TPU v7x, 32 devices: a whole 2x2x4 slice. The times are simulated.
32 devices in a mesh: seq: 8 (over z, core), fsdp: 4 (over y, x).
Axes of the slice: x: 2, y: 2, z: 4, core: 2. Of those that a mesh axis runs over, the one named last changes fastest.
Arguments:
- queries: bfloat16 [4, 1024, 1024], P('fsdp', 'seq'), may hold values from -6 to 6
- keys: bfloat16 [4, 1024, 1024], P('fsdp', 'seq'), may hold values from -6 to 6
- values: bfloat16 [4, 1024, 1024], P('fsdp', 'seq'), may hold values from -6 to 6
- d_out: bfloat16 [4, 1024, 2048], P('fsdp', 'seq'), may hold values from -6 to 6
- w_out: bfloat16 [1024, 2048], P('fsdp'), may hold values from -0.1875 to 0.1875
- pattern: int32 [8, 4], replicated, may hold values from 0 to 7, as said below
- valid: int32 [4, 8], P('fsdp'), may hold values from 2 to 128, as said below
Outputs:
- d_queries: bfloat16 [4, 1024, 1024], P('fsdp', 'seq')
- d_keys: bfloat16 [4, 1024, 1024], P('fsdp', 'seq')
- d_values: bfloat16 [4, 1024, 1024], P('fsdp', 'seq')
Inputs may be any that keep to these rules, and one draw needn't show every extreme that they name: Row b of the pattern, for a query block of shard p, lists the first block of shard p, block b itself, one block of shard p - 1 and one block of shard p + 1; at the first and last shard the missing neighbour's entry repeats the first block of shard p. A block listed twice is attended once. The valid patches of a shard are its first ones; every sample has a shard whose 128 patches are all valid.
All inputs are finite; a program needn't handle non-finite values.
Results may differ from a plain program's by a relative error of at most 0.018.
Values may be sent and summed in bfloat16 or wider, within the bound.
No kernel may reach another device: no remote copies, remote signals or barrier semaphores. Data moves between devices by JAX's collectives and lax.ppermute only.
A program may use at most 64 MiB of HBM per device.

v0:
```python
import jax
import jax.numpy as jnp
from jax import lax
from jax.sharding import PartitionSpec as P

HEADS = 8
HD = 128
BLOCK = 128
BLK_DEV = 1


def with_halo(cells, sides, width):
    for axis, dim in sides:
        count = lax.axis_size(axis)
        ends = count - 1
        head = lax.slice_in_dim(cells, 0, width, axis=dim)
        tail = lax.slice_in_dim(cells, cells.shape[dim] - width, cells.shape[dim], axis=dim)
        cells = jnp.concatenate(
            [
                lax.ppermute(tail, axis, [(i, (i + 1) % count) for i in range(ends)]),
                cells,
                lax.ppermute(head, axis, [((i + 1) % count, i) for i in range(ends)]),
            ],
            axis=dim,
        )
    return cells


def head_split(rows):
    return rows.reshape(rows.shape[0], HEADS, HD)


def allowed_mask(pattern, valid_row, query_shard, key_shard, query_span, key_span, pad_value):
    per_shard = BLK_DEV * BLOCK
    padded = jnp.pad(pattern, ((BLK_DEV, BLK_DEV), (0, 0)), constant_values=pad_value)
    listed_rows = lax.dynamic_slice_in_dim(
        padded, (query_shard + 1) * BLK_DEV, query_span * BLK_DEV, 0
    )
    key_blocks = key_shard * BLK_DEV + jnp.arange(key_span * BLK_DEV, dtype=jnp.int32)
    listed = jnp.any(listed_rows[:, :, None] == key_blocks[None, None, :], axis=1)
    key_pos = jnp.arange(key_span * per_shard, dtype=jnp.int32)
    owner = key_shard + key_pos // per_shard
    shards = jnp.arange(valid_row.shape[0], dtype=jnp.int32)
    owner_count = jnp.sum(
        jnp.where(owner[:, None] == shards[None, :], valid_row[None, :], 0), axis=1
    )
    key_ok = key_pos % per_shard < owner_count
    rows_q = query_span * BLK_DEV
    rows_k = key_span * BLK_DEV
    spread = jnp.broadcast_to(listed[:, None, :, None], (rows_q, BLOCK, rows_k, BLOCK))
    return spread.reshape(rows_q * BLOCK, rows_k * BLOCK) & key_ok[None, :]


def body(queries, keys, values, d_out, w_out, pattern, valid):
    shard = lax.axis_index("seq")
    tok = queries.shape[1]
    width = queries.shape[2]
    valid_row = valid[0]
    pad_value = -(pattern.shape[0] + BLK_DEV + 1)
    scale = HD ** (-0.5)
    cotangent_rows = d_out[0]
    d_attn = jnp.einsum(
        "td,rd->tr",
        cotangent_rows,
        lax.all_gather(w_out, "fsdp", axis=0, tiled=True),
        preferred_element_type=jnp.float32,
    ).astype(jnp.bfloat16)
    band_keys, band_values = (
        with_halo(keys, (("seq", 1),), tok),
        with_halo(values, (("seq", 1),), tok),
    )
    q_heads = head_split(queries[0])
    d_heads = head_split(d_attn)
    k_heads = head_split(band_keys[0])
    v_heads = head_split(band_values[0])
    mask = allowed_mask(pattern, valid_row, shard, shard - 1, 1, 3, pad_value)
    score = jnp.einsum("qhd,khd->hqk", q_heads, k_heads, preferred_element_type=jnp.float32) * scale
    score = jnp.where(mask[None], score, -jnp.inf)
    top = jnp.max(score, axis=2, keepdims=True)
    lse = top + jnp.log(jnp.sum(jnp.exp(score - top), axis=2, keepdims=True))
    prob = jnp.exp(score - lse)
    prob_b = prob.astype(jnp.bfloat16)
    out_rows = jnp.einsum("hqk,khd->hqd", prob_b, v_heads, preferred_element_type=jnp.float32)
    delta = jnp.sum(jnp.transpose(d_heads, (1, 0, 2)) * out_rows, axis=2, keepdims=True)
    d_prob = jnp.einsum("qhd,khd->hqk", d_heads, v_heads, preferred_element_type=jnp.float32)
    d_score = (prob * (d_prob - delta)).astype(jnp.bfloat16)
    d_query = (
        jnp.einsum("hqk,khd->qhd", d_score, k_heads, preferred_element_type=jnp.float32) * scale
    )
    d_query = d_query.reshape(tok, width).astype(jnp.bfloat16)[None]
    lse_rows = jnp.transpose(lse[:, :, 0])[None]
    delta_rows = jnp.transpose(delta[:, :, 0])[None]
    band_queries, band_cotangent = (
        with_halo(queries, (("seq", 1),), tok),
        with_halo(d_attn[None], (("seq", 1),), tok),
    )
    band_lse, band_delta = (
        with_halo(lse_rows, (("seq", 1),), tok),
        with_halo(delta_rows, (("seq", 1),), tok),
    )
    far_q = head_split(band_queries[0])
    far_d = head_split(band_cotangent[0])
    own_k = head_split(keys[0])
    own_v = head_split(values[0])
    mask_keys = allowed_mask(pattern, valid_row, shard - 1, shard, 3, 1, pad_value)
    score_keys = (
        jnp.einsum("qhd,khd->hqk", far_q, own_k, preferred_element_type=jnp.float32) * scale
    )
    score_keys = jnp.where(mask_keys[None], score_keys, -jnp.inf)
    prob_keys = jnp.exp(score_keys - jnp.transpose(band_lse[0])[:, :, None])
    prob_keys_b = prob_keys.astype(jnp.bfloat16)
    d_prob_keys = jnp.einsum("qhd,khd->hqk", far_d, own_v, preferred_element_type=jnp.float32)
    d_score_keys = (prob_keys * (d_prob_keys - jnp.transpose(band_delta[0])[:, :, None])).astype(
        jnp.bfloat16
    )
    key_grad = (
        jnp.einsum("hqk,qhd->khd", d_score_keys, far_q, preferred_element_type=jnp.float32) * scale
    )
    value_grad = jnp.einsum("hqk,qhd->khd", prob_keys_b, far_d, preferred_element_type=jnp.float32)
    key_grad = key_grad.reshape(tok, width)
    value_grad = value_grad.reshape(tok, width)
    return (d_query, key_grad.astype(jnp.bfloat16)[None], value_grad.astype(jnp.bfloat16)[None])


def solution(mesh):
    in_specs = (
        P("fsdp", "seq", None),
        P("fsdp", "seq", None),
        P("fsdp", "seq", None),
        P("fsdp", "seq", None),
        P("fsdp", None),
        P(),
        P("fsdp", None),
    )
    out_specs = (P("fsdp", "seq", None), P("fsdp", "seq", None), P("fsdp", "seq", None))
    return jax.shard_map(body, mesh=mesh, in_specs=in_specs, out_specs=out_specs, check_vma=False)
```

profile of v0, /device:TPU:1, one launch (start us, length us, event | category | flops | bytes accessed | tf_op | source)
XLA Modules:
  0.0 103.1 jit_solution(704263394182010868)
XLA Ops:
  8.0 1.1 %copy.73 = bf16[1,128,1024]{1,2,0:T(8,128)(2,1)S(1)} copy(bf16[1,128,1024]{2,1,0:T(8,128)(2,1)} %param.9) | data formatting | bytes 524288 | tf_op args[2]
  9.1 2.0 %collective-permute-start.3 = (bf16[1,128,1024]{1,2,0:T(8,128)(2,1)S(1)}, bf16[1,128,1024]{1,2,0:T(8,128)(2,1)}, u32[]{:S(2)}, u32[]{:S(2)}) collective-permute-start(bf16[1,128,1024]{1,2,0:T(8,128)(2,1)S(1)} %copy.73), channel_id=1, source_target_pairs={{4,0},{8,4},{12,8},{16,12},{20,16},{24,20},{28,24},{5,1},{9,5},{13... | collective-permute-start | bytes 786440 | tf_op jit(solution)/shard_map/ppermute | solution.py:22
  11.1 4.6 %collective-permute-start.2 = (bf16[1,128,1024]{1,2,0:T(8,128)(2,1)S(1)}, bf16[1,128,1024]{1,2,0:T(8,128)(2,1)}, u32[]{:S(2)}, u32[]{:S(2)}) collective-permute-start(bf16[1,128,1024]{1,2,0:T(8,128)(2,1)S(1)} %copy.73), channel_id=1, source_target_pairs={{0,4},{4,8},{8,12},{12,16},{16,20},{20,24},{24,28},{1,5},{5,9},{9,... | collective-permute-start | bytes 786440 | tf_op jit(solution)/shard_map/ppermute | solution.py:20
  15.8 1.9 %collective-permute-start.1 = (bf16[1,128,1024]{1,2,0:T(8,128)(2,1)S(1)}, bf16[1,128,1024]{1,2,0:T(8,128)(2,1)S(1)}, u32[]{:S(2)}, u32[]{:S(2)}) collective-permute-start(bf16[1,128,1024]{1,2,0:T(8,128)(2,1)S(1)} %copy.68), channel_id=1, source_target_pairs={{4,0},{8,4},{12,8},{16,12},{20,16},{24,20},{28,24},{5,1},{9,5},{13... | collective-permute-start | bytes 786440 | tf_op jit(solution)/shard_map/ppermute | solution.py:22
  17.7 3.6 %collective-permute-start = (bf16[1,128,1024]{1,2,0:T(8,128)(2,1)S(1)}, bf16[1,128,1024]{1,2,0:T(8,128)(2,1)S(1)}, u32[]{:S(2)}, u32[]{:S(2)}) collective-permute-start(bf16[1,128,1024]{1,2,0:T(8,128)(2,1)S(1)} %copy.68), channel_id=1, source_target_pairs={{0,4},{4,8},{8,12},{12,16},{16,20},{20,24},{24,28},{1,5},{5,9},{9,... | collective-permute-start | bytes 786440 | tf_op jit(solution)/shard_map/ppermute | solution.py:20
  21.6 1.9 %collective-permute-start.5 = (bf16[1,128,1024]{1,2,0:T(8,128)(2,1)S(1)}, bf16[1,128,1024]{1,2,0:T(8,128)(2,1)}, u32[]{:S(2)}, u32[]{:S(2)}) collective-permute-start(bf16[1,128,1024]{1,2,0:T(8,128)(2,1)S(1)} %copy.82), channel_id=1, source_target_pairs={{4,0},{8,4},{12,8},{16,12},{20,16},{24,20},{28,24},{5,1},{9,5},{13... | collective-permute-start | bytes 786440 | tf_op jit(solution)/shard_map/ppermute | solution.py:22
  25.2 3.6 %collective-permute-start.4 = (bf16[1,128,1024]{1,2,0:T(8,128)(2,1)S(1)}, bf16[1,128,1024]{1,2,0:T(8,128)(2,1)S(1)}, u32[]{:S(2)}, u32[]{:S(2)}) collective-permute-start(bf16[1,128,1024]{1,2,0:T(8,128)(2,1)S(1)} %copy.82), channel_id=1, source_target_pairs={{0,4},{4,8},{8,12},{12,16},{16,20},{20,24},{24,28},{1,5},{5,9},{9,... | collective-permute-start | bytes 786440 | tf_op jit(solution)/shard_map/ppermute | solution.py:20
  29.8 1.9 %collective-permute-start.7 = (f32[1,128,8]{1,2,0:T(8,128)S(1)}, f32[1,128,8]{1,2,0:T(8,128)S(1)}, u32[]{:S(2)}, u32[]{:S(2)}) collective-permute-start(f32[1,128,8]{1,2,0:T(8,128)S(1)} %bitcast.117), channel_id=1, source_target_pairs={{4,0},{8,4},{12,8},{16,12},{20,16},{24,20},{28,24},{5,1},{9,5},{13... | collective-permute-start | bytes 12296 | tf_op jit(solution)/shard_map/ppermute | solution.py:22
  31.7 3.6 %collective-permute-start.6 = (f32[1,128,8]{1,2,0:T(8,128)S(1)}, f32[1,128,8]{1,2,0:T(8,128)S(1)}, u32[]{:S(2)}, u32[]{:S(2)}) collective-permute-start(f32[1,128,8]{1,2,0:T(8,128)S(1)} %bitcast.118), channel_id=1, source_target_pairs={{0,4},{4,8},{8,12},{12,16},{16,20},{20,24},{24,28},{1,5},{5,9},{9,... | collective-permute-start | bytes 12296 | tf_op jit(solution)/shard_map/ppermute | solution.py:20
  35.4 1.1 %pad_maximum_fusion.2 = bf16[1,384,1024]{1,2,0:T(8,128)(2,1)S(1)} fusion(bf16[1,128,1024]{1,2,0:T(8,128)(2,1)} %collective-permute-done.5, bf16[1,128,1024]{1,2,0:T(8,128)(2,1)S(1)} %copy.82, bf16[1,128,1024]{1,2,0:T(8,128)(2,1)S(1)} %collective-permute-done.4), kind=kLoop, calls=%fused_computation.23 | loop fusion | flops 2359296 | bytes 1572864 | tf_op jit(solution)/shard_map/concatenate | solution.py:18
  36.5 1.6 %fusion.33 = f32[8,384,128]{2,1,0:T(8,128)} fusion(bf16[384,8,128]{0,2,1:T(8,128)(2,1)S(1)} %bitcast.103, bf16[128,8,128]{2,1,0:T(8,128)(2,1)S(1)} %bitcast.106), kind=kOutput, calls=%fused_computation.43 | convolution fusion | flops 100663296 | bytes 2621440 | tf_op jit(solution)/shard_map/qhd,khd->hqk/dot_general | solution.py:107
  38.1 2.0 %pad_maximum_fusion.1 = bf16[1,384,1024]{1,2,0:T(8,128)(2,1)} fusion(bf16[1,128,1024]{1,2,0:T(8,128)(2,1)} %collective-permute-done.3, bf16[1,128,1024]{1,2,0:T(8,128)(2,1)S(1)} %copy.73, bf16[1,128,1024]{1,2,0:T(8,128)(2,1)} %collective-permute-done.2), kind=kLoop, calls=%fused_computation.22 | loop fusion | flops 2359296 | bytes 1572864 | tf_op jit(solution)/shard_map/concatenate | solution.py:18
  40.2 24.6 %all-gather.2.cloned.1.call-done = bf16[1024,2048]{1,0:T(8,128)(2,1)} async-done(((bf16[256,2048]{1,0:T(8,128)(2,1)}), bf16[1024,2048]{1,0:T(8,128)(2,1)}) %all-gather.2.cloned.1.call-update) | async-done | bytes 4194320 | tf_op jit(solution)/shard_map/all_gather | solution.py:65
  64.7 3.7 %convolution_convert_fusion.1 = bf16[128,1024]{1,0:T(8,128)(2,1)S(1)} fusion(bf16[1024,2048]{1,0:T(8,128)(2,1)} %all-gather.2.cloned.1.call-done, bf16[1,128,2048]{2,1,0:T(8,128)(2,1)S(1)} %copy-done), kind=kOutput, calls=%fused_computation.18 | convolution fusion | flops 537001984 | bytes 4980736 | tf_op jit(solution)/shard_map/td,rd->tr/dot_general | solution.py:62
  68.4 2.6 %collective-permute-start.9 = (bf16[1,128,1024]{2,1,0:T(8,128)(2,1)S(1)}, bf16[1,128,1024]{2,1,0:T(8,128)(2,1)}, u32[]{:S(2)}, u32[]{:S(2)}) collective-permute-start(bf16[1,128,1024]{2,1,0:T(8,128)(2,1)S(1)} %bitcast.100), channel_id=1, source_target_pairs={{4,0},{8,4},{12,8},{16,12},{20,16},{24,20},{28,24},{5,1},{9,5},{13... | collective-permute-start | bytes 786440 | tf_op jit(solution)/shard_map/ppermute | solution.py:22
  71.0 3.0 %collective-permute-start.8 = (bf16[1,128,1024]{2,1,0:T(8,128)(2,1)S(1)}, bf16[1,128,1024]{2,1,0:T(8,128)(2,1)}, u32[]{:S(2)}, u32[]{:S(2)}) collective-permute-start(bf16[1,128,1024]{2,1,0:T(8,128)(2,1)S(1)} %bitcast.101), channel_id=1, source_target_pairs={{0,4},{4,8},{8,12},{12,16},{16,20},{20,24},{24,28},{1,5},{5,9},{9,... | collective-permute-start | bytes 786440 | tf_op jit(solution)/shard_map/ppermute | solution.py:20
  74.8 1.1 %copy.78 = bf16[128,8,128]{0,2,1:T(8,128)(2,1)S(1)} copy(bf16[128,8,128]{2,1,0:T(8,128)(2,1)} %bitcast.113) | data formatting | bytes 524288 | tf_op jit(solution)/shard_map/reshape | solution.py:30
  76.0 1.5 %fusion.9 = f32[8,128]{1,0:T(8,128)S(1)} fusion(bf16[384,8,128]{0,2,1:T(8,128)(2,1)} %bitcast.98, f32[8,384,128]{2,1,0:T(8,128)S(1)} %get-tuple-element.16, f32[8,128]{1,0:T(8,128)S(1)} %log_add_fusion, bf16[128,8,128]{0,2,1:T(8,128)(2,1)S(1)} %copy.78), kind=kOutput, calls=%fused_computation.20 | convolution fusion | flops 101841920 | bytes 2629632 | tf_op jit(solution)/shard_map/hqk,khd->hqd/dot_general | solution.py:83
  77.5 2.0 %collective-permute-start.11 = (f32[1,128,8]{1,2,0:T(8,128)S(1)}, f32[1,128,8]{1,2,0:T(8,128)S(1)}, u32[]{:S(2)}, u32[]{:S(2)}) collective-permute-start(f32[1,128,8]{1,2,0:T(8,128)S(1)} %bitcast.120), channel_id=1, source_target_pairs={{4,0},{8,4},{12,8},{16,12},{20,16},{24,20},{28,24},{5,1},{9,5},{13... | collective-permute-start | bytes 12296 | tf_op jit(solution)/shard_map/ppermute | solution.py:22
  79.5 3.6 %collective-permute-start.10 = (f32[1,128,8]{1,2,0:T(8,128)S(1)}, f32[1,128,8]{1,2,0:T(8,128)S(1)}, u32[]{:S(2)}, u32[]{:S(2)}) collective-permute-start(f32[1,128,8]{1,2,0:T(8,128)S(1)} %bitcast.121), channel_id=1, source_target_pairs={{0,4},{4,8},{8,12},{12,16},{16,20},{20,24},{24,28},{1,5},{5,9},{9,... | collective-permute-start | bytes 12296 | tf_op jit(solution)/shard_map/ppermute | solution.py:20
  83.1 1.9 %fusion.7 = bf16[8,128,128]{2,1,0:T(8,128)(2,1)S(1)} fusion(bf16[384,8,128]{0,2,1:T(8,128)(2,1)S(1)} %bitcast.97, bf16[384,8,128]{0,2,1:T(8,128)(2,1)} %bitcast.99, f32[8,384,128]{2,1,0:T(8,128)S(1)} %get-tuple-element.16, f32[8,128]{1,0:T(8,128)S(1)} %fusion.9, f32[8,128]{1,0:T(8,128)S(1)} %log_add_fusion, bf16[128,1024]{1,0:T(8,128)(2,1)S(1)} %convolution_convert_fusion.1), kind=kOutput, calls=%fused_computation.16 | convolution fusion | flops 203161600 | bytes 3678208 | tf_op jit(solution)/shard_map/hqk,khd->qhd/dot_general | solution.py:88
  85.8 1.0 copy.107
  90.2 2.1 %convolution_convert_fusion = bf16[8,128,128]{2,1,0:T(8,128)(2,1)S(1)} fusion(bf16[384,8,128]{2,0,1:T(8,128)(2,1)} %copy_dynamic-update-slice_fusion, f32[8,384,128]{2,1,0:T(8,128)S(1)} %copy-done.3, f32[8,384]{1,0:T(8,128)S(1)} %maximum_bitcast_fusion, pred[384,128]{1,0:T(8,128)(4,1)S(1)} %broadcast_and_fusion), kind=kOutput, calls=%fused_computation.17 | convolution fusion | flops 102367232 | bytes 2682880 | tf_op jit(solution)/shard_map/hqk,qhd->khd/dot_general | solution.py:119
  93.2 2.2 %fusion.6 = bf16[8,128,128]{2,1,0:T(8,128)(2,1)S(1)} fusion(bf16[384,8,128]{0,2,1:T(8,128)(2,1)S(1)} %bitcast.104, f32[8,384,128]{2,1,0:T(8,128)S(1)} %copy-done.3, f32[8,384]{1,0:T(8,128)S(1)} %maximum_bitcast_fusion.1, f32[8,384]{1,0:T(8,128)S(1)} %maximum_bitcast_fusion, pred[384,128]{1,0:T(8,128)(4,1)S(1)} %broadcast_and_fusion, ...), kind=kOutput, calls=%fused_computation.15 | convolution fusion | flops 203948032 | bytes 3743744 | tf_op jit(solution)/shard_map/hqk,qhd->khd/dot_general | solution.py:117
  (65 shorter events, 10.3 us)
Async XLA Ops:
  7.2 57.6 %copy-start = (bf16[1,128,2048]{2,1,0:T(8,128)(2,1)S(1)}, bf16[1,128,2048]{2,1,0:T(8,128)(2,1)}, u32[]{:S(2)}) copy-start(bf16[1,128,2048]{2,1,0:T(8,128)(2,1)} %param.10) | copy-start | bytes 1572868
  7.2 17.1 %copy-start.4 = (bf16[1,128,1024]{2,1,0:T(8,128)(2,1)S(1)}, bf16[1,128,1024]{2,1,0:T(8,128)(2,1)}, u32[]{:S(2)}) copy-start(bf16[1,128,1024]{2,1,0:T(8,128)(2,1)} %param.9) | copy-start | bytes 786436
  7.2 8.4 %copy-start.5 = (bf16[1,128,1024]{2,1,0:T(8,128)(2,1)S(1)}, bf16[1,128,1024]{2,1,0:T(8,128)(2,1)}, u32[]{:S(2)}) copy-start(bf16[1,128,1024]{2,1,0:T(8,128)(2,1)} %param.8) | copy-start | bytes 786436
  7.2 14.2 %copy-start.6 = (bf16[1,128,1024]{2,1,0:T(8,128)(2,1)S(1)}, bf16[1,128,1024]{2,1,0:T(8,128)(2,1)}, u32[]{:S(2)}) copy-start(bf16[1,128,1024]{2,1,0:T(8,128)(2,1)} %param.7) | copy-start | bytes 786436
  7.2 16.3 %copy-start.8 = (s32[8,4]{0,1:T(4,128)S(1)}, s32[8,4]{0,1:T(4,128)}, u32[]{:S(2)}) copy-start(s32[8,4]{0,1:T(4,128)} %param.12) | copy-start | bytes 388
  7.2 16.6 %copy-start.9 = (s32[1,8]{1,0:T(1,128)S(1)}, s32[1,8]{1,0:T(1,128)}, u32[]{:S(2)}) copy-start(s32[1,8]{1,0:T(1,128)} %param.13) | copy-start | bytes 100
  7.2 57.5 %all-gather.2.cloned.1.call-start = ((), (), s32[]{:S(2)}) async-start(), calls=%async_computation | async-start | bytes 5242880 | tf_op jit(solution)/shard_map/all_gather | solution.py:65
  9.1 29.0 %collective-permute-start.3 = (bf16[1,128,1024]{1,2,0:T(8,128)(2,1)S(1)}, bf16[1,128,1024]{1,2,0:T(8,128)(2,1)}, u32[]{:S(2)}, u32[]{:S(2)}) collective-permute-start(bf16[1,128,1024]{1,2,0:T(8,128)(2,1)S(1)} %copy.73), channel_id=1, source_target_pairs={{4,0},{8,4},{12,8},{16,12},{20,16},{24,20},{28,24},{5,1},{9,5},{13... | collective-permute-start | bytes 786440 | tf_op jit(solution)/shard_map/ppermute | solution.py:22
  11.1 27.0 %collective-permute-start.2 = (bf16[1,128,1024]{1,2,0:T(8,128)(2,1)S(1)}, bf16[1,128,1024]{1,2,0:T(8,128)(2,1)}, u32[]{:S(2)}, u32[]{:S(2)}) collective-permute-start(bf16[1,128,1024]{1,2,0:T(8,128)(2,1)S(1)} %copy.73), channel_id=1, source_target_pairs={{0,4},{4,8},{8,12},{12,16},{16,20},{20,24},{24,28},{1,5},{5,9},{9,... | collective-permute-start | bytes 786440 | tf_op jit(solution)/shard_map/ppermute | solution.py:20
  15.8 9.4 %collective-permute-start.1 = (bf16[1,128,1024]{1,2,0:T(8,128)(2,1)S(1)}, bf16[1,128,1024]{1,2,0:T(8,128)(2,1)S(1)}, u32[]{:S(2)}, u32[]{:S(2)}) collective-permute-start(bf16[1,128,1024]{1,2,0:T(8,128)(2,1)S(1)} %copy.68), channel_id=1, source_target_pairs={{4,0},{8,4},{12,8},{16,12},{20,16},{24,20},{28,24},{5,1},{9,5},{13... | collective-permute-start | bytes 786440 | tf_op jit(solution)/shard_map/ppermute | solution.py:22
  17.7 11.2 %collective-permute-start = (bf16[1,128,1024]{1,2,0:T(8,128)(2,1)S(1)}, bf16[1,128,1024]{1,2,0:T(8,128)(2,1)S(1)}, u32[]{:S(2)}, u32[]{:S(2)}) collective-permute-start(bf16[1,128,1024]{1,2,0:T(8,128)(2,1)S(1)} %copy.68), channel_id=1, source_target_pairs={{0,4},{4,8},{8,12},{12,16},{16,20},{20,24},{24,28},{1,5},{5,9},{9,... | collective-permute-start | bytes 786440 | tf_op jit(solution)/shard_map/ppermute | solution.py:20
  21.6 10.1 %collective-permute-start.5 = (bf16[1,128,1024]{1,2,0:T(8,128)(2,1)S(1)}, bf16[1,128,1024]{1,2,0:T(8,128)(2,1)}, u32[]{:S(2)}, u32[]{:S(2)}) collective-permute-start(bf16[1,128,1024]{1,2,0:T(8,128)(2,1)S(1)} %copy.82), channel_id=1, source_target_pairs={{4,0},{8,4},{12,8},{16,12},{20,16},{24,20},{28,24},{5,1},{9,5},{13... | collective-permute-start | bytes 786440 | tf_op jit(solution)/shard_map/ppermute | solution.py:22
  25.2 10.1 %collective-permute-start.4 = (bf16[1,128,1024]{1,2,0:T(8,128)(2,1)S(1)}, bf16[1,128,1024]{1,2,0:T(8,128)(2,1)S(1)}, u32[]{:S(2)}, u32[]{:S(2)}) collective-permute-start(bf16[1,128,1024]{1,2,0:T(8,128)(2,1)S(1)} %copy.82), channel_id=1, source_target_pairs={{0,4},{4,8},{8,12},{12,16},{16,20},{20,24},{24,28},{1,5},{5,9},{9,... | collective-permute-start | bytes 786440 | tf_op jit(solution)/shard_map/ppermute | solution.py:20
  29.8 10.4 %collective-permute-start.7 = (f32[1,128,8]{1,2,0:T(8,128)S(1)}, f32[1,128,8]{1,2,0:T(8,128)S(1)}, u32[]{:S(2)}, u32[]{:S(2)}) collective-permute-start(f32[1,128,8]{1,2,0:T(8,128)S(1)} %bitcast.117), channel_id=1, source_target_pairs={{4,0},{8,4},{12,8},{16,12},{20,16},{24,20},{28,24},{5,1},{9,5},{13... | collective-permute-start | bytes 12296 | tf_op jit(solution)/shard_map/ppermute | solution.py:22
  31.7 8.4 %collective-permute-start.6 = (f32[1,128,8]{1,2,0:T(8,128)S(1)}, f32[1,128,8]{1,2,0:T(8,128)S(1)}, u32[]{:S(2)}, u32[]{:S(2)}) collective-permute-start(f32[1,128,8]{1,2,0:T(8,128)S(1)} %bitcast.118), channel_id=1, source_target_pairs={{0,4},{4,8},{8,12},{12,16},{16,20},{20,24},{24,28},{1,5},{5,9},{9,... | collective-permute-start | bytes 12296 | tf_op jit(solution)/shard_map/ppermute | solution.py:20
  36.4 3.7 %copy-start.1 = (bf16[1,384,1024]{1,2,0:T(8,128)(2,1)}, bf16[1,384,1024]{1,2,0:T(8,128)(2,1)S(1)}, u32[]{:S(2)}) copy-start(bf16[1,384,1024]{1,2,0:T(8,128)(2,1)S(1)} %pad_maximum_fusion.2) | copy-start | bytes 2359300
  68.4 17.4 %collective-permute-start.9 = (bf16[1,128,1024]{2,1,0:T(8,128)(2,1)S(1)}, bf16[1,128,1024]{2,1,0:T(8,128)(2,1)}, u32[]{:S(2)}, u32[]{:S(2)}) collective-permute-start(bf16[1,128,1024]{2,1,0:T(8,128)(2,1)S(1)} %bitcast.100), channel_id=1, source_target_pairs={{4,0},{8,4},{12,8},{16,12},{20,16},{24,20},{28,24},{5,1},{9,5},{13... | collective-permute-start | bytes 786440 | tf_op jit(solution)/shard_map/ppermute | solution.py:22
  71.0 15.8 %collective-permute-start.8 = (bf16[1,128,1024]{2,1,0:T(8,128)(2,1)S(1)}, bf16[1,128,1024]{2,1,0:T(8,128)(2,1)}, u32[]{:S(2)}, u32[]{:S(2)}) collective-permute-start(bf16[1,128,1024]{2,1,0:T(8,128)(2,1)S(1)} %bitcast.101), channel_id=1, source_target_pairs={{0,4},{4,8},{8,12},{12,16},{16,20},{20,24},{24,28},{1,5},{5,9},{9,... | collective-permute-start | bytes 786440 | tf_op jit(solution)/shard_map/ppermute | solution.py:20
  77.5 8.3 %collective-permute-start.11 = (f32[1,128,8]{1,2,0:T(8,128)S(1)}, f32[1,128,8]{1,2,0:T(8,128)S(1)}, u32[]{:S(2)}, u32[]{:S(2)}) collective-permute-start(f32[1,128,8]{1,2,0:T(8,128)S(1)} %bitcast.120), channel_id=1, source_target_pairs={{4,0},{8,4},{12,8},{16,12},{20,16},{24,20},{28,24},{5,1},{9,5},{13... | collective-permute-start | bytes 12296 | tf_op jit(solution)/shard_map/ppermute | solution.py:22
  79.5 6.3 %collective-permute-start.10 = (f32[1,128,8]{1,2,0:T(8,128)S(1)}, f32[1,128,8]{1,2,0:T(8,128)S(1)}, u32[]{:S(2)}, u32[]{:S(2)}) collective-permute-start(f32[1,128,8]{1,2,0:T(8,128)S(1)} %bitcast.121), channel_id=1, source_target_pairs={{0,4},{4,8},{8,12},{12,16},{16,20},{20,24},{24,28},{1,5},{5,9},{9,... | collective-permute-start | bytes 12296 | tf_op jit(solution)/shard_map/ppermute | solution.py:20
  85.0 5.2 %copy-start.3 = (f32[8,384,128]{2,1,0:T(8,128)S(1)}, f32[8,384,128]{2,1,0:T(8,128)}, u32[]{:S(2)}) copy-start(f32[8,384,128]{2,1,0:T(8,128)} %fusion.33) | copy-start | bytes 4718596
  90.2 3.0 %copy-start.2 = (bf16[1,384,1024]{1,2,0:T(8,128)(2,1)S(1)}, bf16[1,384,1024]{1,2,0:T(8,128)(2,1)}, u32[]{:S(2)}) copy-start(bf16[1,384,1024]{1,2,0:T(8,128)(2,1)} %copy-done.1) | copy-start | bytes 2359300
  90.2 3.0 %copy-start.7 = (bf16[16,8,8,128]{3,2,1,0:T(8,128)(2,1)S(1)}, bf16[16,8,8,128]{3,2,1,0:T(8,128)(2,1)}, u32[]{:S(2)}) copy-start(bf16[16,8,8,128]{3,2,1,0:T(8,128)(2,1)} %copy.108) | copy-start | bytes 786436
Sparse Core Ops, SparseCore 0:
  9.9 54.7 all-gather.1
where the time goes:
time: 104 us; the launch traced here: 103 us
  starting transfers between devices  34.4 us (33%)
  waiting for transfers between devices  25.3 us (24%)
  between operations  14.4 us (14%)
  matrix products  13.6 us (13%)
  local copies, waits for them, and re-layouts  11.4 us (11%)
  other arithmetic  4.01 us (4%)
    all_gather x1, waiting for transfers between devices, body(): lax.all_gather(w_out, 'fsdp', axis=0, tiled=True)  24.6 us
    ppermute x6, starting transfers between devices, with_halo(): lax.ppermute(tail, axis, [(i, (i + 1) % count) for i in range(ends)])  22.1 us
    ppermute x6, starting transfers between devices, with_halo(): lax.ppermute(head, axis, [((i + 1) % count, i) for i in range(ends)])  12.3 us
    unnamed x34, local copies, waits for them, and re-layouts  9.16 us
    dot_general x1, matrix products, body(): jnp.einsum('td,rd->tr', cotangent_rows, lax.all_gather(w_out, 'fsdp', axi...  3.7 us
    concatenate x3, other arithmetic, with_halo(): jnp.concatenate([lax.ppermute(tail, axis, [(i, (i + 1) % count) for i in...  3.21 us
    dot_general x1, matrix products, body(): jnp.einsum('hqk,qhd->khd', d_score_keys, far_q, preferred_element_type=jn...  2.25 us
    dot_general x1, matrix products, body(): jnp.einsum('hqk,qhd->khd', prob_keys_b, far_d, preferred_element_type=jnp...  2.13 us
  transfers between devices with their start and end apart: 13, of which 1 were waited for; matrix products, arithmetic and copies ran while one was open for 15% of the time, Pallas kernels for 0%

commit v1 on v0

v1 whole, which is shorter than its diff:
```python
import functools

import jax
import jax.numpy as jnp
from jax import lax
from jax.experimental import pallas as pl
from jax.experimental.pallas import tpu as pltpu
from jax.sharding import PartitionSpec as P

HD = 128
F32 = jnp.float32
BF16 = jnp.bfloat16
NT = (((1,), (1,)), ((), ()))
NN = (((1,), (0,)), ((), ()))
TN = (((0,), (0,)), ((), ()))


def dot(a, b, dims):
    return lax.dot_general(a, b, dims, preferred_element_type=F32)


def swap(n, offset):
    pairs = []
    for i in range(offset, n - 1, 2):
        pairs += [(i, i + 1), (i + 1, i)]
    return pairs


def key_limits(pat_ref, val_ref):
    shard = lax.axis_index("seq")
    count = val_ref.shape[1]
    odd = lax.rem(shard, 2)
    blocks = (shard, shard + 1 - 2 * odd, shard - 1 + 2 * odd)
    limits = []
    for block in blocks:
        listed = pat_ref[shard, 0] == block
        for entry in range(1, pat_ref.shape[1]):
            listed = jnp.logical_or(listed, pat_ref[shard, entry] == block)
        inside = jnp.logical_and(block >= 0, block < count)
        held = val_ref[0, jnp.clip(block, 0, count - 1)]
        limits.append(jnp.where(jnp.logical_and(listed, inside), held, 0))
    return limits


def attention_kernel(
    plan, head_ref, pat_ref, val_ref, q_ref, k_ref, v_ref, core_ref, far_ref, dy_ref, *refs
):
    w_refs = refs[: len(plan)]
    dq_ref, own_ref, to_core_ref, to_far_ref = refs[len(plan) :]
    scale = HD ** (-0.5)
    rows = lax.broadcasted_iota(jnp.int32, (HD, HD), 0)
    open_keys = jnp.concatenate([rows < limit for limit in key_limits(pat_ref, val_ref)], axis=0)
    index = 0
    for w_ref, heads in zip(w_refs, plan):
        for head in range(heads):
            cols = pl.ds(pl.multiple_of(head_ref[index, 0] * HD, HD), HD)
            dest = pl.ds(pl.multiple_of(head_ref[index, 1] * HD, HD), HD)
            index += 1
            d = dot(dy_ref[0], w_ref[head * HD : (head + 1) * HD, :], NT).astype(BF16)
            q = q_ref[0, :, cols]
            k = jnp.concatenate([k_ref[0, :, cols], core_ref[0, :, cols], far_ref[0, :, cols]], 0)
            v = jnp.concatenate([v_ref[0, :, cols], core_ref[1, :, cols], far_ref[1, :, cols]], 0)
            score = jnp.where(open_keys, dot(k, q, NT) * scale, -jnp.inf)
            top = jnp.max(score, axis=0, keepdims=True)
            raised = jnp.exp(score - top)
            prob = raised * (1.0 / jnp.sum(raised, axis=0, keepdims=True))
            prob_b = prob.astype(BF16)
            d_prob = dot(v, d, NT)
            delta = jnp.sum(prob_b.astype(F32) * d_prob, axis=0, keepdims=True)
            d_score = (prob * (d_prob - delta)).astype(BF16)
            dq_ref[:, dest] = (dot(d_score, k, TN) * scale).astype(BF16)
            dk = dot(d_score, q, NN) * scale
            dv = dot(prob_b, d, NN)
            own_ref[0, :, dest] = dk[:HD]
            own_ref[1, :, dest] = dv[:HD]
            to_core_ref[0, :, dest] = dk[HD : 2 * HD].astype(BF16)
            to_core_ref[1, :, dest] = dv[HD : 2 * HD].astype(BF16)
            to_far_ref[0, :, dest] = dk[2 * HD :].astype(BF16)
            to_far_ref[1, :, dest] = dv[2 * HD :].astype(BF16)


def attention(weights, table, pattern, valid, q, k, v, kv_core, kv_far, d_out):
    plan = tuple(w.shape[0] // HD for w in weights)
    heads = sum(plan)
    tok = q.shape[1]
    smem = pl.BlockSpec(memory_space=pltpu.SMEM)
    vmem = pl.BlockSpec(memory_space=pltpu.VMEM)
    width = heads * HD
    return pl.pallas_call(
        functools.partial(attention_kernel, plan),
        out_shape=(
            jax.ShapeDtypeStruct((tok, width), BF16),
            jax.ShapeDtypeStruct((2, tok, width), F32),
            jax.ShapeDtypeStruct((2, tok, width), BF16),
            jax.ShapeDtypeStruct((2, tok, width), BF16),
        ),
        in_specs=[smem] * 3 + [vmem] * (6 + len(weights)),
        out_specs=(vmem,) * 4,
        cost_estimate=pl.CostEstimate(
            flops=heads * 2 * tok * HD * (d_out.shape[2] + 15 * HD),
            bytes_accessed=heads * 800_000,
            transcendentals=heads * 3 * tok * HD,
        ),
        compiler_params=pltpu.CompilerParams(vmem_limit_bytes=32 * 2**20),
        name="attention",
    )(table, pattern, valid, q, k, v, kv_core, kv_far, d_out, *weights)


def finish_kernel(plan, table_ref, *refs):
    ins, (dq_ref, dk_ref, dv_ref) = refs[:-3], refs[-3:]
    index = 0
    for part, heads in enumerate(plan):
        dq, own, core, far = ins[4 * part : 4 * part + 4]
        for head in range(heads):
            dest = pl.ds(pl.multiple_of(table_ref[index] * HD, HD), HD)
            index += 1
            cols = slice(head * HD, (head + 1) * HD)
            dq_ref[0, :, dest] = dq[:, cols]
            for half, out_ref in enumerate((dk_ref, dv_ref)):
                total = own[half, :, cols] + core[half, :, cols].astype(F32)
                out_ref[0, :, dest] = (total + far[half, :, cols].astype(F32)).astype(BF16)


def finish(parts, table, shape):
    plan = tuple(part[0].shape[1] // HD for part in parts)
    vmem = pl.BlockSpec(memory_space=pltpu.VMEM)
    return pl.pallas_call(
        functools.partial(finish_kernel, plan),
        out_shape=(jax.ShapeDtypeStruct(shape, BF16),) * 3,
        in_specs=[pl.BlockSpec(memory_space=pltpu.SMEM)] + [vmem] * (4 * len(parts)),
        out_specs=(vmem,) * 3,
        compiler_params=pltpu.CompilerParams(vmem_limit_bytes=32 * 2**20),
        name="finish",
    )(table, *[x for part in parts for x in part])


def body(queries, keys, values, d_out, w_out, pattern, valid):
    n_seq, n_fsdp = lax.axis_size("seq"), lax.axis_size("fsdp")
    shard, group = lax.axis_index("seq"), lax.axis_index("fsdp")
    core = lax.rem(shard, 2)
    heads = queries.shape[2] // HD
    near = functools.partial(lax.ppermute, axis_name="seq", perm=swap(n_seq, 0))
    far = functools.partial(lax.ppermute, axis_name="seq", perm=swap(n_seq, 1))

    def flip(x, bit):
        return lax.ppermute(x, "fsdp", [(i, i ^ bit) for i in range(n_fsdp)])

    pipelined = n_fsdp == 4 and w_out.shape[0] == 2 * HD
    if pipelined:
        mine = lax.dynamic_slice_in_dim(w_out, core * HD, HD, 0)
        from_x = flip(mine, 1)
        from_y = flip(mine, 2)

    kv = jnp.concatenate([keys, values], axis=0)
    kv_core, kv_far = near(kv), far(kv)
    run = functools.partial(
        attention,
        pattern=pattern,
        valid=valid,
        q=queries,
        k=keys,
        v=values,
        kv_core=kv_core,
        kv_far=kv_far,
        d_out=d_out,
    )

    def part(weights, table):
        dq, own, to_core, to_far = run(weights, table)
        return dq, own, near(to_core), far(to_far)

    if pipelined:
        half = HD // 2
        diag = jnp.concatenate([flip(from_y[:half], 1), flip(from_x[half:], 2)], axis=0)
        g0, g1, g2, g3 = (2 * (group ^ bit) for bit in range(4))
        pair = lambda g, at: [[g + core, at + core], [g + 1 - core, at + 1 - core]]
        table = lambda rows: jnp.array(rows, jnp.int32)
        parts = [
            part([w_out], jnp.stack([jnp.stack([g0, 0 * g0]), jnp.stack([g0 + 1, 0 * g0 + 1])])),
            part(
                [from_x, near(from_x), from_y, near(from_y)],
                jnp.stack([jnp.stack(r) for r in pair(g1, 0) + pair(g2, 2)]),
            ),
            part([diag, near(diag)], jnp.stack([jnp.stack(r) for r in pair(g3, 0)])),
        ]
        places = jnp.stack([g0, g0 + 1, g1, g1 + 1, g2, g2 + 1, g3, g3 + 1])
    else:
        every = jnp.arange(heads, dtype=jnp.int32)
        full = lax.all_gather(w_out, "fsdp", axis=0, tiled=True)
        parts = [part([full], jnp.stack([every, every], axis=1))]
        places = every
    return finish(parts, places.astype(jnp.int32), queries.shape)


def solution(mesh):
    rows = P("fsdp", "seq", None)
    in_specs = (rows, rows, rows, rows, P("fsdp", None), P(), P("fsdp", None))
    return jax.shard_map(
        body, mesh=mesh, in_specs=in_specs, out_specs=(rows,) * 3, check_vma=False
    )
```

time: 104 us -> 66.2 us (0.64)
  waiting for transfers between devices: 25.3 us -> 8.33 us
  Pallas kernels: 0 us -> 14.2 us
  matrix products: 13.6 us -> 0 us
  between operations: 14.4 us -> 0.85 us
  starting transfers between devices: 34.4 us -> 26.1 us
  local copies, waits for them, and re-layouts: 11.4 us -> 15.8 us
  other arithmetic: 4.01 us -> 0.4 us
    all_gather x1 -> x0, waiting for transfers between devices: 24.6 us -> none  [body(): lax.all_gather(w_out, 'fsdp', axis=0, tiled=True)]
    pallas_call x0 -> x4, Pallas kernels: none -> 14.2 us  [the longest x3 12.1 us: attention(): pl.pallas_call(functools.partial(attention_kernel, plan), out_shape=(jax....]
    dot_general x7 -> x0, matrix products: 13.6 us -> none  [the longest x1 3.7 us: body(): jnp.einsum('td,rd->tr', cotangent_rows, lax.all_gather(w_out, 'fsdp', axi...]
    ppermute x12 -> x15, waiting for transfers between devices: 0.03 us -> 8.33 us  [the longest x4 5.53 us: flip(): return lax.ppermute(x, 'fsdp', [(i, i ^ bit) for i in range(n_fsdp)])]
    ppermute x12 -> x15, starting transfers between devices: 34.4 us -> 26.1 us  [the longest x6 9.78 us: part(): return (dq, own, near(to_core), far(to_far))]
    concatenate x3 -> x0, other arithmetic: 3.21 us -> none  [with_halo(): jnp.concatenate([lax.ppermute(tail, axis, [(i, (i + 1) % count) for i in...]
    slice x0 -> x2, local copies, waits for them, and re-layouts: none -> 2.44 us  [the longest x1 1.67 us: body(): from_x[half:]]
    dynamic_slice x1, local copies, waits for them, and re-layouts: 0.19 us -> 1.93 us  [body(): mine = lax.dynamic_slice_in_dim(w_out, core * HD, HD, 0)]
  transfers between devices with their start and end apart: 13 -> 15, of which waited for: 1 -> 3; matrix products, arithmetic and copies ran while one was open for 15% -> 10% of each run, Pallas kernels for 0% -> 18%
where the time goes in v1:
time: 66.2 us; the launch traced here: 65.7 us
  starting transfers between devices  26.1 us (39%)
  local copies, waits for them, and re-layouts  15.8 us (24%)
  Pallas kernels  14.2 us (21%)
  waiting for transfers between devices  8.33 us (13%)
  between operations  0.85 us (1%)
    pallas_call x3, Pallas kernels, attention(): pl.pallas_call(functools.partial(attention_kernel, plan), out_shape=(jax....  12.1 us
    ppermute x6, starting transfers between devices, part(): return (dq, own, near(to_core), far(to_far))  9.78 us
    unnamed x41, local copies, waits for them, and re-layouts  8.96 us
    ppermute x4, starting transfers between devices, flip(): return lax.ppermute(x, 'fsdp', [(i, i ^ bit) for i in range(n_fsdp)])  5.64 us
    ppermute x4, waiting for transfers between devices, flip(): return lax.ppermute(x, 'fsdp', [(i, i ^ bit) for i in range(n_fsdp)])  5.53 us
    ppermute x2, starting transfers between devices, body(): kv_core, kv_far = (near(kv), far(kv))  4.38 us
    ppermute x6, waiting for transfers between devices, part(): return (dq, own, near(to_core), far(to_far))  2.78 us
    ppermute x1, starting transfers between devices, body(): near(diag)  2.29 us
  transfers between devices with their start and end apart: 15, of which 3 were waited for; matrix products, arithmetic and copies ran while one was open for 10% of the time, Pallas kernels for 18%

profile of v1, /device:TPU:1, one launch (start us, length us, event | category | flops | bytes accessed | tf_op | source)
XLA Modules:
  0.0 65.7 jit_solution(17313309604987147584)
XLA Ops:
  0.7 1.9 %constant_dynamic-slice_fusion = bf16[128,2048]{1,0:T(8,128)(2,1)} fusion(bf16[256,2048]{1,0:T(8,128)(2,1)} %refs_0_.1, s32[]{:T(128)S(6)} %select_n.3), kind=kLoop, calls=%fused_computation.15 | loop fusion | bytes 1048580 | tf_op jit(solution)/shard_map/dynamic_slice | solution.py:150
  2.6 2.1 %collective-permute-start.6 = (bf16[128,2048]{1,0:T(8,128)(2,1)}, bf16[128,2048]{1,0:T(8,128)(2,1)S(1)}, u32[]{:S(2)}, u32[]{:S(2)}) collective-permute-start(bf16[128,2048]{1,0:T(8,128)(2,1)} %constant_dynamic-slice_fusion), channel_id=1, source_target_pairs={{0,2},{1,3},{2,0},{3,1},{4,6},{5,7},{6,4},{7,5},{8,10},{9,11},{10,... | collective-permute-start | bytes 1572872 | tf_op jit(solution)/shard_map/ppermute | solution.py:146
  4.7 1.2 %collective-permute-start.4 = (bf16[128,2048]{1,0:T(8,128)(2,1)}, bf16[128,2048]{1,0:T(8,128)(2,1)}, u32[]{:S(2)}, u32[]{:S(2)}) collective-permute-start(bf16[128,2048]{1,0:T(8,128)(2,1)} %constant_dynamic-slice_fusion), channel_id=1, source_target_pairs={{0,1},{1,0},{2,3},{3,2},{4,5},{5,4},{6,7},{7,6},{8,9},{9,8},{10,11... | collective-permute-start | bytes 1572872 | tf_op jit(solution)/shard_map/ppermute | solution.py:146
  7.3 4.3 %collective-permute-start.1 = (bf16[2,128,1024]{2,1,0:T(8,128)(2,1)}, bf16[2,128,1024]{2,1,0:T(8,128)(2,1)S(1)}, u32[]{:S(2)}, u32[]{:S(2)}) collective-permute-start(bf16[2,128,1024]{2,1,0:T(8,128)(2,1)} %constant_dynamic-update-slice_fusion), channel_id=1, source_target_pairs={{4,8},{8,4},{12,16},{16,12},{20,24},{24,20},{5,9},{9,5},{13,17},{1... | collective-permute-start | bytes 1572872 | tf_op jit(solution)/shard_map/ppermute | solution.py:155
  11.7 4.9 %collective-permute-done.6.refs_2_ = bf16[128,2048]{1,0:T(8,128)(2,1)S(1)} collective-permute-done((bf16[128,2048]{1,0:T(8,128)(2,1)}, bf16[128,2048]{1,0:T(8,128)(2,1)S(1)}, u32[]{:S(2)}, u32[]{:S(2)}) %collective-permute-start.6) | collective-permute-done | bytes 524320 | tf_op jit(solution)/shard_map/ppermute | solution.py:146
  17.4 1.1 %collective-permute-start.10 = (bf16[64,2048]{1,0:T(8,128)(2,1)}, bf16[64,2048]{1,0:T(8,128)(2,1)S(1)}, u32[]{:S(2)}, u32[]{:S(2)}) collective-permute-start(bf16[64,2048]{1,0:T(8,128)(2,1)} %slice.8), channel_id=1, source_target_pairs={{0,1},{1,0},{2,3},{3,2},{4,5},{5,4},{6,7},{7,6},{8,9},{9,8},{10,11... | collective-permute-start | bytes 786440 | tf_op jit(solution)/shard_map/ppermute | solution.py:146
  18.7 1.7 %slice.9 = bf16[64,2048]{1,0:T(8,128)(2,1)} slice(bf16[128,2048]{1,0:T(8,128)(2,1)} %collective-permute-done.4.refs_0_), slice={[64:128], [0:2048]} | slice | bytes 524288 | tf_op jit(solution)/shard_map/slice | solution.py:174
  20.3 1.2 %collective-permute-start.11 = (bf16[64,2048]{1,0:T(8,128)(2,1)}, bf16[64,2048]{1,0:T(8,128)(2,1)}, u32[]{:S(2)}, u32[]{:S(2)}) collective-permute-start(bf16[64,2048]{1,0:T(8,128)(2,1)} %slice.9), channel_id=1, source_target_pairs={{0,2},{1,3},{2,0},{3,1},{4,6},{5,7},{6,4},{7,5},{8,10},{9,11},{10,... | collective-permute-start | bytes 786440 | tf_op jit(solution)/shard_map/ppermute | solution.py:146
  21.6 2.0 %collective-permute-start.7 = (bf16[128,2048]{1,0:T(8,128)(2,1)}, bf16[128,2048]{1,0:T(8,128)(2,1)}, u32[]{:S(2)}, u32[]{:S(2)}) collective-permute-start(bf16[128,2048]{1,0:T(8,128)(2,1)} %copy-done.5), channel_id=1, source_target_pairs={{0,4},{4,0},{8,12},{12,8},{16,20},{20,16},{24,28},{28,24},{1,5},{5... | collective-permute-start | bytes 1572872 | tf_op jit(solution)/shard_map/ppermute | solution.py:181
  24.3 2.0 %collective-permute-start.5 = (bf16[128,2048]{1,0:T(8,128)(2,1)}, bf16[128,2048]{1,0:T(8,128)(2,1)}, u32[]{:S(2)}, u32[]{:S(2)}) collective-permute-start(bf16[128,2048]{1,0:T(8,128)(2,1)} %collective-permute-done.4.refs_0_), channel_id=1, source_target_pairs={{0,4},{4,0},{8,12},{12,8},{16,20},{20,16},{24,28},{28,24},{1,5},{5... | collective-permute-start | bytes 1572872 | tf_op jit(solution)/shard_map/ppermute | solution.py:181
  27.0 1.7 %constant_dynamic-update-slice_fusion.2.refs_0_ = bf16[128,2048]{1,0:T(8,128)(2,1)} fusion(bf16[128,2048]{1,0:T(8,128)(2,1)} %constant_dynamic-update-slice_fusion.3, bf16[64,2048]{1,0:T(8,128)(2,1)} %collective-permute-done.11), kind=kLoop, calls=%fused_computation.2 | loop fusion | bytes 524288 | tf_op jit(solution)/shard_map/concatenate | solution.py:174
  28.7 2.3 %collective-permute-start.12 = (bf16[128,2048]{1,0:T(8,128)(2,1)}, bf16[128,2048]{1,0:T(8,128)(2,1)}, u32[]{:S(2)}, u32[]{:S(2)}) collective-permute-start(bf16[128,2048]{1,0:T(8,128)(2,1)} %constant_dynamic-update-slice_fusion.2.refs_0_), channel_id=1, source_target_pairs={{0,4},{4,0},{8,12},{12,8},{16,20},{20,16},{24,28},{28,24},{1,5},{5... | collective-permute-start | bytes 1572872 | tf_op jit(solution)/shard_map/ppermute | solution.py:184
  32.6 3.0 %attention.3 = (bf16[128,256]{1,0:T(8,128)(2,1)S(1)}, f32[2,128,256]{2,1,0:T(8,128)S(1)}, bf16[2,128,256]{2,1,0:T(8,128)(2,1)S(1)}, bf16[2,128,256]{2,1,0:T(8,128)(2,1)}) custom-call(s32[2,2]{1,0:T(2,128)S(1)} %pad_add_fusion.1.head_ref, s32[8,4]{1,0:T(8,128)S(1)} %copy.10.pat_ref, s32[1,8]{1,0:T(1,128)S(1)} %copy-done.17, ...), custom_call_target="tpu_custom_call" | custom-call | flops 260046848 | bytes 1600000 | tf_op jit(solution)/shard_map/attention/pallas_call | solution.py:89
  36.9 5.5 %attention.4 = (bf16[128,512]{1,0:T(8,128)(2,1)S(1)}, f32[2,128,512]{2,1,0:T(8,128)S(1)}, bf16[2,128,512]{2,1,0:T(8,128)(2,1)}, bf16[2,128,512]{2,1,0:T(8,128)(2,1)}) custom-call(s32[4,2]{1,0:T(4,128)S(1)} %pad_add_fusion.head_ref, s32[8,4]{1,0:T(8,128)S(1)} %copy.10.pat_ref, s32[1,8]{1,0:T(1,128)S(1)} %copy-done.17, bf16[1,128,1024]{2,1,0:T(8,128)(2,1)S(1)} %copy-done.4, ...), custom_call_target="tpu_custom_call" | custom-call | flops 520093696 | bytes 3200000 | tf_op jit(solution)/shard_map/attention/pallas_call | solution.py:89
  42.9 3.1 %collective-permute-start.9 = (bf16[2,128,512]{2,1,0:T(8,128)(2,1)}, bf16[2,128,512]{2,1,0:T(8,128)(2,1)}, u32[]{:S(2)}, u32[]{:S(2)}) collective-permute-start(bf16[2,128,512]{2,1,0:T(8,128)(2,1)} %get-tuple-element.22), channel_id=1, source_target_pairs={{4,8},{8,4},{12,16},{16,12},{20,24},{24,20},{5,9},{9,5},{13,17},{1... | collective-permute-start | bytes 786440 | tf_op jit(solution)/shard_map/ppermute | solution.py:170
  46.0 2.6 %collective-permute-start.3 = (bf16[2,128,256]{2,1,0:T(8,128)(2,1)}, bf16[2,128,256]{2,1,0:T(8,128)(2,1)}, u32[]{:S(2)}, u32[]{:S(2)}) collective-permute-start(bf16[2,128,256]{2,1,0:T(8,128)(2,1)} %get-tuple-element.18), channel_id=1, source_target_pairs={{4,8},{8,4},{12,16},{16,12},{20,24},{24,20},{5,9},{9,5},{13,17},{1... | collective-permute-start | bytes 393224 | tf_op jit(solution)/shard_map/ppermute | solution.py:170
  48.6 3.6 %attention.5 = (bf16[128,256]{1,0:T(8,128)(2,1)S(1)}, f32[2,128,256]{2,1,0:T(8,128)S(1)}, bf16[2,128,256]{2,1,0:T(8,128)(2,1)}, bf16[2,128,256]{2,1,0:T(8,128)(2,1)}) custom-call(s32[2,2]{1,0:T(2,128)S(1)} %pad_add_fusion.2.head_ref, s32[8,4]{1,0:T(8,128)S(1)} %copy.10.pat_ref, s32[1,8]{1,0:T(1,128)S(1)} %copy-done.17, bf16[1,128,1024]{2,1,0:T(8,128)(2,1)S(1)} %copy-done.4, ...), custom_call_target="tpu_custom_call" | custom-call | flops 260046848 | bytes 1600000 | tf_op jit(solution)/shard_map/attention/pallas_call | solution.py:89
  53.6 3.6 %collective-permute-start.14 = (bf16[2,128,256]{2,1,0:T(8,128)(2,1)}, bf16[2,128,256]{2,1,0:T(8,128)(2,1)S(1)}, u32[]{:S(2)}, u32[]{:S(2)}) collective-permute-start(bf16[2,128,256]{2,1,0:T(8,128)(2,1)} %get-tuple-element.26), channel_id=1, source_target_pairs={{4,8},{8,4},{12,16},{16,12},{20,24},{24,20},{5,9},{9,5},{13,17},{1... | collective-permute-start | bytes 393224 | tf_op jit(solution)/shard_map/ppermute | solution.py:170
  57.3 2.8 %collective-permute-done.14.refs_11_ = bf16[2,128,256]{2,1,0:T(8,128)(2,1)S(1)} collective-permute-done((bf16[2,128,256]{2,1,0:T(8,128)(2,1)}, bf16[2,128,256]{2,1,0:T(8,128)(2,1)S(1)}, u32[]{:S(2)}, u32[]{:S(2)}) %collective-permute-start.14) | collective-permute-done | bytes 131104 | tf_op jit(solution)/shard_map/ppermute | solution.py:170
  60.1 0.9 %copy-done.10 = f32[2,128,256]{2,1,0:T(8,128)S(1)} copy-done((f32[2,128,256]{2,1,0:T(8,128)S(1)}, f32[2,128,256]{2,1,0:T(8,128)}, u32[]{:S(2)}) %copy-start.10) | copy-done | bytes 262168
  61.0 0.9 %copy-done.12 = bf16[128,512]{1,0:T(8,128)(2,1)S(1)} copy-done((bf16[128,512]{1,0:T(8,128)(2,1)S(1)}, bf16[128,512]{1,0:T(8,128)(2,1)}, u32[]{:S(2)}) %copy-start.12) | copy-done | bytes 131096
  61.9 0.8 %copy-done.14 = bf16[128,256]{1,0:T(8,128)(2,1)S(1)} copy-done((bf16[128,256]{1,0:T(8,128)(2,1)S(1)}, bf16[128,256]{1,0:T(8,128)(2,1)}, u32[]{:S(2)}) %copy-start.14) | copy-done | bytes 65560
  62.8 0.8 %copy-done.16 = bf16[128,256]{1,0:T(8,128)(2,1)S(1)} copy-done((bf16[128,256]{1,0:T(8,128)(2,1)S(1)}, bf16[128,256]{1,0:T(8,128)(2,1)}, u32[]{:S(2)}) %copy-start.16) | copy-done | bytes 65560
  63.6 2.1 %finish.1 = (bf16[1,128,1024]{2,1,0:T(8,128)(2,1)}, bf16[1,128,1024]{2,1,0:T(8,128)(2,1)}, bf16[1,128,1024]{2,1,0:T(8,128)(2,1)}) custom-call(s32[8]{0:T(128)S(1)} %stack.126.table_ref, bf16[128,256]{1,0:T(8,128)(2,1)S(1)} %copy-done.14, f32[2,128,256]{2,1,0:T(8,128)S(1)} %copy-done.8, bf16[2,128,256]{2,1,0:T(8,128)(2,1)S(1)} %collective-permute-done.2.refs_2_, ...), custom_call_target="tpu_custom_call" | custom-call | tf_op jit(solution)/shard_map/finish/pallas_call | solution.py:127
  (65 shorter events, 8.6 us)
Async XLA Ops:
  0.6 5.2 %copy-start.1 = (bf16[1,128,1024]{2,1,0:T(8,128)(2,1)S(1)}, bf16[1,128,1024]{2,1,0:T(8,128)(2,1)}, u32[]{:S(2)}) copy-start(bf16[1,128,1024]{2,1,0:T(8,128)(2,1)} %k_ref.5) | copy-start | bytes 786436
  2.6 4.0 %copy-start.2 = (bf16[1,128,1024]{2,1,0:T(8,128)(2,1)S(1)}, bf16[1,128,1024]{2,1,0:T(8,128)(2,1)}, u32[]{:S(2)}) copy-start(bf16[1,128,1024]{2,1,0:T(8,128)(2,1)} %v_ref.5) | copy-start | bytes 786436
  2.6 14.0 %collective-permute-start.6 = (bf16[128,2048]{1,0:T(8,128)(2,1)}, bf16[128,2048]{1,0:T(8,128)(2,1)S(1)}, u32[]{:S(2)}, u32[]{:S(2)}) collective-permute-start(bf16[128,2048]{1,0:T(8,128)(2,1)} %constant_dynamic-slice_fusion), channel_id=1, source_target_pairs={{0,2},{1,3},{2,0},{3,1},{4,6},{5,7},{6,4},{7,5},{8,10},{9,11},{10,... | collective-permute-start | bytes 1572872 | tf_op jit(solution)/shard_map/ppermute | solution.py:146
  4.7 14.0 %collective-permute-start.4 = (bf16[128,2048]{1,0:T(8,128)(2,1)}, bf16[128,2048]{1,0:T(8,128)(2,1)}, u32[]{:S(2)}, u32[]{:S(2)}) collective-permute-start(bf16[128,2048]{1,0:T(8,128)(2,1)} %constant_dynamic-slice_fusion), channel_id=1, source_target_pairs={{0,1},{1,0},{2,3},{3,2},{4,5},{5,4},{6,7},{7,6},{8,9},{9,8},{10,11... | collective-permute-start | bytes 1572872 | tf_op jit(solution)/shard_map/ppermute | solution.py:146
  7.3 24.7 %collective-permute-start.1 = (bf16[2,128,1024]{2,1,0:T(8,128)(2,1)}, bf16[2,128,1024]{2,1,0:T(8,128)(2,1)S(1)}, u32[]{:S(2)}, u32[]{:S(2)}) collective-permute-start(bf16[2,128,1024]{2,1,0:T(8,128)(2,1)} %constant_dynamic-update-slice_fusion), channel_id=1, source_target_pairs={{4,8},{8,4},{12,16},{16,12},{20,24},{24,20},{5,9},{9,5},{13,17},{1... | collective-permute-start | bytes 1572872 | tf_op jit(solution)/shard_map/ppermute | solution.py:155
  11.6 20.4 %collective-permute-start = (bf16[2,128,1024]{2,1,0:T(8,128)(2,1)}, bf16[2,128,1024]{2,1,0:T(8,128)(2,1)S(1)}, u32[]{:S(2)}, u32[]{:S(2)}) collective-permute-start(bf16[2,128,1024]{2,1,0:T(8,128)(2,1)} %constant_dynamic-update-slice_fusion), channel_id=1, source_target_pairs={{0,4},{4,0},{8,12},{12,8},{16,20},{20,16},{24,28},{28,24},{1,5},{5... | collective-permute-start | bytes 1572872 | tf_op jit(solution)/shard_map/ppermute | solution.py:155
  11.7 20.3 %copy-start.3 = (bf16[256,2048]{1,0:T(8,128)(2,1)S(1)}, bf16[256,2048]{1,0:T(8,128)(2,1)}, u32[]{:S(2)}) copy-start(bf16[256,2048]{1,0:T(8,128)(2,1)} %refs_0_.1) | copy-start | bytes 3145732
  16.6 3.7 %copy-start.5 = (bf16[128,2048]{1,0:T(8,128)(2,1)}, bf16[128,2048]{1,0:T(8,128)(2,1)S(1)}, u32[]{:S(2)}) copy-start(bf16[128,2048]{1,0:T(8,128)(2,1)S(1)} %collective-permute-done.6.refs_2_) | copy-start | bytes 1572868
  17.4 6.9 %collective-permute-start.10 = (bf16[64,2048]{1,0:T(8,128)(2,1)}, bf16[64,2048]{1,0:T(8,128)(2,1)S(1)}, u32[]{:S(2)}, u32[]{:S(2)}) collective-permute-start(bf16[64,2048]{1,0:T(8,128)(2,1)} %slice.8), channel_id=1, source_target_pairs={{0,1},{1,0},{2,3},{3,2},{4,5},{5,4},{6,7},{7,6},{8,9},{9,8},{10,11... | collective-permute-start | bytes 786440 | tf_op jit(solution)/shard_map/ppermute | solution.py:146
  20.3 6.7 %collective-permute-start.11 = (bf16[64,2048]{1,0:T(8,128)(2,1)}, bf16[64,2048]{1,0:T(8,128)(2,1)}, u32[]{:S(2)}, u32[]{:S(2)}) collective-permute-start(bf16[64,2048]{1,0:T(8,128)(2,1)} %slice.9), channel_id=1, source_target_pairs={{0,2},{1,3},{2,0},{3,1},{4,6},{5,7},{6,4},{7,5},{8,10},{9,11},{10,... | collective-permute-start | bytes 786440 | tf_op jit(solution)/shard_map/ppermute | solution.py:146
  21.6 10.4 %copy-start = (bf16[1,128,2048]{2,1,0:T(8,128)(2,1)S(1)}, bf16[1,128,2048]{2,1,0:T(8,128)(2,1)}, u32[]{:S(2)}) copy-start(bf16[1,128,2048]{2,1,0:T(8,128)(2,1)} %dy_ref.5) | copy-start | bytes 1572868
  21.6 15.3 %collective-permute-start.7 = (bf16[128,2048]{1,0:T(8,128)(2,1)}, bf16[128,2048]{1,0:T(8,128)(2,1)}, u32[]{:S(2)}, u32[]{:S(2)}) collective-permute-start(bf16[128,2048]{1,0:T(8,128)(2,1)} %copy-done.5), channel_id=1, source_target_pairs={{0,4},{4,0},{8,12},{12,8},{16,20},{20,16},{24,28},{28,24},{1,5},{5... | collective-permute-start | bytes 1572872 | tf_op jit(solution)/shard_map/ppermute | solution.py:181
  24.3 12.7 %collective-permute-start.5 = (bf16[128,2048]{1,0:T(8,128)(2,1)}, bf16[128,2048]{1,0:T(8,128)(2,1)}, u32[]{:S(2)}, u32[]{:S(2)}) collective-permute-start(bf16[128,2048]{1,0:T(8,128)(2,1)} %collective-permute-done.4.refs_0_), channel_id=1, source_target_pairs={{0,4},{4,0},{8,12},{12,8},{16,20},{20,16},{24,28},{28,24},{1,5},{5... | collective-permute-start | bytes 1572872 | tf_op jit(solution)/shard_map/ppermute | solution.py:181
  27.0 5.0 %copy-start.4 = (bf16[1,128,1024]{2,1,0:T(8,128)(2,1)S(1)}, bf16[1,128,1024]{2,1,0:T(8,128)(2,1)}, u32[]{:S(2)}) copy-start(bf16[1,128,1024]{2,1,0:T(8,128)(2,1)} %q_ref.5) | copy-start | bytes 786436
  28.7 19.9 %collective-permute-start.12 = (bf16[128,2048]{1,0:T(8,128)(2,1)}, bf16[128,2048]{1,0:T(8,128)(2,1)}, u32[]{:S(2)}, u32[]{:S(2)}) collective-permute-start(bf16[128,2048]{1,0:T(8,128)(2,1)} %constant_dynamic-update-slice_fusion.2.refs_0_), channel_id=1, source_target_pairs={{0,4},{4,0},{8,12},{12,8},{16,20},{20,16},{24,28},{28,24},{1,5},{5... | collective-permute-start | bytes 1572872 | tf_op jit(solution)/shard_map/ppermute | solution.py:184
  32.0 5.0 %copy-start.6 = (bf16[128,2048]{1,0:T(8,128)(2,1)S(1)}, bf16[128,2048]{1,0:T(8,128)(2,1)}, u32[]{:S(2)}) copy-start(bf16[128,2048]{1,0:T(8,128)(2,1)} %copy-done.5) | copy-start | bytes 1572868
  36.9 16.7 %collective-permute-start.2 = (bf16[2,128,256]{2,1,0:T(8,128)(2,1)S(1)}, bf16[2,128,256]{2,1,0:T(8,128)(2,1)S(1)}, u32[]{:S(2)}, u32[]{:S(2)}) collective-permute-start(bf16[2,128,256]{2,1,0:T(8,128)(2,1)S(1)} %get-tuple-element.17), channel_id=1, source_target_pairs={{0,4},{4,0},{8,12},{12,8},{16,20},{20,16},{24,28},{28,24},{1,5},{5... | collective-permute-start | bytes 393224 | tf_op jit(solution)/shard_map/ppermute | solution.py:170
  42.4 9.9 %copy-start.11 = (bf16[128,512]{1,0:T(8,128)(2,1)}, bf16[128,512]{1,0:T(8,128)(2,1)S(1)}, u32[]{:S(2)}) copy-start(bf16[128,512]{1,0:T(8,128)(2,1)S(1)} %get-tuple-element.19.refs_4_) | copy-start | bytes 393220
  42.4 14.9 %collective-permute-start.8 = (bf16[2,128,512]{2,1,0:T(8,128)(2,1)}, bf16[2,128,512]{2,1,0:T(8,128)(2,1)S(1)}, u32[]{:S(2)}, u32[]{:S(2)}) collective-permute-start(bf16[2,128,512]{2,1,0:T(8,128)(2,1)} %get-tuple-element.21), channel_id=1, source_target_pairs={{0,4},{4,0},{8,12},{12,8},{16,20},{20,16},{24,28},{28,24},{1,5},{5... | collective-permute-start | bytes 786440 | tf_op jit(solution)/shard_map/ppermute | solution.py:170
  42.9 14.4 %collective-permute-start.9 = (bf16[2,128,512]{2,1,0:T(8,128)(2,1)}, bf16[2,128,512]{2,1,0:T(8,128)(2,1)}, u32[]{:S(2)}, u32[]{:S(2)}) collective-permute-start(bf16[2,128,512]{2,1,0:T(8,128)(2,1)} %get-tuple-element.22), channel_id=1, source_target_pairs={{4,8},{8,4},{12,16},{16,12},{20,24},{24,20},{5,9},{9,5},{13,17},{1... | collective-permute-start | bytes 786440 | tf_op jit(solution)/shard_map/ppermute | solution.py:170
  46.0 14.1 %copy-start.8 = (f32[2,128,256]{2,1,0:T(8,128)S(1)}, f32[2,128,256]{2,1,0:T(8,128)}, u32[]{:S(2)}) copy-start(f32[2,128,256]{2,1,0:T(8,128)} %copy-done.7) | copy-start | bytes 786436
  46.0 11.3 %collective-permute-start.3 = (bf16[2,128,256]{2,1,0:T(8,128)(2,1)}, bf16[2,128,256]{2,1,0:T(8,128)(2,1)}, u32[]{:S(2)}, u32[]{:S(2)}) collective-permute-start(bf16[2,128,256]{2,1,0:T(8,128)(2,1)} %get-tuple-element.18), channel_id=1, source_target_pairs={{4,8},{8,4},{12,16},{16,12},{20,24},{24,20},{5,9},{9,5},{13,17},{1... | collective-permute-start | bytes 393224 | tf_op jit(solution)/shard_map/ppermute | solution.py:170
  53.6 3.7 %collective-permute-start.13 = (bf16[2,128,256]{2,1,0:T(8,128)(2,1)}, bf16[2,128,256]{2,1,0:T(8,128)(2,1)S(1)}, u32[]{:S(2)}, u32[]{:S(2)}) collective-permute-start(bf16[2,128,256]{2,1,0:T(8,128)(2,1)} %get-tuple-element.25), channel_id=1, source_target_pairs={{0,4},{4,0},{8,12},{12,8},{16,20},{20,16},{24,28},{28,24},{1,5},{5... | collective-permute-start | bytes 393224 | tf_op jit(solution)/shard_map/ppermute | solution.py:170
  53.6 6.5 %collective-permute-start.14 = (bf16[2,128,256]{2,1,0:T(8,128)(2,1)}, bf16[2,128,256]{2,1,0:T(8,128)(2,1)S(1)}, u32[]{:S(2)}, u32[]{:S(2)}) collective-permute-start(bf16[2,128,256]{2,1,0:T(8,128)(2,1)} %get-tuple-element.26), channel_id=1, source_target_pairs={{4,8},{8,4},{12,16},{16,12},{20,24},{24,20},{5,9},{9,5},{13,17},{1... | collective-permute-start | bytes 393224 | tf_op jit(solution)/shard_map/ppermute | solution.py:170
  (10 other events, 7.5 us)

commit v2 on v1

v2 whole, which is shorter than its diff:
```python
import functools

import jax
import jax.numpy as jnp
from jax import lax
from jax.experimental import pallas as pl
from jax.experimental.pallas import tpu as pltpu
from jax.sharding import PartitionSpec as P

HD = 128
PAIR = 2 * HD
F32 = jnp.float32
BF16 = jnp.bfloat16
NT = (((1,), (1,)), ((), ()))
NN = (((1,), (0,)), ((), ()))
TN = (((0,), (0,)), ((), ()))
ANY = pl.BlockSpec(memory_space=pl.ANY)
VMEM = pl.BlockSpec(memory_space=pltpu.VMEM)
SMEM = pl.BlockSpec(memory_space=pltpu.SMEM)
PARAMS = pltpu.CompilerParams(vmem_limit_bytes=40 * 2**20)


def dot(a, b, dims):
    return lax.dot_general(a, b, dims, preferred_element_type=F32)


def swap(n, offset):
    pairs = []
    for i in range(offset, n - 1, 2):
        pairs += [(i, i + 1), (i + 1, i)]
    return pairs


def place():
    return lax.rem(lax.axis_index("seq"), 2), lax.axis_index("fsdp")


def run_copies(copies):
    for copy in copies:
        copy.start()
    for copy in copies:
        copy.wait()


def prep_kernel(w_ref, k_ref, v_ref, first_ref, second_ref, kv_ref, sems):
    core, _ = place()
    half = first_ref.shape[0]
    pairs = [
        (w_ref.at[pl.ds(pl.multiple_of(core * half, half), half), :], first_ref),
        (w_ref.at[pl.ds(pl.multiple_of((1 - core) * half, half), half), :], second_ref),
        (k_ref, kv_ref.at[pl.ds(0, 1)]),
        (v_ref, kv_ref.at[pl.ds(1, 1)]),
    ]
    run_copies([pltpu.make_async_copy(s, d, sems.at[i]) for i, (s, d) in enumerate(pairs)])


def prep(w_out, keys, values):
    half = jax.ShapeDtypeStruct((w_out.shape[0] // 2, w_out.shape[1]), BF16)
    return pl.pallas_call(
        prep_kernel,
        out_shape=(half, half, jax.ShapeDtypeStruct((2,) + keys.shape[1:], BF16)),
        in_specs=[ANY] * 3,
        out_specs=(ANY,) * 3,
        scratch_shapes=[pltpu.SemaphoreType.DMA((4,))],
        compiler_params=PARAMS,
        name="prep",
    )(w_out, keys, values)


def key_limits(pat_ref, val_ref):
    shard = lax.axis_index("seq")
    count = val_ref.shape[1]
    odd = lax.rem(shard, 2)
    blocks = (shard, shard + 1 - 2 * odd, shard - 1 + 2 * odd)
    limits = []
    for block in blocks:
        listed = pat_ref[shard, 0] == block
        for entry in range(1, pat_ref.shape[1]):
            listed = jnp.logical_or(listed, pat_ref[shard, entry] == block)
        inside = jnp.logical_and(block >= 0, block < count)
        held = val_ref[0, jnp.clip(block, 0, count - 1)]
        limits.append(jnp.where(jnp.logical_and(listed, inside), held, 0))
    return limits


def diagonal(x):
    zero = jnp.zeros((x.shape[0], HD), x.dtype)
    return jnp.concatenate(
        [
            jnp.concatenate([x[:, :HD], zero], axis=1),
            jnp.concatenate([zero, x[:, HD:]], axis=1),
        ],
        axis=0,
    )


def attention_kernel(chunks, pieces, pat_ref, val_ref, q_ref, k_ref, v_ref, core_ref, far_ref, dy_ref, *refs):
    core, group = place()
    slots = chunks(core, group)
    plan = pieces(core)
    n_w = len(refs) - 4 - 5
    w_refs = refs[:n_w]
    dq_ref, own_ref, to_core_ref, to_far_ref, dy, w, q, kv, sems = refs[n_w:]
    scale = HD ** (-0.5)
    tok = q.shape[1]
    copies = []

    def fetch(source, target):
        copy = pltpu.make_async_copy(source, target, sems.at[len(copies)])
        copy.start()
        copies.append(copy)
        return copy

    first = [fetch(dy_ref.at[0], dy)]
    waits = []
    for slot, (chunk, _) in enumerate(slots):
        wanted = [
            fetch(
                w_refs[index].at[pl.ds(row, rows), :],
                w.at[slot, pl.ds(to, rows), :],
            )
            for index, row, to, rows in plan[slot]
        ]
        cols = pl.ds(pl.multiple_of(chunk * PAIR, PAIR), PAIR)
        wanted.append(fetch(q_ref.at[0, :, cols], q.at[slot]))
        for side, source in enumerate((k_ref, v_ref)):
            wanted.append(fetch(source.at[0, :, cols], kv.at[slot, side, pl.ds(0, tok), :]))
            wanted.append(fetch(core_ref.at[side, :, cols], kv.at[slot, side, pl.ds(tok, tok), :]))
            wanted.append(fetch(far_ref.at[side, :, cols], kv.at[slot, side, pl.ds(2 * tok, tok), :]))
        waits.append(wanted)

    rows = lax.broadcasted_iota(jnp.int32, (tok, PAIR), 0)
    open_keys = jnp.concatenate([rows < limit for limit in key_limits(pat_ref, val_ref)], axis=0)
    for slot in range(len(slots)):
        for copy in first + waits[slot]:
            copy.wait()
        first = []
        cols = pl.ds(pl.multiple_of(slots[slot][1] * PAIR, PAIR), PAIR)
        d = diagonal(dot(dy[...], w[slot], NT).astype(BF16))
        qd = diagonal(q[slot])
        k, v = kv[slot, 0], kv[slot, 1]
        score = jnp.where(open_keys, dot(k, qd, NT) * scale, -jnp.inf)
        top = jnp.max(score, axis=0, keepdims=True)
        raised = jnp.exp(score - top)
        prob = raised * (1.0 / jnp.sum(raised, axis=0, keepdims=True))
        prob_b = prob.astype(BF16)
        d_prob = dot(v, d, NT)
        delta = jnp.sum(prob_b.astype(F32) * d_prob, axis=0, keepdims=True)
        d_score = (prob * (d_prob - delta)).astype(BF16)
        both = dot(d_score, k, TN) * scale
        dq_ref[:, cols] = jnp.concatenate([both[:tok, :HD], both[tok:, HD:]], axis=1).astype(BF16)
        for side, grad in enumerate((dot(d_score, qd, NN) * scale, dot(prob_b, d, NN))):
            own_ref[side, :, cols] = grad[:tok]
            to_core_ref[side, :, cols] = grad[tok : 2 * tok].astype(BF16)
            to_far_ref[side, :, cols] = grad[2 * tok :].astype(BF16)


def attention(name, chunks, pieces, weights, pattern, valid, q, k, v, kv_core, kv_far, d_out):
    count = len(chunks(0, 0))
    tok, depth = q.shape[1], d_out.shape[2]
    width = count * PAIR
    n_copies = 1 + sum(len(slot) + 7 for slot in pieces(0))
    return pl.pallas_call(
        functools.partial(attention_kernel, chunks, pieces),
        out_shape=(
            jax.ShapeDtypeStruct((tok, width), BF16),
            jax.ShapeDtypeStruct((2, tok, width), F32),
            jax.ShapeDtypeStruct((2, tok, width), BF16),
            jax.ShapeDtypeStruct((2, tok, width), BF16),
        ),
        in_specs=[SMEM] * 2 + [ANY] * (6 + len(weights)),
        out_specs=(VMEM,) * 4,
        scratch_shapes=[
            pltpu.VMEM((tok, depth), BF16),
            pltpu.VMEM((count, PAIR, depth), BF16),
            pltpu.VMEM((count, tok, PAIR), BF16),
            pltpu.VMEM((count, 2, 3 * tok, PAIR), BF16),
            pltpu.SemaphoreType.DMA((n_copies,)),
        ],
        cost_estimate=pl.CostEstimate(
            flops=count * 4 * tok * HD * (depth + 15 * HD),
            bytes_accessed=count * 1_800_000,
            transcendentals=count * 6 * tok * HD,
        ),
        compiler_params=PARAMS,
        name=name,
    )(pattern, valid, q, k, v, kv_core, kv_far, d_out, *weights)


def finish_kernel(chunks, n_parts, n_old, *refs):
    core, group = place()
    ins = refs[: 4 * n_parts]
    outs = refs[4 * n_parts + n_old : 4 * n_parts + n_old + 3]
    stage, sems = refs[-2:]
    tok = stage.shape[1]
    copies = []
    slot = 0
    for part in range(n_parts):
        dq, own, near, far = ins[4 * part : 4 * part + 4]
        for at in range(dq.shape[1] // PAIR):
            cols = slice(at * PAIR, (at + 1) * PAIR)
            chunk = chunks(core, group)[slot]
            dest = pl.ds(pl.multiple_of(chunk * PAIR, PAIR), PAIR)
            stage[3 * slot] = dq[:, cols]
            for side in range(2):
                total = own[side, :, cols] + near[side, :, cols].astype(F32)
                stage[3 * slot + 1 + side] = (total + far[side, :, cols].astype(F32)).astype(BF16)
            for index in range(3):
                copy = pltpu.make_async_copy(
                    stage.at[3 * slot + index], outs[index].at[0, :, dest], sems.at[3 * slot + index]
                )
                copy.start()
                copies.append(copy)
            slot += 1
    for copy in copies:
        copy.wait()


def finish(name, chunks, parts, shape, old=()):
    count = len(chunks(0, 0))
    ins = [x for part in parts for x in part]
    out = jax.ShapeDtypeStruct(shape, BF16)
    return pl.pallas_call(
        functools.partial(finish_kernel, chunks, len(parts), len(old)),
        out_shape=(out,) * 3,
        in_specs=[VMEM] * len(ins) + [ANY] * len(old),
        out_specs=(ANY,) * 3,
        scratch_shapes=[
            pltpu.VMEM((3 * count, shape[1], PAIR), BF16),
            pltpu.SemaphoreType.DMA((3 * count,)),
        ],
        input_output_aliases={len(ins) + i: i for i in range(len(old))},
        compiler_params=PARAMS,
        name=name,
    )(*ins, *old)


def body(queries, keys, values, d_out, w_out, pattern, valid):
    n_seq, n_fsdp = lax.axis_size("seq"), lax.axis_size("fsdp")
    n_chunks = queries.shape[2] // PAIR
    near = functools.partial(lax.ppermute, axis_name="seq", perm=swap(n_seq, 0))
    far = functools.partial(lax.ppermute, axis_name="seq", perm=swap(n_seq, 1))

    def cross(x, bits):
        pairs = [
            (s * n_fsdp + g, s * n_fsdp + (g ^ bits[s % 2]))
            for s in range(n_seq)
            for g in range(n_fsdp)
        ]
        return lax.ppermute(x, ("seq", "fsdp"), pairs)

    def part(name, chunks, pieces, weights, halo):
        dq, own, to_core, to_far = attention(
            name, chunks, pieces, weights, pattern, valid, queries, keys, values, *halo, d_out
        )
        return dq, own, near(to_core), far(to_far)

    first, second, kv = prep(w_out, keys, values)
    if n_fsdp == 4 and n_chunks == 4 and w_out.shape[0] == PAIR:
        got_a = cross(first, (1, 2))
        got_b = cross(second, (1, 2))
        halo = near(kv), far(kv)
        part_a = part("heads_own", lambda core, group: [(group, 0)], lambda core: [[(0, 0, 0, PAIR)]], [w_out], halo)
        got_d = cross(got_a, (2, 1))
        got_b, part_a = lax.optimization_barrier((got_b, part_a))
        halves = lambda first, at: [(first, 0, at * HD, HD), (first + 1, 0, (1 - at) * HD, HD)]
        part_b = part(
            "heads_side",
            lambda core, group: [(group ^ (1 + core), core), (group ^ (2 - core), 1 - core)],
            lambda core: [halves(0, core), halves(2, 1 - core)],
            [got_a, got_b, near(got_a), near(got_b)],
            halo,
        )
        part_c = part(
            "heads_far",
            lambda core, group: [(group ^ 3, 0)],
            lambda core: [halves(0, core)],
            [got_d, near(got_d)],
            halo,
        )
        ab = lambda core, group: [group, group ^ 1, group ^ 2]
        last = lambda core, group: [group ^ 3]
        old = finish("finish_first", ab, [part_a, part_b], queries.shape)
        return finish("finish_last", last, [part_c], queries.shape, old)
    full = lax.all_gather(w_out, "fsdp", axis=0, tiled=True)
    halo = near(kv), far(kv)
    chunks = lambda core, group: [(slot, slot) for slot in range(n_chunks)]
    order = lambda core, group: list(range(n_chunks))
    pieces = lambda core: [[(0, slot * PAIR, 0, PAIR)] for slot in range(n_chunks)]
    return finish("finish", order, [part("heads_all", chunks, pieces, [full], halo)], queries.shape)


def solution(mesh):
    rows = P("fsdp", "seq", None)
    in_specs = (rows, rows, rows, rows, P("fsdp", None), P(), P("fsdp", None))
    return jax.shard_map(
        body, mesh=mesh, in_specs=in_specs, out_specs=(rows,) * 3, check_vma=False
    )
```

time: 66.2 us -> 51.6 us (0.78)
  local copies, waits for them, and re-layouts: 15.8 us -> 6.12 us
  starting transfers between devices: 26.1 us -> 19.8 us
  waiting for transfers between devices: 8.33 us -> 11.8 us
  Pallas kernels: 14.2 us -> 12.6 us
    ppermute x9 -> x8, starting transfers between devices: 16.4 us -> 9.46 us  [the longest x3 4.87 us: cross(): return lax.ppermute(x, ('seq', 'fsdp'), pairs)]
    unnamed x41 -> x23, local copies, waits for them, and re-layouts: 8.96 us -> 6.12 us
    slice x2 -> x0, local copies, waits for them, and re-layouts: 2.44 us -> none  [the longest x1 1.67 us: body(): from_x[half:]]
    concatenate x2 -> x0, local copies, waits for them, and re-layouts: 2.4 us -> none  [the longest x1 1.69 us: body(): jnp.concatenate([flip(from_y[:half], 1), flip(from_x[half:], 2)], axis=0)]
    dynamic_slice x1 -> x0, local copies, waits for them, and re-layouts: 1.93 us -> none  [body(): mine = lax.dynamic_slice_in_dim(w_out, core * HD, HD, 0)]
    ppermute x9 -> x8, waiting for transfers between devices: 5.55 us -> 7.46 us  [the longest x2 3.54 us: body(): halo = (near(kv), far(kv))]
    ppermute x6, waiting for transfers between devices: 2.78 us -> 4.34 us  [part(): return (dq, own, near(to_core), far(to_far))]
    pallas_call x4 -> x6, Pallas kernels: 14.2 us -> 12.6 us  [the longest x3 9.85 us: attention(): pl.pallas_call(functools.partial(attention_kernel, chunks, pieces), out_s...]
  transfers between devices with their start and end apart: 15 -> 14, of which waited for: 3 -> 5; matrix products, arithmetic and copies ran while one was open for 10% -> 0% of each run, Pallas kernels for 18% -> 21%
where the time goes in v2:
time: 51.6 us; the launch traced here: 51.2 us
  starting transfers between devices  19.8 us (38%)
  Pallas kernels  12.6 us (24%)
  waiting for transfers between devices  11.8 us (23%)
  local copies, waits for them, and re-layouts  6.12 us (12%)
  between operations  0.83 us (2%)
    ppermute x6, starting transfers between devices, part(): return (dq, own, near(to_core), far(to_far))  10.4 us
    pallas_call x3, Pallas kernels, attention(): pl.pallas_call(functools.partial(attention_kernel, chunks, pieces), out_s...  9.85 us
    unnamed x23, local copies, waits for them, and re-layouts  6.12 us
    ppermute x3, starting transfers between devices, cross(): return lax.ppermute(x, ('seq', 'fsdp'), pairs)  4.87 us
    ppermute x6, waiting for transfers between devices, part(): return (dq, own, near(to_core), far(to_far))  4.34 us
    ppermute x2, starting transfers between devices, body(): halo = (near(kv), far(kv))  4.01 us
    ppermute x2, waiting for transfers between devices, body(): halo = (near(kv), far(kv))  3.54 us
    ppermute x1, waiting for transfers between devices, body(): near(got_b)  2.27 us
  transfers between devices with their start and end apart: 14, of which 5 were waited for; matrix products, arithmetic and copies ran while one was open for 0% of the time, Pallas kernels for 21%

profile of v2, /device:TPU:1, one launch (start us, length us, event | category | flops | bytes accessed | tf_op | source)
XLA Modules:
  0.0 51.2 jit_solution(14399406416378892506)
XLA Ops:
  0.7 1.3 %copy-done.1 = bf16[256,2048]{1,0:T(8,128)(2,1)S(1)} copy-done((bf16[256,2048]{1,0:T(8,128)(2,1)S(1)}, bf16[256,2048]{1,0:T(8,128)(2,1)}, u32[]{:S(2)}) %copy-start.1) | copy-done | bytes 1048600
  1.9 0.9 %copy-done.3 = bf16[1,128,1024]{2,1,0:T(8,128)(2,1)S(1)} copy-done((bf16[1,128,1024]{2,1,0:T(8,128)(2,1)S(1)}, bf16[1,128,1024]{2,1,0:T(8,128)(2,1)}, u32[]{:S(2)}) %copy-start.3) | copy-done | bytes 262168
  2.9 0.9 %copy-done.5 = bf16[1,128,1024]{2,1,0:T(8,128)(2,1)S(1)} copy-done((bf16[1,128,1024]{2,1,0:T(8,128)(2,1)S(1)}, bf16[1,128,1024]{2,1,0:T(8,128)(2,1)}, u32[]{:S(2)}) %copy-start.5) | copy-done | bytes 262168
  3.8 1.1 %prep.1 = (bf16[128,2048]{1,0:T(8,128)(2,1)S(1)}, bf16[128,2048]{1,0:T(8,128)(2,1)}, bf16[2,128,1024]{2,1,0:T(8,128)(2,1)}) custom-call(bf16[256,2048]{1,0:T(8,128)(2,1)S(1)} %copy-done.1, bf16[1,128,1024]{2,1,0:T(8,128)(2,1)S(1)} %copy-done.3, bf16[1,128,1024]{2,1,0:T(8,128)(2,1)S(1)} %copy-done.5), custom_call_target="tpu_custom_call" | custom-call | tf_op jit(solution)/shard_map/prep/pallas_call | solution.py:59
  4.9 2.1 %collective-permute-start.2 = (bf16[128,2048]{1,0:T(8,128)(2,1)S(1)}, bf16[128,2048]{1,0:T(8,128)(2,1)}, u32[]{:S(2)}, u32[]{:S(2)}) collective-permute-start(bf16[128,2048]{1,0:T(8,128)(2,1)S(1)} %get-tuple-element.27), channel_id=1, source_target_pairs={{0,1},{1,0},{2,3},{3,2},{4,6},{5,7},{6,4},{7,5},{8,9},{9,8},{10,11... | collective-permute-start | bytes 1572872 | tf_op jit(solution)/shard_map/ppermute | solution.py:250
  7.0 0.9 %collective-permute-start = (bf16[2,128,1024]{2,1,0:T(8,128)(2,1)}, bf16[2,128,1024]{2,1,0:T(8,128)(2,1)S(1)}, u32[]{:S(2)}, u32[]{:S(2)}) collective-permute-start(bf16[2,128,1024]{2,1,0:T(8,128)(2,1)} %get-tuple-element.26), channel_id=1, source_target_pairs={{0,4},{4,0},{8,12},{12,8},{16,20},{20,16},{24,28},{28,24},{1,5},{5... | collective-permute-start | bytes 1572872 | tf_op jit(solution)/shard_map/ppermute | solution.py:262
  8.0 3.1 %collective-permute-start.1 = (bf16[2,128,1024]{2,1,0:T(8,128)(2,1)}, bf16[2,128,1024]{2,1,0:T(8,128)(2,1)S(1)}, u32[]{:S(2)}, u32[]{:S(2)}) collective-permute-start(bf16[2,128,1024]{2,1,0:T(8,128)(2,1)} %get-tuple-element.26), channel_id=1, source_target_pairs={{4,8},{8,4},{12,16},{16,12},{20,24},{24,20},{5,9},{9,5},{13,17},{1... | collective-permute-start | bytes 1572872 | tf_op jit(solution)/shard_map/ppermute | solution.py:262
  11.1 1.3 %collective-permute-start.7 = (bf16[128,2048]{1,0:T(8,128)(2,1)}, bf16[128,2048]{1,0:T(8,128)(2,1)}, u32[]{:S(2)}, u32[]{:S(2)}) collective-permute-start(bf16[128,2048]{1,0:T(8,128)(2,1)} %get-tuple-element.32), channel_id=1, source_target_pairs={{0,1},{1,0},{2,3},{3,2},{4,6},{5,7},{6,4},{7,5},{8,9},{9,8},{10,11... | collective-permute-start | bytes 1572872 | tf_op jit(solution)/shard_map/ppermute | solution.py:250
  12.4 1.6 %collective-permute-done.2.refs_0_ = bf16[128,2048]{1,0:T(8,128)(2,1)} collective-permute-done((bf16[128,2048]{1,0:T(8,128)(2,1)S(1)}, bf16[128,2048]{1,0:T(8,128)(2,1)}, u32[]{:S(2)}, u32[]{:S(2)}) %collective-permute-start.2) | collective-permute-done | bytes 524320 | tf_op jit(solution)/shard_map/ppermute | solution.py:250
  14.0 1.4 %collective-permute-start.3 = (bf16[128,2048]{1,0:T(8,128)(2,1)}, bf16[128,2048]{1,0:T(8,128)(2,1)S(1)}, u32[]{:S(2)}, u32[]{:S(2)}) collective-permute-start(bf16[128,2048]{1,0:T(8,128)(2,1)} %collective-permute-done.2.refs_0_), channel_id=1, source_target_pairs={{0,2},{1,3},{2,0},{3,1},{4,5},{5,4},{6,7},{7,6},{8,10},{9,11},{10,... | collective-permute-start | bytes 1572872 | tf_op jit(solution)/shard_map/ppermute | solution.py:250
  15.5 3.5 %collective-permute-done.1.far_ref = bf16[2,128,1024]{2,1,0:T(8,128)(2,1)S(1)} collective-permute-done((bf16[2,128,1024]{2,1,0:T(8,128)(2,1)}, bf16[2,128,1024]{2,1,0:T(8,128)(2,1)S(1)}, u32[]{:S(2)}, u32[]{:S(2)}) %collective-permute-start.1) | collective-permute-done | bytes 524320 | tf_op jit(solution)/shard_map/ppermute | solution.py:262
  19.1 0.9 %copy-done.4 = bf16[1,128,1024]{2,1,0:T(8,128)(2,1)S(1)} copy-done((bf16[1,128,1024]{2,1,0:T(8,128)(2,1)S(1)}, bf16[1,128,1024]{2,1,0:T(8,128)(2,1)}, u32[]{:S(2)}) %copy-start.4) | copy-done | bytes 262168
  20.0 0.9 %copy-done.6 = bf16[1,128,1024]{2,1,0:T(8,128)(2,1)S(1)} copy-done((bf16[1,128,1024]{2,1,0:T(8,128)(2,1)S(1)}, bf16[1,128,1024]{2,1,0:T(8,128)(2,1)}, u32[]{:S(2)}) %copy-start.6) | copy-done | bytes 262168
  21.0 0.9 %copy-done.7 = bf16[1,128,1024]{2,1,0:T(8,128)(2,1)S(1)} copy-done((bf16[1,128,1024]{2,1,0:T(8,128)(2,1)S(1)}, bf16[1,128,1024]{2,1,0:T(8,128)(2,1)}, u32[]{:S(2)}) %copy-start.7) | copy-done | bytes 262168
  21.9 2.4 %heads_own.1 = (bf16[128,256]{1,0:T(8,128)(2,1)S(1)}, f32[2,128,256]{2,1,0:T(8,128)S(1)}, bf16[2,128,256]{2,1,0:T(8,128)(2,1)S(1)}, bf16[2,128,256]{2,1,0:T(8,128)(2,1)S(1)}) custom-call(s32[8,4]{1,0:T(8,128)S(1)} %copy.13.pat_ref, s32[1,8]{1,0:T(1,128)S(1)} %copy-done.9, bf16[1,128,1024]{2,1,0:T(8,128)(2,1)S(1)} %copy-done.7, ...), custom_call_target="tpu_custom_call" | custom-call | flops 260046848 | bytes 1800000 | tf_op jit(solution)/shard_map/heads_own/pallas_call | solution.py:163
  24.4 3.6 %collective-permute-start.9 = (bf16[2,128,256]{2,1,0:T(8,128)(2,1)S(1)}, bf16[2,128,256]{2,1,0:T(8,128)(2,1)S(1)}, u32[]{:S(2)}, u32[]{:S(2)}) collective-permute-start(bf16[2,128,256]{2,1,0:T(8,128)(2,1)S(1)} %get-tuple-element.36), channel_id=1, source_target_pairs={{4,8},{8,4},{12,16},{16,12},{20,24},{24,20},{5,9},{9,5},{13,17},{1... | collective-permute-start | bytes 393224 | tf_op jit(solution)/shard_map/ppermute | solution.py:256
  28.1 2.6 %collective-permute-done.9.refs_3_ = bf16[2,128,256]{2,1,0:T(8,128)(2,1)S(1)} collective-permute-done((bf16[2,128,256]{2,1,0:T(8,128)(2,1)S(1)}, bf16[2,128,256]{2,1,0:T(8,128)(2,1)S(1)}, u32[]{:S(2)}, u32[]{:S(2)}) %collective-permute-start.9) | collective-permute-done | bytes 131104 | tf_op jit(solution)/shard_map/ppermute | solution.py:256
  31.2 2.3 %collective-permute-done.11.refs_3_ = bf16[128,2048]{1,0:T(8,128)(2,1)S(1)} collective-permute-done((bf16[128,2048]{1,0:T(8,128)(2,1)}, bf16[128,2048]{1,0:T(8,128)(2,1)S(1)}, u32[]{:S(2)}, u32[]{:S(2)}) %collective-permute-start.11) | collective-permute-done | bytes 524320 | tf_op jit(solution)/shard_map/ppermute | solution.py:271
  33.5 5.0 %heads_side.1 = (bf16[128,512]{1,0:T(8,128)(2,1)S(1)}, f32[2,128,512]{2,1,0:T(8,128)S(1)}, bf16[2,128,512]{2,1,0:T(8,128)(2,1)S(1)}, bf16[2,128,512]{2,1,0:T(8,128)(2,1)S(1)}) custom-call(s32[8,4]{1,0:T(8,128)S(1)} %copy.13.pat_ref, s32[1,8]{1,0:T(1,128)S(1)} %copy-done.9, bf16[1,128,1024]{2,1,0:T(8,128)(2,1)S(1)} %copy-done.8, ...), custom_call_target="tpu_custom_call" | custom-call | flops 520093696 | bytes 3600000 | tf_op jit(solution)/shard_map/heads_side/pallas_call | solution.py:163
  38.7 2.9 %collective-permute-start.13 = (bf16[2,128,512]{2,1,0:T(8,128)(2,1)S(1)}, bf16[2,128,512]{2,1,0:T(8,128)(2,1)S(1)}, u32[]{:S(2)}, u32[]{:S(2)}) collective-permute-start(bf16[2,128,512]{2,1,0:T(8,128)(2,1)S(1)} %get-tuple-element.45), channel_id=1, source_target_pairs={{4,8},{8,4},{12,16},{16,12},{20,24},{24,20},{5,9},{9,5},{13,17},{1... | collective-permute-start | bytes 786440 | tf_op jit(solution)/shard_map/ppermute | solution.py:256
  41.7 2.4 %heads_far.1 = (bf16[128,256]{1,0:T(8,128)(2,1)S(1)}, f32[2,128,256]{2,1,0:T(8,128)S(1)}, bf16[2,128,256]{2,1,0:T(8,128)(2,1)S(1)}, bf16[2,128,256]{2,1,0:T(8,128)(2,1)S(1)}) custom-call(s32[8,4]{1,0:T(8,128)S(1)} %copy.13.pat_ref, s32[1,8]{1,0:T(1,128)S(1)} %copy-done.9, bf16[1,128,1024]{2,1,0:T(8,128)(2,1)S(1)} %copy-done.8, ...), custom_call_target="tpu_custom_call" | custom-call | flops 260046848 | bytes 1800000 | tf_op jit(solution)/shard_map/heads_far/pallas_call | solution.py:163
  44.2 3.6 %collective-permute-start.6 = (bf16[2,128,256]{2,1,0:T(8,128)(2,1)S(1)}, bf16[2,128,256]{2,1,0:T(8,128)(2,1)S(1)}, u32[]{:S(2)}, u32[]{:S(2)}) collective-permute-start(bf16[2,128,256]{2,1,0:T(8,128)(2,1)S(1)} %get-tuple-element.31), channel_id=1, source_target_pairs={{4,8},{8,4},{12,16},{16,12},{20,24},{24,20},{5,9},{9,5},{13,17},{1... | collective-permute-start | bytes 393224 | tf_op jit(solution)/shard_map/ppermute | solution.py:256
  47.8 0.9 %finish_first.1 = (bf16[1,128,1024]{2,1,0:T(8,128)(2,1)}, bf16[1,128,1024]{2,1,0:T(8,128)(2,1)}, bf16[1,128,1024]{2,1,0:T(8,128)(2,1)}) custom-call(bf16[128,256]{1,0:T(8,128)(2,1)S(1)} %get-tuple-element.37.refs_0_, f32[2,128,256]{2,1,0:T(8,128)S(1)} %get-tuple-element.38.refs_1_, bf16[2,128,256]{2,1,0:T(8,128)(2,1)S(1)} %collective-permute-done.8.refs_2_, ...), custom_call_target="tpu_custom_call" | custom-call | tf_op jit(solution)/shard_map/finish_first/pallas_call | solution.py:223
  48.7 1.7 %collective-permute-done.6.refs_3_ = bf16[2,128,256]{2,1,0:T(8,128)(2,1)S(1)} collective-permute-done((bf16[2,128,256]{2,1,0:T(8,128)(2,1)S(1)}, bf16[2,128,256]{2,1,0:T(8,128)(2,1)S(1)}, u32[]{:S(2)}, u32[]{:S(2)}) %collective-permute-start.6) | collective-permute-done | bytes 131104 | tf_op jit(solution)/shard_map/ppermute | solution.py:256
  (33 shorter events, 1.8 us)
Async XLA Ops:
  0.6 18.4 %copy-start = (bf16[1,128,2048]{2,1,0:T(8,128)(2,1)S(1)}, bf16[1,128,2048]{2,1,0:T(8,128)(2,1)}, u32[]{:S(2)}) copy-start(bf16[1,128,2048]{2,1,0:T(8,128)(2,1)} %dy_ref.5) | copy-start | bytes 1572868
  0.6 1.3 %copy-start.1 = (bf16[256,2048]{1,0:T(8,128)(2,1)S(1)}, bf16[256,2048]{1,0:T(8,128)(2,1)}, u32[]{:S(2)}) copy-start(bf16[256,2048]{1,0:T(8,128)(2,1)} %refs_0_.1) | copy-start | bytes 3145732
  1.9 0.9 %copy-start.3 = (bf16[1,128,1024]{2,1,0:T(8,128)(2,1)S(1)}, bf16[1,128,1024]{2,1,0:T(8,128)(2,1)}, u32[]{:S(2)}) copy-start(bf16[1,128,1024]{2,1,0:T(8,128)(2,1)} %k_ref.7) | copy-start | bytes 786436
  2.9 0.9 %copy-start.5 = (bf16[1,128,1024]{2,1,0:T(8,128)(2,1)S(1)}, bf16[1,128,1024]{2,1,0:T(8,128)(2,1)}, u32[]{:S(2)}) copy-start(bf16[1,128,1024]{2,1,0:T(8,128)(2,1)} %v_ref.7) | copy-start | bytes 786436
  3.8 15.2 %copy-start.2 = (bf16[256,2048]{1,0:T(8,128)(2,1)S(1)}, bf16[256,2048]{1,0:T(8,128)(2,1)}, u32[]{:S(2)}) copy-start(bf16[256,2048]{1,0:T(8,128)(2,1)} %refs_0_.1) | copy-start | bytes 3145732
  4.9 10.6 %copy-start.10 = (s32[8,4]{0,1:T(4,128)S(1)}, s32[8,4]{0,1:T(4,128)}, u32[]{:S(2)}) copy-start(s32[8,4]{0,1:T(4,128)} %param.12) | copy-start | bytes 388
  4.9 9.1 %collective-permute-start.2 = (bf16[128,2048]{1,0:T(8,128)(2,1)S(1)}, bf16[128,2048]{1,0:T(8,128)(2,1)}, u32[]{:S(2)}, u32[]{:S(2)}) collective-permute-start(bf16[128,2048]{1,0:T(8,128)(2,1)S(1)} %get-tuple-element.27), channel_id=1, source_target_pairs={{0,1},{1,0},{2,3},{3,2},{4,6},{5,7},{6,4},{7,5},{8,9},{9,8},{10,11... | collective-permute-start | bytes 1572872 | tf_op jit(solution)/shard_map/ppermute | solution.py:250
  7.0 8.5 %collective-permute-start = (bf16[2,128,1024]{2,1,0:T(8,128)(2,1)}, bf16[2,128,1024]{2,1,0:T(8,128)(2,1)S(1)}, u32[]{:S(2)}, u32[]{:S(2)}) collective-permute-start(bf16[2,128,1024]{2,1,0:T(8,128)(2,1)} %get-tuple-element.26), channel_id=1, source_target_pairs={{0,4},{4,0},{8,12},{12,8},{16,20},{20,16},{24,28},{28,24},{1,5},{5... | collective-permute-start | bytes 1572872 | tf_op jit(solution)/shard_map/ppermute | solution.py:262
  8.0 11.1 %collective-permute-start.1 = (bf16[2,128,1024]{2,1,0:T(8,128)(2,1)}, bf16[2,128,1024]{2,1,0:T(8,128)(2,1)S(1)}, u32[]{:S(2)}, u32[]{:S(2)}) collective-permute-start(bf16[2,128,1024]{2,1,0:T(8,128)(2,1)} %get-tuple-element.26), channel_id=1, source_target_pairs={{4,8},{8,4},{12,16},{16,12},{20,24},{24,20},{5,9},{9,5},{13,17},{1... | collective-permute-start | bytes 1572872 | tf_op jit(solution)/shard_map/ppermute | solution.py:262
  11.1 8.0 %copy-start.9 = (s32[1,8]{1,0:T(1,128)S(1)}, s32[1,8]{1,0:T(1,128)}, u32[]{:S(2)}) copy-start(s32[1,8]{1,0:T(1,128)} %val_ref.5) | copy-start | bytes 100
  11.1 17.0 %collective-permute-start.7 = (bf16[128,2048]{1,0:T(8,128)(2,1)}, bf16[128,2048]{1,0:T(8,128)(2,1)}, u32[]{:S(2)}, u32[]{:S(2)}) collective-permute-start(bf16[128,2048]{1,0:T(8,128)(2,1)} %get-tuple-element.32), channel_id=1, source_target_pairs={{0,1},{1,0},{2,3},{3,2},{4,6},{5,7},{6,4},{7,5},{8,9},{9,8},{10,11... | collective-permute-start | bytes 1572872 | tf_op jit(solution)/shard_map/ppermute | solution.py:250
  14.0 16.7 %collective-permute-start.3 = (bf16[128,2048]{1,0:T(8,128)(2,1)}, bf16[128,2048]{1,0:T(8,128)(2,1)S(1)}, u32[]{:S(2)}, u32[]{:S(2)}) collective-permute-start(bf16[128,2048]{1,0:T(8,128)(2,1)} %collective-permute-done.2.refs_0_), channel_id=1, source_target_pairs={{0,2},{1,3},{2,0},{3,1},{4,5},{5,4},{6,7},{7,6},{8,10},{9,11},{10,... | collective-permute-start | bytes 1572872 | tf_op jit(solution)/shard_map/ppermute | solution.py:250
  19.1 1.0 %copy-start.4 = (bf16[1,128,1024]{2,1,0:T(8,128)(2,1)S(1)}, bf16[1,128,1024]{2,1,0:T(8,128)(2,1)}, u32[]{:S(2)}) copy-start(bf16[1,128,1024]{2,1,0:T(8,128)(2,1)} %k_ref.7) | copy-start | bytes 786436
  20.0 0.9 %copy-start.6 = (bf16[1,128,1024]{2,1,0:T(8,128)(2,1)S(1)}, bf16[1,128,1024]{2,1,0:T(8,128)(2,1)}, u32[]{:S(2)}) copy-start(bf16[1,128,1024]{2,1,0:T(8,128)(2,1)} %v_ref.7) | copy-start | bytes 786436
  21.9 11.6 %copy-start.8 = (bf16[1,128,1024]{2,1,0:T(8,128)(2,1)S(1)}, bf16[1,128,1024]{2,1,0:T(8,128)(2,1)}, u32[]{:S(2)}) copy-start(bf16[1,128,1024]{2,1,0:T(8,128)(2,1)} %q_ref.5) | copy-start | bytes 786436
  24.3 3.8 %collective-permute-start.8 = (bf16[2,128,256]{2,1,0:T(8,128)(2,1)S(1)}, bf16[2,128,256]{2,1,0:T(8,128)(2,1)S(1)}, u32[]{:S(2)}, u32[]{:S(2)}) collective-permute-start(bf16[2,128,256]{2,1,0:T(8,128)(2,1)S(1)} %get-tuple-element.35), channel_id=1, source_target_pairs={{0,4},{4,0},{8,12},{12,8},{16,20},{20,16},{24,28},{28,24},{1,5},{5... | collective-permute-start | bytes 393224 | tf_op jit(solution)/shard_map/ppermute | solution.py:256
  24.4 6.3 %collective-permute-start.9 = (bf16[2,128,256]{2,1,0:T(8,128)(2,1)S(1)}, bf16[2,128,256]{2,1,0:T(8,128)(2,1)S(1)}, u32[]{:S(2)}, u32[]{:S(2)}) collective-permute-start(bf16[2,128,256]{2,1,0:T(8,128)(2,1)S(1)} %get-tuple-element.36), channel_id=1, source_target_pairs={{4,8},{8,4},{12,16},{16,12},{20,24},{24,20},{5,9},{9,5},{13,17},{1... | collective-permute-start | bytes 393224 | tf_op jit(solution)/shard_map/ppermute | solution.py:256
  28.0 3.2 %collective-permute-start.10 = (bf16[128,2048]{1,0:T(8,128)(2,1)}, bf16[128,2048]{1,0:T(8,128)(2,1)S(1)}, u32[]{:S(2)}, u32[]{:S(2)}) collective-permute-start(bf16[128,2048]{1,0:T(8,128)(2,1)} %collective-permute-done.2.refs_0_), channel_id=1, source_target_pairs={{0,4},{4,0},{8,12},{12,8},{16,20},{20,16},{24,28},{28,24},{1,5},{5... | collective-permute-start | bytes 1572872 | tf_op jit(solution)/shard_map/ppermute | solution.py:271
  30.7 2.8 %collective-permute-start.11 = (bf16[128,2048]{1,0:T(8,128)(2,1)}, bf16[128,2048]{1,0:T(8,128)(2,1)S(1)}, u32[]{:S(2)}, u32[]{:S(2)}) collective-permute-start(bf16[128,2048]{1,0:T(8,128)(2,1)} %collective-permute-done.7.refs_1_), channel_id=1, source_target_pairs={{0,4},{4,0},{8,12},{12,8},{16,20},{20,16},{24,28},{28,24},{1,5},{5... | collective-permute-start | bytes 1572872 | tf_op jit(solution)/shard_map/ppermute | solution.py:271
  30.7 10.9 %collective-permute-start.4 = (bf16[128,2048]{1,0:T(8,128)(2,1)S(1)}, bf16[128,2048]{1,0:T(8,128)(2,1)S(1)}, u32[]{:S(2)}, u32[]{:S(2)}) collective-permute-start(bf16[128,2048]{1,0:T(8,128)(2,1)S(1)} %collective-permute-done.3.refs_0_), channel_id=1, source_target_pairs={{0,4},{4,0},{8,12},{12,8},{16,20},{20,16},{24,28},{28,24},{1,5},{5... | collective-permute-start | bytes 1572872 | tf_op jit(solution)/shard_map/ppermute | solution.py:278
  38.5 9.2 %collective-permute-start.12 = (bf16[2,128,512]{2,1,0:T(8,128)(2,1)S(1)}, bf16[2,128,512]{2,1,0:T(8,128)(2,1)S(1)}, u32[]{:S(2)}, u32[]{:S(2)}) collective-permute-start(bf16[2,128,512]{2,1,0:T(8,128)(2,1)S(1)} %get-tuple-element.44), channel_id=1, source_target_pairs={{0,4},{4,0},{8,12},{12,8},{16,20},{20,16},{24,28},{28,24},{1,5},{5... | collective-permute-start | bytes 786440 | tf_op jit(solution)/shard_map/ppermute | solution.py:256
  38.7 9.0 %collective-permute-start.13 = (bf16[2,128,512]{2,1,0:T(8,128)(2,1)S(1)}, bf16[2,128,512]{2,1,0:T(8,128)(2,1)S(1)}, u32[]{:S(2)}, u32[]{:S(2)}) collective-permute-start(bf16[2,128,512]{2,1,0:T(8,128)(2,1)S(1)} %get-tuple-element.45), channel_id=1, source_target_pairs={{4,8},{8,4},{12,16},{16,12},{20,24},{24,20},{5,9},{9,5},{13,17},{1... | collective-permute-start | bytes 786440 | tf_op jit(solution)/shard_map/ppermute | solution.py:256
  44.1 4.6 %collective-permute-start.5 = (bf16[2,128,256]{2,1,0:T(8,128)(2,1)S(1)}, bf16[2,128,256]{2,1,0:T(8,128)(2,1)S(1)}, u32[]{:S(2)}, u32[]{:S(2)}) collective-permute-start(bf16[2,128,256]{2,1,0:T(8,128)(2,1)S(1)} %get-tuple-element.30), channel_id=1, source_target_pairs={{0,4},{4,0},{8,12},{12,8},{16,20},{20,16},{24,28},{28,24},{1,5},{5... | collective-permute-start | bytes 393224 | tf_op jit(solution)/shard_map/ppermute | solution.py:256
  44.2 6.3 %collective-permute-start.6 = (bf16[2,128,256]{2,1,0:T(8,128)(2,1)S(1)}, bf16[2,128,256]{2,1,0:T(8,128)(2,1)S(1)}, u32[]{:S(2)}, u32[]{:S(2)}) collective-permute-start(bf16[2,128,256]{2,1,0:T(8,128)(2,1)S(1)} %get-tuple-element.31), channel_id=1, source_target_pairs={{4,8},{8,4},{12,16},{16,12},{20,24},{24,20},{5,9},{9,5},{13,17},{1... | collective-permute-start | bytes 393224 | tf_op jit(solution)/shard_map/ppermute | solution.py:256
  (1 other events, 0.9 us)

commit v3 on v2

--- a/solution.py
+++ b/solution.py
@@ -14,10 +14,12 @@
 NT = (((1,), (1,)), ((), ()))
 NN = (((1,), (0,)), ((), ()))
 TN = (((0,), (0,)), ((), ()))
+HBM = pl.BlockSpec(memory_space=pltpu.HBM)
 ANY = pl.BlockSpec(memory_space=pl.ANY)
 VMEM = pl.BlockSpec(memory_space=pltpu.VMEM)
 SMEM = pl.BlockSpec(memory_space=pltpu.SMEM)
 PARAMS = pltpu.CompilerParams(vmem_limit_bytes=40 * 2**20)
+WIDE = pltpu.CompilerParams(vmem_limit_bytes=58 * 2**20)
 
 
 def dot(a, b, dims):
@@ -59,12 +61,40 @@
     return pl.pallas_call(
         prep_kernel,
         out_shape=(half, half, jax.ShapeDtypeStruct((2,) + keys.shape[1:], BF16)),
-        in_specs=[ANY] * 3,
+        in_specs=[HBM] * 3,
         out_specs=(ANY,) * 3,
         scratch_shapes=[pltpu.SemaphoreType.DMA((4,))],
-        compiler_params=PARAMS,
+        compiler_params=WIDE,
         name="prep",
     )(w_out, keys, values)
+
+
+def stage_kernel(dy_ref, q_ref, w_ref, turned_ref, q_out, w_rows, dy, sems):
+    pairs = [(dy_ref.at[0], dy), (q_ref.at[0], q_out), (w_ref, w_rows)]
+    copies = [pltpu.make_async_copy(s, d, sems.at[i]) for i, (s, d) in enumerate(pairs)]
+    for copy in copies:
+        copy.start()
+    copies[0].wait()
+    turned_ref[...] = dy[...].T
+    for copy in copies[1:]:
+        copy.wait()
+
+
+def stage(d_out, queries, w_out):
+    tok, depth = d_out.shape[1:]
+    return pl.pallas_call(
+        stage_kernel,
+        out_shape=(
+            jax.ShapeDtypeStruct((depth, tok), BF16),
+            jax.ShapeDtypeStruct(queries.shape[1:], BF16),
+            jax.ShapeDtypeStruct(w_out.shape, BF16),
+        ),
+        in_specs=[HBM] * 3,
+        out_specs=(VMEM,) * 3,
+        scratch_shapes=[pltpu.VMEM((tok, depth), BF16), pltpu.SemaphoreType.DMA((3,))],
+        compiler_params=PARAMS,
+        name="stage",
+    )(d_out, queries, w_out)
 
 
 def key_limits(pat_ref, val_ref):
@@ -94,89 +124,65 @@
     )
 
 
-def attention_kernel(chunks, pieces, pat_ref, val_ref, q_ref, k_ref, v_ref, core_ref, far_ref, dy_ref, *refs):
+def columns(chunk):
+    return pl.ds(pl.multiple_of(chunk * PAIR, PAIR), PAIR)
+
+
+def attention_kernel(steps, pat_ref, val_ref, dy_ref, q_ref, own_kv, core_kv, far_kv, *refs):
     core, group = place()
-    slots = chunks(core, group)
-    plan = pieces(core)
-    n_w = len(refs) - 4 - 5
-    w_refs = refs[:n_w]
-    dq_ref, own_ref, to_core_ref, to_far_ref, dy, w, q, kv, sems = refs[n_w:]
+    w_refs = refs[:-4]
+    dq_ref, own_ref, to_core_ref, to_far_ref = refs[-4:]
     scale = HD ** (-0.5)
-    tok = q.shape[1]
-    copies = []
-
-    def fetch(source, target):
-        copy = pltpu.make_async_copy(source, target, sems.at[len(copies)])
-        copy.start()
-        copies.append(copy)
-        return copy
-
-    first = [fetch(dy_ref.at[0], dy)]
-    waits = []
-    for slot, (chunk, _) in enumerate(slots):
-        wanted = [
-            fetch(
-                w_refs[index].at[pl.ds(row, rows), :],
-                w.at[slot, pl.ds(to, rows), :],
-            )
-            for index, row, to, rows in plan[slot]
-        ]
-        cols = pl.ds(pl.multiple_of(chunk * PAIR, PAIR), PAIR)
-        wanted.append(fetch(q_ref.at[0, :, cols], q.at[slot]))
-        for side, source in enumerate((k_ref, v_ref)):
-            wanted.append(fetch(source.at[0, :, cols], kv.at[slot, side, pl.ds(0, tok), :]))
-            wanted.append(fetch(core_ref.at[side, :, cols], kv.at[slot, side, pl.ds(tok, tok), :]))
-            wanted.append(fetch(far_ref.at[side, :, cols], kv.at[slot, side, pl.ds(2 * tok, tok), :]))
-        waits.append(wanted)
-
+    tok = q_ref.shape[0]
     rows = lax.broadcasted_iota(jnp.int32, (tok, PAIR), 0)
     open_keys = jnp.concatenate([rows < limit for limit in key_limits(pat_ref, val_ref)], axis=0)
-    for slot in range(len(slots)):
-        for copy in first + waits[slot]:
-            copy.wait()
-        first = []
-        cols = pl.ds(pl.multiple_of(slots[slot][1] * PAIR, PAIR), PAIR)
-        d = diagonal(dot(dy[...], w[slot], NT).astype(BF16))
-        qd = diagonal(q[slot])
-        k, v = kv[slot, 0], kv[slot, 1]
+    for chunk, slot, halves, lead in steps(core, group):
+        cols, dest = columns(chunk), columns(slot)
+        w = jnp.concatenate([w_refs[i][row : row + HD, :] for i, row in halves], axis=0)
+        turned = dot(w, dy_ref[...], NN)
+        one, two = turned[:HD], turned[HD:]
+        if not isinstance(lead, int):
+            one, two = jnp.where(lead == 0, one, two), jnp.where(lead == 0, two, one)
+        zero = jnp.zeros_like(one)
+        d = jnp.concatenate(
+            [jnp.concatenate([one, zero], axis=1), jnp.concatenate([zero, two], axis=1)], axis=0
+        ).astype(BF16)
+        qd = diagonal(q_ref[:, cols])
+        k, v = (
+            jnp.concatenate([ref[side, :, cols] for ref in (own_kv, core_kv, far_kv)], axis=0)
+            for side in range(2)
+        )
         score = jnp.where(open_keys, dot(k, qd, NT) * scale, -jnp.inf)
         top = jnp.max(score, axis=0, keepdims=True)
         raised = jnp.exp(score - top)
         prob = raised * (1.0 / jnp.sum(raised, axis=0, keepdims=True))
         prob_b = prob.astype(BF16)
-        d_prob = dot(v, d, NT)
+        d_prob = dot(v, d, NN)
         delta = jnp.sum(prob_b.astype(F32) * d_prob, axis=0, keepdims=True)
         d_score = (prob * (d_prob - delta)).astype(BF16)
         both = dot(d_score, k, TN) * scale
-        dq_ref[:, cols] = jnp.concatenate([both[:tok, :HD], both[tok:, HD:]], axis=1).astype(BF16)
-        for side, grad in enumerate((dot(d_score, qd, NN) * scale, dot(prob_b, d, NN))):
-            own_ref[side, :, cols] = grad[:tok]
-            to_core_ref[side, :, cols] = grad[tok : 2 * tok].astype(BF16)
-            to_far_ref[side, :, cols] = grad[2 * tok :].astype(BF16)
-
-
-def attention(name, chunks, pieces, weights, pattern, valid, q, k, v, kv_core, kv_far, d_out):
-    count = len(chunks(0, 0))
-    tok, depth = q.shape[1], d_out.shape[2]
+        dq_ref[:, dest] = jnp.concatenate([both[:tok, :HD], both[tok:, HD:]], axis=1).astype(BF16)
+        for side, grad in enumerate((dot(d_score, qd, NN) * scale, dot(prob_b, d, NT))):
+            own_ref[side, :, dest] = grad[:tok]
+            to_core_ref[side, :, dest] = grad[tok : 2 * tok].astype(BF16)
+            to_far_ref[side, :, dest] = grad[2 * tok :].astype(BF16)
+
+
+def attention(name, steps, weights, pattern, valid, staged, halo):
+    count = len(steps(0, 0))
+    turned, q = staged
+    depth, tok = turned.shape
     width = count * PAIR
-    n_copies = 1 + sum(len(slot) + 7 for slot in pieces(0))
     return pl.pallas_call(
-        functools.partial(attention_kernel, chunks, pieces),
+        functools.partial(attention_kernel, steps),
         out_shape=(
             jax.ShapeDtypeStruct((tok, width), BF16),
             jax.ShapeDtypeStruct((2, tok, width), F32),
             jax.ShapeDtypeStruct((2, tok, width), BF16),
             jax.ShapeDtypeStruct((2, tok, width), BF16),
         ),
-        in_specs=[SMEM] * 2 + [ANY] * (6 + len(weights)),
+        in_specs=[SMEM] * 2 + [VMEM] * (5 + len(weights)),
         out_specs=(VMEM,) * 4,
-        scratch_shapes=[
-            pltpu.VMEM((tok, depth), BF16),
-            pltpu.VMEM((count, PAIR, depth), BF16),
-            pltpu.VMEM((count, tok, PAIR), BF16),
-            pltpu.VMEM((count, 2, 3 * tok, PAIR), BF16),
-            pltpu.SemaphoreType.DMA((n_copies,)),
-        ],
         cost_estimate=pl.CostEstimate(
             flops=count * 4 * tok * HD * (depth + 15 * HD),
             bytes_accessed=count * 1_800_000,
@@ -184,7 +190,7 @@
         ),
         compiler_params=PARAMS,
         name=name,
-    )(pattern, valid, q, k, v, kv_core, kv_far, d_out, *weights)
+    )(pattern, valid, turned, q, *halo, *weights)
 
 
 def finish_kernel(chunks, n_parts, n_old, *refs):
@@ -249,45 +255,44 @@
         ]
         return lax.ppermute(x, ("seq", "fsdp"), pairs)
 
-    def part(name, chunks, pieces, weights, halo):
-        dq, own, to_core, to_far = attention(
-            name, chunks, pieces, weights, pattern, valid, queries, keys, values, *halo, d_out
-        )
+    def part(name, steps, weights):
+        dq, own, to_core, to_far = attention(name, steps, weights, pattern, valid, staged, halo)
         return dq, own, near(to_core), far(to_far)
 
     first, second, kv = prep(w_out, keys, values)
+    *staged, w_rows = stage(d_out, queries, w_out)
     if n_fsdp == 4 and n_chunks == 4 and w_out.shape[0] == PAIR:
+        second, *staged = lax.optimization_barrier((second, *staged))
         got_a = cross(first, (1, 2))
         got_b = cross(second, (1, 2))
-        halo = near(kv), far(kv)
-        part_a = part("heads_own", lambda core, group: [(group, 0)], lambda core: [[(0, 0, 0, PAIR)]], [w_out], halo)
+        halo = kv, near(kv), far(kv)
         got_d = cross(got_a, (2, 1))
+        part_a = part("heads_own", lambda core, group: [(group, 0, ((0, 0), (0, HD)), 0)], [w_rows])
         got_b, part_a = lax.optimization_barrier((got_b, part_a))
-        halves = lambda first, at: [(first, 0, at * HD, HD), (first + 1, 0, (1 - at) * HD, HD)]
         part_b = part(
             "heads_side",
-            lambda core, group: [(group ^ (1 + core), core), (group ^ (2 - core), 1 - core)],
-            lambda core: [halves(0, core), halves(2, 1 - core)],
+            lambda core, group: [
+                (group ^ (1 + core), core, ((0, 0), (1, 0)), core),
+                (group ^ (2 - core), 1 - core, ((2, 0), (3, 0)), 1 - core),
+            ],
             [got_a, got_b, near(got_a), near(got_b)],
-            halo,
         )
         part_c = part(
             "heads_far",
-            lambda core, group: [(group ^ 3, 0)],
-            lambda core: [halves(0, core)],
+            lambda core, group: [(group ^ 3, 0, ((0, 0), (1, 0)), core)],
             [got_d, near(got_d)],
-            halo,
         )
         ab = lambda core, group: [group, group ^ 1, group ^ 2]
         last = lambda core, group: [group ^ 3]
         old = finish("finish_first", ab, [part_a, part_b], queries.shape)
         return finish("finish_last", last, [part_c], queries.shape, old)
     full = lax.all_gather(w_out, "fsdp", axis=0, tiled=True)
-    halo = near(kv), far(kv)
-    chunks = lambda core, group: [(slot, slot) for slot in range(n_chunks)]
+    halo = kv, near(kv), far(kv)
     order = lambda core, group: list(range(n_chunks))
-    pieces = lambda core: [[(0, slot * PAIR, 0, PAIR)] for slot in range(n_chunks)]
-    return finish("finish", order, [part("heads_all", chunks, pieces, [full], halo)], queries.shape)
+    steps = lambda core, group: [
+        (i, i, ((0, i * PAIR), (0, i * PAIR + HD)), 0) for i in range(n_chunks)
+    ]
+    return finish("finish", order, [part("heads_all", steps, [full])], queries.shape)
 
 
 def solution(mesh):

time: 51.6 us -> 90.4 us (1.75)
  Pallas kernels: 12.6 us -> 57.9 us
  local copies, waits for them, and re-layouts: 6.12 us -> 1.05 us
  waiting for transfers between devices: 11.8 us -> 9.67 us
    pallas_call x1, Pallas kernels: 1.06 us -> 48.8 us  [prep(): pl.pallas_call(prep_kernel, out_shape=(half, half, jax.ShapeDtypeStruct((...]
    unnamed x23 -> x13, local copies, waits for them, and re-layouts: 6.12 us -> 1.05 us
    pallas_call x3 -> x4, Pallas kernels: 9.85 us -> 7.46 us  [the longest x3 7.12 us: attention(): pl.pallas_call(functools.partial(attention_kernel, steps), out_shape=(jax...]
    ppermute x3, waiting for transfers between devices: 1.64 us -> 0.39 us  [cross(): return lax.ppermute(x, ('seq', 'fsdp'), pairs)]
  transfers between devices with their start and end apart: 14 -> 14, of which waited for: 5 -> 5; matrix products, arithmetic and copies ran while one was open for 0% -> 0% of each run, Pallas kernels for 21% -> 9%
where the time goes in v3:
time: 90.4 us; the launch traced here: 90.1 us
  Pallas kernels  57.9 us (64%)
  starting transfers between devices  20.6 us (23%)
  waiting for transfers between devices  9.67 us (11%)
  local copies, waits for them, and re-layouts  1.05 us (1%)
    pallas_call x1, Pallas kernels, prep(): pl.pallas_call(prep_kernel, out_shape=(half, half, jax.ShapeDtypeStruct((...  48.8 us
    ppermute x6, starting transfers between devices, part(): return (dq, own, near(to_core), far(to_far))  11.1 us
    pallas_call x3, Pallas kernels, attention(): pl.pallas_call(functools.partial(attention_kernel, steps), out_shape=(jax...  7.12 us
    ppermute x3, starting transfers between devices, cross(): return lax.ppermute(x, ('seq', 'fsdp'), pairs)  4.87 us
    ppermute x6, waiting for transfers between devices, part(): return (dq, own, near(to_core), far(to_far))  4.35 us
    ppermute x2, starting transfers between devices, body(): halo = (kv, near(kv), far(kv))  4.14 us
    ppermute x2, waiting for transfers between devices, body(): halo = (kv, near(kv), far(kv))  3.33 us
  transfers between devices with their start and end apart: 14, of which 5 were waited for; matrix products, arithmetic and copies ran while one was open for 0% of the time, Pallas kernels for 9%

profile of v3, /device:TPU:1, one launch (start us, length us, event | category | flops | bytes accessed | tf_op | source)
XLA Modules:
  0.0 90.1 jit_solution(3270005327346037439)
XLA Ops:
  0.7 48.8 %prep.1 = (bf16[128,2048]{1,0:T(8,128)(2,1)}, bf16[128,2048]{1,0:T(8,128)(2,1)}, bf16[2,128,1024]{2,1,0:T(8,128)(2,1)}) custom-call(bf16[256,2048]{1,0:T(8,128)(2,1)} %w_ref.3, bf16[1,128,1024]{2,1,0:T(8,128)(2,1)} %k_ref.1, bf16[1,128,1024]{2,1,0:T(8,128)(2,1)} %v_ref.1), custom_call_target="tpu_custom_call" | custom-call | tf_op jit(solution)/shard_map/prep/pallas_call | solution.py:61
  49.5 2.1 %collective-permute-start.2 = (bf16[128,2048]{1,0:T(8,128)(2,1)}, bf16[128,2048]{1,0:T(8,128)(2,1)}, u32[]{:S(2)}, u32[]{:S(2)}) collective-permute-start(bf16[128,2048]{1,0:T(8,128)(2,1)} %get-tuple-element.38), channel_id=1, source_target_pairs={{0,1},{1,0},{2,3},{3,2},{4,6},{5,7},{6,4},{7,5},{8,9},{9,8},{10,11... | collective-permute-start | bytes 1572872 | tf_op jit(solution)/shard_map/ppermute | solution.py:256
  51.6 0.9 %collective-permute-start = (bf16[2,128,1024]{2,1,0:T(8,128)(2,1)}, bf16[2,128,1024]{2,1,0:T(8,128)(2,1)S(1)}, u32[]{:S(2)}, u32[]{:S(2)}) collective-permute-start(bf16[2,128,1024]{2,1,0:T(8,128)(2,1)} %get-tuple-element.37.own_kv), channel_id=1, source_target_pairs={{0,4},{4,0},{8,12},{12,8},{16,20},{20,16},{24,28},{28,24},{1,5},{5... | collective-permute-start | bytes 1572872 | tf_op jit(solution)/shard_map/ppermute | solution.py:268
  52.5 3.2 %collective-permute-start.1 = (bf16[2,128,1024]{2,1,0:T(8,128)(2,1)}, bf16[2,128,1024]{2,1,0:T(8,128)(2,1)S(1)}, u32[]{:S(2)}, u32[]{:S(2)}) collective-permute-start(bf16[2,128,1024]{2,1,0:T(8,128)(2,1)} %get-tuple-element.37.own_kv), channel_id=1, source_target_pairs={{4,8},{8,4},{12,16},{16,12},{20,24},{24,20},{5,9},{9,5},{13,17},{1... | collective-permute-start | bytes 1572872 | tf_op jit(solution)/shard_map/ppermute | solution.py:268
  55.8 0.9 %copy-done.3 = bf16[1,128,1024]{2,1,0:T(8,128)(2,1)S(1)} copy-done((bf16[1,128,1024]{2,1,0:T(8,128)(2,1)S(1)}, bf16[1,128,1024]{2,1,0:T(8,128)(2,1)}, u32[]{:S(2)}) %copy-start.3) | copy-done | bytes 262168
  56.7 0.3 stage.1
  57.1 1.3 %collective-permute-start.7 = (bf16[128,2048]{1,0:T(8,128)(2,1)}, bf16[128,2048]{1,0:T(8,128)(2,1)}, u32[]{:S(2)}, u32[]{:S(2)}) collective-permute-start(bf16[128,2048]{1,0:T(8,128)(2,1)} %get-tuple-element.43), channel_id=1, source_target_pairs={{0,1},{1,0},{2,3},{3,2},{4,6},{5,7},{6,4},{7,5},{8,9},{9,8},{10,11... | collective-permute-start | bytes 1572872 | tf_op jit(solution)/shard_map/ppermute | solution.py:256
  58.4 0.4 collective-permute-done.2.refs_0_
  58.8 1.4 %collective-permute-start.3 = (bf16[128,2048]{1,0:T(8,128)(2,1)}, bf16[128,2048]{1,0:T(8,128)(2,1)}, u32[]{:S(2)}, u32[]{:S(2)}) collective-permute-start(bf16[128,2048]{1,0:T(8,128)(2,1)} %collective-permute-done.2.refs_0_), channel_id=1, source_target_pairs={{0,2},{1,3},{2,0},{3,1},{4,5},{5,4},{6,7},{7,6},{8,10},{9,11},{10,... | collective-permute-start | bytes 1572872 | tf_op jit(solution)/shard_map/ppermute | solution.py:256
  60.2 0.1 copy.13.pat_ref
  60.3 3.3 %collective-permute-done.1.far_kv = bf16[2,128,1024]{2,1,0:T(8,128)(2,1)S(1)} collective-permute-done((bf16[2,128,1024]{2,1,0:T(8,128)(2,1)}, bf16[2,128,1024]{2,1,0:T(8,128)(2,1)S(1)}, u32[]{:S(2)}, u32[]{:S(2)}) %collective-permute-start.1) | collective-permute-done | bytes 524320 | tf_op jit(solution)/shard_map/ppermute | solution.py:268
  63.6 1.7 %heads_own.1 = (bf16[128,256]{1,0:T(8,128)(2,1)S(1)}, f32[2,128,256]{2,1,0:T(8,128)S(1)}, bf16[2,128,256]{2,1,0:T(8,128)(2,1)S(1)}, bf16[2,128,256]{2,1,0:T(8,128)(2,1)S(1)}) custom-call(s32[8,4]{1,0:T(8,128)S(1)} %copy.13.pat_ref, s32[1,8]{1,0:T(1,128)S(1)} %copy-done.4, bf16[2048,128]{1,0:T(8,128)(2,1)S(1)} %get-tuple-element.35.dy_ref, ...), custom_call_target="tpu_custom_call" | custom-call | flops 260046848 | bytes 1800000 | tf_op jit(solution)/shard_map/heads_own/pallas_call | solution.py:176
  65.4 3.6 %collective-permute-start.9 = (bf16[2,128,256]{2,1,0:T(8,128)(2,1)S(1)}, bf16[2,128,256]{2,1,0:T(8,128)(2,1)S(1)}, u32[]{:S(2)}, u32[]{:S(2)}) collective-permute-start(bf16[2,128,256]{2,1,0:T(8,128)(2,1)S(1)} %get-tuple-element.48), channel_id=1, source_target_pairs={{4,8},{8,4},{12,16},{16,12},{20,24},{24,20},{5,9},{9,5},{13,17},{1... | collective-permute-start | bytes 393224 | tf_op jit(solution)/shard_map/ppermute | solution.py:260
  69.1 2.6 %collective-permute-done.9.refs_3_ = bf16[2,128,256]{2,1,0:T(8,128)(2,1)S(1)} collective-permute-done((bf16[2,128,256]{2,1,0:T(8,128)(2,1)S(1)}, bf16[2,128,256]{2,1,0:T(8,128)(2,1)S(1)}, u32[]{:S(2)}, u32[]{:S(2)}) %collective-permute-start.9) | collective-permute-done | bytes 131104 | tf_op jit(solution)/shard_map/ppermute | solution.py:260
  71.7 0.5 collective-permute-start.4
  72.2 1.6 %collective-permute-done.11.refs_3_ = bf16[128,2048]{1,0:T(8,128)(2,1)S(1)} collective-permute-done((bf16[128,2048]{1,0:T(8,128)(2,1)}, bf16[128,2048]{1,0:T(8,128)(2,1)S(1)}, u32[]{:S(2)}, u32[]{:S(2)}) %collective-permute-start.11) | collective-permute-done | bytes 524320 | tf_op jit(solution)/shard_map/ppermute | solution.py:278
  73.8 3.3 %heads_side.1 = (bf16[128,512]{1,0:T(8,128)(2,1)S(1)}, f32[2,128,512]{2,1,0:T(8,128)S(1)}, bf16[2,128,512]{2,1,0:T(8,128)(2,1)S(1)}, bf16[2,128,512]{2,1,0:T(8,128)(2,1)S(1)}) custom-call(s32[8,4]{1,0:T(8,128)S(1)} %copy.13.pat_ref, s32[1,8]{1,0:T(1,128)S(1)} %copy-done.4, bf16[2048,128]{1,0:T(8,128)(2,1)S(1)} %get-tuple-element.35.dy_ref, ...), custom_call_target="tpu_custom_call" | custom-call | flops 520093696 | bytes 3600000 | tf_op jit(solution)/shard_map/heads_side/pallas_call | solution.py:176
  77.1 0.2 collective-permute-start.12
  77.3 3.6 %collective-permute-start.13 = (bf16[2,128,512]{2,1,0:T(8,128)(2,1)S(1)}, bf16[2,128,512]{2,1,0:T(8,128)(2,1)S(1)}, u32[]{:S(2)}, u32[]{:S(2)}) collective-permute-start(bf16[2,128,512]{2,1,0:T(8,128)(2,1)S(1)} %get-tuple-element.57), channel_id=1, source_target_pairs={{4,8},{8,4},{12,16},{16,12},{20,24},{24,20},{5,9},{9,5},{13,17},{1... | collective-permute-start | bytes 786440 | tf_op jit(solution)/shard_map/ppermute | solution.py:260
  80.9 2.1 %heads_far.1 = (bf16[128,256]{1,0:T(8,128)(2,1)S(1)}, f32[2,128,256]{2,1,0:T(8,128)S(1)}, bf16[2,128,256]{2,1,0:T(8,128)(2,1)S(1)}, bf16[2,128,256]{2,1,0:T(8,128)(2,1)S(1)}) custom-call(s32[8,4]{1,0:T(8,128)S(1)} %copy.13.pat_ref, s32[1,8]{1,0:T(1,128)S(1)} %copy-done.4, bf16[2048,128]{1,0:T(8,128)(2,1)S(1)} %get-tuple-element.35.dy_ref, ...), custom_call_target="tpu_custom_call" | custom-call | flops 260046848 | bytes 1800000 | tf_op jit(solution)/shard_map/heads_far/pallas_call | solution.py:176
  83.1 3.6 %collective-permute-start.6 = (bf16[2,128,256]{2,1,0:T(8,128)(2,1)S(1)}, bf16[2,128,256]{2,1,0:T(8,128)(2,1)S(1)}, u32[]{:S(2)}, u32[]{:S(2)}) collective-permute-start(bf16[2,128,256]{2,1,0:T(8,128)(2,1)S(1)} %get-tuple-element.42), channel_id=1, source_target_pairs={{4,8},{8,4},{12,16},{16,12},{20,24},{24,20},{5,9},{9,5},{13,17},{1... | collective-permute-start | bytes 393224 | tf_op jit(solution)/shard_map/ppermute | solution.py:260
  86.7 0.9 %finish_first.1 = (bf16[1,128,1024]{2,1,0:T(8,128)(2,1)}, bf16[1,128,1024]{2,1,0:T(8,128)(2,1)}, bf16[1,128,1024]{2,1,0:T(8,128)(2,1)}) custom-call(bf16[128,256]{1,0:T(8,128)(2,1)S(1)} %get-tuple-element.49.refs_0_, f32[2,128,256]{2,1,0:T(8,128)S(1)} %get-tuple-element.50.refs_1_, bf16[2,128,256]{2,1,0:T(8,128)(2,1)S(1)} %collective-permute-done.8.refs_2_, ...), custom_call_target="tpu_custom_call" | custom-call | tf_op jit(solution)/shard_map/finish_first/pallas_call | solution.py:229
  87.7 1.7 %collective-permute-done.6.refs_3_ = bf16[2,128,256]{2,1,0:T(8,128)(2,1)S(1)} collective-permute-done((bf16[2,128,256]{2,1,0:T(8,128)(2,1)S(1)}, bf16[2,128,256]{2,1,0:T(8,128)(2,1)S(1)}, u32[]{:S(2)}, u32[]{:S(2)}) %collective-permute-start.6) | collective-permute-done | bytes 131104 | tf_op jit(solution)/shard_map/ppermute | solution.py:260
  89.4 0.7 finish_last.1
  (24 shorter events, 0.3 us)
Async XLA Ops:
  0.6 55.1 %copy-start.1 = (bf16[256,2048]{1,0:T(8,128)(2,1)S(1)}, bf16[256,2048]{1,0:T(8,128)(2,1)}, u32[]{:S(2)}) copy-start(bf16[256,2048]{1,0:T(8,128)(2,1)} %w_ref.3) | copy-start | bytes 3145732
  0.6 55.1 %copy-start.2 = (bf16[1,128,2048]{2,1,0:T(8,128)(2,1)S(1)}, bf16[1,128,2048]{2,1,0:T(8,128)(2,1)}, u32[]{:S(2)}) copy-start(bf16[1,128,2048]{2,1,0:T(8,128)(2,1)} %dy_ref.1) | copy-start | bytes 1572868
  49.5 9.3 %collective-permute-start.2 = (bf16[128,2048]{1,0:T(8,128)(2,1)}, bf16[128,2048]{1,0:T(8,128)(2,1)}, u32[]{:S(2)}, u32[]{:S(2)}) collective-permute-start(bf16[128,2048]{1,0:T(8,128)(2,1)} %get-tuple-element.38), channel_id=1, source_target_pairs={{0,1},{1,0},{2,3},{3,2},{4,6},{5,7},{6,4},{7,5},{8,9},{9,8},{10,11... | collective-permute-start | bytes 1572872 | tf_op jit(solution)/shard_map/ppermute | solution.py:256
  51.6 12.0 %copy-start = (bf16[2,128,1024]{2,1,0:T(8,128)(2,1)S(1)}, bf16[2,128,1024]{2,1,0:T(8,128)(2,1)}, u32[]{:S(2)}) copy-start(bf16[2,128,1024]{2,1,0:T(8,128)(2,1)} %get-tuple-element.37.own_kv) | copy-start | bytes 1572868
  51.6 8.7 %collective-permute-start = (bf16[2,128,1024]{2,1,0:T(8,128)(2,1)}, bf16[2,128,1024]{2,1,0:T(8,128)(2,1)S(1)}, u32[]{:S(2)}, u32[]{:S(2)}) collective-permute-start(bf16[2,128,1024]{2,1,0:T(8,128)(2,1)} %get-tuple-element.37.own_kv), channel_id=1, source_target_pairs={{0,4},{4,0},{8,12},{12,8},{16,20},{20,16},{24,28},{28,24},{1,5},{5... | collective-permute-start | bytes 1572872 | tf_op jit(solution)/shard_map/ppermute | solution.py:268
  52.5 11.1 %collective-permute-start.1 = (bf16[2,128,1024]{2,1,0:T(8,128)(2,1)}, bf16[2,128,1024]{2,1,0:T(8,128)(2,1)S(1)}, u32[]{:S(2)}, u32[]{:S(2)}) collective-permute-start(bf16[2,128,1024]{2,1,0:T(8,128)(2,1)} %get-tuple-element.37.own_kv), channel_id=1, source_target_pairs={{4,8},{8,4},{12,16},{16,12},{20,24},{24,20},{5,9},{9,5},{13,17},{1... | collective-permute-start | bytes 1572872 | tf_op jit(solution)/shard_map/ppermute | solution.py:268
  55.8 1.0 %copy-start.3 = (bf16[1,128,1024]{2,1,0:T(8,128)(2,1)S(1)}, bf16[1,128,1024]{2,1,0:T(8,128)(2,1)}, u32[]{:S(2)}) copy-start(bf16[1,128,1024]{2,1,0:T(8,128)(2,1)} %q_ref.1) | copy-start | bytes 786436
  57.1 3.1 %copy-start.5 = (s32[8,4]{0,1:T(4,128)S(1)}, s32[8,4]{0,1:T(4,128)}, u32[]{:S(2)}) copy-start(s32[8,4]{0,1:T(4,128)} %param.12) | copy-start | bytes 388
  57.1 12.0 %collective-permute-start.7 = (bf16[128,2048]{1,0:T(8,128)(2,1)}, bf16[128,2048]{1,0:T(8,128)(2,1)}, u32[]{:S(2)}, u32[]{:S(2)}) collective-permute-start(bf16[128,2048]{1,0:T(8,128)(2,1)} %get-tuple-element.43), channel_id=1, source_target_pairs={{0,1},{1,0},{2,3},{3,2},{4,6},{5,7},{6,4},{7,5},{8,9},{9,8},{10,11... | collective-permute-start | bytes 1572872 | tf_op jit(solution)/shard_map/ppermute | solution.py:256
  58.8 12.9 %collective-permute-start.3 = (bf16[128,2048]{1,0:T(8,128)(2,1)}, bf16[128,2048]{1,0:T(8,128)(2,1)}, u32[]{:S(2)}, u32[]{:S(2)}) collective-permute-start(bf16[128,2048]{1,0:T(8,128)(2,1)} %collective-permute-done.2.refs_0_), channel_id=1, source_target_pairs={{0,2},{1,3},{2,0},{3,1},{4,5},{5,4},{6,7},{7,6},{8,10},{9,11},{10,... | collective-permute-start | bytes 1572872 | tf_op jit(solution)/shard_map/ppermute | solution.py:256
  60.3 3.3 %copy-start.4 = (s32[1,8]{1,0:T(1,128)S(1)}, s32[1,8]{1,0:T(1,128)}, u32[]{:S(2)}) copy-start(s32[1,8]{1,0:T(1,128)} %val_ref.5) | copy-start | bytes 100
  65.3 3.8 %collective-permute-start.8 = (bf16[2,128,256]{2,1,0:T(8,128)(2,1)S(1)}, bf16[2,128,256]{2,1,0:T(8,128)(2,1)S(1)}, u32[]{:S(2)}, u32[]{:S(2)}) collective-permute-start(bf16[2,128,256]{2,1,0:T(8,128)(2,1)S(1)} %get-tuple-element.47), channel_id=1, source_target_pairs={{0,4},{4,0},{8,12},{12,8},{16,20},{20,16},{24,28},{28,24},{1,5},{5... | collective-permute-start | bytes 393224 | tf_op jit(solution)/shard_map/ppermute | solution.py:260
  65.4 6.3 %collective-permute-start.9 = (bf16[2,128,256]{2,1,0:T(8,128)(2,1)S(1)}, bf16[2,128,256]{2,1,0:T(8,128)(2,1)S(1)}, u32[]{:S(2)}, u32[]{:S(2)}) collective-permute-start(bf16[2,128,256]{2,1,0:T(8,128)(2,1)S(1)} %get-tuple-element.48), channel_id=1, source_target_pairs={{4,8},{8,4},{12,16},{16,12},{20,24},{24,20},{5,9},{9,5},{13,17},{1... | collective-permute-start | bytes 393224 | tf_op jit(solution)/shard_map/ppermute | solution.py:260
  69.0 3.2 %collective-permute-start.10 = (bf16[128,2048]{1,0:T(8,128)(2,1)}, bf16[128,2048]{1,0:T(8,128)(2,1)S(1)}, u32[]{:S(2)}, u32[]{:S(2)}) collective-permute-start(bf16[128,2048]{1,0:T(8,128)(2,1)} %collective-permute-done.2.refs_0_), channel_id=1, source_target_pairs={{0,4},{4,0},{8,12},{12,8},{16,20},{20,16},{24,28},{28,24},{1,5},{5... | collective-permute-start | bytes 1572872 | tf_op jit(solution)/shard_map/ppermute | solution.py:278
  71.7 2.1 %collective-permute-start.11 = (bf16[128,2048]{1,0:T(8,128)(2,1)}, bf16[128,2048]{1,0:T(8,128)(2,1)S(1)}, u32[]{:S(2)}, u32[]{:S(2)}) collective-permute-start(bf16[128,2048]{1,0:T(8,128)(2,1)} %collective-permute-done.7.refs_1_), channel_id=1, source_target_pairs={{0,4},{4,0},{8,12},{12,8},{16,20},{20,16},{24,28},{28,24},{1,5},{5... | collective-permute-start | bytes 1572872 | tf_op jit(solution)/shard_map/ppermute | solution.py:278
  71.7 9.2 %collective-permute-start.4 = (bf16[128,2048]{1,0:T(8,128)(2,1)}, bf16[128,2048]{1,0:T(8,128)(2,1)S(1)}, u32[]{:S(2)}, u32[]{:S(2)}) collective-permute-start(bf16[128,2048]{1,0:T(8,128)(2,1)} %collective-permute-done.3.refs_0_), channel_id=1, source_target_pairs={{0,4},{4,0},{8,12},{12,8},{16,20},{20,16},{24,28},{28,24},{1,5},{5... | collective-permute-start | bytes 1572872 | tf_op jit(solution)/shard_map/ppermute | solution.py:283
  77.1 9.6 %collective-permute-start.12 = (bf16[2,128,512]{2,1,0:T(8,128)(2,1)S(1)}, bf16[2,128,512]{2,1,0:T(8,128)(2,1)S(1)}, u32[]{:S(2)}, u32[]{:S(2)}) collective-permute-start(bf16[2,128,512]{2,1,0:T(8,128)(2,1)S(1)} %get-tuple-element.56), channel_id=1, source_target_pairs={{0,4},{4,0},{8,12},{12,8},{16,20},{20,16},{24,28},{28,24},{1,5},{5... | collective-permute-start | bytes 786440 | tf_op jit(solution)/shard_map/ppermute | solution.py:260
  77.3 9.4 %collective-permute-start.13 = (bf16[2,128,512]{2,1,0:T(8,128)(2,1)S(1)}, bf16[2,128,512]{2,1,0:T(8,128)(2,1)S(1)}, u32[]{:S(2)}, u32[]{:S(2)}) collective-permute-start(bf16[2,128,512]{2,1,0:T(8,128)(2,1)S(1)} %get-tuple-element.57), channel_id=1, source_target_pairs={{4,8},{8,4},{12,16},{16,12},{20,24},{24,20},{5,9},{9,5},{13,17},{1... | collective-permute-start | bytes 786440 | tf_op jit(solution)/shard_map/ppermute | solution.py:260
  83.0 4.6 %collective-permute-start.5 = (bf16[2,128,256]{2,1,0:T(8,128)(2,1)S(1)}, bf16[2,128,256]{2,1,0:T(8,128)(2,1)S(1)}, u32[]{:S(2)}, u32[]{:S(2)}) collective-permute-start(bf16[2,128,256]{2,1,0:T(8,128)(2,1)S(1)} %get-tuple-element.41), channel_id=1, source_target_pairs={{0,4},{4,0},{8,12},{12,8},{16,20},{20,16},{24,28},{28,24},{1,5},{5... | collective-permute-start | bytes 393224 | tf_op jit(solution)/shard_map/ppermute | solution.py:260
  83.1 6.3 %collective-permute-start.6 = (bf16[2,128,256]{2,1,0:T(8,128)(2,1)S(1)}, bf16[2,128,256]{2,1,0:T(8,128)(2,1)S(1)}, u32[]{:S(2)}, u32[]{:S(2)}) collective-permute-start(bf16[2,128,256]{2,1,0:T(8,128)(2,1)S(1)} %get-tuple-element.42), channel_id=1, source_target_pairs={{4,8},{8,4},{12,16},{16,12},{20,24},{24,20},{5,9},{9,5},{13,17},{1... | collective-permute-start | bytes 393224 | tf_op jit(solution)/shard_map/ppermute | solution.py:260

commit v4 on v3

--- a/solution.py
+++ b/solution.py
@@ -9,6 +9,8 @@
 
 HD = 128
 PAIR = 2 * HD
+PIECES = 2
+BRIEF = pl.CostEstimate(flops=1, bytes_accessed=1, transcendentals=0)
 F32 = jnp.float32
 BF16 = jnp.bfloat16
 NT = (((1,), (1,)), ((), ()))
@@ -37,33 +39,54 @@
     return lax.rem(lax.axis_index("seq"), 2), lax.axis_index("fsdp")
 
 
-def run_copies(copies):
-    for copy in copies:
+def relay(pairs, buffers, sems):
+    arrivals, moves = [], []
+    for i, (source, target) in enumerate(pairs):
+        arrivals.append(pltpu.make_async_copy(source, buffers[i], sems.at[0, i]))
+        moves.append(pltpu.make_async_copy(buffers[i], target, sems.at[1, i]))
+    for copy in arrivals:
         copy.start()
-    for copy in copies:
-        copy.wait()
-
-
-def prep_kernel(w_ref, k_ref, v_ref, first_ref, second_ref, kv_ref, sems):
+    for arrival, move in zip(arrivals, moves):
+        arrival.wait()
+        move.start()
+    for move in moves:
+        move.wait()
+
+
+def half_rows(w_ref, half, which, piece):
+    rows = half // PIECES
+    start = pl.multiple_of(which * half + piece * rows, rows)
+    return w_ref.at[pl.ds(start, rows), :]
+
+
+def prep_kernel(w_ref, k_ref, v_ref, first_ref, second_ref, kv_ref, w_buffer, kv_buffer, sems):
     core, _ = place()
     half = first_ref.shape[0]
-    pairs = [
-        (w_ref.at[pl.ds(pl.multiple_of(core * half, half), half), :], first_ref),
-        (w_ref.at[pl.ds(pl.multiple_of((1 - core) * half, half), half), :], second_ref),
-        (k_ref, kv_ref.at[pl.ds(0, 1)]),
-        (v_ref, kv_ref.at[pl.ds(1, 1)]),
-    ]
-    run_copies([pltpu.make_async_copy(s, d, sems.at[i]) for i, (s, d) in enumerate(pairs)])
+    rows = half // PIECES
+    pairs, buffers = [], []
+    for which, target in ((core, first_ref), (1 - core, second_ref)):
+        for i in range(PIECES):
+            pairs.append((half_rows(w_ref, half, which, i), target.at[pl.ds(i * rows, rows), :]))
+            buffers.append(w_buffer.at[len(buffers)])
+    pairs += [(k_ref.at[0], kv_ref.at[0]), (v_ref.at[0], kv_ref.at[1])]
+    relay(pairs, buffers + [kv_buffer.at[0], kv_buffer.at[1]], sems)
 
 
 def prep(w_out, keys, values):
-    half = jax.ShapeDtypeStruct((w_out.shape[0] // 2, w_out.shape[1]), BF16)
+    rows, depth = w_out.shape
+    kv = (2,) + keys.shape[1:]
+    half = jax.ShapeDtypeStruct((rows // 2, depth), BF16)
     return pl.pallas_call(
         prep_kernel,
-        out_shape=(half, half, jax.ShapeDtypeStruct((2,) + keys.shape[1:], BF16)),
+        out_shape=(half, half, jax.ShapeDtypeStruct(kv, BF16)),
         in_specs=[HBM] * 3,
         out_specs=(ANY,) * 3,
-        scratch_shapes=[pltpu.SemaphoreType.DMA((4,))],
+        scratch_shapes=[
+            pltpu.VMEM((2 * PIECES, rows // (2 * PIECES), depth), BF16),
+            pltpu.VMEM(kv, BF16),
+            pltpu.SemaphoreType.DMA((2, 2 + 2 * PIECES)),
+        ],
+        cost_estimate=BRIEF,
         compiler_params=WIDE,
         name="prep",
     )(w_out, keys, values)
@@ -92,6 +115,7 @@
         in_specs=[HBM] * 3,
         out_specs=(VMEM,) * 3,
         scratch_shapes=[pltpu.VMEM((tok, depth), BF16), pltpu.SemaphoreType.DMA((3,))],
+        cost_estimate=BRIEF,
         compiler_params=PARAMS,
         name="stage",
     )(d_out, queries, w_out)
@@ -183,11 +207,7 @@
         ),
         in_specs=[SMEM] * 2 + [VMEM] * (5 + len(weights)),
         out_specs=(VMEM,) * 4,
-        cost_estimate=pl.CostEstimate(
-            flops=count * 4 * tok * HD * (depth + 15 * HD),
-            bytes_accessed=count * 1_800_000,
-            transcendentals=count * 6 * tok * HD,
-        ),
+        cost_estimate=BRIEF,
         compiler_params=PARAMS,
         name=name,
     )(pattern, valid, turned, q, *halo, *weights)
@@ -236,6 +256,7 @@
             pltpu.SemaphoreType.DMA((3 * count,)),
         ],
         input_output_aliases={len(ins) + i: i for i in range(len(old))},
+        cost_estimate=BRIEF,
         compiler_params=PARAMS,
         name=name,
     )(*ins, *old)
@@ -257,7 +278,8 @@
 
     def part(name, steps, weights):
         dq, own, to_core, to_far = attention(name, steps, weights, pattern, valid, staged, halo)
-        return dq, own, near(to_core), far(to_far)
+        back = far(to_far)
+        return dq, own, near(to_core), back
 
     first, second, kv = prep(w_out, keys, values)
     *staged, w_rows = stage(d_out, queries, w_out)
@@ -265,10 +287,12 @@
         second, *staged = lax.optimization_barrier((second, *staged))
         got_a = cross(first, (1, 2))
         got_b = cross(second, (1, 2))
-        halo = kv, near(kv), far(kv)
+        kv_far = far(kv)
+        halo = kv, near(kv), kv_far
         got_d = cross(got_a, (2, 1))
         part_a = part("heads_own", lambda core, group: [(group, 0, ((0, 0), (0, HD)), 0)], [w_rows])
-        got_b, part_a = lax.optimization_barrier((got_b, part_a))
+        got_b, dq = lax.optimization_barrier((got_b, part_a[0]))
+        part_a = (dq,) + part_a[1:]
         part_b = part(
             "heads_side",
             lambda core, group: [

time: 90.4 us -> 46 us (0.51)
  Pallas kernels: 57.9 us -> 11.6 us
  starting transfers between devices: 20.6 us -> 22 us
    pallas_call x1, Pallas kernels: 48.8 us -> 2.5 us  [prep(): pl.pallas_call(prep_kernel, out_shape=(half, half, jax.ShapeDtypeStruct(k...]
    ppermute x3, waiting for transfers between devices: 0.39 us -> 5.2 us  [cross(): return lax.ppermute(x, ('seq', 'fsdp'), pairs)]
    ppermute x8, waiting for transfers between devices: 7.67 us -> 4.95 us  [the longest x1 3.21 us: body(): kv_far = far(kv)]
    ppermute x1, waiting for transfers between devices: 1.6 us -> 0.01 us  [body(): near(got_b)]
  transfers between devices with their start and end apart: 14 -> 14, of which waited for: 5 -> 5; matrix products, arithmetic and copies ran while one was open for 0% -> 0% of each run, Pallas kernels for 9% -> 18%
where the time goes in v4:
time: 46 us; the launch traced here: 45.7 us
  starting transfers between devices  22 us (48%)
  Pallas kernels  11.6 us (25%)
  waiting for transfers between devices  10.2 us (22%)
  local copies, waits for them, and re-layouts  1.05 us (2%)
  between operations  0.83 us (2%)
    ppermute x3, starting transfers between devices, part(): back = far(to_far)  11.1 us
    pallas_call x3, Pallas kernels, attention(): pl.pallas_call(functools.partial(attention_kernel, steps), out_shape=(jax...  7.12 us
    ppermute x3, waiting for transfers between devices, cross(): return lax.ppermute(x, ('seq', 'fsdp'), pairs)  5.2 us
    ppermute x3, starting transfers between devices, cross(): return lax.ppermute(x, ('seq', 'fsdp'), pairs)  4.87 us
    ppermute x1, starting transfers between devices, body(): kv_far = far(kv)  3.21 us
    ppermute x1, waiting for transfers between devices, body(): kv_far = far(kv)  3.21 us
    pallas_call x1, Pallas kernels, prep(): pl.pallas_call(prep_kernel, out_shape=(half, half, jax.ShapeDtypeStruct(k...  2.5 us
    ppermute x3, waiting for transfers between devices, part(): back = far(to_far)  1.73 us
  transfers between devices with their start and end apart: 14, of which 5 were waited for; matrix products, arithmetic and copies ran while one was open for 0% of the time, Pallas kernels for 18%

profile of v4, /device:TPU:1, one launch (start us, length us, event | category | flops | bytes accessed | tf_op | source)
XLA Modules:
  0.0 45.7 jit_solution(4296635085768121945)
XLA Ops:
  0.7 2.5 %prep.1 = (bf16[128,2048]{1,0:T(8,128)(2,1)}, bf16[128,2048]{1,0:T(8,128)(2,1)}, bf16[2,128,1024]{2,1,0:T(8,128)(2,1)}) custom-call(bf16[256,2048]{1,0:T(8,128)(2,1)} %w_ref.3, bf16[1,128,1024]{2,1,0:T(8,128)(2,1)} %k_ref.1, bf16[1,128,1024]{2,1,0:T(8,128)(2,1)} %v_ref.1), custom_call_target="tpu_custom_call" | custom-call | flops 1 | bytes 1 | tf_op jit(solution)/shard_map/prep/pallas_call | solution.py:79
  3.2 2.1 %collective-permute-start.2 = (bf16[128,2048]{1,0:T(8,128)(2,1)}, bf16[128,2048]{1,0:T(8,128)(2,1)}, u32[]{:S(2)}, u32[]{:S(2)}) collective-permute-start(bf16[128,2048]{1,0:T(8,128)(2,1)} %get-tuple-element.35), channel_id=1, source_target_pairs={{0,1},{1,0},{2,3},{3,2},{4,6},{5,7},{6,4},{7,5},{8,9},{9,8},{10,11... | collective-permute-start | bytes 1572872 | tf_op jit(solution)/shard_map/ppermute | solution.py:277
  5.3 0.8 %collective-permute-start = (bf16[2,128,1024]{2,1,0:T(8,128)(2,1)}, bf16[2,128,1024]{2,1,0:T(8,128)(2,1)S(1)}, u32[]{:S(2)}, u32[]{:S(2)}) collective-permute-start(bf16[2,128,1024]{2,1,0:T(8,128)(2,1)} %get-tuple-element.34.own_kv), channel_id=1, source_target_pairs={{0,4},{4,0},{8,12},{12,8},{16,20},{20,16},{24,28},{28,24},{1,5},{5... | collective-permute-start | bytes 1572872 | tf_op jit(solution)/shard_map/ppermute | solution.py:291
  6.1 3.2 %collective-permute-start.1 = (bf16[2,128,1024]{2,1,0:T(8,128)(2,1)}, bf16[2,128,1024]{2,1,0:T(8,128)(2,1)S(1)}, u32[]{:S(2)}, u32[]{:S(2)}) collective-permute-start(bf16[2,128,1024]{2,1,0:T(8,128)(2,1)} %get-tuple-element.34.own_kv), channel_id=1, source_target_pairs={{4,8},{8,4},{12,16},{16,12},{20,24},{24,20},{5,9},{9,5},{13,17},{1... | collective-permute-start | bytes 1572872 | tf_op jit(solution)/shard_map/ppermute | solution.py:290
  9.4 0.9 %copy-done.3 = bf16[1,128,1024]{2,1,0:T(8,128)(2,1)S(1)} copy-done((bf16[1,128,1024]{2,1,0:T(8,128)(2,1)S(1)}, bf16[1,128,1024]{2,1,0:T(8,128)(2,1)}, u32[]{:S(2)}) %copy-start.3) | copy-done | bytes 262168
  10.3 0.3 stage.1
  10.7 1.3 %collective-permute-start.7 = (bf16[128,2048]{1,0:T(8,128)(2,1)}, bf16[128,2048]{1,0:T(8,128)(2,1)}, u32[]{:S(2)}, u32[]{:S(2)}) collective-permute-start(bf16[128,2048]{1,0:T(8,128)(2,1)} %get-tuple-element.40), channel_id=1, source_target_pairs={{0,1},{1,0},{2,3},{3,2},{4,6},{5,7},{6,4},{7,5},{8,9},{9,8},{10,11... | collective-permute-start | bytes 1572872 | tf_op jit(solution)/shard_map/ppermute | solution.py:277
  12.0 0.5 %collective-permute-done.2.refs_0_ = bf16[128,2048]{1,0:T(8,128)(2,1)} collective-permute-done((bf16[128,2048]{1,0:T(8,128)(2,1)}, bf16[128,2048]{1,0:T(8,128)(2,1)}, u32[]{:S(2)}, u32[]{:S(2)}) %collective-permute-start.2) | collective-permute-done | bytes 524320 | tf_op jit(solution)/shard_map/ppermute | solution.py:277
  12.5 1.4 %collective-permute-start.3 = (bf16[128,2048]{1,0:T(8,128)(2,1)}, bf16[128,2048]{1,0:T(8,128)(2,1)}, u32[]{:S(2)}, u32[]{:S(2)}) collective-permute-start(bf16[128,2048]{1,0:T(8,128)(2,1)} %collective-permute-done.2.refs_0_), channel_id=1, source_target_pairs={{0,2},{1,3},{2,0},{3,1},{4,5},{5,4},{6,7},{7,6},{8,10},{9,11},{10,... | collective-permute-start | bytes 1572872 | tf_op jit(solution)/shard_map/ppermute | solution.py:277
  13.9 0.1 copy.13.pat_ref
  14.0 3.2 %collective-permute-done.1.far_kv = bf16[2,128,1024]{2,1,0:T(8,128)(2,1)S(1)} collective-permute-done((bf16[2,128,1024]{2,1,0:T(8,128)(2,1)}, bf16[2,128,1024]{2,1,0:T(8,128)(2,1)S(1)}, u32[]{:S(2)}, u32[]{:S(2)}) %collective-permute-start.1) | collective-permute-done | bytes 524320 | tf_op jit(solution)/shard_map/ppermute | solution.py:290
  17.2 1.7 %heads_own.1 = (bf16[128,256]{1,0:T(8,128)(2,1)S(1)}, f32[2,128,256]{2,1,0:T(8,128)S(1)}, bf16[2,128,256]{2,1,0:T(8,128)(2,1)S(1)}, bf16[2,128,256]{2,1,0:T(8,128)(2,1)S(1)}) custom-call(s32[8,4]{1,0:T(8,128)S(1)} %copy.13.pat_ref, s32[1,8]{1,0:T(1,128)S(1)} %copy-done.4, bf16[2048,128]{1,0:T(8,128)(2,1)S(1)} %get-tuple-element.32.dy_ref, ...), custom_call_target="tpu_custom_call" | custom-call | flops 1 | bytes 1 | tf_op jit(solution)/shard_map/heads_own/pallas_call | solution.py:200
  18.9 2.7 %collective-permute-done.7.refs_1_ = bf16[128,2048]{1,0:T(8,128)(2,1)} collective-permute-done((bf16[128,2048]{1,0:T(8,128)(2,1)}, bf16[128,2048]{1,0:T(8,128)(2,1)}, u32[]{:S(2)}, u32[]{:S(2)}) %collective-permute-start.7) | collective-permute-done | bytes 524320 | tf_op jit(solution)/shard_map/ppermute | solution.py:277
  21.6 0.8 %collective-permute-start.11 = (bf16[128,2048]{1,0:T(8,128)(2,1)}, bf16[128,2048]{1,0:T(8,128)(2,1)S(1)}, u32[]{:S(2)}, u32[]{:S(2)}) collective-permute-start(bf16[128,2048]{1,0:T(8,128)(2,1)} %collective-permute-done.7.refs_1_), channel_id=1, source_target_pairs={{0,4},{4,0},{8,12},{12,8},{16,20},{20,16},{24,28},{28,24},{1,5},{5... | collective-permute-start | bytes 1572872 | tf_op jit(solution)/shard_map/ppermute | solution.py:302
  22.4 2.0 %collective-permute-done.3.refs_0_ = bf16[128,2048]{1,0:T(8,128)(2,1)} collective-permute-done((bf16[128,2048]{1,0:T(8,128)(2,1)}, bf16[128,2048]{1,0:T(8,128)(2,1)}, u32[]{:S(2)}, u32[]{:S(2)}) %collective-permute-start.3) | collective-permute-done | bytes 524320 | tf_op jit(solution)/shard_map/ppermute | solution.py:277
  24.4 1.0 %collective-permute-start.4 = (bf16[128,2048]{1,0:T(8,128)(2,1)}, bf16[128,2048]{1,0:T(8,128)(2,1)S(1)}, u32[]{:S(2)}, u32[]{:S(2)}) collective-permute-start(bf16[128,2048]{1,0:T(8,128)(2,1)} %collective-permute-done.3.refs_0_), channel_id=1, source_target_pairs={{0,4},{4,0},{8,12},{12,8},{16,20},{20,16},{24,28},{28,24},{1,5},{5... | collective-permute-start | bytes 1572872 | tf_op jit(solution)/shard_map/ppermute | solution.py:307
  25.4 3.3 %heads_side.1 = (bf16[128,512]{1,0:T(8,128)(2,1)S(1)}, f32[2,128,512]{2,1,0:T(8,128)S(1)}, bf16[2,128,512]{2,1,0:T(8,128)(2,1)S(1)}, bf16[2,128,512]{2,1,0:T(8,128)(2,1)S(1)}) custom-call(s32[8,4]{1,0:T(8,128)S(1)} %copy.13.pat_ref, s32[1,8]{1,0:T(1,128)S(1)} %copy-done.4, bf16[2048,128]{1,0:T(8,128)(2,1)S(1)} %get-tuple-element.32.dy_ref, ...), custom_call_target="tpu_custom_call" | custom-call | flops 1 | bytes 1 | tf_op jit(solution)/shard_map/heads_side/pallas_call | solution.py:200
  28.8 4.0 %collective-permute-start.13 = (bf16[2,128,512]{2,1,0:T(8,128)(2,1)S(1)}, bf16[2,128,512]{2,1,0:T(8,128)(2,1)S(1)}, u32[]{:S(2)}, u32[]{:S(2)}) collective-permute-start(bf16[2,128,512]{2,1,0:T(8,128)(2,1)S(1)} %get-tuple-element.51), channel_id=1, source_target_pairs={{4,8},{8,4},{12,16},{16,12},{20,24},{24,20},{5,9},{9,5},{13,17},{1... | collective-permute-start | bytes 786440 | tf_op jit(solution)/shard_map/ppermute | solution.py:281
  32.8 3.6 %collective-permute-start.9 = (bf16[2,128,256]{2,1,0:T(8,128)(2,1)S(1)}, bf16[2,128,256]{2,1,0:T(8,128)(2,1)S(1)}, u32[]{:S(2)}, u32[]{:S(2)}) collective-permute-start(bf16[2,128,256]{2,1,0:T(8,128)(2,1)S(1)} %get-tuple-element.46), channel_id=1, source_target_pairs={{4,8},{8,4},{12,16},{16,12},{20,24},{24,20},{5,9},{9,5},{13,17},{1... | collective-permute-start | bytes 393224 | tf_op jit(solution)/shard_map/ppermute | solution.py:281
  36.4 2.1 %heads_far.1 = (bf16[128,256]{1,0:T(8,128)(2,1)S(1)}, f32[2,128,256]{2,1,0:T(8,128)S(1)}, bf16[2,128,256]{2,1,0:T(8,128)(2,1)S(1)}, bf16[2,128,256]{2,1,0:T(8,128)(2,1)S(1)}) custom-call(s32[8,4]{1,0:T(8,128)S(1)} %copy.13.pat_ref, s32[1,8]{1,0:T(1,128)S(1)} %copy-done.4, bf16[2048,128]{1,0:T(8,128)(2,1)S(1)} %get-tuple-element.32.dy_ref, ...), custom_call_target="tpu_custom_call" | custom-call | flops 1 | bytes 1 | tf_op jit(solution)/shard_map/heads_far/pallas_call | solution.py:200
  38.7 3.6 %collective-permute-start.6 = (bf16[2,128,256]{2,1,0:T(8,128)(2,1)S(1)}, bf16[2,128,256]{2,1,0:T(8,128)(2,1)S(1)}, u32[]{:S(2)}, u32[]{:S(2)}) collective-permute-start(bf16[2,128,256]{2,1,0:T(8,128)(2,1)S(1)} %get-tuple-element.39), channel_id=1, source_target_pairs={{4,8},{8,4},{12,16},{16,12},{20,24},{24,20},{5,9},{9,5},{13,17},{1... | collective-permute-start | bytes 393224 | tf_op jit(solution)/shard_map/ppermute | solution.py:281
  42.3 0.9 %finish_first.1 = (bf16[1,128,1024]{2,1,0:T(8,128)(2,1)}, bf16[1,128,1024]{2,1,0:T(8,128)(2,1)}, bf16[1,128,1024]{2,1,0:T(8,128)(2,1)}) custom-call(bf16[128,256]{1,0:T(8,128)(2,1)S(1)} %get-tuple-element.43.refs_0_, f32[2,128,256]{2,1,0:T(8,128)S(1)} %get-tuple-element.44.refs_1_, bf16[2,128,256]{2,1,0:T(8,128)(2,1)S(1)} %collective-permute-done.8.refs_2_, ...), custom_call_target="tpu_custom_call" | custom-call | flops 1 | bytes 1 | tf_op jit(solution)/shard_map/finish_first/pallas_call | solution.py:249
  43.2 1.7 %collective-permute-done.6.refs_3_ = bf16[2,128,256]{2,1,0:T(8,128)(2,1)S(1)} collective-permute-done((bf16[2,128,256]{2,1,0:T(8,128)(2,1)S(1)}, bf16[2,128,256]{2,1,0:T(8,128)(2,1)S(1)}, u32[]{:S(2)}, u32[]{:S(2)}) %collective-permute-start.6) | collective-permute-done | bytes 131104 | tf_op jit(solution)/shard_map/ppermute | solution.py:281
  44.9 0.7 %finish_last.1 = (bf16[1,128,1024]{2,1,0:T(8,128)(2,1)}, bf16[1,128,1024]{2,1,0:T(8,128)(2,1)}, bf16[1,128,1024]{2,1,0:T(8,128)(2,1)}) custom-call(bf16[128,256]{1,0:T(8,128)(2,1)S(1)} %get-tuple-element.36.refs_0_, f32[2,128,256]{2,1,0:T(8,128)S(1)} %get-tuple-element.37.refs_1_, ...), custom_call_target="tpu_custom_call", output_to_operand_aliasing={{0}: (4, {}), {1}: (5, {}), {2}: (6, {})} | custom-call | flops 1 | bytes 1 | tf_op jit(solution)/shard_map/finish_last/pallas_call | solution.py:249
  (24 shorter events, 0.3 us)
Async XLA Ops:
  0.6 8.7 %copy-start.1 = (bf16[256,2048]{1,0:T(8,128)(2,1)S(1)}, bf16[256,2048]{1,0:T(8,128)(2,1)}, u32[]{:S(2)}) copy-start(bf16[256,2048]{1,0:T(8,128)(2,1)} %w_ref.3) | copy-start | bytes 3145732
  0.6 8.7 %copy-start.2 = (bf16[1,128,2048]{2,1,0:T(8,128)(2,1)S(1)}, bf16[1,128,2048]{2,1,0:T(8,128)(2,1)}, u32[]{:S(2)}) copy-start(bf16[1,128,2048]{2,1,0:T(8,128)(2,1)} %dy_ref.1) | copy-start | bytes 1572868
  3.2 9.3 %collective-permute-start.2 = (bf16[128,2048]{1,0:T(8,128)(2,1)}, bf16[128,2048]{1,0:T(8,128)(2,1)}, u32[]{:S(2)}, u32[]{:S(2)}) collective-permute-start(bf16[128,2048]{1,0:T(8,128)(2,1)} %get-tuple-element.35), channel_id=1, source_target_pairs={{0,1},{1,0},{2,3},{3,2},{4,6},{5,7},{6,4},{7,5},{8,9},{9,8},{10,11... | collective-permute-start | bytes 1572872 | tf_op jit(solution)/shard_map/ppermute | solution.py:277
  5.3 11.9 %copy-start = (bf16[2,128,1024]{2,1,0:T(8,128)(2,1)S(1)}, bf16[2,128,1024]{2,1,0:T(8,128)(2,1)}, u32[]{:S(2)}) copy-start(bf16[2,128,1024]{2,1,0:T(8,128)(2,1)} %get-tuple-element.34.own_kv) | copy-start | bytes 1572868
  5.3 8.7 %collective-permute-start = (bf16[2,128,1024]{2,1,0:T(8,128)(2,1)}, bf16[2,128,1024]{2,1,0:T(8,128)(2,1)S(1)}, u32[]{:S(2)}, u32[]{:S(2)}) collective-permute-start(bf16[2,128,1024]{2,1,0:T(8,128)(2,1)} %get-tuple-element.34.own_kv), channel_id=1, source_target_pairs={{0,4},{4,0},{8,12},{12,8},{16,20},{20,16},{24,28},{28,24},{1,5},{5... | collective-permute-start | bytes 1572872 | tf_op jit(solution)/shard_map/ppermute | solution.py:291
  6.1 11.1 %collective-permute-start.1 = (bf16[2,128,1024]{2,1,0:T(8,128)(2,1)}, bf16[2,128,1024]{2,1,0:T(8,128)(2,1)S(1)}, u32[]{:S(2)}, u32[]{:S(2)}) collective-permute-start(bf16[2,128,1024]{2,1,0:T(8,128)(2,1)} %get-tuple-element.34.own_kv), channel_id=1, source_target_pairs={{4,8},{8,4},{12,16},{16,12},{20,24},{24,20},{5,9},{9,5},{13,17},{1... | collective-permute-start | bytes 1572872 | tf_op jit(solution)/shard_map/ppermute | solution.py:290
  9.3 1.0 %copy-start.3 = (bf16[1,128,1024]{2,1,0:T(8,128)(2,1)S(1)}, bf16[1,128,1024]{2,1,0:T(8,128)(2,1)}, u32[]{:S(2)}) copy-start(bf16[1,128,1024]{2,1,0:T(8,128)(2,1)} %q_ref.1) | copy-start | bytes 786436
  10.7 3.3 %copy-start.5 = (s32[8,4]{0,1:T(4,128)S(1)}, s32[8,4]{0,1:T(4,128)}, u32[]{:S(2)}) copy-start(s32[8,4]{0,1:T(4,128)} %param.12) | copy-start | bytes 388
  10.7 10.9 %collective-permute-start.7 = (bf16[128,2048]{1,0:T(8,128)(2,1)}, bf16[128,2048]{1,0:T(8,128)(2,1)}, u32[]{:S(2)}, u32[]{:S(2)}) collective-permute-start(bf16[128,2048]{1,0:T(8,128)(2,1)} %get-tuple-element.40), channel_id=1, source_target_pairs={{0,1},{1,0},{2,3},{3,2},{4,6},{5,7},{6,4},{7,5},{8,9},{9,8},{10,11... | collective-permute-start | bytes 1572872 | tf_op jit(solution)/shard_map/ppermute | solution.py:277
  12.5 11.9 %collective-permute-start.3 = (bf16[128,2048]{1,0:T(8,128)(2,1)}, bf16[128,2048]{1,0:T(8,128)(2,1)}, u32[]{:S(2)}, u32[]{:S(2)}) collective-permute-start(bf16[128,2048]{1,0:T(8,128)(2,1)} %collective-permute-done.2.refs_0_), channel_id=1, source_target_pairs={{0,2},{1,3},{2,0},{3,1},{4,5},{5,4},{6,7},{7,6},{8,10},{9,11},{10,... | collective-permute-start | bytes 1572872 | tf_op jit(solution)/shard_map/ppermute | solution.py:277
  14.0 3.2 %copy-start.4 = (s32[1,8]{1,0:T(1,128)S(1)}, s32[1,8]{1,0:T(1,128)}, u32[]{:S(2)}) copy-start(s32[1,8]{1,0:T(1,128)} %val_ref.5) | copy-start | bytes 100
  21.6 3.8 %collective-permute-start.11 = (bf16[128,2048]{1,0:T(8,128)(2,1)}, bf16[128,2048]{1,0:T(8,128)(2,1)S(1)}, u32[]{:S(2)}, u32[]{:S(2)}) collective-permute-start(bf16[128,2048]{1,0:T(8,128)(2,1)} %collective-permute-done.7.refs_1_), channel_id=1, source_target_pairs={{0,4},{4,0},{8,12},{12,8},{16,20},{20,16},{24,28},{28,24},{1,5},{5... | collective-permute-start | bytes 1572872 | tf_op jit(solution)/shard_map/ppermute | solution.py:302
  22.4 3.0 %collective-permute-start.10 = (bf16[128,2048]{1,0:T(8,128)(2,1)}, bf16[128,2048]{1,0:T(8,128)(2,1)S(1)}, u32[]{:S(2)}, u32[]{:S(2)}) collective-permute-start(bf16[128,2048]{1,0:T(8,128)(2,1)} %collective-permute-done.2.refs_0_), channel_id=1, source_target_pairs={{0,4},{4,0},{8,12},{12,8},{16,20},{20,16},{24,28},{28,24},{1,5},{5... | collective-permute-start | bytes 1572872 | tf_op jit(solution)/shard_map/ppermute | solution.py:302
  24.4 12.0 %collective-permute-start.4 = (bf16[128,2048]{1,0:T(8,128)(2,1)}, bf16[128,2048]{1,0:T(8,128)(2,1)S(1)}, u32[]{:S(2)}, u32[]{:S(2)}) collective-permute-start(bf16[128,2048]{1,0:T(8,128)(2,1)} %collective-permute-done.3.refs_0_), channel_id=1, source_target_pairs={{0,4},{4,0},{8,12},{12,8},{16,20},{20,16},{24,28},{28,24},{1,5},{5... | collective-permute-start | bytes 1572872 | tf_op jit(solution)/shard_map/ppermute | solution.py:307
  28.7 13.5 %collective-permute-start.12 = (bf16[2,128,512]{2,1,0:T(8,128)(2,1)S(1)}, bf16[2,128,512]{2,1,0:T(8,128)(2,1)S(1)}, u32[]{:S(2)}, u32[]{:S(2)}) collective-permute-start(bf16[2,128,512]{2,1,0:T(8,128)(2,1)S(1)} %get-tuple-element.50), channel_id=1, source_target_pairs={{0,4},{4,0},{8,12},{12,8},{16,20},{20,16},{24,28},{28,24},{1,5},{5... | collective-permute-start | bytes 786440 | tf_op jit(solution)/shard_map/ppermute | solution.py:282
  28.8 13.5 %collective-permute-start.13 = (bf16[2,128,512]{2,1,0:T(8,128)(2,1)S(1)}, bf16[2,128,512]{2,1,0:T(8,128)(2,1)S(1)}, u32[]{:S(2)}, u32[]{:S(2)}) collective-permute-start(bf16[2,128,512]{2,1,0:T(8,128)(2,1)S(1)} %get-tuple-element.51), channel_id=1, source_target_pairs={{4,8},{8,4},{12,16},{16,12},{20,24},{24,20},{5,9},{9,5},{13,17},{1... | collective-permute-start | bytes 786440 | tf_op jit(solution)/shard_map/ppermute | solution.py:281
  32.8 5.9 %collective-permute-start.8 = (bf16[2,128,256]{2,1,0:T(8,128)(2,1)S(1)}, bf16[2,128,256]{2,1,0:T(8,128)(2,1)S(1)}, u32[]{:S(2)}, u32[]{:S(2)}) collective-permute-start(bf16[2,128,256]{2,1,0:T(8,128)(2,1)S(1)} %get-tuple-element.45), channel_id=1, source_target_pairs={{0,4},{4,0},{8,12},{12,8},{16,20},{20,16},{24,28},{28,24},{1,5},{5... | collective-permute-start | bytes 393224 | tf_op jit(solution)/shard_map/ppermute | solution.py:282
  32.8 9.4 %collective-permute-start.9 = (bf16[2,128,256]{2,1,0:T(8,128)(2,1)S(1)}, bf16[2,128,256]{2,1,0:T(8,128)(2,1)S(1)}, u32[]{:S(2)}, u32[]{:S(2)}) collective-permute-start(bf16[2,128,256]{2,1,0:T(8,128)(2,1)S(1)} %get-tuple-element.46), channel_id=1, source_target_pairs={{4,8},{8,4},{12,16},{16,12},{20,24},{24,20},{5,9},{9,5},{13,17},{1... | collective-permute-start | bytes 393224 | tf_op jit(solution)/shard_map/ppermute | solution.py:281
  38.6 4.6 %collective-permute-start.5 = (bf16[2,128,256]{2,1,0:T(8,128)(2,1)S(1)}, bf16[2,128,256]{2,1,0:T(8,128)(2,1)S(1)}, u32[]{:S(2)}, u32[]{:S(2)}) collective-permute-start(bf16[2,128,256]{2,1,0:T(8,128)(2,1)S(1)} %get-tuple-element.38), channel_id=1, source_target_pairs={{0,4},{4,0},{8,12},{12,8},{16,20},{20,16},{24,28},{28,24},{1,5},{5... | collective-permute-start | bytes 393224 | tf_op jit(solution)/shard_map/ppermute | solution.py:282
  38.7 6.3 %collective-permute-start.6 = (bf16[2,128,256]{2,1,0:T(8,128)(2,1)S(1)}, bf16[2,128,256]{2,1,0:T(8,128)(2,1)S(1)}, u32[]{:S(2)}, u32[]{:S(2)}) collective-permute-start(bf16[2,128,256]{2,1,0:T(8,128)(2,1)S(1)} %get-tuple-element.39), channel_id=1, source_target_pairs={{4,8},{8,4},{12,16},{16,12},{20,24},{24,20},{5,9},{9,5},{13,17},{1... | collective-permute-start | bytes 393224 | tf_op jit(solution)/shard_map/ppermute | solution.py:281

commit v5 on v4

--- a/solution.py
+++ b/solution.py
@@ -9,7 +9,6 @@
 
 HD = 128
 PAIR = 2 * HD
-PIECES = 2
 BRIEF = pl.CostEstimate(flops=1, bytes_accessed=1, transcendentals=0)
 F32 = jnp.float32
 BF16 = jnp.bfloat16
@@ -53,43 +52,40 @@
         move.wait()
 
 
-def half_rows(w_ref, half, which, piece):
-    rows = half // PIECES
-    start = pl.multiple_of(which * half + piece * rows, rows)
-    return w_ref.at[pl.ds(start, rows), :]
-
-
-def prep_kernel(w_ref, k_ref, v_ref, first_ref, second_ref, kv_ref, w_buffer, kv_buffer, sems):
+def join_kernel(k_ref, v_ref, kv_ref, buffer, sems):
+    relay([(k_ref.at[0], kv_ref.at[0]), (v_ref.at[0], kv_ref.at[1])], [buffer.at[0], buffer.at[1]], sems)
+
+
+def join(keys, values):
+    shape = (2,) + keys.shape[1:]
+    return pl.pallas_call(
+        join_kernel,
+        out_shape=jax.ShapeDtypeStruct(shape, BF16),
+        in_specs=[HBM] * 2,
+        out_specs=ANY,
+        scratch_shapes=[pltpu.VMEM(shape, BF16), pltpu.SemaphoreType.DMA((2, 2))],
+        cost_estimate=BRIEF,
+        compiler_params=WIDE,
+        name="join",
+    )(keys, values)
+
+
+def onward_kernel(w_ref, out_ref):
     core, _ = place()
-    half = first_ref.shape[0]
-    rows = half // PIECES
-    pairs, buffers = [], []
-    for which, target in ((core, first_ref), (1 - core, second_ref)):
-        for i in range(PIECES):
-            pairs.append((half_rows(w_ref, half, which, i), target.at[pl.ds(i * rows, rows), :]))
-            buffers.append(w_buffer.at[len(buffers)])
-    pairs += [(k_ref.at[0], kv_ref.at[0]), (v_ref.at[0], kv_ref.at[1])]
-    relay(pairs, buffers + [kv_buffer.at[0], kv_buffer.at[1]], sems)
-
-
-def prep(w_out, keys, values):
-    rows, depth = w_out.shape
-    kv = (2,) + keys.shape[1:]
-    half = jax.ShapeDtypeStruct((rows // 2, depth), BF16)
-    return pl.pallas_call(
-        prep_kernel,
-        out_shape=(half, half, jax.ShapeDtypeStruct(kv, BF16)),
-        in_specs=[HBM] * 3,
-        out_specs=(ANY,) * 3,
-        scratch_shapes=[
-            pltpu.VMEM((2 * PIECES, rows // (2 * PIECES), depth), BF16),
-            pltpu.VMEM(kv, BF16),
-            pltpu.SemaphoreType.DMA((2, 2 + 2 * PIECES)),
-        ],
-        cost_estimate=BRIEF,
-        compiler_params=WIDE,
-        name="prep",
-    )(w_out, keys, values)
+    half = out_ref.shape[0]
+    out_ref[...] = w_ref[pl.ds(pl.multiple_of(core * half, half), half), :]
+
+
+def onward(got):
+    return pl.pallas_call(
+        onward_kernel,
+        out_shape=jax.ShapeDtypeStruct((got.shape[0] // 2, got.shape[1]), BF16),
+        in_specs=[VMEM],
+        out_specs=VMEM,
+        cost_estimate=BRIEF,
+        compiler_params=PARAMS,
+        name="onward",
+    )(got)
 
 
 def stage_kernel(dy_ref, q_ref, w_ref, turned_ref, q_out, w_rows, dy, sems):
@@ -152,10 +148,12 @@
     return pl.ds(pl.multiple_of(chunk * PAIR, PAIR), PAIR)
 
 
-def attention_kernel(steps, pat_ref, val_ref, dy_ref, q_ref, own_kv, core_kv, far_kv, *refs):
+def attention_kernel(steps, carried, pat_ref, val_ref, dy_ref, q_ref, own_kv, core_kv, far_kv, *refs):
     core, group = place()
-    w_refs = refs[:-4]
-    dq_ref, own_ref, to_core_ref, to_far_ref = refs[-4:]
+    w_refs, earlier, outs = refs[: -4 - carried], refs[-4 - carried : -4], refs[-4:]
+    dq_ref, own_ref, to_core_ref, to_far_ref = outs
+    for old, out in zip(earlier, outs):
+        out[..., : old.shape[-1]] = old[...]
     scale = HD ** (-0.5)
     tok = q_ref.shape[0]
     rows = lax.broadcasted_iota(jnp.int32, (tok, PAIR), 0)
@@ -192,25 +190,25 @@
             to_far_ref[side, :, dest] = grad[2 * tok :].astype(BF16)
 
 
-def attention(name, steps, weights, pattern, valid, staged, halo):
+def attention(name, steps, weights, earlier, pattern, valid, staged, halo):
     count = len(steps(0, 0))
     turned, q = staged
     depth, tok = turned.shape
-    width = count * PAIR
-    return pl.pallas_call(
-        functools.partial(attention_kernel, steps),
+    width = count * PAIR + (earlier[0].shape[1] if earlier else 0)
+    return pl.pallas_call(
+        functools.partial(attention_kernel, steps, len(earlier)),
         out_shape=(
             jax.ShapeDtypeStruct((tok, width), BF16),
             jax.ShapeDtypeStruct((2, tok, width), F32),
             jax.ShapeDtypeStruct((2, tok, width), BF16),
             jax.ShapeDtypeStruct((2, tok, width), BF16),
         ),
-        in_specs=[SMEM] * 2 + [VMEM] * (5 + len(weights)),
+        in_specs=[SMEM] * 2 + [VMEM] * (5 + len(weights) + len(earlier)),
         out_specs=(VMEM,) * 4,
         cost_estimate=BRIEF,
         compiler_params=PARAMS,
         name=name,
-    )(pattern, valid, turned, q, *halo, *weights)
+    )(pattern, valid, turned, q, *halo, *weights, *earlier)
 
 
 def finish_kernel(chunks, n_parts, n_old, *refs):
@@ -276,47 +274,53 @@
         ]
         return lax.ppermute(x, ("seq", "fsdp"), pairs)
 
-    def part(name, steps, weights):
-        dq, own, to_core, to_far = attention(name, steps, weights, pattern, valid, staged, halo)
+    def heads(name, steps, weights, earlier=()):
+        return attention(name, steps, weights, earlier, pattern, valid, staged, halo)
+
+    def exchange(part):
+        dq, own, to_core, to_far = part
         back = far(to_far)
         return dq, own, near(to_core), back
 
-    first, second, kv = prep(w_out, keys, values)
+    kv = join(keys, values)
     *staged, w_rows = stage(d_out, queries, w_out)
     if n_fsdp == 4 and n_chunks == 4 and w_out.shape[0] == PAIR:
-        second, *staged = lax.optimization_barrier((second, *staged))
-        got_a = cross(first, (1, 2))
-        got_b = cross(second, (1, 2))
+        got = cross(w_out, (1, 2))
         kv_far = far(kv)
         halo = kv, near(kv), kv_far
-        got_d = cross(got_a, (2, 1))
-        part_a = part("heads_own", lambda core, group: [(group, 0, ((0, 0), (0, HD)), 0)], [w_rows])
-        got_b, dq = lax.optimization_barrier((got_b, part_a[0]))
-        part_a = (dq,) + part_a[1:]
-        part_b = part(
+        part = heads("heads_own", lambda core, group: [(group, 0, ((0, 0), (0, HD)), 0)], [w_rows])
+        got, dq = lax.optimization_barrier((got, part[0]))
+        part = (dq, *part[1:])
+        got_d = cross(onward(got), (2, 1))
+        part = heads(
             "heads_side",
             lambda core, group: [
-                (group ^ (1 + core), core, ((0, 0), (1, 0)), core),
-                (group ^ (2 - core), 1 - core, ((2, 0), (3, 0)), 1 - core),
+                (group ^ (1 + core), 1 + core, ((0, 0), (0, HD)), 0),
+                (group ^ (2 - core), 2 - core, ((1, 0), (1, HD)), 0),
             ],
-            [got_a, got_b, near(got_a), near(got_b)],
+            [got, near(got)],
+            part,
         )
-        part_c = part(
-            "heads_far",
-            lambda core, group: [(group ^ 3, 0, ((0, 0), (1, 0)), core)],
-            [got_d, near(got_d)],
+        got_d, dq = lax.optimization_barrier((got_d, part[0]))
+        sums = exchange((dq, *part[1:]))
+        last_sums = exchange(
+            heads(
+                "heads_far",
+                lambda core, group: [(group ^ 3, 0, ((0, 0), (1, 0)), core)],
+                [got_d, near(got_d)],
+            )
         )
         ab = lambda core, group: [group, group ^ 1, group ^ 2]
         last = lambda core, group: [group ^ 3]
-        old = finish("finish_first", ab, [part_a, part_b], queries.shape)
-        return finish("finish_last", last, [part_c], queries.shape, old)
+        old = finish("finish_first", ab, [sums], queries.shape)
+        return finish("finish_last", last, [last_sums], queries.shape, old)
     full = lax.all_gather(w_out, "fsdp", axis=0, tiled=True)
     halo = kv, near(kv), far(kv)
     order = lambda core, group: list(range(n_chunks))
     steps = lambda core, group: [
         (i, i, ((0, i * PAIR), (0, i * PAIR + HD)), 0) for i in range(n_chunks)
     ]
-    return finish("finish", order, [part("heads_all", steps, [full])], queries.shape)
+    return finish("finish", order, [exchange(heads("heads_all", steps, [full]))], queries.shape)
 
 
 def solution(mesh):

time: 46 us -> 42.7 us (0.928)
  starting transfers between devices: 22 us -> 16 us
  local copies, waits for them, and re-layouts: 1.05 us -> 4.95 us
  Pallas kernels: 11.6 us -> 9.87 us
  waiting for transfers between devices: 10.2 us -> 10.7 us
    ppermute x8 -> x5, starting transfers between devices: 12.2 us -> 7.56 us  [the longest x2 7.41 us: exchange(): back = far(to_far)]
    unnamed x13 -> x17, local copies, waits for them, and re-layouts: 1.05 us -> 4.95 us
    ppermute x3 -> x2, waiting for transfers between devices: 5.2 us -> 3.11 us  [cross(): return lax.ppermute(x, ('seq', 'fsdp'), pairs)]
    ppermute x3 -> x2, starting transfers between devices: 4.87 us -> 2.9 us  [cross(): return lax.ppermute(x, ('seq', 'fsdp'), pairs)]
    ppermute x8 -> x5, waiting for transfers between devices: 1.75 us -> 3.59 us  [the longest x1 1.82 us: body(): near(got)]
    pallas_call x4 -> x5, Pallas kernels: 9.62 us -> 7.86 us  [the longest x3 6.04 us: attention(): pl.pallas_call(functools.partial(attention_kernel, steps, len(earlier)),...]
    ppermute x1, waiting for transfers between devices: 3.21 us -> 4.04 us  [body(): kv_far = far(kv)]
  transfers between devices with their start and end apart: 14 -> 10, of which waited for: 5 -> 5; matrix products, arithmetic and copies ran while one was open for 0% -> 0% of each run, Pallas kernels for 18% -> 22%
where the time goes in v5:
time: 42.7 us; the launch traced here: 42.4 us
  starting transfers between devices  16 us (37%)
  waiting for transfers between devices  10.7 us (25%)
  Pallas kernels  9.87 us (23%)
  local copies, waits for them, and re-layouts  4.95 us (12%)
  between operations  0.8 us (2%)
    ppermute x2, starting transfers between devices, exchange(): back = far(to_far)  7.41 us
    pallas_call x3, Pallas kernels, attention(): pl.pallas_call(functools.partial(attention_kernel, steps, len(earlier)),...  6.04 us
    unnamed x17, local copies, waits for them, and re-layouts  4.95 us
    ppermute x1, waiting for transfers between devices, body(): kv_far = far(kv)  4.04 us
    ppermute x1, starting transfers between devices, body(): kv_far = far(kv)  3.23 us
    ppermute x2, waiting for transfers between devices, cross(): return lax.ppermute(x, ('seq', 'fsdp'), pairs)  3.11 us
    ppermute x2, starting transfers between devices, cross(): return lax.ppermute(x, ('seq', 'fsdp'), pairs)  2.9 us
    ppermute x1, waiting for transfers between devices, body(): near(got)  1.82 us
  transfers between devices with their start and end apart: 10, of which 5 were waited for; matrix products, arithmetic and copies ran while one was open for 0% of the time, Pallas kernels for 22%

profile of v5, /device:TPU:1, one launch (start us, length us, event | category | flops | bytes accessed | tf_op | source)
XLA Modules:
  0.0 42.4 jit_solution(2124470484466770134)
XLA Ops:
  0.6 2.1 %collective-permute-start.2 = (bf16[256,2048]{1,0:T(8,128)(2,1)}, bf16[256,2048]{1,0:T(8,128)(2,1)S(1)}, u32[]{:S(2)}, u32[]{:S(2)}) collective-permute-start(bf16[256,2048]{1,0:T(8,128)(2,1)} %w_ref.1), channel_id=1, source_target_pairs={{0,1},{1,0},{2,3},{3,2},{4,6},{5,7},{6,4},{7,5},{8,9},{9,8},{10,11... | collective-permute-start | bytes 3145736 | tf_op jit(solution)/shard_map/ppermute | solution.py:275
  2.8 1.8 %join.1.own_kv = bf16[2,128,1024]{2,1,0:T(8,128)(2,1)} custom-call(bf16[1,128,1024]{2,1,0:T(8,128)(2,1)} %k_ref.1, bf16[1,128,1024]{2,1,0:T(8,128)(2,1)} %v_ref.1), custom_call_target="tpu_custom_call" | custom-call | flops 1 | bytes 1 | tf_op jit(solution)/shard_map/join/pallas_call | solution.py:61
  4.6 1.0 %collective-permute-start = (bf16[2,128,1024]{2,1,0:T(8,128)(2,1)}, bf16[2,128,1024]{2,1,0:T(8,128)(2,1)S(1)}, u32[]{:S(2)}, u32[]{:S(2)}) collective-permute-start(bf16[2,128,1024]{2,1,0:T(8,128)(2,1)} %join.1.own_kv), channel_id=1, source_target_pairs={{0,4},{4,0},{8,12},{12,8},{16,20},{20,16},{24,28},{28,24},{1,5},{5... | collective-permute-start | bytes 1572872 | tf_op jit(solution)/shard_map/ppermute | solution.py:290
  5.6 3.2 %collective-permute-start.1 = (bf16[2,128,1024]{2,1,0:T(8,128)(2,1)}, bf16[2,128,1024]{2,1,0:T(8,128)(2,1)S(1)}, u32[]{:S(2)}, u32[]{:S(2)}) collective-permute-start(bf16[2,128,1024]{2,1,0:T(8,128)(2,1)} %join.1.own_kv), channel_id=1, source_target_pairs={{4,8},{8,4},{12,16},{16,12},{20,24},{24,20},{5,9},{9,5},{13,17},{1... | collective-permute-start | bytes 1572872 | tf_op jit(solution)/shard_map/ppermute | solution.py:289
  8.8 1.0 %copy-done.4 = bf16[1,128,2048]{2,1,0:T(8,128)(2,1)S(1)} copy-done((bf16[1,128,2048]{2,1,0:T(8,128)(2,1)S(1)}, bf16[1,128,2048]{2,1,0:T(8,128)(2,1)}, u32[]{:S(2)}) %copy-start.4) | copy-done | bytes 524312
  9.9 0.9 %copy-done.5 = bf16[1,128,1024]{2,1,0:T(8,128)(2,1)S(1)} copy-done((bf16[1,128,1024]{2,1,0:T(8,128)(2,1)S(1)}, bf16[1,128,1024]{2,1,0:T(8,128)(2,1)}, u32[]{:S(2)}) %copy-start.5) | copy-done | bytes 262168
  10.8 0.3 stage.1
  11.2 1.0 %copy-done.1 = bf16[256,2048]{1,0:T(8,128)(2,1)} copy-done((bf16[256,2048]{1,0:T(8,128)(2,1)}, bf16[256,2048]{1,0:T(8,128)(2,1)S(1)}, u32[]{:S(2)}) %copy-start.1) | copy-done | bytes 1048600
  12.3 4.0 %collective-permute-done.1.far_kv = bf16[2,128,1024]{2,1,0:T(8,128)(2,1)S(1)} collective-permute-done((bf16[2,128,1024]{2,1,0:T(8,128)(2,1)}, bf16[2,128,1024]{2,1,0:T(8,128)(2,1)S(1)}, u32[]{:S(2)}, u32[]{:S(2)}) %collective-permute-start.1) | collective-permute-done | bytes 524320 | tf_op jit(solution)/shard_map/ppermute | solution.py:289
  16.3 0.7 %copy-done.6 = s32[1,8]{1,0:T(1,128)S(1)} copy-done((s32[1,8]{1,0:T(1,128)S(1)}, s32[1,8]{1,0:T(1,128)}, u32[]{:S(2)}) %copy-start.6) | copy-done | bytes 56
  17.0 1.2 %copy-done.2 = bf16[256,2048]{1,0:T(8,128)(2,1)S(1)} copy-done((bf16[256,2048]{1,0:T(8,128)(2,1)S(1)}, bf16[256,2048]{1,0:T(8,128)(2,1)}, u32[]{:S(2)}) %copy-start.2) | copy-done | bytes 1048600
  18.2 1.7 %heads_own.1 = (bf16[128,256]{1,0:T(8,128)(2,1)S(1)}, f32[2,128,256]{2,1,0:T(8,128)S(1)}, bf16[2,128,256]{2,1,0:T(8,128)(2,1)S(1)}, bf16[2,128,256]{2,1,0:T(8,128)(2,1)S(1)}) custom-call(s32[8,4]{1,0:T(8,128)S(1)} %copy.15.pat_ref, s32[1,8]{1,0:T(1,128)S(1)} %copy-done.6, bf16[2048,128]{1,0:T(8,128)(2,1)S(1)} %get-tuple-element.25.dy_ref, ...), custom_call_target="tpu_custom_call" | custom-call | flops 1 | bytes 1 | tf_op jit(solution)/shard_map/heads_own/pallas_call | solution.py:198
  20.0 0.8 %collective-permute-start.3 = (bf16[128,2048]{1,0:T(8,128)(2,1)S(1)}, bf16[128,2048]{1,0:T(8,128)(2,1)S(1)}, u32[]{:S(2)}, u32[]{:S(2)}) collective-permute-start(bf16[128,2048]{1,0:T(8,128)(2,1)S(1)} %onward.1), channel_id=1, source_target_pairs={{0,2},{1,3},{2,0},{3,1},{4,5},{5,4},{6,7},{7,6},{8,10},{9,11},{10,... | collective-permute-start | bytes 1572872 | tf_op jit(solution)/shard_map/ppermute | solution.py:275
  20.8 1.8 %collective-permute-done.4.refs_1_ = bf16[256,2048]{1,0:T(8,128)(2,1)S(1)} collective-permute-done((bf16[256,2048]{1,0:T(8,128)(2,1)S(1)}, bf16[256,2048]{1,0:T(8,128)(2,1)S(1)}, u32[]{:S(2)}, u32[]{:S(2)}) %collective-permute-start.4) | collective-permute-done | bytes 1048608 | tf_op jit(solution)/shard_map/ppermute | solution.py:301
  22.6 2.7 %heads_side.1 = (bf16[128,768]{1,0:T(8,128)(2,1)S(1)}, f32[2,128,768]{2,1,0:T(8,128)S(1)}, bf16[2,128,768]{2,1,0:T(8,128)(2,1)S(1)}, bf16[2,128,768]{2,1,0:T(8,128)(2,1)S(1)}) custom-call(s32[8,4]{1,0:T(8,128)S(1)} %copy.15.pat_ref, s32[1,8]{1,0:T(1,128)S(1)} %copy-done.6, bf16[2048,128]{1,0:T(8,128)(2,1)S(1)} %get-tuple-element.25.dy_ref, ...), custom_call_target="tpu_custom_call" | custom-call | flops 1 | bytes 1 | tf_op jit(solution)/shard_map/heads_side/pallas_call | solution.py:198
  25.3 3.1 %collective-permute-done.3.refs_0_ = bf16[128,2048]{1,0:T(8,128)(2,1)S(1)} collective-permute-done((bf16[128,2048]{1,0:T(8,128)(2,1)S(1)}, bf16[128,2048]{1,0:T(8,128)(2,1)S(1)}, u32[]{:S(2)}, u32[]{:S(2)}) %collective-permute-start.3) | collective-permute-done | bytes 524320 | tf_op jit(solution)/shard_map/ppermute | solution.py:275
  28.4 1.3 %collective-permute-start.5 = (bf16[128,2048]{1,0:T(8,128)(2,1)S(1)}, bf16[128,2048]{1,0:T(8,128)(2,1)S(1)}, u32[]{:S(2)}, u32[]{:S(2)}) collective-permute-start(bf16[128,2048]{1,0:T(8,128)(2,1)S(1)} %collective-permute-done.3.refs_0_), channel_id=1, source_target_pairs={{0,4},{4,0},{8,12},{12,8},{16,20},{20,16},{24,28},{28,24},{1,5},{5... | collective-permute-start | bytes 1572872 | tf_op jit(solution)/shard_map/ppermute | solution.py:310
  29.7 3.8 %collective-permute-start.9 = (bf16[2,128,768]{2,1,0:T(8,128)(2,1)S(1)}, bf16[2,128,768]{2,1,0:T(8,128)(2,1)S(1)}, u32[]{:S(2)}, u32[]{:S(2)}) collective-permute-start(bf16[2,128,768]{2,1,0:T(8,128)(2,1)S(1)} %get-tuple-element.43), channel_id=1, source_target_pairs={{4,8},{8,4},{12,16},{16,12},{20,24},{24,20},{5,9},{9,5},{13,17},{1... | collective-permute-start | bytes 1179656 | tf_op jit(solution)/shard_map/ppermute | solution.py:282
  33.6 1.7 %heads_far.1 = (bf16[128,256]{1,0:T(8,128)(2,1)S(1)}, f32[2,128,256]{2,1,0:T(8,128)S(1)}, bf16[2,128,256]{2,1,0:T(8,128)(2,1)S(1)}, bf16[2,128,256]{2,1,0:T(8,128)(2,1)S(1)}) custom-call(s32[8,4]{1,0:T(8,128)S(1)} %copy.15.pat_ref, s32[1,8]{1,0:T(1,128)S(1)} %copy-done.6, bf16[2048,128]{1,0:T(8,128)(2,1)S(1)} %get-tuple-element.25.dy_ref, ...), custom_call_target="tpu_custom_call" | custom-call | flops 1 | bytes 1 | tf_op jit(solution)/shard_map/heads_far/pallas_call | solution.py:198
  35.4 3.6 %collective-permute-start.7 = (bf16[2,128,256]{2,1,0:T(8,128)(2,1)S(1)}, bf16[2,128,256]{2,1,0:T(8,128)(2,1)S(1)}, u32[]{:S(2)}, u32[]{:S(2)}) collective-permute-start(bf16[2,128,256]{2,1,0:T(8,128)(2,1)S(1)} %get-tuple-element.39), channel_id=1, source_target_pairs={{4,8},{8,4},{12,16},{16,12},{20,24},{24,20},{5,9},{9,5},{13,17},{1... | collective-permute-start | bytes 393224 | tf_op jit(solution)/shard_map/ppermute | solution.py:282
  38.9 0.1 collective-permute-done.9.refs_3_
  39.0 0.9 %finish_first.1 = (bf16[1,128,1024]{2,1,0:T(8,128)(2,1)}, bf16[1,128,1024]{2,1,0:T(8,128)(2,1)}, bf16[1,128,1024]{2,1,0:T(8,128)(2,1)}) custom-call(bf16[128,768]{1,0:T(8,128)(2,1)S(1)} %get-tuple-element.40.refs_0_, f32[2,128,768]{2,1,0:T(8,128)S(1)} %get-tuple-element.41.refs_1_, bf16[2,128,768]{2,1,0:T(8,128)(2,1)S(1)} %collective-permute-done.8.refs_2_, ...), custom_call_target="tpu_custom_call" | custom-call | flops 1 | bytes 1 | tf_op jit(solution)/shard_map/finish_first/pallas_call | solution.py:247
  40.0 1.7 %collective-permute-done.7.refs_3_ = bf16[2,128,256]{2,1,0:T(8,128)(2,1)S(1)} collective-permute-done((bf16[2,128,256]{2,1,0:T(8,128)(2,1)S(1)}, bf16[2,128,256]{2,1,0:T(8,128)(2,1)S(1)}, u32[]{:S(2)}, u32[]{:S(2)}) %collective-permute-start.7) | collective-permute-done | bytes 131104 | tf_op jit(solution)/shard_map/ppermute | solution.py:282
  41.6 0.7 %finish_last.1 = (bf16[1,128,1024]{2,1,0:T(8,128)(2,1)}, bf16[1,128,1024]{2,1,0:T(8,128)(2,1)}, bf16[1,128,1024]{2,1,0:T(8,128)(2,1)}) custom-call(bf16[128,256]{1,0:T(8,128)(2,1)S(1)} %get-tuple-element.36.refs_0_, f32[2,128,256]{2,1,0:T(8,128)S(1)} %get-tuple-element.37.refs_1_, ...), custom_call_target="tpu_custom_call", output_to_operand_aliasing={{0}: (4, {}), {1}: (5, {}), {2}: (6, {})} | custom-call | flops 1 | bytes 1 | tf_op jit(solution)/shard_map/finish_last/pallas_call | solution.py:247
  (21 shorter events, 0.3 us)
Async XLA Ops:
  0.6 8.2 %copy-start.3 = (bf16[256,2048]{1,0:T(8,128)(2,1)S(1)}, bf16[256,2048]{1,0:T(8,128)(2,1)}, u32[]{:S(2)}) copy-start(bf16[256,2048]{1,0:T(8,128)(2,1)} %w_ref.1) | copy-start | bytes 3145732
  0.6 19.2 %collective-permute-start.2 = (bf16[256,2048]{1,0:T(8,128)(2,1)}, bf16[256,2048]{1,0:T(8,128)(2,1)S(1)}, u32[]{:S(2)}, u32[]{:S(2)}) collective-permute-start(bf16[256,2048]{1,0:T(8,128)(2,1)} %w_ref.1), channel_id=1, source_target_pairs={{0,1},{1,0},{2,3},{3,2},{4,6},{5,7},{6,4},{7,5},{8,9},{9,8},{10,11... | collective-permute-start | bytes 3145736 | tf_op jit(solution)/shard_map/ppermute | solution.py:275
  4.6 11.7 %copy-start = (bf16[2,128,1024]{2,1,0:T(8,128)(2,1)S(1)}, bf16[2,128,1024]{2,1,0:T(8,128)(2,1)}, u32[]{:S(2)}) copy-start(bf16[2,128,1024]{2,1,0:T(8,128)(2,1)} %join.1.own_kv) | copy-start | bytes 1572868
  4.6 7.7 %collective-permute-start = (bf16[2,128,1024]{2,1,0:T(8,128)(2,1)}, bf16[2,128,1024]{2,1,0:T(8,128)(2,1)S(1)}, u32[]{:S(2)}, u32[]{:S(2)}) collective-permute-start(bf16[2,128,1024]{2,1,0:T(8,128)(2,1)} %join.1.own_kv), channel_id=1, source_target_pairs={{0,4},{4,0},{8,12},{12,8},{16,20},{20,16},{24,28},{28,24},{1,5},{5... | collective-permute-start | bytes 1572872 | tf_op jit(solution)/shard_map/ppermute | solution.py:290
  5.6 10.7 %collective-permute-start.1 = (bf16[2,128,1024]{2,1,0:T(8,128)(2,1)}, bf16[2,128,1024]{2,1,0:T(8,128)(2,1)S(1)}, u32[]{:S(2)}, u32[]{:S(2)}) collective-permute-start(bf16[2,128,1024]{2,1,0:T(8,128)(2,1)} %join.1.own_kv), channel_id=1, source_target_pairs={{4,8},{8,4},{12,16},{16,12},{20,24},{24,20},{5,9},{9,5},{13,17},{1... | collective-permute-start | bytes 1572872 | tf_op jit(solution)/shard_map/ppermute | solution.py:289
  8.8 1.0 %copy-start.4 = (bf16[1,128,2048]{2,1,0:T(8,128)(2,1)S(1)}, bf16[1,128,2048]{2,1,0:T(8,128)(2,1)}, u32[]{:S(2)}) copy-start(bf16[1,128,2048]{2,1,0:T(8,128)(2,1)} %dy_ref.1) | copy-start | bytes 1572868
  9.9 0.9 %copy-start.5 = (bf16[1,128,1024]{2,1,0:T(8,128)(2,1)S(1)}, bf16[1,128,1024]{2,1,0:T(8,128)(2,1)}, u32[]{:S(2)}) copy-start(bf16[1,128,1024]{2,1,0:T(8,128)(2,1)} %q_ref.1) | copy-start | bytes 786436
  10.8 1.4 %copy-start.7 = (s32[8,4]{0,1:T(4,128)S(1)}, s32[8,4]{0,1:T(4,128)}, u32[]{:S(2)}) copy-start(s32[8,4]{0,1:T(4,128)} %param.12) | copy-start | bytes 388
  11.2 1.0 %copy-start.1 = (bf16[256,2048]{1,0:T(8,128)(2,1)}, bf16[256,2048]{1,0:T(8,128)(2,1)S(1)}, u32[]{:S(2)}) copy-start(bf16[256,2048]{1,0:T(8,128)(2,1)S(1)} %get-tuple-element.27.refs_0_) | copy-start | bytes 3145732
  16.3 0.7 %copy-start.6 = (s32[1,8]{1,0:T(1,128)S(1)}, s32[1,8]{1,0:T(1,128)}, u32[]{:S(2)}) copy-start(s32[1,8]{1,0:T(1,128)} %val_ref.5) | copy-start | bytes 100
  17.0 1.2 %copy-start.2 = (bf16[256,2048]{1,0:T(8,128)(2,1)S(1)}, bf16[256,2048]{1,0:T(8,128)(2,1)}, u32[]{:S(2)}) copy-start(bf16[256,2048]{1,0:T(8,128)(2,1)} %copy-done.1) | copy-start | bytes 3145732
  19.9 2.7 %collective-permute-start.4 = (bf16[256,2048]{1,0:T(8,128)(2,1)S(1)}, bf16[256,2048]{1,0:T(8,128)(2,1)S(1)}, u32[]{:S(2)}, u32[]{:S(2)}) collective-permute-start(bf16[256,2048]{1,0:T(8,128)(2,1)S(1)} %collective-permute-done.2.w_ref.refs_0_), channel_id=1, source_target_pairs={{0,4},{4,0},{8,12},{12,8},{16,20},{20,16},{24,28},{28,24},{1,5},{5... | collective-permute-start | bytes 3145736 | tf_op jit(solution)/shard_map/ppermute | solution.py:301
  20.0 8.4 %collective-permute-start.3 = (bf16[128,2048]{1,0:T(8,128)(2,1)S(1)}, bf16[128,2048]{1,0:T(8,128)(2,1)S(1)}, u32[]{:S(2)}, u32[]{:S(2)}) collective-permute-start(bf16[128,2048]{1,0:T(8,128)(2,1)S(1)} %onward.1), channel_id=1, source_target_pairs={{0,2},{1,3},{2,0},{3,1},{4,5},{5,4},{6,7},{7,6},{8,10},{9,11},{10,... | collective-permute-start | bytes 1572872 | tf_op jit(solution)/shard_map/ppermute | solution.py:275
  28.4 5.2 %collective-permute-start.5 = (bf16[128,2048]{1,0:T(8,128)(2,1)S(1)}, bf16[128,2048]{1,0:T(8,128)(2,1)S(1)}, u32[]{:S(2)}, u32[]{:S(2)}) collective-permute-start(bf16[128,2048]{1,0:T(8,128)(2,1)S(1)} %collective-permute-done.3.refs_0_), channel_id=1, source_target_pairs={{0,4},{4,0},{8,12},{12,8},{16,20},{20,16},{24,28},{28,24},{1,5},{5... | collective-permute-start | bytes 1572872 | tf_op jit(solution)/shard_map/ppermute | solution.py:310
  29.7 9.2 %collective-permute-start.8 = (bf16[2,128,768]{2,1,0:T(8,128)(2,1)S(1)}, bf16[2,128,768]{2,1,0:T(8,128)(2,1)S(1)}, u32[]{:S(2)}, u32[]{:S(2)}) collective-permute-start(bf16[2,128,768]{2,1,0:T(8,128)(2,1)S(1)} %get-tuple-element.42), channel_id=1, source_target_pairs={{0,4},{4,0},{8,12},{12,8},{16,20},{20,16},{24,28},{28,24},{1,5},{5... | collective-permute-start | bytes 1179656 | tf_op jit(solution)/shard_map/ppermute | solution.py:283
  29.7 9.3 %collective-permute-start.9 = (bf16[2,128,768]{2,1,0:T(8,128)(2,1)S(1)}, bf16[2,128,768]{2,1,0:T(8,128)(2,1)S(1)}, u32[]{:S(2)}, u32[]{:S(2)}) collective-permute-start(bf16[2,128,768]{2,1,0:T(8,128)(2,1)S(1)} %get-tuple-element.43), channel_id=1, source_target_pairs={{4,8},{8,4},{12,16},{16,12},{20,24},{24,20},{5,9},{9,5},{13,17},{1... | collective-permute-start | bytes 1179656 | tf_op jit(solution)/shard_map/ppermute | solution.py:282
  35.3 4.7 %collective-permute-start.6 = (bf16[2,128,256]{2,1,0:T(8,128)(2,1)S(1)}, bf16[2,128,256]{2,1,0:T(8,128)(2,1)S(1)}, u32[]{:S(2)}, u32[]{:S(2)}) collective-permute-start(bf16[2,128,256]{2,1,0:T(8,128)(2,1)S(1)} %get-tuple-element.38), channel_id=1, source_target_pairs={{0,4},{4,0},{8,12},{12,8},{16,20},{20,16},{24,28},{28,24},{1,5},{5... | collective-permute-start | bytes 393224 | tf_op jit(solution)/shard_map/ppermute | solution.py:283
  35.4 6.3 %collective-permute-start.7 = (bf16[2,128,256]{2,1,0:T(8,128)(2,1)S(1)}, bf16[2,128,256]{2,1,0:T(8,128)(2,1)S(1)}, u32[]{:S(2)}, u32[]{:S(2)}) collective-permute-start(bf16[2,128,256]{2,1,0:T(8,128)(2,1)S(1)} %get-tuple-element.39), channel_id=1, source_target_pairs={{4,8},{8,4},{12,16},{16,12},{20,24},{24,20},{5,9},{9,5},{13,17},{1... | collective-permute-start | bytes 393224 | tf_op jit(solution)/shard_map/ppermute | solution.py:282

commit v6 on v5

--- a/solution.py
+++ b/solution.py
@@ -88,35 +88,6 @@
     )(got)
 
 
-def stage_kernel(dy_ref, q_ref, w_ref, turned_ref, q_out, w_rows, dy, sems):
-    pairs = [(dy_ref.at[0], dy), (q_ref.at[0], q_out), (w_ref, w_rows)]
-    copies = [pltpu.make_async_copy(s, d, sems.at[i]) for i, (s, d) in enumerate(pairs)]
-    for copy in copies:
-        copy.start()
-    copies[0].wait()
-    turned_ref[...] = dy[...].T
-    for copy in copies[1:]:
-        copy.wait()
-
-
-def stage(d_out, queries, w_out):
-    tok, depth = d_out.shape[1:]
-    return pl.pallas_call(
-        stage_kernel,
-        out_shape=(
-            jax.ShapeDtypeStruct((depth, tok), BF16),
-            jax.ShapeDtypeStruct(queries.shape[1:], BF16),
-            jax.ShapeDtypeStruct(w_out.shape, BF16),
-        ),
-        in_specs=[HBM] * 3,
-        out_specs=(VMEM,) * 3,
-        scratch_shapes=[pltpu.VMEM((tok, depth), BF16), pltpu.SemaphoreType.DMA((3,))],
-        cost_estimate=BRIEF,
-        compiler_params=PARAMS,
-        name="stage",
-    )(d_out, queries, w_out)
-
-
 def key_limits(pat_ref, val_ref):
     shard = lax.axis_index("seq")
     count = val_ref.shape[1]
@@ -133,6 +104,39 @@
     return limits
 
 
+def stage_kernel(pat_ref, val_ref, dy_ref, q_ref, turned_ref, q_out, limit_ref, dy, sems):
+    copies = [
+        pltpu.make_async_copy(dy_ref.at[0], dy, sems.at[0]),
+        pltpu.make_async_copy(q_ref.at[0], q_out, sems.at[1]),
+    ]
+    for copy in copies:
+        copy.start()
+    limit_ref[...] = jnp.zeros_like(limit_ref)
+    for row, limit in enumerate(key_limits(pat_ref, val_ref)):
+        limit_ref[row : row + 1, :] = jnp.full((1, PAIR), limit, jnp.int32)
+    copies[0].wait()
+    turned_ref[...] = dy[...].T
+    copies[1].wait()
+
+
+def stage(d_out, queries, pattern, valid):
+    tok, depth = d_out.shape[1:]
+    return pl.pallas_call(
+        stage_kernel,
+        out_shape=(
+            jax.ShapeDtypeStruct((depth, tok), BF16),
+            jax.ShapeDtypeStruct(queries.shape[1:], BF16),
+            jax.ShapeDtypeStruct((8, PAIR), jnp.int32),
+        ),
+        in_specs=[SMEM] * 2 + [HBM] * 2,
+        out_specs=(VMEM,) * 3,
+        scratch_shapes=[pltpu.VMEM((tok, depth), BF16), pltpu.SemaphoreType.DMA((2,))],
+        cost_estimate=BRIEF,
+        compiler_params=PARAMS,
+        name="stage",
+    )(pattern, valid, d_out, queries)
+
+
 def diagonal(x):
     zero = jnp.zeros((x.shape[0], HD), x.dtype)
     return jnp.concatenate(
@@ -148,7 +152,7 @@
     return pl.ds(pl.multiple_of(chunk * PAIR, PAIR), PAIR)
 
 
-def attention_kernel(steps, carried, pat_ref, val_ref, dy_ref, q_ref, own_kv, core_kv, far_kv, *refs):
+def attention_kernel(steps, carried, dy_ref, q_ref, limit_ref, own_kv, core_kv, far_kv, *refs):
     core, group = place()
     w_refs, earlier, outs = refs[: -4 - carried], refs[-4 - carried : -4], refs[-4:]
     dq_ref, own_ref, to_core_ref, to_far_ref = outs
@@ -157,7 +161,7 @@
     scale = HD ** (-0.5)
     tok = q_ref.shape[0]
     rows = lax.broadcasted_iota(jnp.int32, (tok, PAIR), 0)
-    open_keys = jnp.concatenate([rows < limit for limit in key_limits(pat_ref, val_ref)], axis=0)
+    open_keys = jnp.concatenate([rows < limit_ref[i : i + 1, :] for i in range(3)], axis=0)
     for chunk, slot, halves, lead in steps(core, group):
         cols, dest = columns(chunk), columns(slot)
         w = jnp.concatenate([w_refs[i][row : row + HD, :] for i, row in halves], axis=0)
@@ -190,10 +194,9 @@
             to_far_ref[side, :, dest] = grad[2 * tok :].astype(BF16)
 
 
-def attention(name, steps, weights, earlier, pattern, valid, staged, halo):
+def attention(name, steps, weights, earlier, staged, halo):
     count = len(steps(0, 0))
-    turned, q = staged
-    depth, tok = turned.shape
+    tok = staged[0].shape[1]
     width = count * PAIR + (earlier[0].shape[1] if earlier else 0)
     return pl.pallas_call(
         functools.partial(attention_kernel, steps, len(earlier)),
@@ -203,12 +206,12 @@
             jax.ShapeDtypeStruct((2, tok, width), BF16),
             jax.ShapeDtypeStruct((2, tok, width), BF16),
         ),
-        in_specs=[SMEM] * 2 + [VMEM] * (5 + len(weights) + len(earlier)),
+        in_specs=[VMEM] * (6 + len(weights) + len(earlier)),
         out_specs=(VMEM,) * 4,
         cost_estimate=BRIEF,
         compiler_params=PARAMS,
         name=name,
-    )(pattern, valid, turned, q, *halo, *weights, *earlier)
+    )(*staged, *halo, *weights, *earlier)
 
 
 def finish_kernel(chunks, n_parts, n_old, *refs):
@@ -275,7 +278,7 @@
         return lax.ppermute(x, ("seq", "fsdp"), pairs)
 
     def heads(name, steps, weights, earlier=()):
-        return attention(name, steps, weights, earlier, pattern, valid, staged, halo)
+        return attention(name, steps, weights, earlier, staged, halo)
 
     def exchange(part):
         dq, own, to_core, to_far = part
@@ -283,15 +286,14 @@
         return dq, own, near(to_core), back
 
     kv = join(keys, values)
-    *staged, w_rows = stage(d_out, queries, w_out)
+    staged = stage(d_out, queries, pattern, valid)
     if n_fsdp == 4 and n_chunks == 4 and w_out.shape[0] == PAIR:
         got = cross(w_out, (1, 2))
-        kv_far = far(kv)
-        halo = kv, near(kv), kv_far
-        part = heads("heads_own", lambda core, group: [(group, 0, ((0, 0), (0, HD)), 0)], [w_rows])
-        got, dq = lax.optimization_barrier((got, part[0]))
-        part = (dq, *part[1:])
+        early = got, kv, near(kv), far(kv), *staged
+        got, *early = lax.optimization_barrier(early)
+        halo, staged = early[:3], early[3:]
         got_d = cross(onward(got), (2, 1))
+        part = heads("heads_own", lambda core, group: [(group, 0, ((0, 0), (0, HD)), 0)], [w_out])
         part = heads(
             "heads_side",
             lambda core, group: [

time: 42.7 us -> 38.6 us (0.904)
  local copies, waits for them, and re-layouts: 4.95 us -> 0.11 us
  waiting for transfers between devices: 10.7 us -> 12 us
  Pallas kernels: 9.87 us -> 8.68 us
  starting transfers between devices: 16 us -> 16.8 us
    unnamed x17 -> x13, local copies, waits for them, and re-layouts: 4.95 us -> 0.11 us
    ppermute x2, waiting for transfers between devices: 4.05 us -> 6.6 us  [body(): early = (got, kv, near(kv), far(kv), *staged)]
    ppermute x1, waiting for transfers between devices: 1.82 us -> 0.01 us  [body(): near(got)]
    pallas_call x3, Pallas kernels: 6.04 us -> 4.3 us  [attention(): pl.pallas_call(functools.partial(attention_kernel, steps, len(earlier)),...]
    ppermute x2, starting transfers between devices: 2.9 us -> 3.94 us  [cross(): return lax.ppermute(x, ('seq', 'fsdp'), pairs)]
    ppermute x1, starting transfers between devices: 1.33 us -> 0.7 us  [body(): near(got_d)]
    pallas_call x1, Pallas kernels: 0.35 us -> 0.9 us  [stage(): pl.pallas_call(stage_kernel, out_shape=(jax.ShapeDtypeStruct((depth, tok)...]
    ppermute x2, waiting for transfers between devices: 3.11 us -> 3.63 us  [cross(): return lax.ppermute(x, ('seq', 'fsdp'), pairs)]
  transfers between devices with their start and end apart: 10 -> 10, of which waited for: 5 -> 4; matrix products, arithmetic and copies ran while one was open for 0% -> 0% of each run, Pallas kernels for 22% -> 21%
where the time goes in v6:
time: 38.6 us; the launch traced here: 38.3 us
  starting transfers between devices  16.8 us (44%)
  waiting for transfers between devices  12 us (31%)
  Pallas kernels  8.68 us (22%)
  between operations  0.8 us (2%)
    ppermute x2, starting transfers between devices, exchange(): back = far(to_far)  7.57 us
    ppermute x2, waiting for transfers between devices, body(): early = (got, kv, near(kv), far(kv), *staged)  6.6 us
    pallas_call x3, Pallas kernels, attention(): pl.pallas_call(functools.partial(attention_kernel, steps, len(earlier)),...  4.3 us
    ppermute x2, starting transfers between devices, body(): early = (got, kv, near(kv), far(kv), *staged)  4.09 us
    ppermute x2, starting transfers between devices, cross(): return lax.ppermute(x, ('seq', 'fsdp'), pairs)  3.94 us
    ppermute x2, waiting for transfers between devices, cross(): return lax.ppermute(x, ('seq', 'fsdp'), pairs)  3.63 us
    pallas_call x1, Pallas kernels, join(): pl.pallas_call(join_kernel, out_shape=jax.ShapeDtypeStruct(shape, BF16),...  1.77 us
    ppermute x2, waiting for transfers between devices, exchange(): back = far(to_far)  1.74 us
  transfers between devices with their start and end apart: 10, of which 4 were waited for; matrix products, arithmetic and copies ran while one was open for 0% of the time, Pallas kernels for 21%

profile of v6, /device:TPU:1, one launch (start us, length us, event | category | flops | bytes accessed | tf_op | source)
XLA Modules:
  0.0 38.3 jit_solution(4341028876418135650)
XLA Ops:
  0.7 2.1 %collective-permute-start = (bf16[256,2048]{1,0:T(8,128)(2,1)}, bf16[256,2048]{1,0:T(8,128)(2,1)S(1)}, u32[]{:S(2)}, u32[]{:S(2)}) collective-permute-start(bf16[256,2048]{1,0:T(8,128)(2,1)} %refs_0_.1), channel_id=1, source_target_pairs={{0,1},{1,0},{2,3},{3,2},{4,6},{5,7},{6,4},{7,5},{8,9},{9,8},{10,11... | collective-permute-start | bytes 3145736 | tf_op jit(solution)/shard_map/ppermute | solution.py:278
  2.8 1.8 %join.1.own_kv = bf16[2,128,1024]{2,1,0:T(8,128)(2,1)} custom-call(bf16[1,128,1024]{2,1,0:T(8,128)(2,1)} %k_ref.1, bf16[1,128,1024]{2,1,0:T(8,128)(2,1)} %v_ref.1), custom_call_target="tpu_custom_call" | custom-call | flops 1 | bytes 1 | tf_op jit(solution)/shard_map/join/pallas_call | solution.py:61
  4.6 0.0 copy-start.4
  4.6 1.0 %collective-permute-start.1 = (bf16[2,128,1024]{2,1,0:T(8,128)(2,1)}, bf16[2,128,1024]{2,1,0:T(8,128)(2,1)S(1)}, u32[]{:S(2)}, u32[]{:S(2)}) collective-permute-start(bf16[2,128,1024]{2,1,0:T(8,128)(2,1)} %join.1.own_kv), channel_id=1, source_target_pairs={{0,4},{4,0},{8,12},{12,8},{16,20},{20,16},{24,28},{28,24},{1,5},{5... | collective-permute-start | bytes 1572872 | tf_op jit(solution)/shard_map/ppermute | solution.py:292
  5.6 3.1 %collective-permute-start.2 = (bf16[2,128,1024]{2,1,0:T(8,128)(2,1)}, bf16[2,128,1024]{2,1,0:T(8,128)(2,1)S(1)}, u32[]{:S(2)}, u32[]{:S(2)}) collective-permute-start(bf16[2,128,1024]{2,1,0:T(8,128)(2,1)} %join.1.own_kv), channel_id=1, source_target_pairs={{4,8},{8,4},{12,16},{16,12},{20,24},{24,20},{5,9},{9,5},{13,17},{1... | collective-permute-start | bytes 1572872 | tf_op jit(solution)/shard_map/ppermute | solution.py:292
  8.7 0.1 copy.13.pat_ref
  8.8 0.9 %stage.1 = (bf16[2048,128]{1,0:T(8,128)(2,1)S(1)}, bf16[128,1024]{1,0:T(8,128)(2,1)S(1)}, s32[8,256]{1,0:T(8,128)S(1)}) custom-call(s32[8,4]{1,0:T(8,128)S(1)} %copy.13.pat_ref, s32[1,8]{1,0:T(1,128)S(1)} %copy-done.4, bf16[1,128,2048]{2,1,0:T(8,128)(2,1)S(1)} %copy-done.2, bf16[1,128,1024]{2,1,0:T(8,128)(2,1)S(1)} %copy-done.3), custom_call_target="tpu_custom_call" | custom-call | flops 1 | bytes 1 | tf_op jit(solution)/shard_map/stage/pallas_call | solution.py:124
  9.7 6.6 %collective-permute-done.2.far_kv = bf16[2,128,1024]{2,1,0:T(8,128)(2,1)S(1)} collective-permute-done((bf16[2,128,1024]{2,1,0:T(8,128)(2,1)}, bf16[2,128,1024]{2,1,0:T(8,128)(2,1)S(1)}, u32[]{:S(2)}, u32[]{:S(2)}) %collective-permute-start.2) | collective-permute-done | bytes 524320 | tf_op jit(solution)/shard_map/ppermute | solution.py:292
  16.3 0.0 collective-permute-done.w_ref.refs_0_
  16.3 0.4 %collective-permute-start.4 = (bf16[256,2048]{1,0:T(8,128)(2,1)S(1)}, bf16[256,2048]{1,0:T(8,128)(2,1)S(1)}, u32[]{:S(2)}, u32[]{:S(2)}) collective-permute-start(bf16[256,2048]{1,0:T(8,128)(2,1)S(1)} %collective-permute-done.w_ref.refs_0_), channel_id=1, source_target_pairs={{0,4},{4,0},{8,12},{12,8},{16,20},{20,16},{24,28},{28,24},{1,5},{5... | collective-permute-start | bytes 3145736 | tf_op jit(solution)/shard_map/ppermute | solution.py:303
  16.8 1.8 %collective-permute-start.3 = (bf16[128,2048]{1,0:T(8,128)(2,1)S(1)}, bf16[128,2048]{1,0:T(8,128)(2,1)S(1)}, u32[]{:S(2)}, u32[]{:S(2)}) collective-permute-start(bf16[128,2048]{1,0:T(8,128)(2,1)S(1)} %onward.1), channel_id=1, source_target_pairs={{0,2},{1,3},{2,0},{3,1},{4,5},{5,4},{6,7},{7,6},{8,10},{9,11},{10,... | collective-permute-start | bytes 1572872 | tf_op jit(solution)/shard_map/ppermute | solution.py:278
  18.6 1.1 %heads_own.1 = (bf16[128,256]{1,0:T(8,128)(2,1)S(1)}, f32[2,128,256]{2,1,0:T(8,128)S(1)}, bf16[2,128,256]{2,1,0:T(8,128)(2,1)S(1)}, bf16[2,128,256]{2,1,0:T(8,128)(2,1)S(1)}) custom-call(bf16[2048,128]{1,0:T(8,128)(2,1)S(1)} %get-tuple-element.33.dy_ref, bf16[128,1024]{1,0:T(8,128)(2,1)S(1)} %get-tuple-element.34.q_ref, ...), custom_call_target="tpu_custom_call" | custom-call | flops 1 | bytes 1 | tf_op jit(solution)/shard_map/heads_own/pallas_call | solution.py:201
  19.7 2.1 %heads_side.1 = (bf16[128,768]{1,0:T(8,128)(2,1)S(1)}, f32[2,128,768]{2,1,0:T(8,128)S(1)}, bf16[2,128,768]{2,1,0:T(8,128)(2,1)S(1)}, bf16[2,128,768]{2,1,0:T(8,128)(2,1)S(1)}) custom-call(bf16[2048,128]{1,0:T(8,128)(2,1)S(1)} %get-tuple-element.33.dy_ref, bf16[128,1024]{1,0:T(8,128)(2,1)S(1)} %get-tuple-element.34.q_ref, ...), custom_call_target="tpu_custom_call" | custom-call | flops 1 | bytes 1 | tf_op jit(solution)/shard_map/heads_side/pallas_call | solution.py:201
  21.8 3.6 %collective-permute-done.3.refs_0_ = bf16[128,2048]{1,0:T(8,128)(2,1)S(1)} collective-permute-done((bf16[128,2048]{1,0:T(8,128)(2,1)S(1)}, bf16[128,2048]{1,0:T(8,128)(2,1)S(1)}, u32[]{:S(2)}, u32[]{:S(2)}) %collective-permute-start.3) | collective-permute-done | bytes 524320 | tf_op jit(solution)/shard_map/ppermute | solution.py:278
  25.4 0.7 %collective-permute-start.5 = (bf16[128,2048]{1,0:T(8,128)(2,1)S(1)}, bf16[128,2048]{1,0:T(8,128)(2,1)S(1)}, u32[]{:S(2)}, u32[]{:S(2)}) collective-permute-start(bf16[128,2048]{1,0:T(8,128)(2,1)S(1)} %collective-permute-done.3.refs_0_), channel_id=1, source_target_pairs={{0,4},{4,0},{8,12},{12,8},{16,20},{20,16},{24,28},{28,24},{1,5},{5... | collective-permute-start | bytes 1572872 | tf_op jit(solution)/shard_map/ppermute | solution.py:312
  26.1 0.0 collective-permute-start.8
  26.1 4.0 %collective-permute-start.9 = (bf16[2,128,768]{2,1,0:T(8,128)(2,1)S(1)}, bf16[2,128,768]{2,1,0:T(8,128)(2,1)S(1)}, u32[]{:S(2)}, u32[]{:S(2)}) collective-permute-start(bf16[2,128,768]{2,1,0:T(8,128)(2,1)S(1)} %get-tuple-element.53), channel_id=1, source_target_pairs={{4,8},{8,4},{12,16},{16,12},{20,24},{24,20},{5,9},{9,5},{13,17},{1... | collective-permute-start | bytes 1179656 | tf_op jit(solution)/shard_map/ppermute | solution.py:285
  30.1 1.1 %heads_far.1 = (bf16[128,256]{1,0:T(8,128)(2,1)S(1)}, f32[2,128,256]{2,1,0:T(8,128)S(1)}, bf16[2,128,256]{2,1,0:T(8,128)(2,1)S(1)}, bf16[2,128,256]{2,1,0:T(8,128)(2,1)S(1)}) custom-call(bf16[2048,128]{1,0:T(8,128)(2,1)S(1)} %get-tuple-element.33.dy_ref, bf16[128,1024]{1,0:T(8,128)(2,1)S(1)} %get-tuple-element.34.q_ref, ...), custom_call_target="tpu_custom_call" | custom-call | flops 1 | bytes 1 | tf_op jit(solution)/shard_map/heads_far/pallas_call | solution.py:201
  31.2 0.1 collective-permute-start.6
  31.3 3.6 %collective-permute-start.7 = (bf16[2,128,256]{2,1,0:T(8,128)(2,1)S(1)}, bf16[2,128,256]{2,1,0:T(8,128)(2,1)S(1)}, u32[]{:S(2)}, u32[]{:S(2)}) collective-permute-start(bf16[2,128,256]{2,1,0:T(8,128)(2,1)S(1)} %get-tuple-element.49), channel_id=1, source_target_pairs={{4,8},{8,4},{12,16},{16,12},{20,24},{24,20},{5,9},{9,5},{13,17},{1... | collective-permute-start | bytes 393224 | tf_op jit(solution)/shard_map/ppermute | solution.py:285
  34.9 0.7 %collective-permute-done.9.refs_3_ = bf16[2,128,768]{2,1,0:T(8,128)(2,1)S(1)} collective-permute-done((bf16[2,128,768]{2,1,0:T(8,128)(2,1)S(1)}, bf16[2,128,768]{2,1,0:T(8,128)(2,1)S(1)}, u32[]{:S(2)}, u32[]{:S(2)}) %collective-permute-start.9) | collective-permute-done | bytes 393248 | tf_op jit(solution)/shard_map/ppermute | solution.py:285
  35.6 0.9 %finish_first.1 = (bf16[1,128,1024]{2,1,0:T(8,128)(2,1)}, bf16[1,128,1024]{2,1,0:T(8,128)(2,1)}, bf16[1,128,1024]{2,1,0:T(8,128)(2,1)}) custom-call(bf16[128,768]{1,0:T(8,128)(2,1)S(1)} %get-tuple-element.50.refs_0_, f32[2,128,768]{2,1,0:T(8,128)S(1)} %get-tuple-element.51.refs_1_, bf16[2,128,768]{2,1,0:T(8,128)(2,1)S(1)} %collective-permute-done.8.refs_2_, ...), custom_call_target="tpu_custom_call" | custom-call | flops 1 | bytes 1 | tf_op jit(solution)/shard_map/finish_first/pallas_call | solution.py:250
  36.5 1.1 %collective-permute-done.7.refs_3_ = bf16[2,128,256]{2,1,0:T(8,128)(2,1)S(1)} collective-permute-done((bf16[2,128,256]{2,1,0:T(8,128)(2,1)S(1)}, bf16[2,128,256]{2,1,0:T(8,128)(2,1)S(1)}, u32[]{:S(2)}, u32[]{:S(2)}) %collective-permute-start.7) | collective-permute-done | bytes 131104 | tf_op jit(solution)/shard_map/ppermute | solution.py:285
  37.6 0.7 %finish_last.1 = (bf16[1,128,1024]{2,1,0:T(8,128)(2,1)}, bf16[1,128,1024]{2,1,0:T(8,128)(2,1)}, bf16[1,128,1024]{2,1,0:T(8,128)(2,1)}) custom-call(bf16[128,256]{1,0:T(8,128)(2,1)S(1)} %get-tuple-element.46.refs_0_, f32[2,128,256]{2,1,0:T(8,128)S(1)} %get-tuple-element.47.refs_1_, ...), custom_call_target="tpu_custom_call", output_to_operand_aliasing={{0}: (4, {}), {1}: (5, {}), {2}: (6, {})} | custom-call | flops 1 | bytes 1 | tf_op jit(solution)/shard_map/finish_last/pallas_call | solution.py:250
  (17 shorter events, 0.1 us)
Async XLA Ops:
  0.6 8.1 %copy-start.5 = (s32[8,4]{0,1:T(4,128)S(1)}, s32[8,4]{0,1:T(4,128)}, u32[]{:S(2)}) copy-start(s32[8,4]{0,1:T(4,128)} %param.12) | copy-start | bytes 388
  0.6 8.1 %copy-start.2 = (bf16[1,128,2048]{2,1,0:T(8,128)(2,1)S(1)}, bf16[1,128,2048]{2,1,0:T(8,128)(2,1)}, u32[]{:S(2)}) copy-start(bf16[1,128,2048]{2,1,0:T(8,128)(2,1)} %dy_ref.1) | copy-start | bytes 1572868
  0.7 8.1 %copy-start.3 = (bf16[1,128,1024]{2,1,0:T(8,128)(2,1)S(1)}, bf16[1,128,1024]{2,1,0:T(8,128)(2,1)}, u32[]{:S(2)}) copy-start(bf16[1,128,1024]{2,1,0:T(8,128)(2,1)} %q_ref.1) | copy-start | bytes 786436
  0.7 15.7 %collective-permute-start = (bf16[256,2048]{1,0:T(8,128)(2,1)}, bf16[256,2048]{1,0:T(8,128)(2,1)S(1)}, u32[]{:S(2)}, u32[]{:S(2)}) collective-permute-start(bf16[256,2048]{1,0:T(8,128)(2,1)} %refs_0_.1), channel_id=1, source_target_pairs={{0,1},{1,0},{2,3},{3,2},{4,6},{5,7},{6,4},{7,5},{8,9},{9,8},{10,11... | collective-permute-start | bytes 3145736 | tf_op jit(solution)/shard_map/ppermute | solution.py:278
  4.6 4.2 %copy-start.4 = (s32[1,8]{1,0:T(1,128)S(1)}, s32[1,8]{1,0:T(1,128)}, u32[]{:S(2)}) copy-start(s32[1,8]{1,0:T(1,128)} %val_ref.1) | copy-start | bytes 100
  4.6 5.1 %collective-permute-start.1 = (bf16[2,128,1024]{2,1,0:T(8,128)(2,1)}, bf16[2,128,1024]{2,1,0:T(8,128)(2,1)S(1)}, u32[]{:S(2)}, u32[]{:S(2)}) collective-permute-start(bf16[2,128,1024]{2,1,0:T(8,128)(2,1)} %join.1.own_kv), channel_id=1, source_target_pairs={{0,4},{4,0},{8,12},{12,8},{16,20},{20,16},{24,28},{28,24},{1,5},{5... | collective-permute-start | bytes 1572872 | tf_op jit(solution)/shard_map/ppermute | solution.py:292
  5.6 10.7 %collective-permute-start.2 = (bf16[2,128,1024]{2,1,0:T(8,128)(2,1)}, bf16[2,128,1024]{2,1,0:T(8,128)(2,1)S(1)}, u32[]{:S(2)}, u32[]{:S(2)}) collective-permute-start(bf16[2,128,1024]{2,1,0:T(8,128)(2,1)} %join.1.own_kv), channel_id=1, source_target_pairs={{4,8},{8,4},{12,16},{16,12},{20,24},{24,20},{5,9},{9,5},{13,17},{1... | collective-permute-start | bytes 1572872 | tf_op jit(solution)/shard_map/ppermute | solution.py:292
  8.8 9.8 %copy-start.1 = (bf16[256,2048]{1,0:T(8,128)(2,1)S(1)}, bf16[256,2048]{1,0:T(8,128)(2,1)}, u32[]{:S(2)}) copy-start(bf16[256,2048]{1,0:T(8,128)(2,1)} %refs_0_.1) | copy-start | bytes 3145732
  16.3 2.2 %copy-start = (bf16[2,128,1024]{2,1,0:T(8,128)(2,1)S(1)}, bf16[2,128,1024]{2,1,0:T(8,128)(2,1)}, u32[]{:S(2)}) copy-start(bf16[2,128,1024]{2,1,0:T(8,128)(2,1)} %join.1.own_kv) | copy-start | bytes 1572868
  16.3 3.3 %collective-permute-start.4 = (bf16[256,2048]{1,0:T(8,128)(2,1)S(1)}, bf16[256,2048]{1,0:T(8,128)(2,1)S(1)}, u32[]{:S(2)}, u32[]{:S(2)}) collective-permute-start(bf16[256,2048]{1,0:T(8,128)(2,1)S(1)} %collective-permute-done.w_ref.refs_0_), channel_id=1, source_target_pairs={{0,4},{4,0},{8,12},{12,8},{16,20},{20,16},{24,28},{28,24},{1,5},{5... | collective-permute-start | bytes 3145736 | tf_op jit(solution)/shard_map/ppermute | solution.py:303
  16.8 8.7 %collective-permute-start.3 = (bf16[128,2048]{1,0:T(8,128)(2,1)S(1)}, bf16[128,2048]{1,0:T(8,128)(2,1)S(1)}, u32[]{:S(2)}, u32[]{:S(2)}) collective-permute-start(bf16[128,2048]{1,0:T(8,128)(2,1)S(1)} %onward.1), channel_id=1, source_target_pairs={{0,2},{1,3},{2,0},{3,1},{4,5},{5,4},{6,7},{7,6},{8,10},{9,11},{10,... | collective-permute-start | bytes 1572872 | tf_op jit(solution)/shard_map/ppermute | solution.py:278
  25.4 4.7 %collective-permute-start.5 = (bf16[128,2048]{1,0:T(8,128)(2,1)S(1)}, bf16[128,2048]{1,0:T(8,128)(2,1)S(1)}, u32[]{:S(2)}, u32[]{:S(2)}) collective-permute-start(bf16[128,2048]{1,0:T(8,128)(2,1)S(1)} %collective-permute-done.3.refs_0_), channel_id=1, source_target_pairs={{0,4},{4,0},{8,12},{12,8},{16,20},{20,16},{24,28},{28,24},{1,5},{5... | collective-permute-start | bytes 1572872 | tf_op jit(solution)/shard_map/ppermute | solution.py:312
  26.1 8.8 %collective-permute-start.8 = (bf16[2,128,768]{2,1,0:T(8,128)(2,1)S(1)}, bf16[2,128,768]{2,1,0:T(8,128)(2,1)S(1)}, u32[]{:S(2)}, u32[]{:S(2)}) collective-permute-start(bf16[2,128,768]{2,1,0:T(8,128)(2,1)S(1)} %get-tuple-element.52), channel_id=1, source_target_pairs={{0,4},{4,0},{8,12},{12,8},{16,20},{20,16},{24,28},{28,24},{1,5},{5... | collective-permute-start | bytes 1179656 | tf_op jit(solution)/shard_map/ppermute | solution.py:286
  26.1 9.4 %collective-permute-start.9 = (bf16[2,128,768]{2,1,0:T(8,128)(2,1)S(1)}, bf16[2,128,768]{2,1,0:T(8,128)(2,1)S(1)}, u32[]{:S(2)}, u32[]{:S(2)}) collective-permute-start(bf16[2,128,768]{2,1,0:T(8,128)(2,1)S(1)} %get-tuple-element.53), channel_id=1, source_target_pairs={{4,8},{8,4},{12,16},{16,12},{20,24},{24,20},{5,9},{9,5},{13,17},{1... | collective-permute-start | bytes 1179656 | tf_op jit(solution)/shard_map/ppermute | solution.py:285
  31.2 5.3 %collective-permute-start.6 = (bf16[2,128,256]{2,1,0:T(8,128)(2,1)S(1)}, bf16[2,128,256]{2,1,0:T(8,128)(2,1)S(1)}, u32[]{:S(2)}, u32[]{:S(2)}) collective-permute-start(bf16[2,128,256]{2,1,0:T(8,128)(2,1)S(1)} %get-tuple-element.48), channel_id=1, source_target_pairs={{0,4},{4,0},{8,12},{12,8},{16,20},{20,16},{24,28},{28,24},{1,5},{5... | collective-permute-start | bytes 393224 | tf_op jit(solution)/shard_map/ppermute | solution.py:286
  31.3 6.3 %collective-permute-start.7 = (bf16[2,128,256]{2,1,0:T(8,128)(2,1)S(1)}, bf16[2,128,256]{2,1,0:T(8,128)(2,1)S(1)}, u32[]{:S(2)}, u32[]{:S(2)}) collective-permute-start(bf16[2,128,256]{2,1,0:T(8,128)(2,1)S(1)} %get-tuple-element.49), channel_id=1, source_target_pairs={{4,8},{8,4},{12,16},{16,12},{20,24},{24,20},{5,9},{9,5},{13,17},{1... | collective-permute-start | bytes 393224 | tf_op jit(solution)/shard_map/ppermute | solution.py:285

commit v7 on v5

v7 whole, which is shorter than its diff:
```python
import functools

import jax
import jax.numpy as jnp
from jax import lax
from jax.experimental import pallas as pl
from jax.experimental.pallas import tpu as pltpu
from jax.sharding import PartitionSpec as P

HD = 128
PAIR = 2 * HD
EXTRA = 16
PIECE = 64
BRIEF = pl.CostEstimate(flops=1, bytes_accessed=1, transcendentals=0)
F32 = jnp.float32
BF16 = jnp.bfloat16
NT = (((1,), (1,)), ((), ()))
NN = (((1,), (0,)), ((), ()))
TN = (((0,), (0,)), ((), ()))
HBM = pl.BlockSpec(memory_space=pltpu.HBM)
ANY = pl.BlockSpec(memory_space=pl.ANY)
VMEM = pl.BlockSpec(memory_space=pltpu.VMEM)
SMEM = pl.BlockSpec(memory_space=pltpu.SMEM)
PARAMS = pltpu.CompilerParams(vmem_limit_bytes=40 * 2**20)
WIDE = pltpu.CompilerParams(vmem_limit_bytes=58 * 2**20)
SCALE = HD ** (-0.5)


def dot(a, b, dims):
    return lax.dot_general(a, b, dims, preferred_element_type=F32)


def swap(n, offset):
    pairs = []
    for i in range(offset, n - 1, 2):
        pairs += [(i, i + 1), (i + 1, i)]
    return pairs


def place():
    return lax.rem(lax.axis_index("seq"), 2), lax.axis_index("fsdp")


def columns(chunk):
    return pl.ds(pl.multiple_of(chunk * PAIR, PAIR), PAIR)


def call(kernel, name, out_shape, in_specs, out_specs, scratch, *args):
    return pl.pallas_call(
        kernel,
        out_shape=out_shape,
        in_specs=in_specs,
        out_specs=out_specs,
        scratch_shapes=scratch,
        cost_estimate=BRIEF,
        compiler_params=PARAMS,
        name=name,
    )(*args)


def key_limits(pat_ref, val_ref):
    shard = lax.axis_index("seq")
    count = val_ref.shape[1]
    odd = lax.rem(shard, 2)
    blocks = (shard, shard + 1 - 2 * odd, shard - 1 + 2 * odd)
    limits = []
    for row, block in [(shard, block) for block in blocks] + [(block, shard) for block in blocks[1:]]:
        held = jnp.clip(row, 0, count - 1)
        listed = pat_ref[held, 0] == block
        for entry in range(1, pat_ref.shape[1]):
            listed = jnp.logical_or(listed, pat_ref[held, entry] == block)
        inside = jnp.logical_and(row == held, jnp.logical_and(block >= 0, block < count))
        keys = val_ref[0, jnp.clip(block, 0, count - 1)]
        limits.append(jnp.where(jnp.logical_and(listed, inside), keys, 0))
    return limits


def pack_kernel(last, pat_ref, val_ref, dy_ref, q_ref, limit_ref, both_ref):
    core, group = place()
    depth = dy_ref.shape[2]
    limit_ref[...] = jnp.zeros_like(limit_ref)
    for row, limit in enumerate(key_limits(pat_ref, val_ref)):
        limit_ref[row : row + 1, :] = jnp.full((1, PAIR), limit, jnp.int32)
    both_ref[:, :depth] = dy_ref[0]
    both_ref[:, depth:] = q_ref[0, :, columns(last(core, group))]


def pack(last, pattern, valid, d_out, queries):
    tok, depth = d_out.shape[1:]
    return call(
        functools.partial(pack_kernel, last),
        "pack",
        (
            jax.ShapeDtypeStruct((8, PAIR), jnp.int32),
            jax.ShapeDtypeStruct((tok, depth + PAIR), BF16),
        ),
        [SMEM] * 2 + [VMEM] * 2,
        (VMEM,) * 2,
        [],
        pattern,
        valid,
        d_out,
        queries,
    )


def join_kernel(k_ref, v_ref, kv_ref, buffer, sems):
    arrivals, moves = [], []
    for side, ref in enumerate((k_ref, v_ref)):
        for row in range(0, ref.shape[1], PIECE):
            rows = pl.ds(row, PIECE)
            held, i = buffer.at[side, rows, :], len(moves)
            arrivals.append(pltpu.make_async_copy(ref.at[0, rows, :], held, sems.at[0, i]))
            moves.append(pltpu.make_async_copy(held, kv_ref.at[side, rows, :], sems.at[1, i]))
    for copy in arrivals:
        copy.start()
    for arrival, move in zip(arrivals, moves):
        arrival.wait()
        move.start()
    for move in moves:
        move.wait()


def join(keys, values):
    shape = (2,) + keys.shape[1:]
    copies = 2 * (shape[1] // PIECE)
    return pl.pallas_call(
        join_kernel,
        out_shape=jax.ShapeDtypeStruct(shape, BF16),
        in_specs=[HBM] * 2,
        out_specs=ANY,
        scratch_shapes=[pltpu.VMEM(shape, BF16), pltpu.SemaphoreType.DMA((2, copies))],
        cost_estimate=BRIEF,
        compiler_params=WIDE,
        name="join",
    )(keys, values)


def onward_kernel(w_ref, *out_refs):
    core, _ = place()
    half = w_ref.shape[0] // 2
    start = pl.multiple_of(core * half, half)
    for i, ref in enumerate(out_refs[:2]):
        rows = ref.shape[0]
        ref[...] = w_ref[pl.ds(start + i * rows, rows), :]
    for ref, first in zip(out_refs[2:], (start, half - start)):
        ref[...] = w_ref[pl.ds(pl.multiple_of(first, half), half), :]


def onward(got):
    rows, depth = got.shape
    shapes = [jax.ShapeDtypeStruct((rows // part, depth), BF16) for part in (4, 4, 2, 2)]
    return call(onward_kernel, "onward", tuple(shapes), [VMEM], (VMEM,) * 4, [], got)


def diagonal(x):
    zero = jnp.zeros((x.shape[0], HD), x.dtype)
    return jnp.concatenate(
        [
            jnp.concatenate([x[:, :HD], zero], axis=1),
            jnp.concatenate([zero, x[:, HD:]], axis=1),
        ],
        axis=0,
    )


def diagonal_turned(one, two):
    zero = jnp.zeros_like(one)
    return jnp.concatenate(
        [jnp.concatenate([one, zero], axis=1), jnp.concatenate([zero, two], axis=1)], axis=0
    )


def in_order(rows, lead):
    one, two = rows[:HD], rows[HD:]
    if isinstance(lead, int):
        return (one, two) if lead == 0 else (two, one)
    return jnp.where(lead == 0, one, two), jnp.where(lead == 0, two, one)


def key_mask(limit_ref, rows, first, count):
    index = lax.broadcasted_iota(jnp.int32, (rows, PAIR), 0)
    return jnp.concatenate(
        [index < limit_ref[i : i + 1, :] for i in range(first, first + count)], axis=0
    )


def softmax(k, qd, open_keys):
    score = jnp.where(open_keys, dot(k, qd, NT) * SCALE, -jnp.inf)
    top = jnp.max(score, axis=0, keepdims=True)
    raised = jnp.exp(score - top)
    total = jnp.sum(raised, axis=0, keepdims=True)
    return raised * (1.0 / total), top, total


def stacked(refs, side, cols):
    return jnp.concatenate([ref[side, :, cols] for ref in refs], axis=0)


def heads_kernel(steps, last, dy_ref, q_ref, limit_ref, *refs):
    core, group = place()
    kv_refs, w_refs = refs[:3], refs[3:-4]
    dq_ref, own_ref, to_core_ref, to_far_ref = refs[-4:]
    tok = q_ref.shape[1]
    open_keys = key_mask(limit_ref, tok, 0, 3)
    todo = steps(core, group)
    for chunk, slot, pieces, lead in todo:
        cols, dest = columns(chunk), columns(slot)
        w = jnp.concatenate([w_refs[i][row : row + rows, :] for i, row, rows in pieces], axis=0)
        d = diagonal_turned(*in_order(dot(w, dy_ref[0], NT).astype(BF16), lead))
        qd = diagonal(q_ref[0, :, cols])
        k, v = stacked(kv_refs, 0, cols), stacked(kv_refs, 1, cols)
        prob, _, _ = softmax(k, qd, open_keys)
        prob_b = prob.astype(BF16)
        d_prob = dot(v, d, NN)
        delta = jnp.sum(prob_b.astype(F32) * d_prob, axis=0, keepdims=True)
        d_score = (prob * (d_prob - delta)).astype(BF16)
        both = dot(d_score, k, TN) * SCALE
        dq_ref[:, dest] = jnp.concatenate([both[:tok, :HD], both[tok:, HD:]], axis=1).astype(BF16)
        for side, grad in enumerate((dot(d_score, qd, NN) * SCALE, dot(prob_b, d, NT))):
            own_ref[side, :, dest] = grad[:tok]
            to_core_ref[side, :tok, dest] = grad[tok : 2 * tok].astype(BF16)
            to_far_ref[side, :tok, dest] = grad[2 * tok :].astype(BF16)
    for ref in (to_core_ref, to_far_ref):
        ref[:, tok:, : len(todo) * PAIR] = jnp.zeros((2, EXTRA, len(todo) * PAIR), BF16)
    if last is not None:
        cols = columns(last(core, group))
        prob, top, total = softmax(stacked(kv_refs, 0, cols), diagonal(q_ref[0, :, cols]), open_keys)
        out = dot(stacked(kv_refs, 1, cols), prob.astype(BF16), TN)
        lse = top + jnp.log(total)
        place_ = slice(len(todo) * PAIR, len(todo) * PAIR + HD)
        for head in range(2):
            span = slice(head * HD, (head + 1) * HD)
            rest = lse[:, span]
            terms = []
            for _ in range(3):
                terms.append(rest.astype(BF16))
                rest = rest - terms[-1].astype(F32)
            terms.append(jnp.zeros((EXTRA - 3, HD), BF16))
            tail = jnp.concatenate(terms, axis=0)
            for ref in (to_core_ref, to_far_ref):
                ref[head, :tok, place_] = out[span, span].astype(BF16)
                ref[head, tok:, place_] = tail


def heads(name, steps, last, weights, d_out, q, limits, blocks):
    tok = q.shape[1]
    width = len(steps(0, 0)) * PAIR
    message = (2, tok + EXTRA, width if last is None else width + HD)
    return call(
        functools.partial(heads_kernel, steps, last),
        name,
        (
            jax.ShapeDtypeStruct((tok, width), BF16),
            jax.ShapeDtypeStruct((2, tok, width), F32),
            jax.ShapeDtypeStruct(message, BF16),
            jax.ShapeDtypeStruct(message, BF16),
        ),
        [VMEM] * (6 + len(weights)),
        (VMEM,) * 4,
        [],
        d_out,
        q,
        limits,
        *blocks,
        *weights,
    )


def last_kernel(last, dy_ref, q_ref, limit_ref, *refs):
    core, group = place()
    kv_refs = refs[:3]
    near_dy, far_dy, near_message, far_message, *w_refs, dq_ref, dk_ref, dv_ref = refs[3:]
    tok, depth = q_ref.shape[1], dy_ref.shape[2]
    cols = columns(last(core, group))
    w = jnp.concatenate([ref[...] for ref in w_refs], axis=0)
    dy = jnp.concatenate([dy_ref[0], near_dy[:, :depth], far_dy[:, :depth]], axis=0)
    turned = in_order(dot(w, dy, NT).astype(BF16), core)

    def of(block):
        span = slice(block * tok, (block + 1) * tok)
        return [half[:, span] for half in turned]

    k, v = stacked(kv_refs, 0, cols), stacked(kv_refs, 1, cols)
    qd = diagonal(q_ref[0, :, cols])
    d = diagonal_turned(*of(0))
    prob, _, _ = softmax(k, qd, key_mask(limit_ref, tok, 0, 3))
    prob_b = prob.astype(BF16)
    d_prob = dot(v, d, NN)
    delta = jnp.sum(prob_b.astype(F32) * d_prob, axis=0, keepdims=True)
    d_score = (prob * (d_prob - delta)).astype(BF16)
    both = dot(d_score, k, TN) * SCALE
    dq_ref[...] = jnp.concatenate([both[:tok, :HD], both[tok:, HD:]], axis=1).astype(BF16)
    scores, probs, queries, cotangents = [d_score[:tok]], [prob_b[:tok]], [qd], [d]
    for block, (dy_far, message) in enumerate(((near_dy, near_message), (far_dy, far_message)), 1):
        qd = diagonal(dy_far[:, depth:])
        one, two = of(block)
        d = diagonal_turned(one, two)
        at = slice(message.shape[2] - HD, message.shape[2])
        lse = jnp.concatenate(
            [
                sum(message[head, tok + term : tok + term + 1, at].astype(F32) for term in range(3))
                for head in range(2)
            ],
            axis=1,
        )
        delta = jnp.concatenate(
            [
                jnp.sum(t.astype(F32) * message[head, :tok, at].astype(F32), axis=0, keepdims=True)
                for head, t in enumerate((one, two))
            ],
            axis=1,
        )
        score = dot(k[:tok], qd, NT) * SCALE
        score = jnp.where(key_mask(limit_ref, tok, 2 + block, 1), score, -jnp.inf)
        prob = jnp.exp(score - lse)
        scores.append((prob * (dot(v[:tok], d, NN) - delta)).astype(BF16))
        probs.append(prob.astype(BF16))
        queries.append(qd)
        cotangents.append(d)
    scores, probs = jnp.concatenate(scores, axis=1), jnp.concatenate(probs, axis=1)
    dk_ref[...] = (dot(scores, jnp.concatenate(queries, axis=0), NN) * SCALE).astype(BF16)
    dv_ref[...] = dot(probs, jnp.concatenate(cotangents, axis=1), NT).astype(BF16)


def last_heads(last, d_out, q, limits, blocks, halo, messages, weights):
    tok = q.shape[1]
    return call(
        functools.partial(last_kernel, last),
        "heads_last",
        (jax.ShapeDtypeStruct((tok, PAIR), BF16),) * 3,
        [VMEM] * (10 + len(weights)),
        (VMEM,) * 3,
        [],
        d_out,
        q,
        limits,
        *blocks,
        *halo,
        *messages,
        *weights,
    )


def finish_kernel(chunks, widths, *refs):
    core, group = place()
    outs, stage, sems = refs[-5:-2], refs[-2], refs[-1]
    tok = stage.shape[1]
    copies = []
    slot = at = 0
    for width, summed in widths:
        part = refs[at : at + (3 if summed else 4)]
        at += len(part)
        for step in range(width // PAIR):
            cols = slice(step * PAIR, (step + 1) * PAIR)
            dest = columns(chunks(core, group)[slot])
            stage[3 * slot] = part[0][:, cols]
            for side in range(2):
                if summed:
                    total = part[1 + side][:, cols]
                else:
                    _, own, near, far = part
                    total = own[side, :, cols] + near[side, :tok, cols].astype(F32)
                    total = (total + far[side, :tok, cols].astype(F32)).astype(BF16)
                stage[3 * slot + 1 + side] = total
            for index in range(3):
                copy = pltpu.make_async_copy(
                    stage.at[3 * slot + index], outs[index].at[0, :, dest], sems.at[3 * slot + index]
                )
                copy.start()
                copies.append(copy)
            slot += 1
    for copy in copies:
        copy.wait()


def finish(chunks, parts, shape):
    count = len(chunks(0, 0))
    ins = [x for part in parts for x in part]
    widths = tuple((part[0].shape[1], len(part) == 3) for part in parts)
    return call(
        functools.partial(finish_kernel, chunks, widths),
        "finish",
        (jax.ShapeDtypeStruct(shape, BF16),) * 3,
        [VMEM] * len(ins),
        (ANY,) * 3,
        [
            pltpu.VMEM((3 * count, shape[1], PAIR), BF16),
            pltpu.SemaphoreType.DMA((3 * count,)),
        ],
        *ins,
    )


def body(queries, keys, values, d_out, w_out, pattern, valid):
    n_seq, n_fsdp = lax.axis_size("seq"), lax.axis_size("fsdp")
    n_chunks = queries.shape[2] // PAIR
    near = functools.partial(lax.ppermute, axis_name="seq", perm=swap(n_seq, 0))
    far = functools.partial(lax.ppermute, axis_name="seq", perm=swap(n_seq, 1))

    def cross(x, bits):
        pairs = [
            (s * n_fsdp + g, s * n_fsdp + (g ^ bits[s % 2]))
            for s in range(n_seq)
            for g in range(n_fsdp)
        ]
        return lax.ppermute(x, ("seq", "fsdp"), pairs)

    def exchange(part):
        dq, own, to_core, to_far = part
        back = far(to_far)
        return dq, own, near(to_core), back

    kv = join(keys, values)
    far_kv, near_kv = far(kv), near(kv)
    if n_fsdp == 4 and n_chunks == 4 and w_out.shape[0] == PAIR:
        last = lambda core, group: group ^ 3
        got = cross(w_out, (1, 2))
        limits, both = pack(last, pattern, valid, d_out, queries)
        far_both, near_both = far(both), near(both)
        ours = d_out, queries, limits, (kv, near_kv, far_kv)
        own = heads(
            "heads_own",
            lambda core, group: [(group, 0, ((0, 0, PAIR),), 0)],
            last,
            [w_out],
            *ours,
        )
        got, dq, near_both = lax.optimization_barrier((got, own[0], near_both))
        own = exchange((dq, *own[1:]))
        *pieces, mine, other = onward(got)
        got_d = [cross(piece, (2, 1)) for piece in pieces]
        far_both, near_got = lax.optimization_barrier((far_both, (near(mine), near(other))))
        side = heads(
            "heads_side",
            lambda core, group: [
                (group ^ (1 + core), core, ((0, 0, HD), (0, HD, HD)), 0),
                (
                    group ^ (2 - core),
                    1 - core,
                    ((1, 0, HD), (2, 0, HD)),
                    1 - core,
                ),
            ],
            None,
            [got, *near_got],
            *ours,
        )
        got_d, dq, messages = lax.optimization_barrier((got_d, side[0], own[2:]))
        own = (*own[:2], *messages)
        side = exchange((dq, *side[1:]))
        third = last_heads(last, *ours, (near_both, far_both), messages, (*got_d, *[near(x) for x in got_d]))
        order = lambda core, group: [group, group ^ 1, group ^ 2, group ^ 3]
        return finish(order, [own, side, third], queries.shape)
    full = lax.all_gather(w_out, "fsdp", axis=0, tiled=True)
    limits, _ = pack(lambda core, group: 0, pattern, valid, d_out, queries)
    steps = lambda core, group: [
        (i, i, ((0, i * PAIR, PAIR),), 0) for i in range(n_chunks)
    ]
    ours = d_out, queries, limits, (kv, near_kv, far_kv)
    part = exchange(heads("heads_all", steps, None, [full], *ours))
    return finish(lambda core, group: list(range(n_chunks)), [part], queries.shape)


def solution(mesh):
    rows = P("fsdp", "seq", None)
    in_specs = (rows, rows, rows, rows, P("fsdp", None), P(), P("fsdp", None))
    return jax.shard_map(
        body, mesh=mesh, in_specs=in_specs, out_specs=(rows,) * 3, check_vma=False
    )
```

time: 42.7 us -> 41.4 us (0.970)
  starting transfers between devices: 16 us -> 19.8 us
  waiting for transfers between devices: 10.7 us -> 7.68 us
  local copies, waits for them, and re-layouts: 4.95 us -> 3.81 us
  Pallas kernels: 9.87 us -> 8.94 us
    ppermute x4 -> x8, starting transfers between devices: 5.63 us -> 8.94 us  [the longest x2 4.57 us: body(): far_both, near_both = (far(both), near(both))]
    ppermute x2 -> x3, waiting for transfers between devices: 3.11 us -> 0.01 us  [cross(): return lax.ppermute(x, ('seq', 'fsdp'), pairs)]
    unnamed x17, local copies, waits for them, and re-layouts: 4.95 us -> 3.81 us
    pallas_call x7 -> x6, Pallas kernels: 8.1 us -> 7.14 us  [call(): pl.pallas_call(kernel, out_shape=out_shape, in_specs=in_specs, out_specs=...]
    ppermute x4 -> x8, waiting for transfers between devices: 5.87 us -> 6.74 us  [the longest x2 3.88 us: body(): far_kv, near_kv = (far(kv), near(kv))]
    ppermute x2, waiting for transfers between devices: 1.76 us -> 0.93 us  [exchange(): back = far(to_far)]
    ppermute x2 -> x3, starting transfers between devices: 2.9 us -> 3.6 us  [cross(): return lax.ppermute(x, ('seq', 'fsdp'), pairs)]
  transfers between devices with their start and end apart: 10 -> 15, of which waited for: 5 -> 5; matrix products, arithmetic and copies ran while one was open for 0% -> 2% of each run, Pallas kernels for 22% -> 19%
where the time goes in v7:
time: 41.4 us; the launch traced here: 41.1 us
  starting transfers between devices  19.8 us (48%)
  Pallas kernels  8.94 us (22%)
  waiting for transfers between devices  7.68 us (19%)
  local copies, waits for them, and re-layouts  3.81 us (9%)
  between operations  0.87 us (2%)
    ppermute x2, starting transfers between devices, exchange(): back = far(to_far)  7.15 us
    pallas_call x6, Pallas kernels, call(): pl.pallas_call(kernel, out_shape=out_shape, in_specs=in_specs, out_specs=...  7.14 us
    ppermute x2, starting transfers between devices, body(): far_both, near_both = (far(both), near(both))  4.57 us
    ppermute x2, waiting for transfers between devices, body(): far_kv, near_kv = (far(kv), near(kv))  3.88 us
    unnamed x17, local copies, waits for them, and re-layouts  3.81 us
    ppermute x3, starting transfers between devices, cross(): return lax.ppermute(x, ('seq', 'fsdp'), pairs)  3.6 us
    ppermute x2, starting transfers between devices, body(): far_kv, near_kv = (far(kv), near(kv))  3.23 us
    pallas_call x1, Pallas kernels, join(): pl.pallas_call(join_kernel, out_shape=jax.ShapeDtypeStruct(shape, BF16),...  1.8 us
  transfers between devices with their start and end apart: 15, of which 5 were waited for; matrix products, arithmetic and copies ran while one was open for 2% of the time, Pallas kernels for 19%

profile of v7, /device:TPU:1, one launch (start us, length us, event | category | flops | bytes accessed | tf_op | source)
XLA Modules:
  0.0 41.1 jit_solution(7297701792980709140)
XLA Ops:
  0.6 2.1 %collective-permute-start = (bf16[256,2048]{1,0:T(8,128)(2,1)}, bf16[256,2048]{1,0:T(8,128)(2,1)S(1)}, u32[]{:S(2)}, u32[]{:S(2)}) collective-permute-start(bf16[256,2048]{1,0:T(8,128)(2,1)} %refs_3_.1), channel_id=1, source_target_pairs={{0,1},{1,0},{2,3},{3,2},{4,6},{5,7},{6,4},{7,5},{8,9},{9,8},{10,11... | collective-permute-start | bytes 3145736 | tf_op jit(solution)/shard_map/ppermute | solution.py:407
  2.8 0.8 %copy.10.pat_ref = s32[8,4]{1,0:T(8,128)S(1)} copy(s32[8,4]{0,1:T(4,128)} %param.12) | data formatting | bytes 256 | tf_op args[5]
  3.5 1.0 %copy-done = bf16[1,128,2048]{2,1,0:T(8,128)(2,1)S(1)} copy-done((bf16[1,128,2048]{2,1,0:T(8,128)(2,1)S(1)}, bf16[1,128,2048]{2,1,0:T(8,128)(2,1)}, u32[]{:S(2)}) %copy-start) | copy-done | bytes 524312
  4.6 0.9 %copy-done.4 = bf16[1,128,1024]{2,1,0:T(8,128)(2,1)S(1)} copy-done((bf16[1,128,1024]{2,1,0:T(8,128)(2,1)S(1)}, bf16[1,128,1024]{2,1,0:T(8,128)(2,1)}, u32[]{:S(2)}) %copy-start.4) | copy-done | bytes 262168
  5.5 0.7 %pack.1 = (s32[8,256]{1,0:T(8,128)S(1)}, bf16[128,2304]{1,0:T(8,128)(2,1)S(1)}) custom-call(s32[8,4]{1,0:T(8,128)S(1)} %copy.10.pat_ref, s32[1,8]{1,0:T(1,128)S(1)} %copy-done.7, bf16[1,128,2048]{2,1,0:T(8,128)(2,1)S(1)} %copy-done, bf16[1,128,1024]{2,1,0:T(8,128)(2,1)S(1)} %copy-done.4), custom_call_target="tpu_custom_call" | custom-call | flops 1 | bytes 1 | tf_op jit(solution)/shard_map/pack/pallas_call | solution.py:49
  6.2 1.0 %collective-permute-start.3 = (bf16[128,2304]{1,0:T(8,128)(2,1)S(1)}, bf16[128,2304]{1,0:T(8,128)(2,1)S(1)}, u32[]{:S(2)}, u32[]{:S(2)}) collective-permute-start(bf16[128,2304]{1,0:T(8,128)(2,1)S(1)} %get-tuple-element.33), channel_id=1, source_target_pairs={{0,4},{4,0},{8,12},{12,8},{16,20},{20,16},{24,28},{28,24},{1,5},{5... | collective-permute-start | bytes 1769480 | tf_op jit(solution)/shard_map/ppermute | solution.py:420
  7.2 1.8 %join.1.refs_0_ = bf16[2,128,1024]{2,1,0:T(8,128)(2,1)} custom-call(bf16[1,128,1024]{2,1,0:T(8,128)(2,1)} %k_ref.1, bf16[1,128,1024]{2,1,0:T(8,128)(2,1)} %v_ref.1), custom_call_target="tpu_custom_call" | custom-call | flops 1 | bytes 1 | tf_op jit(solution)/shard_map/join/pallas_call | solution.py:127
  9.0 3.2 %collective-permute-start.2 = (bf16[2,128,1024]{2,1,0:T(8,128)(2,1)}, bf16[2,128,1024]{2,1,0:T(8,128)(2,1)S(1)}, u32[]{:S(2)}, u32[]{:S(2)}) collective-permute-start(bf16[2,128,1024]{2,1,0:T(8,128)(2,1)} %join.1.refs_0_), channel_id=1, source_target_pairs={{4,8},{8,4},{12,16},{16,12},{20,24},{24,20},{5,9},{9,5},{13,17},{1... | collective-permute-start | bytes 1572872 | tf_op jit(solution)/shard_map/ppermute | solution.py:415
  12.3 3.6 %collective-permute-start.6 = (bf16[128,2304]{1,0:T(8,128)(2,1)S(1)}, bf16[128,2304]{1,0:T(8,128)(2,1)S(1)}, u32[]{:S(2)}, u32[]{:S(2)}) collective-permute-start(bf16[128,2304]{1,0:T(8,128)(2,1)S(1)} %get-tuple-element.33), channel_id=1, source_target_pairs={{4,8},{8,4},{12,16},{16,12},{20,24},{24,20},{5,9},{9,5},{13,17},{1... | collective-permute-start | bytes 1769480 | tf_op jit(solution)/shard_map/ppermute | solution.py:420
  15.8 3.9 %collective-permute-done.2.refs_2_ = bf16[2,128,1024]{2,1,0:T(8,128)(2,1)S(1)} collective-permute-done((bf16[2,128,1024]{2,1,0:T(8,128)(2,1)}, bf16[2,128,1024]{2,1,0:T(8,128)(2,1)S(1)}, u32[]{:S(2)}, u32[]{:S(2)}) %collective-permute-start.2) | collective-permute-done | bytes 524320 | tf_op jit(solution)/shard_map/ppermute | solution.py:415
  19.8 1.0 %copy-done.2 = bf16[2,128,1024]{2,1,0:T(8,128)(2,1)S(1)} copy-done((bf16[2,128,1024]{2,1,0:T(8,128)(2,1)S(1)}, bf16[2,128,1024]{2,1,0:T(8,128)(2,1)}, u32[]{:S(2)}) %copy-start.2) | copy-done | bytes 524312
  20.8 1.6 %heads_own.1 = (bf16[128,256]{1,0:T(8,128)(2,1)S(1)}, f32[2,128,256]{2,1,0:T(8,128)S(1)}, bf16[2,144,384]{2,1,0:T(8,128)(2,1)S(1)}, bf16[2,144,384]{2,1,0:T(8,128)(2,1)S(1)}) custom-call(bf16[1,128,2048]{2,1,0:T(8,128)(2,1)S(1)} %copy-done.1, bf16[1,128,1024]{2,1,0:T(8,128)(2,1)S(1)} %copy-done.5, s32[8,256]{1,0:T(8,128)S(1)} %get-tuple-element.31.limit_ref, ...), custom_call_target="tpu_custom_call" | custom-call | flops 1 | bytes 1 | tf_op jit(solution)/shard_map/heads_own/pallas_call | solution.py:49
  22.6 0.5 %collective-permute-start.8 = (bf16[128,2048]{1,0:T(8,128)(2,1)S(1)}, bf16[128,2048]{1,0:T(8,128)(2,1)S(1)}, u32[]{:S(2)}, u32[]{:S(2)}) collective-permute-start(bf16[128,2048]{1,0:T(8,128)(2,1)S(1)} %get-tuple-element.40), channel_id=1, source_target_pairs={{0,4},{4,0},{8,12},{12,8},{16,20},{20,16},{24,28},{28,24},{1,5},{5... | collective-permute-start | bytes 1572872 | tf_op jit(solution)/shard_map/ppermute | solution.py:433
  23.5 1.1 %collective-permute-start.5 = (bf16[64,2048]{1,0:T(8,128)(2,1)S(1)}, bf16[64,2048]{1,0:T(8,128)(2,1)S(1)}, u32[]{:S(2)}, u32[]{:S(2)}) collective-permute-start(bf16[64,2048]{1,0:T(8,128)(2,1)S(1)} %get-tuple-element.38), channel_id=1, source_target_pairs={{0,2},{1,3},{2,0},{3,1},{4,5},{5,4},{6,7},{7,6},{8,10},{9,11},{10,... | collective-permute-start | bytes 786440 | tf_op jit(solution)/shard_map/ppermute | solution.py:407
  24.6 1.5 %collective-permute-done.6.refs_4_ = bf16[128,2304]{1,0:T(8,128)(2,1)S(1)} collective-permute-done((bf16[128,2304]{1,0:T(8,128)(2,1)S(1)}, bf16[128,2304]{1,0:T(8,128)(2,1)S(1)}, u32[]{:S(2)}, u32[]{:S(2)}) %collective-permute-start.6) | collective-permute-done | bytes 589856 | tf_op jit(solution)/shard_map/ppermute | solution.py:420
  26.1 3.6 %collective-permute-start.10 = (bf16[2,144,384]{2,1,0:T(8,128)(2,1)S(1)}, bf16[2,144,384]{2,1,0:T(8,128)(2,1)S(1)}, u32[]{:S(2)}, u32[]{:S(2)}) collective-permute-start(bf16[2,144,384]{2,1,0:T(8,128)(2,1)S(1)} %get-tuple-element.45), channel_id=1, source_target_pairs={{4,8},{8,4},{12,16},{16,12},{20,24},{24,20},{5,9},{9,5},{13,17},{1... | collective-permute-start | bytes 663560 | tf_op jit(solution)/shard_map/ppermute | solution.py:411
  29.7 2.2 %heads_side.1 = (bf16[128,512]{1,0:T(8,128)(2,1)S(1)}, f32[2,128,512]{2,1,0:T(8,128)S(1)}, bf16[2,144,512]{2,1,0:T(8,128)(2,1)S(1)}, bf16[2,144,512]{2,1,0:T(8,128)(2,1)S(1)}) custom-call(bf16[1,128,2048]{2,1,0:T(8,128)(2,1)S(1)} %copy-done.1, bf16[1,128,1024]{2,1,0:T(8,128)(2,1)S(1)} %copy-done.5, s32[8,256]{1,0:T(8,128)S(1)} %get-tuple-element.31.limit_ref, ...), custom_call_target="tpu_custom_call" | custom-call | flops 1 | bytes 1 | tf_op jit(solution)/shard_map/heads_side/pallas_call | solution.py:49
  32.0 3.6 %collective-permute-start.12 = (bf16[2,144,512]{2,1,0:T(8,128)(2,1)S(1)}, bf16[2,144,512]{2,1,0:T(8,128)(2,1)S(1)}, u32[]{:S(2)}, u32[]{:S(2)}) collective-permute-start(bf16[2,144,512]{2,1,0:T(8,128)(2,1)S(1)} %get-tuple-element.51), channel_id=1, source_target_pairs={{4,8},{8,4},{12,16},{16,12},{20,24},{24,20},{5,9},{9,5},{13,17},{1... | collective-permute-start | bytes 884744 | tf_op jit(solution)/shard_map/ppermute | solution.py:411
  35.7 0.5 %collective-permute-start.14 = (bf16[64,2048]{1,0:T(8,128)(2,1)S(1)}, bf16[64,2048]{1,0:T(8,128)(2,1)S(1)}, u32[]{:S(2)}, u32[]{:S(2)}) collective-permute-start(bf16[64,2048]{1,0:T(8,128)(2,1)S(1)} %collective-permute-done.5.refs_8_), channel_id=1, source_target_pairs={{0,4},{4,0},{8,12},{12,8},{16,20},{20,16},{24,28},{28,24},{1,5},{5... | collective-permute-start | bytes 786440 | tf_op jit(solution)/shard_map/ppermute | solution.py:452
  36.2 1.0 %collective-permute-done.13.refs_9_ = bf16[64,2048]{1,0:T(8,128)(2,1)S(1)} collective-permute-done((bf16[64,2048]{1,0:T(8,128)(2,1)S(1)}, bf16[64,2048]{1,0:T(8,128)(2,1)S(1)}, u32[]{:S(2)}, u32[]{:S(2)}) %collective-permute-start.13) | collective-permute-done | bytes 262176 | tf_op jit(solution)/shard_map/ppermute | solution.py:452
  37.2 0.4 collective-permute-done.14.refs_10_
  37.6 1.5 %heads_last.1 = (bf16[128,256]{1,0:T(8,128)(2,1)S(1)}, bf16[128,256]{1,0:T(8,128)(2,1)S(1)}, bf16[128,256]{1,0:T(8,128)(2,1)S(1)}) custom-call(bf16[1,128,2048]{2,1,0:T(8,128)(2,1)S(1)} %copy-done.1, bf16[1,128,1024]{2,1,0:T(8,128)(2,1)S(1)} %copy-done.5, s32[8,256]{1,0:T(8,128)S(1)} %get-tuple-element.31.limit_ref, bf16[2,128,1024]{2,1,0:T(8,128)(2,1)S(1)} %copy-done.3, ...), custom_call_target="tpu_custom_call" | custom-call | flops 1 | bytes 1 | tf_op jit(solution)/shard_map/heads_last/pallas_call | solution.py:49
  39.1 0.9 %collective-permute-done.12.refs_7_ = bf16[2,144,512]{2,1,0:T(8,128)(2,1)S(1)} collective-permute-done((bf16[2,144,512]{2,1,0:T(8,128)(2,1)S(1)}, bf16[2,144,512]{2,1,0:T(8,128)(2,1)S(1)}, u32[]{:S(2)}, u32[]{:S(2)}) %collective-permute-start.12) | collective-permute-done | bytes 294944 | tf_op jit(solution)/shard_map/ppermute | solution.py:411
  40.0 1.0 %finish.1 = (bf16[1,128,1024]{2,1,0:T(8,128)(2,1)}, bf16[1,128,1024]{2,1,0:T(8,128)(2,1)}, bf16[1,128,1024]{2,1,0:T(8,128)(2,1)}) custom-call(bf16[128,256]{1,0:T(8,128)(2,1)S(1)} %get-tuple-element.34.refs_0_, f32[2,128,256]{2,1,0:T(8,128)S(1)} %get-tuple-element.35.refs_1_, bf16[2,144,384]{2,1,0:T(8,128)(2,1)S(1)} %collective-permute-done.9.refs_5_.refs_2_, ...), custom_call_target="tpu_custom_call" | custom-call | flops 1 | bytes 1 | tf_op jit(solution)/shard_map/finish/pallas_call | solution.py:49
  (30 shorter events, 0.8 us)
Async XLA Ops:
  0.6 2.9 %copy-start.7 = (s32[1,8]{1,0:T(1,128)S(1)}, s32[1,8]{1,0:T(1,128)}, u32[]{:S(2)}) copy-start(s32[1,8]{1,0:T(1,128)} %val_ref.1) | copy-start | bytes 100
  0.6 21.8 %collective-permute-start = (bf16[256,2048]{1,0:T(8,128)(2,1)}, bf16[256,2048]{1,0:T(8,128)(2,1)S(1)}, u32[]{:S(2)}, u32[]{:S(2)}) collective-permute-start(bf16[256,2048]{1,0:T(8,128)(2,1)} %refs_3_.1), channel_id=1, source_target_pairs={{0,1},{1,0},{2,3},{3,2},{4,6},{5,7},{6,4},{7,5},{8,9},{9,8},{10,11... | collective-permute-start | bytes 3145736 | tf_op jit(solution)/shard_map/ppermute | solution.py:407
  3.5 1.0 %copy-start = (bf16[1,128,2048]{2,1,0:T(8,128)(2,1)S(1)}, bf16[1,128,2048]{2,1,0:T(8,128)(2,1)}, u32[]{:S(2)}) copy-start(bf16[1,128,2048]{2,1,0:T(8,128)(2,1)} %dy_ref.7) | copy-start | bytes 1572868
  4.6 0.9 %copy-start.4 = (bf16[1,128,1024]{2,1,0:T(8,128)(2,1)S(1)}, bf16[1,128,1024]{2,1,0:T(8,128)(2,1)}, u32[]{:S(2)}) copy-start(bf16[1,128,1024]{2,1,0:T(8,128)(2,1)} %q_ref.7) | copy-start | bytes 786436
  5.5 14.2 %copy-start.6 = (bf16[256,2048]{1,0:T(8,128)(2,1)S(1)}, bf16[256,2048]{1,0:T(8,128)(2,1)}, u32[]{:S(2)}) copy-start(bf16[256,2048]{1,0:T(8,128)(2,1)} %refs_3_.1) | copy-start | bytes 3145732
  6.2 13.5 %copy-start.1 = (bf16[1,128,2048]{2,1,0:T(8,128)(2,1)S(1)}, bf16[1,128,2048]{2,1,0:T(8,128)(2,1)}, u32[]{:S(2)}) copy-start(bf16[1,128,2048]{2,1,0:T(8,128)(2,1)} %dy_ref.7) | copy-start | bytes 1572868
  6.2 13.5 %copy-start.5 = (bf16[1,128,1024]{2,1,0:T(8,128)(2,1)S(1)}, bf16[1,128,1024]{2,1,0:T(8,128)(2,1)}, u32[]{:S(2)}) copy-start(bf16[1,128,1024]{2,1,0:T(8,128)(2,1)} %q_ref.7) | copy-start | bytes 786436
  6.2 16.2 %collective-permute-start.3 = (bf16[128,2304]{1,0:T(8,128)(2,1)S(1)}, bf16[128,2304]{1,0:T(8,128)(2,1)S(1)}, u32[]{:S(2)}, u32[]{:S(2)}) collective-permute-start(bf16[128,2304]{1,0:T(8,128)(2,1)S(1)} %get-tuple-element.33), channel_id=1, source_target_pairs={{0,4},{4,0},{8,12},{12,8},{16,20},{20,16},{24,28},{28,24},{1,5},{5... | collective-permute-start | bytes 1769480 | tf_op jit(solution)/shard_map/ppermute | solution.py:420
  9.0 10.7 %collective-permute-start.2 = (bf16[2,128,1024]{2,1,0:T(8,128)(2,1)}, bf16[2,128,1024]{2,1,0:T(8,128)(2,1)S(1)}, u32[]{:S(2)}, u32[]{:S(2)}) collective-permute-start(bf16[2,128,1024]{2,1,0:T(8,128)(2,1)} %join.1.refs_0_), channel_id=1, source_target_pairs={{4,8},{8,4},{12,16},{16,12},{20,24},{24,20},{5,9},{9,5},{13,17},{1... | collective-permute-start | bytes 1572872 | tf_op jit(solution)/shard_map/ppermute | solution.py:415
  12.2 7.5 %collective-permute-start.1 = (bf16[2,128,1024]{2,1,0:T(8,128)(2,1)}, bf16[2,128,1024]{2,1,0:T(8,128)(2,1)S(1)}, u32[]{:S(2)}, u32[]{:S(2)}) collective-permute-start(bf16[2,128,1024]{2,1,0:T(8,128)(2,1)} %join.1.refs_0_), channel_id=1, source_target_pairs={{0,4},{4,0},{8,12},{12,8},{16,20},{20,16},{24,28},{28,24},{1,5},{5... | collective-permute-start | bytes 1572872 | tf_op jit(solution)/shard_map/ppermute | solution.py:415
  12.3 13.8 %collective-permute-start.6 = (bf16[128,2304]{1,0:T(8,128)(2,1)S(1)}, bf16[128,2304]{1,0:T(8,128)(2,1)S(1)}, u32[]{:S(2)}, u32[]{:S(2)}) collective-permute-start(bf16[128,2304]{1,0:T(8,128)(2,1)S(1)} %get-tuple-element.33), channel_id=1, source_target_pairs={{4,8},{8,4},{12,16},{16,12},{20,24},{24,20},{5,9},{9,5},{13,17},{1... | collective-permute-start | bytes 1769480 | tf_op jit(solution)/shard_map/ppermute | solution.py:420
  19.7 1.0 %copy-start.2 = (bf16[2,128,1024]{2,1,0:T(8,128)(2,1)S(1)}, bf16[2,128,1024]{2,1,0:T(8,128)(2,1)}, u32[]{:S(2)}) copy-start(bf16[2,128,1024]{2,1,0:T(8,128)(2,1)} %join.1.refs_0_) | copy-start | bytes 1572868
  22.4 7.2 %copy-start.3 = (bf16[2,128,1024]{2,1,0:T(8,128)(2,1)S(1)}, bf16[2,128,1024]{2,1,0:T(8,128)(2,1)}, u32[]{:S(2)}) copy-start(bf16[2,128,1024]{2,1,0:T(8,128)(2,1)} %join.1.refs_0_) | copy-start | bytes 1572868
  22.6 3.5 %collective-permute-start.7 = (bf16[128,2048]{1,0:T(8,128)(2,1)S(1)}, bf16[128,2048]{1,0:T(8,128)(2,1)S(1)}, u32[]{:S(2)}, u32[]{:S(2)}) collective-permute-start(bf16[128,2048]{1,0:T(8,128)(2,1)S(1)} %get-tuple-element.39), channel_id=1, source_target_pairs={{0,4},{4,0},{8,12},{12,8},{16,20},{20,16},{24,28},{28,24},{1,5},{5... | collective-permute-start | bytes 1572872 | tf_op jit(solution)/shard_map/ppermute | solution.py:433
  22.6 7.0 %collective-permute-start.8 = (bf16[128,2048]{1,0:T(8,128)(2,1)S(1)}, bf16[128,2048]{1,0:T(8,128)(2,1)S(1)}, u32[]{:S(2)}, u32[]{:S(2)}) collective-permute-start(bf16[128,2048]{1,0:T(8,128)(2,1)S(1)} %get-tuple-element.40), channel_id=1, source_target_pairs={{0,4},{4,0},{8,12},{12,8},{16,20},{20,16},{24,28},{28,24},{1,5},{5... | collective-permute-start | bytes 1572872 | tf_op jit(solution)/shard_map/ppermute | solution.py:433
  23.1 12.5 %collective-permute-start.4 = (bf16[64,2048]{1,0:T(8,128)(2,1)S(1)}, bf16[64,2048]{1,0:T(8,128)(2,1)S(1)}, u32[]{:S(2)}, u32[]{:S(2)}) collective-permute-start(bf16[64,2048]{1,0:T(8,128)(2,1)S(1)} %get-tuple-element.37), channel_id=1, source_target_pairs={{0,2},{1,3},{2,0},{3,1},{4,5},{5,4},{6,7},{7,6},{8,10},{9,11},{10,... | collective-permute-start | bytes 786440 | tf_op jit(solution)/shard_map/ppermute | solution.py:407
  23.5 12.1 %collective-permute-start.5 = (bf16[64,2048]{1,0:T(8,128)(2,1)S(1)}, bf16[64,2048]{1,0:T(8,128)(2,1)S(1)}, u32[]{:S(2)}, u32[]{:S(2)}) collective-permute-start(bf16[64,2048]{1,0:T(8,128)(2,1)S(1)} %get-tuple-element.38), channel_id=1, source_target_pairs={{0,2},{1,3},{2,0},{3,1},{4,5},{5,4},{6,7},{7,6},{8,10},{9,11},{10,... | collective-permute-start | bytes 786440 | tf_op jit(solution)/shard_map/ppermute | solution.py:407
  26.0 6.0 %collective-permute-start.9 = (bf16[2,144,384]{2,1,0:T(8,128)(2,1)S(1)}, bf16[2,144,384]{2,1,0:T(8,128)(2,1)S(1)}, u32[]{:S(2)}, u32[]{:S(2)}) collective-permute-start(bf16[2,144,384]{2,1,0:T(8,128)(2,1)S(1)} %get-tuple-element.44), channel_id=1, source_target_pairs={{0,4},{4,0},{8,12},{12,8},{16,20},{20,16},{24,28},{28,24},{1,5},{5... | collective-permute-start | bytes 663560 | tf_op jit(solution)/shard_map/ppermute | solution.py:412
  26.1 9.5 %collective-permute-start.10 = (bf16[2,144,384]{2,1,0:T(8,128)(2,1)S(1)}, bf16[2,144,384]{2,1,0:T(8,128)(2,1)S(1)}, u32[]{:S(2)}, u32[]{:S(2)}) collective-permute-start(bf16[2,144,384]{2,1,0:T(8,128)(2,1)S(1)} %get-tuple-element.45), channel_id=1, source_target_pairs={{4,8},{8,4},{12,16},{16,12},{20,24},{24,20},{5,9},{9,5},{13,17},{1... | collective-permute-start | bytes 663560 | tf_op jit(solution)/shard_map/ppermute | solution.py:411
  31.9 7.2 %collective-permute-start.11 = (bf16[2,144,512]{2,1,0:T(8,128)(2,1)S(1)}, bf16[2,144,512]{2,1,0:T(8,128)(2,1)S(1)}, u32[]{:S(2)}, u32[]{:S(2)}) collective-permute-start(bf16[2,144,512]{2,1,0:T(8,128)(2,1)S(1)} %get-tuple-element.50), channel_id=1, source_target_pairs={{0,4},{4,0},{8,12},{12,8},{16,20},{20,16},{24,28},{28,24},{1,5},{5... | collective-permute-start | bytes 884744 | tf_op jit(solution)/shard_map/ppermute | solution.py:412
  32.0 8.0 %collective-permute-start.12 = (bf16[2,144,512]{2,1,0:T(8,128)(2,1)S(1)}, bf16[2,144,512]{2,1,0:T(8,128)(2,1)S(1)}, u32[]{:S(2)}, u32[]{:S(2)}) collective-permute-start(bf16[2,144,512]{2,1,0:T(8,128)(2,1)S(1)} %get-tuple-element.51), channel_id=1, source_target_pairs={{4,8},{8,4},{12,16},{16,12},{20,24},{24,20},{5,9},{9,5},{13,17},{1... | collective-permute-start | bytes 884744 | tf_op jit(solution)/shard_map/ppermute | solution.py:411
  35.6 1.6 %collective-permute-start.13 = (bf16[64,2048]{1,0:T(8,128)(2,1)S(1)}, bf16[64,2048]{1,0:T(8,128)(2,1)S(1)}, u32[]{:S(2)}, u32[]{:S(2)}) collective-permute-start(bf16[64,2048]{1,0:T(8,128)(2,1)S(1)} %collective-permute-done.4.refs_7_), channel_id=1, source_target_pairs={{0,4},{4,0},{8,12},{12,8},{16,20},{20,16},{24,28},{28,24},{1,5},{5... | collective-permute-start | bytes 786440 | tf_op jit(solution)/shard_map/ppermute | solution.py:452
  35.7 1.9 %collective-permute-start.14 = (bf16[64,2048]{1,0:T(8,128)(2,1)S(1)}, bf16[64,2048]{1,0:T(8,128)(2,1)S(1)}, u32[]{:S(2)}, u32[]{:S(2)}) collective-permute-start(bf16[64,2048]{1,0:T(8,128)(2,1)S(1)} %collective-permute-done.5.refs_8_), channel_id=1, source_target_pairs={{0,4},{4,0},{8,12},{12,8},{16,20},{20,16},{24,28},{28,24},{1,5},{5... | collective-permute-start | bytes 786440 | tf_op jit(solution)/shard_map/ppermute | solution.py:452

commit v8 on v7

v8 whole, which is shorter than its diff:
```python
import functools

import jax
import jax.numpy as jnp
from jax import lax
from jax.experimental import pallas as pl
from jax.experimental.pallas import tpu as pltpu
from jax.sharding import PartitionSpec as P

HD = 128
PAIR = 2 * HD
PIECE = 64
BRIEF = pl.CostEstimate(flops=1, bytes_accessed=1, transcendentals=0)
F32 = jnp.float32
BF16 = jnp.bfloat16
NT = (((1,), (1,)), ((), ()))
NN = (((1,), (0,)), ((), ()))
TN = (((0,), (0,)), ((), ()))
HBM = pl.BlockSpec(memory_space=pltpu.HBM)
ANY = pl.BlockSpec(memory_space=pl.ANY)
VMEM = pl.BlockSpec(memory_space=pltpu.VMEM)
SMEM = pl.BlockSpec(memory_space=pltpu.SMEM)
PARAMS = pltpu.CompilerParams(vmem_limit_bytes=40 * 2**20)
WIDE = pltpu.CompilerParams(vmem_limit_bytes=58 * 2**20)
SCALE = HD ** (-0.5)


def dot(a, b, dims):
    return lax.dot_general(a, b, dims, preferred_element_type=F32)


def swap(n, offset):
    pairs = []
    for i in range(offset, n - 1, 2):
        pairs += [(i, i + 1), (i + 1, i)]
    return pairs


def place():
    return lax.rem(lax.axis_index("seq"), 2), lax.axis_index("fsdp")


def columns(chunk):
    return pl.ds(pl.multiple_of(chunk * PAIR, PAIR), PAIR)


def call(kernel, name, out_shape, in_specs, out_specs, scratch, *args):
    return pl.pallas_call(
        kernel,
        out_shape=out_shape,
        in_specs=in_specs,
        out_specs=out_specs,
        scratch_shapes=scratch,
        cost_estimate=BRIEF,
        compiler_params=PARAMS,
        name=name,
    )(*args)


def key_limits(pat_ref, val_ref):
    shard = lax.axis_index("seq")
    count = val_ref.shape[1]

    def pair(block):
        return block + 1 - 2 * lax.rem(block + 2, 2)

    def far(block):
        return block - 1 + 2 * lax.rem(block + 2, 2)

    wanted = [(shard, block) for block in (shard, pair(shard), far(shard))]
    for row, other in ((pair(shard), far(pair(shard))), (far(shard), pair(far(shard)))):
        wanted += [(row, block) for block in (row, shard, other)]
    limits = []
    for row, block in wanted:
        held = jnp.clip(row, 0, count - 1)
        listed = pat_ref[held, 0] == block
        for entry in range(1, pat_ref.shape[1]):
            listed = jnp.logical_or(listed, pat_ref[held, entry] == block)
        inside = jnp.logical_and(row == held, jnp.logical_and(block >= 0, block < count))
        keys = val_ref[0, jnp.clip(block, 0, count - 1)]
        limits.append(jnp.where(jnp.logical_and(listed, inside), keys, 0))
    return limits


def limits_kernel(pat_ref, val_ref, limit_ref):
    limit_ref[...] = jnp.zeros_like(limit_ref)
    for row, limit in enumerate(key_limits(pat_ref, val_ref)):
        limit_ref[row : row + 1, :] = jnp.full((1, PAIR), limit, jnp.int32)


def limits_of(pattern, valid):
    shape = jax.ShapeDtypeStruct((16, PAIR), jnp.int32)
    return call(limits_kernel, "limits", shape, [SMEM] * 2, VMEM, [], pattern, valid)


def join_kernel(last, k_ref, v_ref, dy_ref, q_ref, kv_ref, both_ref, kv, both, sems):
    core, group = place()
    tok, depth = dy_ref.shape[1:]
    width = k_ref.shape[2]
    steps = []
    for sources, held, target in (
        (((k_ref, slice(None), width), (v_ref, slice(None), width)), kv, kv_ref),
        (
            ((dy_ref, slice(None), depth), (q_ref, columns(last(core, group)), PAIR)),
            both,
            both_ref,
        ),
    ):
        for row in range(0, tok, PIECE):
            rows = pl.ds(row, PIECE)
            to = 0
            for source, cols, size in sources:
                at = (rows, pl.ds(to, size))
                steps.append((source.at[0, rows, cols], held.at[at], target.at[at]))
                to += size
    arrivals, moves = [], []
    for i, (source, held, target) in enumerate(steps):
        arrivals.append(pltpu.make_async_copy(source, held, sems.at[0, i]))
        moves.append(pltpu.make_async_copy(held, target, sems.at[1, i]))
    for copy in arrivals:
        copy.start()
    for arrival, move in zip(arrivals, moves):
        arrival.wait()
        move.start()
    for move in moves:
        move.wait()


def join(last, keys, values, d_out, queries):
    tok, depth = d_out.shape[1:]
    kv, both = (tok, 2 * keys.shape[2]), (tok, depth + PAIR)
    return pl.pallas_call(
        functools.partial(join_kernel, last),
        out_shape=(jax.ShapeDtypeStruct(kv, BF16), jax.ShapeDtypeStruct(both, BF16)),
        in_specs=[HBM] * 4,
        out_specs=(ANY,) * 2,
        scratch_shapes=[
            pltpu.VMEM(kv, BF16),
            pltpu.VMEM(both, BF16),
            pltpu.SemaphoreType.DMA((2, 4 * (tok // PIECE))),
        ],
        cost_estimate=BRIEF,
        compiler_params=WIDE,
        name="join",
    )(keys, values, d_out, queries)


def hand_on_kernel(last, *refs):
    core, group = place()
    *before, kv_ref, out_ref = refs
    chunk = last(core, group)
    cols = [columns(chunk), columns(chunk + kv_ref.shape[1] // (2 * PAIR))]
    to = 0
    for piece in [ref[...] for ref in before] + [kv_ref[:, at] for at in cols]:
        out_ref[:, to : to + piece.shape[1]] = piece
        to += piece.shape[1]


def hand_on(name, last, kv, *before):
    width = sum(x.shape[1] for x in before) + 2 * PAIR
    shape = jax.ShapeDtypeStruct((kv.shape[0], width), BF16)
    kernel = functools.partial(hand_on_kernel, last)
    return call(kernel, name, shape, [VMEM] * (len(before) + 1), VMEM, [], *before, kv)


def onward_kernel(w_ref, *out_refs):
    core, _ = place()
    half = w_ref.shape[0] // 2
    start = pl.multiple_of(core * half, half)
    for i, ref in enumerate(out_refs[:2]):
        rows = ref.shape[0]
        ref[...] = w_ref[pl.ds(start + i * rows, rows), :]
    for ref, first in zip(out_refs[2:], (start, half - start)):
        ref[...] = w_ref[pl.ds(pl.multiple_of(first, half), half), :]


def onward(got):
    rows, depth = got.shape
    shapes = [jax.ShapeDtypeStruct((rows // part, depth), BF16) for part in (4, 4, 2, 2)]
    return call(onward_kernel, "onward", tuple(shapes), [VMEM], (VMEM,) * 4, [], got)


def diagonal(x):
    zero = jnp.zeros((x.shape[0], HD), x.dtype)
    return jnp.concatenate(
        [
            jnp.concatenate([x[:, :HD], zero], axis=1),
            jnp.concatenate([zero, x[:, HD:]], axis=1),
        ],
        axis=0,
    )


def diagonal_turned(one, two):
    zero = jnp.zeros_like(one)
    return jnp.concatenate(
        [jnp.concatenate([one, zero], axis=1), jnp.concatenate([zero, two], axis=1)], axis=0
    )


def in_order(rows, lead):
    one, two = rows[:HD], rows[HD:]
    if isinstance(lead, int):
        return (one, two) if lead == 0 else (two, one)
    return jnp.where(lead == 0, one, two), jnp.where(lead == 0, two, one)


def key_mask(limit_ref, rows, first, count):
    index = lax.broadcasted_iota(jnp.int32, (rows, PAIR), 0)
    return jnp.concatenate(
        [index < limit_ref[i : i + 1, :] for i in range(first, first + count)], axis=0
    )


def scores_of(k, v, qd, d, open_keys):
    score = jnp.where(open_keys, dot(k, qd, NT) * SCALE, -jnp.inf)
    top = jnp.maximum(jnp.max(score, axis=0, keepdims=True), -1e30)
    raised = jnp.exp(score - top)
    total = jnp.maximum(jnp.sum(raised, axis=0, keepdims=True), 1.0)
    prob = raised * (1.0 / total)
    prob_b = prob.astype(BF16)
    d_prob = dot(v, d, NN)
    delta = jnp.sum(prob_b.astype(F32) * d_prob, axis=0, keepdims=True)
    return prob_b, (prob * (d_prob - delta)).astype(BF16)


def query_grad(d_score, k, tok):
    both = dot(d_score, k, TN) * SCALE
    return jnp.concatenate([both[:tok, :HD], both[tok:, HD:]], axis=1).astype(BF16)


def stacked(refs, cols):
    return jnp.concatenate([ref[:, cols] for ref in refs], axis=0)


def heads_kernel(steps, carried, dy_ref, q_ref, limit_ref, *refs):
    core, group = place()
    kv_refs, w_refs = refs[:3], refs[3 : -4 - carried]
    earlier, outs = refs[-4 - carried : -4], refs[-4:]
    dq_ref, own_ref, to_core_ref, to_far_ref = outs
    for old, out in zip(earlier, outs):
        out[..., : old.shape[-1]] = old[...]
    tok = q_ref.shape[1]
    values_at = kv_refs[0].shape[1] // (2 * PAIR)
    open_keys = key_mask(limit_ref, tok, 0, 3)
    for chunk, slot, pieces, lead in steps(core, group):
        cols, dest = columns(chunk), columns(slot)
        w = jnp.concatenate([w_refs[i][row : row + rows, :] for i, row, rows in pieces], axis=0)
        d = diagonal_turned(*in_order(dot(w, dy_ref[0], NT).astype(BF16), lead))
        qd = diagonal(q_ref[0, :, cols])
        k, v = stacked(kv_refs, cols), stacked(kv_refs, columns(chunk + values_at))
        prob_b, d_score = scores_of(k, v, qd, d, open_keys)
        dq_ref[:, dest] = query_grad(d_score, k, tok)
        for side, grad in enumerate((dot(d_score, qd, NN) * SCALE, dot(prob_b, d, NT))):
            own_ref[side, :, dest] = grad[:tok]
            to_core_ref[side, :, dest] = grad[tok : 2 * tok].astype(BF16)
            to_far_ref[side, :, dest] = grad[2 * tok :].astype(BF16)


def heads(name, steps, weights, earlier, d_out, q, limits, blocks):
    tok = q.shape[1]
    width = len(steps(0, 0)) * PAIR + (earlier[0].shape[1] if earlier else 0)
    return call(
        functools.partial(heads_kernel, steps, len(earlier)),
        name,
        (
            jax.ShapeDtypeStruct((tok, width), BF16),
            jax.ShapeDtypeStruct((2, tok, width), F32),
            jax.ShapeDtypeStruct((2, tok, width), BF16),
            jax.ShapeDtypeStruct((2, tok, width), BF16),
        ),
        [VMEM] * (6 + len(weights) + len(earlier)),
        (VMEM,) * 4,
        [],
        d_out,
        q,
        limits,
        *blocks,
        *weights,
        *earlier,
    )


def last_kernel(last, dy_ref, q_ref, limit_ref, *refs):
    core, group = place()
    kv_refs = refs[:3]
    near_both, far_both, near_next, *w_refs, dq_ref, dk_ref, dv_ref = refs[3:]
    tok, depth = q_ref.shape[1], dy_ref.shape[2]
    chunk = last(core, group)
    cols = columns(chunk)
    value_cols = columns(chunk + kv_refs[0].shape[1] // (2 * PAIR))
    w = jnp.concatenate([ref[...] for ref in w_refs], axis=0)
    dy = jnp.concatenate([dy_ref[0], near_both[:, :depth], far_both[:, :depth]], axis=0)
    turned = in_order(dot(w, dy, NT).astype(BF16), core)
    own, near, far = ([ref[:, at] for at in (cols, value_cols)] for ref in kv_refs)
    past_near = [near_next[:, :PAIR], near_next[:, PAIR:]]
    past_far = [far_both[:, depth + PAIR : depth + 2 * PAIR], far_both[:, depth + 2 * PAIR :]]
    at_queries = slice(depth, depth + PAIR)
    probs, scores, queries, cotangents = [], [], [], []
    for block, (q, parts) in enumerate(
        (
            (q_ref[0, :, cols], (own, near, far)),
            (near_both[:, at_queries], (near, own, past_near)),
            (far_both[:, at_queries], (far, own, past_far)),
        )
    ):
        k, v = (jnp.concatenate([part[side] for part in parts], axis=0) for side in range(2))
        qd = diagonal(q)
        d = diagonal_turned(*[half[:, block * tok : (block + 1) * tok] for half in turned])
        prob_b, d_score = scores_of(k, v, qd, d, key_mask(limit_ref, tok, 3 * block, 3))
        if block == 0:
            dq_ref[...] = query_grad(d_score, k, tok)
        mine = slice(0, tok) if block == 0 else slice(tok, 2 * tok)
        probs.append(prob_b[mine])
        scores.append(d_score[mine])
        queries.append(qd)
        cotangents.append(d)
    scores, probs = jnp.concatenate(scores, axis=1), jnp.concatenate(probs, axis=1)
    dk_ref[...] = (dot(scores, jnp.concatenate(queries, axis=0), NN) * SCALE).astype(BF16)
    dv_ref[...] = dot(probs, jnp.concatenate(cotangents, axis=1), NT).astype(BF16)


def last_heads(last, d_out, q, limits, blocks, halo, weights):
    tok = q.shape[1]
    return call(
        functools.partial(last_kernel, last),
        "heads_last",
        (jax.ShapeDtypeStruct((tok, PAIR), BF16),) * 3,
        [VMEM] * (9 + len(weights)),
        (VMEM,) * 3,
        [],
        d_out,
        q,
        limits,
        *blocks,
        *halo,
        *weights,
    )


def finish_kernel(chunks, widths, *refs):
    core, group = place()
    outs, stage, sems = refs[-5:-2], refs[-2], refs[-1]
    tok = stage.shape[1]
    copies = []
    slot = at = 0
    for width, summed in widths:
        part = refs[at : at + (3 if summed else 4)]
        at += len(part)
        for step in range(width // PAIR):
            cols = slice(step * PAIR, (step + 1) * PAIR)
            dest = columns(chunks(core, group)[slot])
            stage[3 * slot] = part[0][:, cols]
            for side in range(2):
                if summed:
                    total = part[1 + side][:, cols]
                else:
                    _, own, near, far = part
                    total = own[side, :, cols] + near[side, :, cols].astype(F32)
                    total = (total + far[side, :, cols].astype(F32)).astype(BF16)
                stage[3 * slot + 1 + side] = total
            for index in range(3):
                copy = pltpu.make_async_copy(
                    stage.at[3 * slot + index], outs[index].at[0, :, dest], sems.at[3 * slot + index]
                )
                copy.start()
                copies.append(copy)
            slot += 1
    for copy in copies:
        copy.wait()


def finish(chunks, parts, shape):
    count = len(chunks(0, 0))
    ins = [x for part in parts for x in part]
    widths = tuple((part[0].shape[1], len(part) == 3) for part in parts)
    return call(
        functools.partial(finish_kernel, chunks, widths),
        "finish",
        (jax.ShapeDtypeStruct(shape, BF16),) * 3,
        [VMEM] * len(ins),
        (ANY,) * 3,
        [
            pltpu.VMEM((3 * count, shape[1], PAIR), BF16),
            pltpu.SemaphoreType.DMA((3 * count,)),
        ],
        *ins,
    )


def body(queries, keys, values, d_out, w_out, pattern, valid):
    n_seq, n_fsdp = lax.axis_size("seq"), lax.axis_size("fsdp")
    n_chunks = queries.shape[2] // PAIR
    near = functools.partial(lax.ppermute, axis_name="seq", perm=swap(n_seq, 0))
    far = functools.partial(lax.ppermute, axis_name="seq", perm=swap(n_seq, 1))

    def cross(x, bits):
        pairs = [
            (s * n_fsdp + g, s * n_fsdp + (g ^ bits[s % 2]))
            for s in range(n_seq)
            for g in range(n_fsdp)
        ]
        return lax.ppermute(x, ("seq", "fsdp"), pairs)

    def exchange(part):
        dq, own, to_core, to_far = part
        back = far(to_far)
        return dq, own, near(to_core), back

    last = lambda core, group: group ^ 3 if n_fsdp == 4 else 0
    kv, both = join(last, keys, values, d_out, queries)
    limits = limits_of(pattern, valid)
    far_kv, near_kv = far(kv), near(kv)
    ours = d_out, queries, limits, (kv, near_kv, far_kv)
    if n_fsdp == 4 and n_chunks == 4 and w_out.shape[0] == PAIR:
        got = cross(w_out, (1, 2))
        near_both = near(both)
        far_both = far(hand_on("hand_far", last, near_kv, both))
        near_next = near(hand_on("hand_near", last, far_kv))
        own = heads("heads_own", lambda core, group: [(group, 0, ((0, 0, PAIR),), 0)], [w_out], (), *ours)
        got, dq, near_both, near_next = lax.optimization_barrier((got, own[0], near_both, near_next))
        *pieces, mine, other = onward(got)
        got_d = [cross(piece, (2, 1)) for piece in pieces]
        far_both, near_got = lax.optimization_barrier((far_both, (near(mine), near(other))))
        side = heads(
            "heads_side",
            lambda core, group: [
                (group ^ (1 + core), 1 + core, ((0, 0, HD), (0, HD, HD)), 0),
                (group ^ (2 - core), 2 - core, ((1, 0, HD), (2, 0, HD)), 1 - core),
            ],
            [got, *near_got],
            (dq, *own[1:]),
            *ours,
        )
        got_d, dq = lax.optimization_barrier((got_d, side[0]))
        sums = exchange((dq, *side[1:]))
        halo = near_both, far_both, near_next
        third = last_heads(last, *ours, halo, (*got_d, *[near(x) for x in got_d]))
        order = lambda core, group: [group, group ^ 1, group ^ 2, group ^ 3]
        return finish(order, [sums, third], queries.shape)
    full = lax.all_gather(w_out, "fsdp", axis=0, tiled=True)
    steps = lambda core, group: [
        (i, i, ((0, i * PAIR, PAIR),), 0) for i in range(n_chunks)
    ]
    part = exchange(heads("heads_all", steps, [full], (), *ours))
    return finish(lambda core, group: list(range(n_chunks)), [part], queries.shape)


def solution(mesh):
    rows = P("fsdp", "seq", None)
    in_specs = (rows, rows, rows, rows, P("fsdp", None), P(), P("fsdp", None))
    return jax.shard_map(
        body, mesh=mesh, in_specs=in_specs, out_specs=(rows,) * 3, check_vma=False
    )
```

time: 41.4 us -> 37.7 us (0.911)
  Pallas kernels: 8.94 us -> 12.4 us
  waiting for transfers between devices: 7.68 us -> 4.25 us
  starting transfers between devices: 19.8 us -> 16.6 us
  local copies, waits for them, and re-layouts: 3.81 us -> 2.94 us
    ppermute x2 -> x1, starting transfers between devices: 7.15 us -> 3.72 us  [exchange(): back = far(to_far)]
    pallas_call x6 -> x8, Pallas kernels: 7.14 us -> 10.3 us  [call(): pl.pallas_call(kernel, out_shape=out_shape, in_specs=in_specs, out_specs=...]
    ppermute x2, waiting for transfers between devices: 3.88 us -> 1.77 us  [body(): far_kv, near_kv = (far(kv), near(kv))]
    ppermute x2 -> x1, waiting for transfers between devices: 0.93 us -> 0.01 us  [exchange(): back = far(to_far)]
    unnamed x17 -> x15, local copies, waits for them, and re-layouts: 3.81 us -> 2.94 us
    ppermute x2, starting transfers between devices: 3.23 us -> 4.09 us  [body(): far_kv, near_kv = (far(kv), near(kv))]
    ppermute x4 -> x5, starting transfers between devices: 5.14 us -> 4.56 us  [the longest x1 3.7 us: body(): far_both = far(hand_on('hand_far', last, near_kv, both))]
    ppermute x4 -> x5, waiting for transfers between devices: 2.85 us -> 2.47 us  [the longest x2 1.53 us: body(): third = last_heads(last, *ours, halo, (*got_d, *[near(x) for x in got_d]))]
  transfers between devices with their start and end apart: 15 -> 14, of which waited for: 5 -> 4; matrix products, arithmetic and copies ran while one was open for 2% -> 0% of each run, Pallas kernels for 19% -> 31%
where the time goes in v8:
time: 37.7 us; the launch traced here: 37.1 us
  starting transfers between devices  16.6 us (44%)
  Pallas kernels  12.4 us (33%)
  waiting for transfers between devices  4.25 us (11%)
  local copies, waits for them, and re-layouts  2.94 us (8%)
  between operations  0.84 us (2%)
    pallas_call x8, Pallas kernels, call(): pl.pallas_call(kernel, out_shape=out_shape, in_specs=in_specs, out_specs=...  10.3 us
    ppermute x2, starting transfers between devices, body(): far_kv, near_kv = (far(kv), near(kv))  4.09 us
    ppermute x1, starting transfers between devices, exchange(): back = far(to_far)  3.72 us
    ppermute x1, starting transfers between devices, body(): far_both = far(hand_on('hand_far', last, near_kv, both))  3.7 us
    ppermute x3, starting transfers between devices, cross(): return lax.ppermute(x, ('seq', 'fsdp'), pairs)  3.6 us
    unnamed x15, local copies, waits for them, and re-layouts  2.94 us
    pallas_call x1, Pallas kernels, join(): pl.pallas_call(functools.partial(join_kernel, last), out_shape=(jax.Shape...  2.17 us
    ppermute x2, waiting for transfers between devices, body(): far_kv, near_kv = (far(kv), near(kv))  1.77 us
  transfers between devices with their start and end apart: 14, of which 4 were waited for; matrix products, arithmetic and copies ran while one was open for 0% of the time, Pallas kernels for 31%

profile of v8, /device:TPU:1, one launch (start us, length us, event | category | flops | bytes accessed | tf_op | source)
XLA Modules:
  0.0 37.1 jit_solution(15005961749415310005)
XLA Ops:
  0.6 2.1 %collective-permute-start = (bf16[256,2048]{1,0:T(8,128)(2,1)}, bf16[256,2048]{1,0:T(8,128)(2,1)S(1)}, u32[]{:S(2)}, u32[]{:S(2)}) collective-permute-start(bf16[256,2048]{1,0:T(8,128)(2,1)} %refs_3_.1), channel_id=1, source_target_pairs={{0,1},{1,0},{2,3},{3,2},{4,6},{5,7},{6,4},{7,5},{8,9},{9,8},{10,11... | collective-permute-start | bytes 3145736 | tf_op jit(solution)/shard_map/ppermute | solution.py:403
  2.8 2.2 %join.1 = (bf16[128,2048]{1,0:T(8,128)(2,1)}, bf16[128,2304]{1,0:T(8,128)(2,1)}) custom-call(bf16[1,128,1024]{2,1,0:T(8,128)(2,1)} %k_ref.1, bf16[1,128,1024]{2,1,0:T(8,128)(2,1)} %v_ref.1, bf16[1,128,2048]{2,1,0:T(8,128)(2,1)} %dy_ref.7, bf16[1,128,1024]{2,1,0:T(8,128)(2,1)} %q_ref.7), custom_call_target="tpu_custom_call" | custom-call | flops 1 | bytes 1 | tf_op jit(solution)/shard_map/join/pallas_call | solution.py:132
  4.9 1.0 %collective-permute-start.1 = (bf16[128,2048]{1,0:T(8,128)(2,1)}, bf16[128,2048]{1,0:T(8,128)(2,1)S(1)}, u32[]{:S(2)}, u32[]{:S(2)}) collective-permute-start(bf16[128,2048]{1,0:T(8,128)(2,1)} %get-tuple-element.30.refs_0_), channel_id=1, source_target_pairs={{0,4},{4,0},{8,12},{12,8},{16,20},{20,16},{24,28},{28,24},{1,5},{5... | collective-permute-start | bytes 1572872 | tf_op jit(solution)/shard_map/ppermute | solution.py:413
  5.9 3.1 %collective-permute-start.2 = (bf16[128,2048]{1,0:T(8,128)(2,1)}, bf16[128,2048]{1,0:T(8,128)(2,1)S(1)}, u32[]{:S(2)}, u32[]{:S(2)}) collective-permute-start(bf16[128,2048]{1,0:T(8,128)(2,1)} %get-tuple-element.30.refs_0_), channel_id=1, source_target_pairs={{4,8},{8,4},{12,16},{16,12},{20,24},{24,20},{5,9},{9,5},{13,17},{1... | collective-permute-start | bytes 1572872 | tf_op jit(solution)/shard_map/ppermute | solution.py:413
  9.1 1.1 %copy-done.4 = bf16[128,2304]{1,0:T(8,128)(2,1)S(1)} copy-done((bf16[128,2304]{1,0:T(8,128)(2,1)S(1)}, bf16[128,2304]{1,0:T(8,128)(2,1)}, u32[]{:S(2)}) %copy-start.4) | copy-done | bytes 589848
  10.2 1.0 %hand_far.1 = bf16[128,2816]{1,0:T(8,128)(2,1)} custom-call(bf16[128,2304]{1,0:T(8,128)(2,1)S(1)} %copy-done.4, bf16[128,2048]{1,0:T(8,128)(2,1)S(1)} %collective-permute-done.1.refs_1_), custom_call_target="tpu_custom_call" | custom-call | flops 1 | bytes 1 | tf_op jit(solution)/shard_map/hand_far/pallas_call | solution.py:48
  11.2 3.7 %collective-permute-start.7 = (bf16[128,2816]{1,0:T(8,128)(2,1)}, bf16[128,2816]{1,0:T(8,128)(2,1)}, u32[]{:S(2)}, u32[]{:S(2)}) collective-permute-start(bf16[128,2816]{1,0:T(8,128)(2,1)} %hand_far.1), channel_id=1, source_target_pairs={{4,8},{8,4},{12,16},{16,12},{20,24},{24,20},{5,9},{9,5},{13,17},{1... | collective-permute-start | bytes 2162696 | tf_op jit(solution)/shard_map/ppermute | solution.py:418
  14.9 1.8 %collective-permute-done.2.refs_2_.refs_0_ = bf16[128,2048]{1,0:T(8,128)(2,1)S(1)} collective-permute-done((bf16[128,2048]{1,0:T(8,128)(2,1)}, bf16[128,2048]{1,0:T(8,128)(2,1)S(1)}, u32[]{:S(2)}, u32[]{:S(2)}) %collective-permute-start.2) | collective-permute-done | bytes 524320 | tf_op jit(solution)/shard_map/ppermute | solution.py:413
  16.6 0.7 %hand_near.1 = bf16[128,512]{1,0:T(8,128)(2,1)} custom-call(bf16[128,2048]{1,0:T(8,128)(2,1)S(1)} %collective-permute-done.2.refs_2_.refs_0_), custom_call_target="tpu_custom_call" | custom-call | flops 1 | bytes 1 | tf_op jit(solution)/shard_map/hand_near/pallas_call | solution.py:48
  17.4 0.6 %copy-done.5 = s32[1,8]{1,0:T(1,128)S(1)} copy-done((s32[1,8]{1,0:T(1,128)S(1)}, s32[1,8]{1,0:T(1,128)}, u32[]{:S(2)}) %copy-start.5) | copy-done | bytes 56
  18.0 0.7 %limits.1.limit_ref = s32[16,256]{1,0:T(8,128)S(1)} custom-call(s32[8,4]{1,0:T(8,128)S(1)} %copy.10.pat_ref, s32[1,8]{1,0:T(1,128)S(1)} %copy-done.5), custom_call_target="tpu_custom_call" | custom-call | flops 1 | bytes 1 | tf_op jit(solution)/shard_map/limits/pallas_call | solution.py:48
  18.7 1.2 %copy-done.3 = bf16[256,2048]{1,0:T(8,128)(2,1)S(1)} copy-done((bf16[256,2048]{1,0:T(8,128)(2,1)S(1)}, bf16[256,2048]{1,0:T(8,128)(2,1)}, u32[]{:S(2)}) %copy-start.3) | copy-done | bytes 1048600
  19.9 1.4 %heads_own.1 = (bf16[128,256]{1,0:T(8,128)(2,1)S(1)}, f32[2,128,256]{2,1,0:T(8,128)S(1)}, bf16[2,128,256]{2,1,0:T(8,128)(2,1)S(1)}, bf16[2,128,256]{2,1,0:T(8,128)(2,1)S(1)}) custom-call(bf16[1,128,2048]{2,1,0:T(8,128)(2,1)S(1)} %copy-done, bf16[1,128,1024]{2,1,0:T(8,128)(2,1)S(1)} %copy-done.2, s32[16,256]{1,0:T(8,128)S(1)} %limits.1.limit_ref, ...), custom_call_target="tpu_custom_call" | custom-call | flops 1 | bytes 1 | tf_op jit(solution)/shard_map/heads_own/pallas_call | solution.py:48
  21.6 0.5 %collective-permute-start.9 = (bf16[128,2048]{1,0:T(8,128)(2,1)S(1)}, bf16[128,2048]{1,0:T(8,128)(2,1)S(1)}, u32[]{:S(2)}, u32[]{:S(2)}) collective-permute-start(bf16[128,2048]{1,0:T(8,128)(2,1)S(1)} %get-tuple-element.37), channel_id=1, source_target_pairs={{0,4},{4,0},{8,12},{12,8},{16,20},{20,16},{24,28},{28,24},{1,5},{5... | collective-permute-start | bytes 1572872 | tf_op jit(solution)/shard_map/ppermute | solution.py:424
  22.1 0.6 %collective-permute-start.5 = (bf16[64,2048]{1,0:T(8,128)(2,1)S(1)}, bf16[64,2048]{1,0:T(8,128)(2,1)S(1)}, u32[]{:S(2)}, u32[]{:S(2)}) collective-permute-start(bf16[64,2048]{1,0:T(8,128)(2,1)S(1)} %get-tuple-element.34), channel_id=1, source_target_pairs={{0,2},{1,3},{2,0},{3,1},{4,5},{5,4},{6,7},{7,6},{8,10},{9,11},{10,... | collective-permute-start | bytes 786440 | tf_op jit(solution)/shard_map/ppermute | solution.py:403
  22.7 0.9 %collective-permute-start.6 = (bf16[64,2048]{1,0:T(8,128)(2,1)S(1)}, bf16[64,2048]{1,0:T(8,128)(2,1)S(1)}, u32[]{:S(2)}, u32[]{:S(2)}) collective-permute-start(bf16[64,2048]{1,0:T(8,128)(2,1)S(1)} %get-tuple-element.35), channel_id=1, source_target_pairs={{0,2},{1,3},{2,0},{3,1},{4,5},{5,4},{6,7},{7,6},{8,10},{9,11},{10,... | collective-permute-start | bytes 786440 | tf_op jit(solution)/shard_map/ppermute | solution.py:403
  23.5 0.9 %collective-permute-done.7.refs_4_ = bf16[128,2816]{1,0:T(8,128)(2,1)} collective-permute-done((bf16[128,2816]{1,0:T(8,128)(2,1)}, bf16[128,2816]{1,0:T(8,128)(2,1)}, u32[]{:S(2)}, u32[]{:S(2)}) %collective-permute-start.7) | collective-permute-done | bytes 720928 | tf_op jit(solution)/shard_map/ppermute | solution.py:418
  24.5 2.2 %heads_side.1 = (bf16[128,768]{1,0:T(8,128)(2,1)S(1)}, f32[2,128,768]{2,1,0:T(8,128)S(1)}, bf16[2,128,768]{2,1,0:T(8,128)(2,1)S(1)}, bf16[2,128,768]{2,1,0:T(8,128)(2,1)S(1)}) custom-call(bf16[1,128,2048]{2,1,0:T(8,128)(2,1)S(1)} %copy-done, bf16[1,128,1024]{2,1,0:T(8,128)(2,1)S(1)} %copy-done.2, s32[16,256]{1,0:T(8,128)S(1)} %limits.1.limit_ref, ...), custom_call_target="tpu_custom_call" | custom-call | flops 1 | bytes 1 | tf_op jit(solution)/shard_map/heads_side/pallas_call | solution.py:48
  26.8 3.7 %collective-permute-start.11 = (bf16[2,128,768]{2,1,0:T(8,128)(2,1)S(1)}, bf16[2,128,768]{2,1,0:T(8,128)(2,1)S(1)}, u32[]{:S(2)}, u32[]{:S(2)}) collective-permute-start(bf16[2,128,768]{2,1,0:T(8,128)(2,1)S(1)} %get-tuple-element.48), channel_id=1, source_target_pairs={{4,8},{8,4},{12,16},{16,12},{20,24},{24,20},{5,9},{9,5},{13,17},{1... | collective-permute-start | bytes 1179656 | tf_op jit(solution)/shard_map/ppermute | solution.py:407
  30.5 0.8 %collective-permute-start.12 = (bf16[64,2048]{1,0:T(8,128)(2,1)S(1)}, bf16[64,2048]{1,0:T(8,128)(2,1)S(1)}, u32[]{:S(2)}, u32[]{:S(2)}) collective-permute-start(bf16[64,2048]{1,0:T(8,128)(2,1)S(1)} %collective-permute-done.5.refs_6_), channel_id=1, source_target_pairs={{0,4},{4,0},{8,12},{12,8},{16,20},{20,16},{24,28},{28,24},{1,5},{5... | collective-permute-start | bytes 786440 | tf_op jit(solution)/shard_map/ppermute | solution.py:438
  31.3 1.2 %collective-permute-done.12.refs_8_ = bf16[64,2048]{1,0:T(8,128)(2,1)S(1)} collective-permute-done((bf16[64,2048]{1,0:T(8,128)(2,1)S(1)}, bf16[64,2048]{1,0:T(8,128)(2,1)S(1)}, u32[]{:S(2)}, u32[]{:S(2)}) %collective-permute-start.12) | collective-permute-done | bytes 262176 | tf_op jit(solution)/shard_map/ppermute | solution.py:438
  32.5 0.4 %collective-permute-done.13.refs_9_ = bf16[64,2048]{1,0:T(8,128)(2,1)S(1)} collective-permute-done((bf16[64,2048]{1,0:T(8,128)(2,1)S(1)}, bf16[64,2048]{1,0:T(8,128)(2,1)S(1)}, u32[]{:S(2)}, u32[]{:S(2)}) %collective-permute-start.13) | collective-permute-done | bytes 262176 | tf_op jit(solution)/shard_map/ppermute | solution.py:438
  32.9 3.2 %heads_last.1 = (bf16[128,256]{1,0:T(8,128)(2,1)S(1)}, bf16[128,256]{1,0:T(8,128)(2,1)S(1)}, bf16[128,256]{1,0:T(8,128)(2,1)S(1)}) custom-call(bf16[1,128,2048]{2,1,0:T(8,128)(2,1)S(1)} %copy-done, bf16[1,128,1024]{2,1,0:T(8,128)(2,1)S(1)} %copy-done.2, s32[16,256]{1,0:T(8,128)S(1)} %limits.1.limit_ref, bf16[128,2048]{1,0:T(8,128)(2,1)S(1)} %copy-done.1, ...), custom_call_target="tpu_custom_call" | custom-call | flops 1 | bytes 1 | tf_op jit(solution)/shard_map/heads_last/pallas_call | solution.py:48
  36.1 1.0 %finish.1 = (bf16[1,128,1024]{2,1,0:T(8,128)(2,1)}, bf16[1,128,1024]{2,1,0:T(8,128)(2,1)}, bf16[1,128,1024]{2,1,0:T(8,128)(2,1)}) custom-call(bf16[128,768]{1,0:T(8,128)(2,1)S(1)} %get-tuple-element.45.refs_0_, f32[2,128,768]{2,1,0:T(8,128)S(1)} %get-tuple-element.46.refs_1_, bf16[2,128,768]{2,1,0:T(8,128)(2,1)S(1)} %collective-permute-done.10.refs_2_, ...), custom_call_target="tpu_custom_call" | custom-call | flops 1 | bytes 1 | tf_op jit(solution)/shard_map/finish/pallas_call | solution.py:48
  (28 shorter events, 0.5 us)
Async XLA Ops:
  0.6 20.7 %collective-permute-start = (bf16[256,2048]{1,0:T(8,128)(2,1)}, bf16[256,2048]{1,0:T(8,128)(2,1)S(1)}, u32[]{:S(2)}, u32[]{:S(2)}) collective-permute-start(bf16[256,2048]{1,0:T(8,128)(2,1)} %refs_3_.1), channel_id=1, source_target_pairs={{0,1},{1,0},{2,3},{3,2},{4,6},{5,7},{6,4},{7,5},{8,9},{9,8},{10,11... | collective-permute-start | bytes 3145736 | tf_op jit(solution)/shard_map/ppermute | solution.py:403
  4.9 4.2 %collective-permute-start.1 = (bf16[128,2048]{1,0:T(8,128)(2,1)}, bf16[128,2048]{1,0:T(8,128)(2,1)S(1)}, u32[]{:S(2)}, u32[]{:S(2)}) collective-permute-start(bf16[128,2048]{1,0:T(8,128)(2,1)} %get-tuple-element.30.refs_0_), channel_id=1, source_target_pairs={{0,4},{4,0},{8,12},{12,8},{16,20},{20,16},{24,28},{28,24},{1,5},{5... | collective-permute-start | bytes 1572872 | tf_op jit(solution)/shard_map/ppermute | solution.py:413
  5.9 10.7 %collective-permute-start.2 = (bf16[128,2048]{1,0:T(8,128)(2,1)}, bf16[128,2048]{1,0:T(8,128)(2,1)S(1)}, u32[]{:S(2)}, u32[]{:S(2)}) collective-permute-start(bf16[128,2048]{1,0:T(8,128)(2,1)} %get-tuple-element.30.refs_0_), channel_id=1, source_target_pairs={{4,8},{8,4},{12,16},{16,12},{20,24},{24,20},{5,9},{9,5},{13,17},{1... | collective-permute-start | bytes 1572872 | tf_op jit(solution)/shard_map/ppermute | solution.py:413
  9.0 12.3 %collective-permute-start.3 = (bf16[128,2304]{1,0:T(8,128)(2,1)}, bf16[128,2304]{1,0:T(8,128)(2,1)}, u32[]{:S(2)}, u32[]{:S(2)}) collective-permute-start(bf16[128,2304]{1,0:T(8,128)(2,1)} %get-tuple-element.32.refs_0_), channel_id=1, source_target_pairs={{0,4},{4,0},{8,12},{12,8},{16,20},{20,16},{24,28},{28,24},{1,5},{5... | collective-permute-start | bytes 1769480 | tf_op jit(solution)/shard_map/ppermute | solution.py:417
  9.1 1.1 %copy-start.4 = (bf16[128,2304]{1,0:T(8,128)(2,1)S(1)}, bf16[128,2304]{1,0:T(8,128)(2,1)}, u32[]{:S(2)}) copy-start(bf16[128,2304]{1,0:T(8,128)(2,1)} %get-tuple-element.32.refs_0_) | copy-start | bytes 1769476
  10.2 8.4 %copy-start.1 = (bf16[128,2048]{1,0:T(8,128)(2,1)S(1)}, bf16[128,2048]{1,0:T(8,128)(2,1)}, u32[]{:S(2)}) copy-start(bf16[128,2048]{1,0:T(8,128)(2,1)} %get-tuple-element.30.refs_0_) | copy-start | bytes 1572868
  10.2 8.5 %copy-start.2 = (bf16[1,128,1024]{2,1,0:T(8,128)(2,1)S(1)}, bf16[1,128,1024]{2,1,0:T(8,128)(2,1)}, u32[]{:S(2)}) copy-start(bf16[1,128,1024]{2,1,0:T(8,128)(2,1)} %q_ref.7) | copy-start | bytes 786436
  11.2 6.2 %copy-start.6 = (s32[8,4]{0,1:T(4,128)S(1)}, s32[8,4]{0,1:T(4,128)}, u32[]{:S(2)}) copy-start(s32[8,4]{0,1:T(4,128)} %param.12) | copy-start | bytes 388
  11.2 7.5 %copy-start = (bf16[1,128,2048]{2,1,0:T(8,128)(2,1)S(1)}, bf16[1,128,2048]{2,1,0:T(8,128)(2,1)}, u32[]{:S(2)}) copy-start(bf16[1,128,2048]{2,1,0:T(8,128)(2,1)} %dy_ref.7) | copy-start | bytes 1572868
  11.2 13.3 %collective-permute-start.7 = (bf16[128,2816]{1,0:T(8,128)(2,1)}, bf16[128,2816]{1,0:T(8,128)(2,1)}, u32[]{:S(2)}, u32[]{:S(2)}) collective-permute-start(bf16[128,2816]{1,0:T(8,128)(2,1)} %hand_far.1), channel_id=1, source_target_pairs={{4,8},{8,4},{12,16},{16,12},{20,24},{24,20},{5,9},{9,5},{13,17},{1... | collective-permute-start | bytes 2162696 | tf_op jit(solution)/shard_map/ppermute | solution.py:418
  17.3 0.7 %copy-start.5 = (s32[1,8]{1,0:T(1,128)S(1)}, s32[1,8]{1,0:T(1,128)}, u32[]{:S(2)}) copy-start(s32[1,8]{1,0:T(1,128)} %val_ref.1) | copy-start | bytes 100
  17.3 4.0 %collective-permute-start.4 = (bf16[128,512]{1,0:T(8,128)(2,1)}, bf16[128,512]{1,0:T(8,128)(2,1)S(1)}, u32[]{:S(2)}, u32[]{:S(2)}) collective-permute-start(bf16[128,512]{1,0:T(8,128)(2,1)} %hand_near.1), channel_id=1, source_target_pairs={{0,4},{4,0},{8,12},{12,8},{16,20},{20,16},{24,28},{28,24},{1,5},{5... | collective-permute-start | bytes 393224 | tf_op jit(solution)/shard_map/ppermute | solution.py:419
  18.7 1.2 %copy-start.3 = (bf16[256,2048]{1,0:T(8,128)(2,1)S(1)}, bf16[256,2048]{1,0:T(8,128)(2,1)}, u32[]{:S(2)}) copy-start(bf16[256,2048]{1,0:T(8,128)(2,1)} %refs_3_.1) | copy-start | bytes 3145732
  21.5 3.0 %collective-permute-start.8 = (bf16[128,2048]{1,0:T(8,128)(2,1)S(1)}, bf16[128,2048]{1,0:T(8,128)(2,1)S(1)}, u32[]{:S(2)}, u32[]{:S(2)}) collective-permute-start(bf16[128,2048]{1,0:T(8,128)(2,1)S(1)} %get-tuple-element.36), channel_id=1, source_target_pairs={{0,4},{4,0},{8,12},{12,8},{16,20},{20,16},{24,28},{28,24},{1,5},{5... | collective-permute-start | bytes 1572872 | tf_op jit(solution)/shard_map/ppermute | solution.py:424
  21.6 2.9 %collective-permute-start.9 = (bf16[128,2048]{1,0:T(8,128)(2,1)S(1)}, bf16[128,2048]{1,0:T(8,128)(2,1)S(1)}, u32[]{:S(2)}, u32[]{:S(2)}) collective-permute-start(bf16[128,2048]{1,0:T(8,128)(2,1)S(1)} %get-tuple-element.37), channel_id=1, source_target_pairs={{0,4},{4,0},{8,12},{12,8},{16,20},{20,16},{24,28},{28,24},{1,5},{5... | collective-permute-start | bytes 1572872 | tf_op jit(solution)/shard_map/ppermute | solution.py:424
  22.1 8.5 %collective-permute-start.5 = (bf16[64,2048]{1,0:T(8,128)(2,1)S(1)}, bf16[64,2048]{1,0:T(8,128)(2,1)S(1)}, u32[]{:S(2)}, u32[]{:S(2)}) collective-permute-start(bf16[64,2048]{1,0:T(8,128)(2,1)S(1)} %get-tuple-element.34), channel_id=1, source_target_pairs={{0,2},{1,3},{2,0},{3,1},{4,5},{5,4},{6,7},{7,6},{8,10},{9,11},{10,... | collective-permute-start | bytes 786440 | tf_op jit(solution)/shard_map/ppermute | solution.py:403
  22.7 7.9 %collective-permute-start.6 = (bf16[64,2048]{1,0:T(8,128)(2,1)S(1)}, bf16[64,2048]{1,0:T(8,128)(2,1)S(1)}, u32[]{:S(2)}, u32[]{:S(2)}) collective-permute-start(bf16[64,2048]{1,0:T(8,128)(2,1)S(1)} %get-tuple-element.35), channel_id=1, source_target_pairs={{0,2},{1,3},{2,0},{3,1},{4,5},{5,4},{6,7},{7,6},{8,10},{9,11},{10,... | collective-permute-start | bytes 786440 | tf_op jit(solution)/shard_map/ppermute | solution.py:403
  26.7 9.3 %collective-permute-start.10 = (bf16[2,128,768]{2,1,0:T(8,128)(2,1)S(1)}, bf16[2,128,768]{2,1,0:T(8,128)(2,1)S(1)}, u32[]{:S(2)}, u32[]{:S(2)}) collective-permute-start(bf16[2,128,768]{2,1,0:T(8,128)(2,1)S(1)} %get-tuple-element.47), channel_id=1, source_target_pairs={{0,4},{4,0},{8,12},{12,8},{16,20},{20,16},{24,28},{28,24},{1,5},{5... | collective-permute-start | bytes 1179656 | tf_op jit(solution)/shard_map/ppermute | solution.py:408
  26.8 9.2 %collective-permute-start.11 = (bf16[2,128,768]{2,1,0:T(8,128)(2,1)S(1)}, bf16[2,128,768]{2,1,0:T(8,128)(2,1)S(1)}, u32[]{:S(2)}, u32[]{:S(2)}) collective-permute-start(bf16[2,128,768]{2,1,0:T(8,128)(2,1)S(1)} %get-tuple-element.48), channel_id=1, source_target_pairs={{4,8},{8,4},{12,16},{16,12},{20,24},{24,20},{5,9},{9,5},{13,17},{1... | collective-permute-start | bytes 1179656 | tf_op jit(solution)/shard_map/ppermute | solution.py:407
  30.5 1.9 %collective-permute-start.12 = (bf16[64,2048]{1,0:T(8,128)(2,1)S(1)}, bf16[64,2048]{1,0:T(8,128)(2,1)S(1)}, u32[]{:S(2)}, u32[]{:S(2)}) collective-permute-start(bf16[64,2048]{1,0:T(8,128)(2,1)S(1)} %collective-permute-done.5.refs_6_), channel_id=1, source_target_pairs={{0,4},{4,0},{8,12},{12,8},{16,20},{20,16},{24,28},{28,24},{1,5},{5... | collective-permute-start | bytes 786440 | tf_op jit(solution)/shard_map/ppermute | solution.py:438
  31.3 1.5 %collective-permute-start.13 = (bf16[64,2048]{1,0:T(8,128)(2,1)S(1)}, bf16[64,2048]{1,0:T(8,128)(2,1)S(1)}, u32[]{:S(2)}, u32[]{:S(2)}) collective-permute-start(bf16[64,2048]{1,0:T(8,128)(2,1)S(1)} %collective-permute-done.6.refs_7_), channel_id=1, source_target_pairs={{0,4},{4,0},{8,12},{12,8},{16,20},{20,16},{24,28},{28,24},{1,5},{5... | collective-permute-start | bytes 786440 | tf_op jit(solution)/shard_map/ppermute | solution.py:438

commit v9 on v8

--- a/solution.py
+++ b/solution.py
@@ -212,16 +212,18 @@
     )
 
 
-def scores_of(k, v, qd, d, open_keys):
+def prob_of(k, qd, open_keys):
     score = jnp.where(open_keys, dot(k, qd, NT) * SCALE, -jnp.inf)
     top = jnp.maximum(jnp.max(score, axis=0, keepdims=True), -1e30)
     raised = jnp.exp(score - top)
     total = jnp.maximum(jnp.sum(raised, axis=0, keepdims=True), 1.0)
-    prob = raised * (1.0 / total)
-    prob_b = prob.astype(BF16)
+    return raised * (1.0 / total)
+
+
+def score_grad(prob, prob_b, v, d):
     d_prob = dot(v, d, NN)
     delta = jnp.sum(prob_b.astype(F32) * d_prob, axis=0, keepdims=True)
-    return prob_b, (prob * (d_prob - delta)).astype(BF16)
+    return (prob * (d_prob - delta)).astype(BF16)
 
 
 def query_grad(d_score, k, tok):
@@ -249,7 +251,9 @@
         d = diagonal_turned(*in_order(dot(w, dy_ref[0], NT).astype(BF16), lead))
         qd = diagonal(q_ref[0, :, cols])
         k, v = stacked(kv_refs, cols), stacked(kv_refs, columns(chunk + values_at))
-        prob_b, d_score = scores_of(k, v, qd, d, open_keys)
+        prob = prob_of(k, qd, open_keys)
+        prob_b = prob.astype(BF16)
+        d_score = score_grad(prob, prob_b, v, d)
         dq_ref[:, dest] = query_grad(d_score, k, tok)
         for side, grad in enumerate((dot(d_score, qd, NN) * SCALE, dot(prob_b, d, NT))):
             own_ref[side, :, dest] = grad[:tok]
@@ -281,35 +285,61 @@
     )
 
 
-def last_kernel(last, dy_ref, q_ref, limit_ref, *refs):
-    core, group = place()
-    kv_refs = refs[:3]
-    near_both, far_both, near_next, *w_refs, dq_ref, dk_ref, dv_ref = refs[3:]
-    tok, depth = q_ref.shape[1], dy_ref.shape[2]
-    chunk = last(core, group)
-    cols = columns(chunk)
-    value_cols = columns(chunk + kv_refs[0].shape[1] // (2 * PAIR))
-    w = jnp.concatenate([ref[...] for ref in w_refs], axis=0)
-    dy = jnp.concatenate([dy_ref[0], near_both[:, :depth], far_both[:, :depth]], axis=0)
-    turned = in_order(dot(w, dy, NT).astype(BF16), core)
+def last_parts(last, q_ref, near_both, far_both, near_next, kv_refs):
+    cols = columns(last(*place()))
+    value_cols = columns(last(*place()) + kv_refs[0].shape[1] // (2 * PAIR))
+    depth = far_both.shape[1] - 3 * PAIR
     own, near, far = ([ref[:, at] for at in (cols, value_cols)] for ref in kv_refs)
     past_near = [near_next[:, :PAIR], near_next[:, PAIR:]]
     past_far = [far_both[:, depth + PAIR : depth + 2 * PAIR], far_both[:, depth + 2 * PAIR :]]
     at_queries = slice(depth, depth + PAIR)
+    return (
+        (q_ref[0, :, cols], (own, near, far)),
+        (near_both[:, at_queries], (near, own, past_near)),
+        (far_both[:, at_queries], (far, own, past_far)),
+    )
+
+
+def joined(parts, side):
+    return jnp.concatenate([part[side] for part in parts], axis=0)
+
+
+def probs_kernel(last, q_ref, limit_ref, *refs):
+    *kv_refs, near_both, far_both, near_next, prob_ref = refs
+    tok = q_ref.shape[1]
+    blocks = last_parts(last, q_ref, near_both, far_both, near_next, kv_refs)
+    for block, (q, parts) in enumerate(blocks):
+        open_keys = key_mask(limit_ref, tok, 3 * block, 3)
+        prob_ref[block] = prob_of(joined(parts, 0), diagonal(q), open_keys)
+
+
+def turn_kernel(dy_ref, near_both, far_both, *refs):
+    *w_refs, out_ref = refs
+    depth = dy_ref.shape[2]
+    w = jnp.concatenate([ref[...] for ref in w_refs], axis=0)
+    dy = jnp.concatenate([dy_ref[0], near_both[:, :depth], far_both[:, :depth]], axis=0)
+    out_ref[...] = dot(w, dy, NT).astype(BF16)
+
+
+def last_kernel(last, dy_ref, q_ref, prob_ref, mine_ref, *refs):
+    core, _ = place()
+    kv_refs = refs[:3]
+    near_both, far_both, near_next, *w_refs, dq_ref, dk_ref, dv_ref = refs[3:]
+    tok, depth = q_ref.shape[1], dy_ref.shape[2]
+    w = jnp.concatenate([ref[...] for ref in w_refs], axis=0)
+    dy = jnp.concatenate([dy_ref[0], near_both[:, :depth], far_both[:, :depth]], axis=0)
+    other = dot(w, dy, NT).astype(BF16)
+    turned = in_order(jnp.concatenate([mine_ref[...], other], axis=0), core)
     probs, scores, queries, cotangents = [], [], [], []
-    for block, (q, parts) in enumerate(
-        (
-            (q_ref[0, :, cols], (own, near, far)),
-            (near_both[:, at_queries], (near, own, past_near)),
-            (far_both[:, at_queries], (far, own, past_far)),
-        )
-    ):
-        k, v = (jnp.concatenate([part[side] for part in parts], axis=0) for side in range(2))
+    blocks = last_parts(last, q_ref, near_both, far_both, near_next, kv_refs)
+    for block, (q, parts) in enumerate(blocks):
         qd = diagonal(q)
         d = diagonal_turned(*[half[:, block * tok : (block + 1) * tok] for half in turned])
-        prob_b, d_score = scores_of(k, v, qd, d, key_mask(limit_ref, tok, 3 * block, 3))
+        prob = prob_ref[block]
+        prob_b = prob.astype(BF16)
+        d_score = score_grad(prob, prob_b, joined(parts, 1), d)
         if block == 0:
-            dq_ref[...] = query_grad(d_score, k, tok)
+            dq_ref[...] = query_grad(d_score, joined(parts, 0), tok)
         mine = slice(0, tok) if block == 0 else slice(tok, 2 * tok)
         probs.append(prob_b[mine])
         scores.append(d_score[mine])
@@ -320,21 +350,45 @@
     dv_ref[...] = dot(probs, jnp.concatenate(cotangents, axis=1), NT).astype(BF16)
 
 
-def last_heads(last, d_out, q, limits, blocks, halo, weights):
+def last_heads(last, d_out, q, limits, blocks, halo, mine, other):
     tok = q.shape[1]
+    prob = call(
+        functools.partial(probs_kernel, last),
+        "probs_last",
+        jax.ShapeDtypeStruct((3, 3 * tok, PAIR), F32),
+        [VMEM] * 8,
+        VMEM,
+        [],
+        q,
+        limits,
+        *blocks,
+        *halo,
+    )
+    turned = call(
+        turn_kernel,
+        "turn",
+        jax.ShapeDtypeStruct((HD, 3 * tok), BF16),
+        [VMEM] * (3 + len(mine)),
+        VMEM,
+        [],
+        d_out,
+        *halo[:2],
+        *mine,
+    )
     return call(
         functools.partial(last_kernel, last),
         "heads_last",
         (jax.ShapeDtypeStruct((tok, PAIR), BF16),) * 3,
-        [VMEM] * (9 + len(weights)),
+        [VMEM] * (10 + len(other)),
         (VMEM,) * 3,
         [],
         d_out,
         q,
-        limits,
+        prob,
+        turned,
         *blocks,
         *halo,
-        *weights,
+        *other,
     )
 
 
@@ -411,17 +465,19 @@
     kv, both = join(last, keys, values, d_out, queries)
     limits = limits_of(pattern, valid)
     far_kv, near_kv = far(kv), near(kv)
-    ours = d_out, queries, limits, (kv, near_kv, far_kv)
     if n_fsdp == 4 and n_chunks == 4 and w_out.shape[0] == PAIR:
         got = cross(w_out, (1, 2))
         near_both = near(both)
         far_both = far(hand_on("hand_far", last, near_kv, both))
-        near_next = near(hand_on("hand_near", last, far_kv))
-        own = heads("heads_own", lambda core, group: [(group, 0, ((0, 0, PAIR),), 0)], [w_out], (), *ours)
-        got, dq, near_both, near_next = lax.optimization_barrier((got, own[0], near_both, near_next))
+        early = got, near_kv, far_kv, limits
+        got, near_kv, far_kv, limits = lax.optimization_barrier(early)
         *pieces, mine, other = onward(got)
         got_d = [cross(piece, (2, 1)) for piece in pieces]
-        far_both, near_got = lax.optimization_barrier((far_both, (near(mine), near(other))))
+        near_next = near(hand_on("hand_near", last, far_kv))
+        ours = d_out, queries, limits, (kv, near_kv, far_kv)
+        own = heads("heads_own", lambda core, group: [(group, 0, ((0, 0, PAIR),), 0)], [w_out], (), *ours)
+        near_got = near(mine), near(other)
+        far_both, near_both, near_got = lax.optimization_barrier((far_both, near_both, near_got))
         side = heads(
             "heads_side",
             lambda core, group: [
@@ -429,16 +485,17 @@
                 (group ^ (2 - core), 2 - core, ((1, 0, HD), (2, 0, HD)), 1 - core),
             ],
             [got, *near_got],
-            (dq, *own[1:]),
+            own,
             *ours,
         )
-        got_d, dq = lax.optimization_barrier((got_d, side[0]))
+        got_d, near_next, dq = lax.optimization_barrier((got_d, near_next, side[0]))
         sums = exchange((dq, *side[1:]))
         halo = near_both, far_both, near_next
-        third = last_heads(last, *ours, halo, (*got_d, *[near(x) for x in got_d]))
+        third = last_heads(last, *ours, halo, got_d, [near(x) for x in got_d])
         order = lambda core, group: [group, group ^ 1, group ^ 2, group ^ 3]
         return finish(order, [sums, third], queries.shape)
     full = lax.all_gather(w_out, "fsdp", axis=0, tiled=True)
+    ours = d_out, queries, limits, (kv, near_kv, far_kv)
     steps = lambda core, group: [
         (i, i, ((0, i * PAIR, PAIR),), 0) for i in range(n_chunks)
     ]

time: 37.7 us -> 40.1 us (1.064)
  Pallas kernels: 12.4 us -> 18.1 us
  local copies, waits for them, and re-layouts: 2.94 us -> 1.33 us
  starting transfers between devices: 16.6 us -> 15.1 us
    pallas_call x8 -> x10, Pallas kernels: 10.3 us -> 15.9 us  [call(): pl.pallas_call(kernel, out_shape=out_shape, in_specs=in_specs, out_specs=...]
    unnamed x15 -> x13, local copies, waits for them, and re-layouts: 2.94 us -> 1.33 us
    ppermute x4, waiting for transfers between devices: 1.54 us -> 0.01 us  [the longest x2 0.01 us: body(): third = last_heads(last, *ours, halo, got_d, [near(x) for x in got_d])]
    ppermute x1, starting transfers between devices: 3.7 us -> 2.57 us  [body(): far_both = far(hand_on('hand_far', last, near_kv, both))]
    ppermute x1, waiting for transfers between devices: 0.93 us -> 1.93 us  [body(): far_both = far(hand_on('hand_far', last, near_kv, both))]
    ppermute x1, starting transfers between devices: 3.72 us -> 3.1 us  [exchange(): back = far(to_far)]
    ppermute x1, starting transfers between devices: 0.07 us -> 0.56 us  [exchange(): return (dq, own, near(to_core), back)]
  transfers between devices with their start and end apart: 14 -> 14, of which waited for: 4 -> 2; matrix products, arithmetic and copies ran while one was open for 0% -> 0% of each run, Pallas kernels for 31% -> 43%
where the time goes in v9:
time: 40.1 us; the launch traced here: 39.6 us
  Pallas kernels  18.1 us (45%)
  starting transfers between devices  15.1 us (38%)
  waiting for transfers between devices  4.12 us (10%)
  local copies, waits for them, and re-layouts  1.33 us (3%)
  between operations  0.86 us (2%)
    pallas_call x10, Pallas kernels, call(): pl.pallas_call(kernel, out_shape=out_shape, in_specs=in_specs, out_specs=...  15.9 us
    ppermute x2, starting transfers between devices, body(): far_kv, near_kv = (far(kv), near(kv))  4.09 us
    ppermute x3, starting transfers between devices, cross(): return lax.ppermute(x, ('seq', 'fsdp'), pairs)  3.6 us
    ppermute x1, starting transfers between devices, exchange(): back = far(to_far)  3.1 us
    ppermute x1, starting transfers between devices, body(): far_both = far(hand_on('hand_far', last, near_kv, both))  2.57 us
    pallas_call x1, Pallas kernels, join(): pl.pallas_call(functools.partial(join_kernel, last), out_shape=(jax.Shape...  2.18 us
    ppermute x2, waiting for transfers between devices, body(): far_kv, near_kv = (far(kv), near(kv))  2.16 us
    ppermute x1, waiting for transfers between devices, body(): far_both = far(hand_on('hand_far', last, near_kv, both))  1.93 us
  transfers between devices with their start and end apart: 14, of which 2 were waited for; matrix products, arithmetic and copies ran while one was open for 0% of the time, Pallas kernels for 43%

profile of v9, /device:TPU:1, one launch (start us, length us, event | category | flops | bytes accessed | tf_op | source)
XLA Modules:
  0.0 39.6 jit_solution(11844084207341944636)
XLA Ops:
  0.6 2.1 %collective-permute-start = (bf16[256,2048]{1,0:T(8,128)(2,1)}, bf16[256,2048]{1,0:T(8,128)(2,1)}, u32[]{:S(2)}, u32[]{:S(2)}) collective-permute-start(bf16[256,2048]{1,0:T(8,128)(2,1)} %refs_3_.1), channel_id=1, source_target_pairs={{0,1},{1,0},{2,3},{3,2},{4,6},{5,7},{6,4},{7,5},{8,9},{9,8},{10,11... | collective-permute-start | bytes 3145736 | tf_op jit(solution)/shard_map/ppermute | solution.py:457
  2.8 2.2 %join.1 = (bf16[128,2048]{1,0:T(8,128)(2,1)}, bf16[128,2304]{1,0:T(8,128)(2,1)}) custom-call(bf16[1,128,1024]{2,1,0:T(8,128)(2,1)} %k_ref.1, bf16[1,128,1024]{2,1,0:T(8,128)(2,1)} %v_ref.1, bf16[1,128,2048]{2,1,0:T(8,128)(2,1)} %dy_ref.9, bf16[1,128,1024]{2,1,0:T(8,128)(2,1)} %q_ref.9), custom_call_target="tpu_custom_call" | custom-call | flops 1 | bytes 1 | tf_op jit(solution)/shard_map/join/pallas_call | solution.py:132
  5.0 1.0 %collective-permute-start.1 = (bf16[128,2048]{1,0:T(8,128)(2,1)}, bf16[128,2048]{1,0:T(8,128)(2,1)S(1)}, u32[]{:S(2)}, u32[]{:S(2)}) collective-permute-start(bf16[128,2048]{1,0:T(8,128)(2,1)} %get-tuple-element.32.refs_0_), channel_id=1, source_target_pairs={{0,4},{4,0},{8,12},{12,8},{16,20},{20,16},{24,28},{28,24},{1,5},{5... | collective-permute-start | bytes 1572872 | tf_op jit(solution)/shard_map/ppermute | solution.py:467
  6.0 3.1 %collective-permute-start.2 = (bf16[128,2048]{1,0:T(8,128)(2,1)}, bf16[128,2048]{1,0:T(8,128)(2,1)S(1)}, u32[]{:S(2)}, u32[]{:S(2)}) collective-permute-start(bf16[128,2048]{1,0:T(8,128)(2,1)} %get-tuple-element.32.refs_0_), channel_id=1, source_target_pairs={{4,8},{8,4},{12,16},{16,12},{20,24},{24,20},{5,9},{9,5},{13,17},{1... | collective-permute-start | bytes 1572872 | tf_op jit(solution)/shard_map/ppermute | solution.py:467
  9.1 2.0 %hand_far.1 = bf16[128,2816]{1,0:T(8,128)(2,1)} custom-call(bf16[128,2304]{1,0:T(8,128)(2,1)} %get-tuple-element.39.refs_0_, bf16[128,2048]{1,0:T(8,128)(2,1)S(1)} %collective-permute-done.1.refs_1_), custom_call_target="tpu_custom_call" | custom-call | flops 1 | bytes 1 | tf_op jit(solution)/shard_map/hand_far/pallas_call | solution.py:48
  11.1 2.6 %collective-permute-start.6 = (bf16[128,2816]{1,0:T(8,128)(2,1)}, bf16[128,2816]{1,0:T(8,128)(2,1)S(1)}, u32[]{:S(2)}, u32[]{:S(2)}) collective-permute-start(bf16[128,2816]{1,0:T(8,128)(2,1)} %hand_far.1), channel_id=1, source_target_pairs={{4,8},{8,4},{12,16},{16,12},{20,24},{24,20},{5,9},{9,5},{13,17},{1... | collective-permute-start | bytes 2162696 | tf_op jit(solution)/shard_map/ppermute | solution.py:471
  13.7 0.1 copy.10.pat_ref
  13.8 0.7 %limits.1.limit_ref = s32[16,256]{1,0:T(8,128)S(1)} custom-call(s32[8,4]{1,0:T(8,128)S(1)} %copy.10.pat_ref, s32[1,8]{1,0:T(1,128)S(1)} %copy-done.4), custom_call_target="tpu_custom_call" | custom-call | flops 1 | bytes 1 | tf_op jit(solution)/shard_map/limits/pallas_call | solution.py:48
  14.5 2.2 %collective-permute-done.2.refs_0_.refs_2_ = bf16[128,2048]{1,0:T(8,128)(2,1)S(1)} collective-permute-done((bf16[128,2048]{1,0:T(8,128)(2,1)}, bf16[128,2048]{1,0:T(8,128)(2,1)S(1)}, u32[]{:S(2)}, u32[]{:S(2)}) %collective-permute-start.2) | collective-permute-done | bytes 524320 | tf_op jit(solution)/shard_map/ppermute | solution.py:467
  16.7 1.3 %onward.1 = (bf16[64,2048]{1,0:T(8,128)(2,1)S(1)}, bf16[64,2048]{1,0:T(8,128)(2,1)S(1)}, bf16[128,2048]{1,0:T(8,128)(2,1)S(1)}, bf16[128,2048]{1,0:T(8,128)(2,1)S(1)}) custom-call(bf16[256,2048]{1,0:T(8,128)(2,1)} %collective-permute-done.w_ref.refs_3_), custom_call_target="tpu_custom_call" | custom-call | flops 1 | bytes 1 | tf_op jit(solution)/shard_map/onward/pallas_call | solution.py:48
  18.0 0.2 collective-permute-start.8
  18.2 0.4 %collective-permute-start.9 = (bf16[128,2048]{1,0:T(8,128)(2,1)S(1)}, bf16[128,2048]{1,0:T(8,128)(2,1)S(1)}, u32[]{:S(2)}, u32[]{:S(2)}) collective-permute-start(bf16[128,2048]{1,0:T(8,128)(2,1)S(1)} %get-tuple-element.41), channel_id=1, source_target_pairs={{0,4},{4,0},{8,12},{12,8},{16,20},{20,16},{24,28},{28,24},{1,5},{5... | collective-permute-start | bytes 1572872 | tf_op jit(solution)/shard_map/ppermute | solution.py:479
  18.6 1.4 %collective-permute-start.3 = (bf16[64,2048]{1,0:T(8,128)(2,1)S(1)}, bf16[64,2048]{1,0:T(8,128)(2,1)S(1)}, u32[]{:S(2)}, u32[]{:S(2)}) collective-permute-start(bf16[64,2048]{1,0:T(8,128)(2,1)S(1)} %get-tuple-element.34), channel_id=1, source_target_pairs={{0,2},{1,3},{2,0},{3,1},{4,5},{5,4},{6,7},{7,6},{8,10},{9,11},{10,... | collective-permute-start | bytes 786440 | tf_op jit(solution)/shard_map/ppermute | solution.py:457
  20.1 1.2 %copy-done.3 = bf16[256,2048]{1,0:T(8,128)(2,1)S(1)} copy-done((bf16[256,2048]{1,0:T(8,128)(2,1)S(1)}, bf16[256,2048]{1,0:T(8,128)(2,1)}, u32[]{:S(2)}) %copy-start.3) | copy-done | bytes 1048600
  21.3 1.4 %heads_own.1 = (bf16[128,256]{1,0:T(8,128)(2,1)S(1)}, f32[2,128,256]{2,1,0:T(8,128)S(1)}, bf16[2,128,256]{2,1,0:T(8,128)(2,1)S(1)}, bf16[2,128,256]{2,1,0:T(8,128)(2,1)S(1)}) custom-call(bf16[1,128,2048]{2,1,0:T(8,128)(2,1)S(1)} %copy-done, bf16[1,128,1024]{2,1,0:T(8,128)(2,1)S(1)} %copy-done.2, s32[16,256]{1,0:T(8,128)S(1)} %limits.1.limit_ref, ...), custom_call_target="tpu_custom_call" | custom-call | flops 1 | bytes 1 | tf_op jit(solution)/shard_map/heads_own/pallas_call | solution.py:48
  22.8 1.9 %collective-permute-done.6.refs_4_.far_both = bf16[128,2816]{1,0:T(8,128)(2,1)S(1)} collective-permute-done((bf16[128,2816]{1,0:T(8,128)(2,1)}, bf16[128,2816]{1,0:T(8,128)(2,1)S(1)}, u32[]{:S(2)}, u32[]{:S(2)}) %collective-permute-start.6) | collective-permute-done | bytes 720928 | tf_op jit(solution)/shard_map/ppermute | solution.py:471
  24.7 3.5 %heads_side.1 = (bf16[128,768]{1,0:T(8,128)(2,1)S(1)}, f32[2,128,768]{2,1,0:T(8,128)S(1)}, bf16[2,128,768]{2,1,0:T(8,128)(2,1)S(1)}, bf16[2,128,768]{2,1,0:T(8,128)(2,1)S(1)}) custom-call(bf16[1,128,2048]{2,1,0:T(8,128)(2,1)S(1)} %copy-done, bf16[1,128,1024]{2,1,0:T(8,128)(2,1)S(1)} %copy-done.2, s32[16,256]{1,0:T(8,128)S(1)} %limits.1.limit_ref, ...), custom_call_target="tpu_custom_call" | custom-call | flops 1 | bytes 1 | tf_op jit(solution)/shard_map/heads_side/pallas_call | solution.py:48
  28.2 0.6 %collective-permute-start.10 = (bf16[2,128,768]{2,1,0:T(8,128)(2,1)S(1)}, bf16[2,128,768]{2,1,0:T(8,128)(2,1)S(1)}, u32[]{:S(2)}, u32[]{:S(2)}) collective-permute-start(bf16[2,128,768]{2,1,0:T(8,128)(2,1)S(1)} %get-tuple-element.51), channel_id=1, source_target_pairs={{0,4},{4,0},{8,12},{12,8},{16,20},{20,16},{24,28},{28,24},{1,5},{5... | collective-permute-start | bytes 1179656 | tf_op jit(solution)/shard_map/ppermute | solution.py:462
  28.7 3.1 %collective-permute-start.11 = (bf16[2,128,768]{2,1,0:T(8,128)(2,1)S(1)}, bf16[2,128,768]{2,1,0:T(8,128)(2,1)S(1)}, u32[]{:S(2)}, u32[]{:S(2)}) collective-permute-start(bf16[2,128,768]{2,1,0:T(8,128)(2,1)S(1)} %get-tuple-element.52), channel_id=1, source_target_pairs={{4,8},{8,4},{12,16},{16,12},{20,24},{24,20},{5,9},{9,5},{13,17},{1... | collective-permute-start | bytes 1179656 | tf_op jit(solution)/shard_map/ppermute | solution.py:461
  32.0 0.5 %collective-permute-start.13 = (bf16[64,2048]{1,0:T(8,128)(2,1)S(1)}, bf16[64,2048]{1,0:T(8,128)(2,1)S(1)}, u32[]{:S(2)}, u32[]{:S(2)}) collective-permute-start(bf16[64,2048]{1,0:T(8,128)(2,1)S(1)} %collective-permute-done.4.refs_1_), channel_id=1, source_target_pairs={{0,4},{4,0},{8,12},{12,8},{16,20},{20,16},{24,28},{28,24},{1,5},{5... | collective-permute-start | bytes 786440 | tf_op jit(solution)/shard_map/ppermute | solution.py:494
  32.5 1.7 %turn.1.mine_ref = bf16[128,384]{1,0:T(8,128)(2,1)S(1)} custom-call(bf16[1,128,2048]{2,1,0:T(8,128)(2,1)S(1)} %copy-done, bf16[128,2304]{1,0:T(8,128)(2,1)} %collective-permute-done.7.refs_3_.near_both, bf16[128,2816]{1,0:T(8,128)(2,1)S(1)} %collective-permute-done.6.refs_4_.far_both, bf16[64,2048]{1,0:T(8,128)(2,1)S(1)} %collective-permute-done.3.refs_0_, ...), custom_call_target="tpu_custom_call" | custom-call | flops 1 | bytes 1 | tf_op jit(solution)/shard_map/turn/pallas_call | solution.py:48
  34.1 1.8 %probs_last.1.prob_ref = f32[3,384,256]{2,1,0:T(8,128)S(1)} custom-call(bf16[1,128,1024]{2,1,0:T(8,128)(2,1)S(1)} %copy-done.2, s32[16,256]{1,0:T(8,128)S(1)} %limits.1.limit_ref, bf16[128,2048]{1,0:T(8,128)(2,1)S(1)} %copy-done.1, bf16[128,2048]{1,0:T(8,128)(2,1)S(1)} %collective-permute-done.1.refs_1_, ...), custom_call_target="tpu_custom_call" | custom-call | flops 1 | bytes 1 | tf_op jit(solution)/shard_map/probs_last/pallas_call | solution.py:48
  35.9 2.6 %heads_last.1 = (bf16[128,256]{1,0:T(8,128)(2,1)S(1)}, bf16[128,256]{1,0:T(8,128)(2,1)S(1)}, bf16[128,256]{1,0:T(8,128)(2,1)S(1)}) custom-call(bf16[1,128,2048]{2,1,0:T(8,128)(2,1)S(1)} %copy-done, bf16[1,128,1024]{2,1,0:T(8,128)(2,1)S(1)} %copy-done.2, f32[3,384,256]{2,1,0:T(8,128)S(1)} %probs_last.1.prob_ref, bf16[128,384]{1,0:T(8,128)(2,1)S(1)} %turn.1.mine_ref, ...), custom_call_target="tpu_custom_call" | custom-call | flops 1 | bytes 1 | tf_op jit(solution)/shard_map/heads_last/pallas_call | solution.py:48
  38.5 1.0 %finish.1 = (bf16[1,128,1024]{2,1,0:T(8,128)(2,1)}, bf16[1,128,1024]{2,1,0:T(8,128)(2,1)}, bf16[1,128,1024]{2,1,0:T(8,128)(2,1)}) custom-call(bf16[128,768]{1,0:T(8,128)(2,1)S(1)} %get-tuple-element.49.refs_0_, f32[2,128,768]{2,1,0:T(8,128)S(1)} %get-tuple-element.50.refs_1_, bf16[2,128,768]{2,1,0:T(8,128)(2,1)S(1)} %collective-permute-done.10.refs_2_, ...), custom_call_target="tpu_custom_call" | custom-call | flops 1 | bytes 1 | tf_op jit(solution)/shard_map/finish/pallas_call | solution.py:48
  (28 shorter events, 0.3 us)
Async XLA Ops:
  0.6 16.0 %collective-permute-start = (bf16[256,2048]{1,0:T(8,128)(2,1)}, bf16[256,2048]{1,0:T(8,128)(2,1)}, u32[]{:S(2)}, u32[]{:S(2)}) collective-permute-start(bf16[256,2048]{1,0:T(8,128)(2,1)} %refs_3_.1), channel_id=1, source_target_pairs={{0,1},{1,0},{2,3},{3,2},{4,6},{5,7},{6,4},{7,5},{8,9},{9,8},{10,11... | collective-permute-start | bytes 3145736 | tf_op jit(solution)/shard_map/ppermute | solution.py:457
  5.0 8.8 %copy-start.5 = (s32[8,4]{0,1:T(4,128)S(1)}, s32[8,4]{0,1:T(4,128)}, u32[]{:S(2)}) copy-start(s32[8,4]{0,1:T(4,128)} %param.12) | copy-start | bytes 388
  5.0 8.9 %copy-start.4 = (s32[1,8]{1,0:T(1,128)S(1)}, s32[1,8]{1,0:T(1,128)}, u32[]{:S(2)}) copy-start(s32[1,8]{1,0:T(1,128)} %val_ref.1) | copy-start | bytes 100
  5.0 4.1 %collective-permute-start.1 = (bf16[128,2048]{1,0:T(8,128)(2,1)}, bf16[128,2048]{1,0:T(8,128)(2,1)S(1)}, u32[]{:S(2)}, u32[]{:S(2)}) collective-permute-start(bf16[128,2048]{1,0:T(8,128)(2,1)} %get-tuple-element.32.refs_0_), channel_id=1, source_target_pairs={{0,4},{4,0},{8,12},{12,8},{16,20},{20,16},{24,28},{28,24},{1,5},{5... | collective-permute-start | bytes 1572872 | tf_op jit(solution)/shard_map/ppermute | solution.py:467
  6.0 10.7 %collective-permute-start.2 = (bf16[128,2048]{1,0:T(8,128)(2,1)}, bf16[128,2048]{1,0:T(8,128)(2,1)S(1)}, u32[]{:S(2)}, u32[]{:S(2)}) collective-permute-start(bf16[128,2048]{1,0:T(8,128)(2,1)} %get-tuple-element.32.refs_0_), channel_id=1, source_target_pairs={{4,8},{8,4},{12,16},{16,12},{20,24},{24,20},{5,9},{9,5},{13,17},{1... | collective-permute-start | bytes 1572872 | tf_op jit(solution)/shard_map/ppermute | solution.py:467
  11.1 9.0 %copy-start = (bf16[1,128,2048]{2,1,0:T(8,128)(2,1)S(1)}, bf16[1,128,2048]{2,1,0:T(8,128)(2,1)}, u32[]{:S(2)}) copy-start(bf16[1,128,2048]{2,1,0:T(8,128)(2,1)} %dy_ref.9) | copy-start | bytes 1572868
  11.1 9.0 %copy-start.1 = (bf16[128,2048]{1,0:T(8,128)(2,1)S(1)}, bf16[128,2048]{1,0:T(8,128)(2,1)}, u32[]{:S(2)}) copy-start(bf16[128,2048]{1,0:T(8,128)(2,1)} %get-tuple-element.32.refs_0_) | copy-start | bytes 1572868
  11.1 9.0 %copy-start.2 = (bf16[1,128,1024]{2,1,0:T(8,128)(2,1)S(1)}, bf16[1,128,1024]{2,1,0:T(8,128)(2,1)}, u32[]{:S(2)}) copy-start(bf16[1,128,1024]{2,1,0:T(8,128)(2,1)} %q_ref.9) | copy-start | bytes 786436
  11.1 13.6 %collective-permute-start.6 = (bf16[128,2816]{1,0:T(8,128)(2,1)}, bf16[128,2816]{1,0:T(8,128)(2,1)S(1)}, u32[]{:S(2)}, u32[]{:S(2)}) collective-permute-start(bf16[128,2816]{1,0:T(8,128)(2,1)} %hand_far.1), channel_id=1, source_target_pairs={{4,8},{8,4},{12,16},{16,12},{20,24},{24,20},{5,9},{9,5},{13,17},{1... | collective-permute-start | bytes 2162696 | tf_op jit(solution)/shard_map/ppermute | solution.py:471
  13.7 6.3 %collective-permute-start.7 = (bf16[128,2304]{1,0:T(8,128)(2,1)}, bf16[128,2304]{1,0:T(8,128)(2,1)}, u32[]{:S(2)}, u32[]{:S(2)}) collective-permute-start(bf16[128,2304]{1,0:T(8,128)(2,1)} %get-tuple-element.39.refs_0_), channel_id=1, source_target_pairs={{0,4},{4,0},{8,12},{12,8},{16,20},{20,16},{24,28},{28,24},{1,5},{5... | collective-permute-start | bytes 1769480 | tf_op jit(solution)/shard_map/ppermute | solution.py:470
  18.0 6.7 %collective-permute-start.8 = (bf16[128,2048]{1,0:T(8,128)(2,1)S(1)}, bf16[128,2048]{1,0:T(8,128)(2,1)S(1)}, u32[]{:S(2)}, u32[]{:S(2)}) collective-permute-start(bf16[128,2048]{1,0:T(8,128)(2,1)S(1)} %get-tuple-element.40), channel_id=1, source_target_pairs={{0,4},{4,0},{8,12},{12,8},{16,20},{20,16},{24,28},{28,24},{1,5},{5... | collective-permute-start | bytes 1572872 | tf_op jit(solution)/shard_map/ppermute | solution.py:479
  18.2 6.5 %collective-permute-start.9 = (bf16[128,2048]{1,0:T(8,128)(2,1)S(1)}, bf16[128,2048]{1,0:T(8,128)(2,1)S(1)}, u32[]{:S(2)}, u32[]{:S(2)}) collective-permute-start(bf16[128,2048]{1,0:T(8,128)(2,1)S(1)} %get-tuple-element.41), channel_id=1, source_target_pairs={{0,4},{4,0},{8,12},{12,8},{16,20},{20,16},{24,28},{28,24},{1,5},{5... | collective-permute-start | bytes 1572872 | tf_op jit(solution)/shard_map/ppermute | solution.py:479
  18.6 13.3 %collective-permute-start.3 = (bf16[64,2048]{1,0:T(8,128)(2,1)S(1)}, bf16[64,2048]{1,0:T(8,128)(2,1)S(1)}, u32[]{:S(2)}, u32[]{:S(2)}) collective-permute-start(bf16[64,2048]{1,0:T(8,128)(2,1)S(1)} %get-tuple-element.34), channel_id=1, source_target_pairs={{0,2},{1,3},{2,0},{3,1},{4,5},{5,4},{6,7},{7,6},{8,10},{9,11},{10,... | collective-permute-start | bytes 786440 | tf_op jit(solution)/shard_map/ppermute | solution.py:457
  20.0 11.9 %collective-permute-start.4 = (bf16[64,2048]{1,0:T(8,128)(2,1)S(1)}, bf16[64,2048]{1,0:T(8,128)(2,1)S(1)}, u32[]{:S(2)}, u32[]{:S(2)}) collective-permute-start(bf16[64,2048]{1,0:T(8,128)(2,1)S(1)} %get-tuple-element.35), channel_id=1, source_target_pairs={{0,2},{1,3},{2,0},{3,1},{4,5},{5,4},{6,7},{7,6},{8,10},{9,11},{10,... | collective-permute-start | bytes 786440 | tf_op jit(solution)/shard_map/ppermute | solution.py:457
  20.1 1.2 %copy-start.3 = (bf16[256,2048]{1,0:T(8,128)(2,1)S(1)}, bf16[256,2048]{1,0:T(8,128)(2,1)}, u32[]{:S(2)}) copy-start(bf16[256,2048]{1,0:T(8,128)(2,1)} %refs_3_.1) | copy-start | bytes 3145732
  24.7 7.2 %collective-permute-start.5 = (bf16[128,512]{1,0:T(8,128)(2,1)S(1)}, bf16[128,512]{1,0:T(8,128)(2,1)S(1)}, u32[]{:S(2)}, u32[]{:S(2)}) collective-permute-start(bf16[128,512]{1,0:T(8,128)(2,1)S(1)} %hand_near.1), channel_id=1, source_target_pairs={{0,4},{4,0},{8,12},{12,8},{16,20},{20,16},{24,28},{28,24},{1,5},{5... | collective-permute-start | bytes 393224 | tf_op jit(solution)/shard_map/ppermute | solution.py:476
  28.2 10.3 %collective-permute-start.10 = (bf16[2,128,768]{2,1,0:T(8,128)(2,1)S(1)}, bf16[2,128,768]{2,1,0:T(8,128)(2,1)S(1)}, u32[]{:S(2)}, u32[]{:S(2)}) collective-permute-start(bf16[2,128,768]{2,1,0:T(8,128)(2,1)S(1)} %get-tuple-element.51), channel_id=1, source_target_pairs={{0,4},{4,0},{8,12},{12,8},{16,20},{20,16},{24,28},{28,24},{1,5},{5... | collective-permute-start | bytes 1179656 | tf_op jit(solution)/shard_map/ppermute | solution.py:462
  28.7 9.8 %collective-permute-start.11 = (bf16[2,128,768]{2,1,0:T(8,128)(2,1)S(1)}, bf16[2,128,768]{2,1,0:T(8,128)(2,1)S(1)}, u32[]{:S(2)}, u32[]{:S(2)}) collective-permute-start(bf16[2,128,768]{2,1,0:T(8,128)(2,1)S(1)} %get-tuple-element.52), channel_id=1, source_target_pairs={{4,8},{8,4},{12,16},{16,12},{20,24},{24,20},{5,9},{9,5},{13,17},{1... | collective-permute-start | bytes 1179656 | tf_op jit(solution)/shard_map/ppermute | solution.py:461
  31.9 4.0 %collective-permute-start.12 = (bf16[64,2048]{1,0:T(8,128)(2,1)S(1)}, bf16[64,2048]{1,0:T(8,128)(2,1)S(1)}, u32[]{:S(2)}, u32[]{:S(2)}) collective-permute-start(bf16[64,2048]{1,0:T(8,128)(2,1)S(1)} %collective-permute-done.3.refs_0_), channel_id=1, source_target_pairs={{0,4},{4,0},{8,12},{12,8},{16,20},{20,16},{24,28},{28,24},{1,5},{5... | collective-permute-start | bytes 786440 | tf_op jit(solution)/shard_map/ppermute | solution.py:494
  32.0 3.9 %collective-permute-start.13 = (bf16[64,2048]{1,0:T(8,128)(2,1)S(1)}, bf16[64,2048]{1,0:T(8,128)(2,1)S(1)}, u32[]{:S(2)}, u32[]{:S(2)}) collective-permute-start(bf16[64,2048]{1,0:T(8,128)(2,1)S(1)} %collective-permute-done.4.refs_1_), channel_id=1, source_target_pairs={{0,4},{4,0},{8,12},{12,8},{16,20},{20,16},{24,28},{28,24},{1,5},{5... | collective-permute-start | bytes 786440 | tf_op jit(solution)/shard_map/ppermute | solution.py:494

commit v10 on v9

--- a/solution.py
+++ b/solution.py
@@ -73,9 +73,9 @@
     limits = []
     for row, block in wanted:
         held = jnp.clip(row, 0, count - 1)
-        listed = pat_ref[held, 0] == block
-        for entry in range(1, pat_ref.shape[1]):
-            listed = jnp.logical_or(listed, pat_ref[held, entry] == block)
+        listed = pat_ref[0, held] == block
+        for entry in range(1, pat_ref.shape[0]):
+            listed = jnp.logical_or(listed, pat_ref[entry, held] == block)
         inside = jnp.logical_and(row == held, jnp.logical_and(block >= 0, block < count))
         keys = val_ref[0, jnp.clip(block, 0, count - 1)]
         limits.append(jnp.where(jnp.logical_and(listed, inside), keys, 0))
@@ -90,7 +90,7 @@
 
 def limits_of(pattern, valid):
     shape = jax.ShapeDtypeStruct((16, PAIR), jnp.int32)
-    return call(limits_kernel, "limits", shape, [SMEM] * 2, VMEM, [], pattern, valid)
+    return call(limits_kernel, "limits", shape, [SMEM] * 2, VMEM, [], pattern.T, valid)
 
 
 def join_kernel(last, k_ref, v_ref, dy_ref, q_ref, kv_ref, both_ref, kv, both, sems):
@@ -477,7 +477,7 @@
         ours = d_out, queries, limits, (kv, near_kv, far_kv)
         own = heads("heads_own", lambda core, group: [(group, 0, ((0, 0, PAIR),), 0)], [w_out], (), *ours)
         near_got = near(mine), near(other)
-        far_both, near_both, near_got = lax.optimization_barrier((far_both, near_both, near_got))
+        near_both, near_got = lax.optimization_barrier((near_both, near_got))
         side = heads(
             "heads_side",
             lambda core, group: [
@@ -489,7 +489,8 @@
             *ours,
         )
         got_d, near_next, dq = lax.optimization_barrier((got_d, near_next, side[0]))
-        sums = exchange((dq, *side[1:]))
+        far_both, messages = lax.optimization_barrier((far_both, side[2:]))
+        sums = exchange((dq, side[1], *messages))
         halo = near_both, far_both, near_next
         third = last_heads(last, *ours, halo, got_d, [near(x) for x in got_d])
         order = lambda core, group: [group, group ^ 1, group ^ 2, group ^ 3]

time: 40.1 us -> 35 us (0.87)
  Pallas kernels: 18.1 us -> 10.5 us
  starting transfers between devices: 15.1 us -> 16.9 us
  waiting for transfers between devices: 4.12 us -> 5.4 us
    pallas_call x10, Pallas kernels: 15.9 us -> 8.31 us  [call(): pl.pallas_call(kernel, out_shape=out_shape, in_specs=in_specs, out_specs=...]
    ppermute x1, waiting for transfers between devices: 0.01 us -> 1.95 us  [exchange(): back = far(to_far)]
    ppermute x1, starting transfers between devices: 2.57 us -> 3.71 us  [body(): far_both = far(hand_on('hand_far', last, near_kv, both))]
    ppermute x1, starting transfers between devices: 0.01 us -> 0.71 us  [body(): near_next = near(hand_on('hand_near', last, far_kv))]
    ppermute x1, starting transfers between devices: 0.56 us -> 0.01 us  [exchange(): return (dq, own, near(to_core), back)]
    ppermute x1, waiting for transfers between devices: 1.93 us -> 1.4 us  [body(): far_both = far(hand_on('hand_far', last, near_kv, both))]
    ppermute x1, starting transfers between devices: 3.1 us -> 3.59 us  [exchange(): back = far(to_far)]
    unnamed x13 -> x14, local copies, waits for them, and re-layouts: 1.33 us -> 1.09 us
  transfers between devices with their start and end apart: 14 -> 14, of which waited for: 2 -> 4; matrix products, arithmetic and copies ran while one was open for 0% -> 0% of each run, Pallas kernels for 43% -> 27%
where the time goes in v10:
time: 35 us; the launch traced here: 34.8 us
  starting transfers between devices  16.9 us (48%)
  Pallas kernels  10.5 us (30%)
  waiting for transfers between devices  5.4 us (15%)
  local copies, waits for them, and re-layouts  1.09 us (3%)
  between operations  0.9 us (3%)
    pallas_call x10, Pallas kernels, call(): pl.pallas_call(kernel, out_shape=out_shape, in_specs=in_specs, out_specs=...  8.31 us
    ppermute x2, starting transfers between devices, body(): far_kv, near_kv = (far(kv), near(kv))  4.09 us
    ppermute x1, starting transfers between devices, body(): far_both = far(hand_on('hand_far', last, near_kv, both))  3.71 us
    ppermute x3, starting transfers between devices, cross(): return lax.ppermute(x, ('seq', 'fsdp'), pairs)  3.6 us
    ppermute x1, starting transfers between devices, exchange(): back = far(to_far)  3.59 us
    pallas_call x1, Pallas kernels, join(): pl.pallas_call(functools.partial(join_kernel, last), out_shape=(jax.Shape...  2.19 us
    ppermute x2, waiting for transfers between devices, body(): far_kv, near_kv = (far(kv), near(kv))  1.95 us
    ppermute x1, waiting for transfers between devices, exchange(): back = far(to_far)  1.95 us
  transfers between devices with their start and end apart: 14, of which 4 were waited for; matrix products, arithmetic and copies ran while one was open for 0% of the time, Pallas kernels for 27%

profile of v10, /device:TPU:1, one launch (start us, length us, event | category | flops | bytes accessed | tf_op | source)
XLA Modules:
  0.0 34.8 jit_solution(18022099061798299372)
XLA Ops:
  0.6 2.1 %collective-permute-start = (bf16[256,2048]{1,0:T(8,128)(2,1)}, bf16[256,2048]{1,0:T(8,128)(2,1)S(1)}, u32[]{:S(2)}, u32[]{:S(2)}) collective-permute-start(bf16[256,2048]{1,0:T(8,128)(2,1)} %refs_3_.1), channel_id=1, source_target_pairs={{0,1},{1,0},{2,3},{3,2},{4,6},{5,7},{6,4},{7,5},{8,9},{9,8},{10,11... | collective-permute-start | bytes 3145736 | tf_op jit(solution)/shard_map/ppermute | solution.py:457
  2.8 2.2 %join.1 = (bf16[128,2048]{1,0:T(8,128)(2,1)}, bf16[128,2304]{1,0:T(8,128)(2,1)}) custom-call(bf16[1,128,1024]{2,1,0:T(8,128)(2,1)} %k_ref.1, bf16[1,128,1024]{2,1,0:T(8,128)(2,1)} %v_ref.1, bf16[1,128,2048]{2,1,0:T(8,128)(2,1)} %dy_ref.9, bf16[1,128,1024]{2,1,0:T(8,128)(2,1)} %q_ref.9), custom_call_target="tpu_custom_call" | custom-call | flops 1 | bytes 1 | tf_op jit(solution)/shard_map/join/pallas_call | solution.py:132
  5.0 1.0 %collective-permute-start.1 = (bf16[128,2048]{1,0:T(8,128)(2,1)}, bf16[128,2048]{1,0:T(8,128)(2,1)S(1)}, u32[]{:S(2)}, u32[]{:S(2)}) collective-permute-start(bf16[128,2048]{1,0:T(8,128)(2,1)} %get-tuple-element.34.refs_0_), channel_id=1, source_target_pairs={{0,4},{4,0},{8,12},{12,8},{16,20},{20,16},{24,28},{28,24},{1,5},{5... | collective-permute-start | bytes 1572872 | tf_op jit(solution)/shard_map/ppermute | solution.py:467
  6.0 3.1 %collective-permute-start.2 = (bf16[128,2048]{1,0:T(8,128)(2,1)}, bf16[128,2048]{1,0:T(8,128)(2,1)S(1)}, u32[]{:S(2)}, u32[]{:S(2)}) collective-permute-start(bf16[128,2048]{1,0:T(8,128)(2,1)} %get-tuple-element.34.refs_0_), channel_id=1, source_target_pairs={{4,8},{8,4},{12,16},{16,12},{20,24},{24,20},{5,9},{9,5},{13,17},{1... | collective-permute-start | bytes 1572872 | tf_op jit(solution)/shard_map/ppermute | solution.py:467
  9.2 1.1 %copy-done.4 = bf16[128,2304]{1,0:T(8,128)(2,1)S(1)} copy-done((bf16[128,2304]{1,0:T(8,128)(2,1)S(1)}, bf16[128,2304]{1,0:T(8,128)(2,1)}, u32[]{:S(2)}) %copy-start.4) | copy-done | bytes 589848
  10.3 3.7 %collective-permute-start.9 = (bf16[128,2816]{1,0:T(8,128)(2,1)S(1)}, bf16[128,2816]{1,0:T(8,128)(2,1)S(1)}, u32[]{:S(2)}, u32[]{:S(2)}) collective-permute-start(bf16[128,2816]{1,0:T(8,128)(2,1)S(1)} %hand_far.1), channel_id=1, source_target_pairs={{4,8},{8,4},{12,16},{16,12},{20,24},{24,20},{5,9},{9,5},{13,17},{1... | collective-permute-start | bytes 2162696 | tf_op jit(solution)/shard_map/ppermute | solution.py:471
  14.1 0.6 %limits.1.limit_ref = s32[16,256]{1,0:T(8,128)S(1)} custom-call(s32[4,8]{1,0:T(4,128)S(1)} %bitcast.1, s32[1,8]{1,0:T(1,128)S(1)} %copy-done.6), custom_call_target="tpu_custom_call" | custom-call | flops 1 | bytes 1 | tf_op jit(solution)/shard_map/limits/pallas_call | solution.py:48
  14.7 1.9 %collective-permute-done.2.refs_0_.refs_2_ = bf16[128,2048]{1,0:T(8,128)(2,1)S(1)} collective-permute-done((bf16[128,2048]{1,0:T(8,128)(2,1)}, bf16[128,2048]{1,0:T(8,128)(2,1)S(1)}, u32[]{:S(2)}, u32[]{:S(2)}) %collective-permute-start.2) | collective-permute-done | bytes 524320 | tf_op jit(solution)/shard_map/ppermute | solution.py:467
  16.7 0.1 onward.1
  16.9 0.5 %collective-permute-start.8 = (bf16[128,2048]{1,0:T(8,128)(2,1)S(1)}, bf16[128,2048]{1,0:T(8,128)(2,1)S(1)}, u32[]{:S(2)}, u32[]{:S(2)}) collective-permute-start(bf16[128,2048]{1,0:T(8,128)(2,1)S(1)} %get-tuple-element.43), channel_id=1, source_target_pairs={{0,4},{4,0},{8,12},{12,8},{16,20},{20,16},{24,28},{28,24},{1,5},{5... | collective-permute-start | bytes 1572872 | tf_op jit(solution)/shard_map/ppermute | solution.py:479
  17.4 1.3 %collective-permute-start.3 = (bf16[64,2048]{1,0:T(8,128)(2,1)S(1)}, bf16[64,2048]{1,0:T(8,128)(2,1)S(1)}, u32[]{:S(2)}, u32[]{:S(2)}) collective-permute-start(bf16[64,2048]{1,0:T(8,128)(2,1)S(1)} %get-tuple-element.36), channel_id=1, source_target_pairs={{0,2},{1,3},{2,0},{3,1},{4,5},{5,4},{6,7},{7,6},{8,10},{9,11},{10,... | collective-permute-start | bytes 786440 | tf_op jit(solution)/shard_map/ppermute | solution.py:457
  18.7 0.2 collective-permute-start.4
  18.9 1.4 %heads_own.1 = (bf16[128,256]{1,0:T(8,128)(2,1)S(1)}, f32[2,128,256]{2,1,0:T(8,128)S(1)}, bf16[2,128,256]{2,1,0:T(8,128)(2,1)S(1)}, bf16[2,128,256]{2,1,0:T(8,128)(2,1)S(1)}) custom-call(bf16[1,128,2048]{2,1,0:T(8,128)(2,1)S(1)} %copy-done, bf16[1,128,1024]{2,1,0:T(8,128)(2,1)S(1)} %copy-done.2, s32[16,256]{1,0:T(8,128)S(1)} %limits.1.limit_ref, ...), custom_call_target="tpu_custom_call" | custom-call | flops 1 | bytes 1 | tf_op jit(solution)/shard_map/heads_own/pallas_call | solution.py:48
  20.3 0.7 %collective-permute-start.5 = (bf16[128,512]{1,0:T(8,128)(2,1)S(1)}, bf16[128,512]{1,0:T(8,128)(2,1)S(1)}, u32[]{:S(2)}, u32[]{:S(2)}) collective-permute-start(bf16[128,512]{1,0:T(8,128)(2,1)S(1)} %hand_near.1), channel_id=1, source_target_pairs={{0,4},{4,0},{8,12},{12,8},{16,20},{20,16},{24,28},{28,24},{1,5},{5... | collective-permute-start | bytes 393224 | tf_op jit(solution)/shard_map/ppermute | solution.py:476
  21.0 2.2 %heads_side.1 = (bf16[128,768]{1,0:T(8,128)(2,1)S(1)}, f32[2,128,768]{2,1,0:T(8,128)S(1)}, bf16[2,128,768]{2,1,0:T(8,128)(2,1)S(1)}, bf16[2,128,768]{2,1,0:T(8,128)(2,1)S(1)}) custom-call(bf16[1,128,2048]{2,1,0:T(8,128)(2,1)S(1)} %copy-done, bf16[1,128,1024]{2,1,0:T(8,128)(2,1)S(1)} %copy-done.2, s32[16,256]{1,0:T(8,128)S(1)} %limits.1.limit_ref, ...), custom_call_target="tpu_custom_call" | custom-call | flops 1 | bytes 1 | tf_op jit(solution)/shard_map/heads_side/pallas_call | solution.py:48
  23.3 1.4 %collective-permute-done.9.refs_4_.far_both = bf16[128,2816]{1,0:T(8,128)(2,1)S(1)} collective-permute-done((bf16[128,2816]{1,0:T(8,128)(2,1)S(1)}, bf16[128,2816]{1,0:T(8,128)(2,1)S(1)}, u32[]{:S(2)}, u32[]{:S(2)}) %collective-permute-start.9) | collective-permute-done | bytes 720928 | tf_op jit(solution)/shard_map/ppermute | solution.py:471
  24.7 3.6 %collective-permute-start.11 = (bf16[2,128,768]{2,1,0:T(8,128)(2,1)S(1)}, bf16[2,128,768]{2,1,0:T(8,128)(2,1)S(1)}, u32[]{:S(2)}, u32[]{:S(2)}) collective-permute-start(bf16[2,128,768]{2,1,0:T(8,128)(2,1)S(1)} %get-tuple-element.56), channel_id=1, source_target_pairs={{4,8},{8,4},{12,16},{16,12},{20,24},{24,20},{5,9},{9,5},{13,17},{1... | collective-permute-start | bytes 1179656 | tf_op jit(solution)/shard_map/ppermute | solution.py:461
  28.4 0.5 %collective-permute-start.13 = (bf16[64,2048]{1,0:T(8,128)(2,1)S(1)}, bf16[64,2048]{1,0:T(8,128)(2,1)S(1)}, u32[]{:S(2)}, u32[]{:S(2)}) collective-permute-start(bf16[64,2048]{1,0:T(8,128)(2,1)S(1)} %collective-permute-done.4.refs_1_), channel_id=1, source_target_pairs={{0,4},{4,0},{8,12},{12,8},{16,20},{20,16},{24,28},{28,24},{1,5},{5... | collective-permute-start | bytes 786440 | tf_op jit(solution)/shard_map/ppermute | solution.py:495
  28.9 0.6 %turn.1.mine_ref = bf16[128,384]{1,0:T(8,128)(2,1)S(1)} custom-call(bf16[1,128,2048]{2,1,0:T(8,128)(2,1)S(1)} %copy-done, bf16[128,2304]{1,0:T(8,128)(2,1)S(1)} %collective-permute-done.6.refs_3_.near_both, bf16[128,2816]{1,0:T(8,128)(2,1)S(1)} %collective-permute-done.9.refs_4_.far_both, bf16[64,2048]{1,0:T(8,128)(2,1)S(1)} %collective-permute-done.3.refs_0_, ...), custom_call_target="tpu_custom_call" | custom-call | flops 1 | bytes 1 | tf_op jit(solution)/shard_map/turn/pallas_call | solution.py:48
  29.5 0.7 %probs_last.1.prob_ref = f32[3,384,256]{2,1,0:T(8,128)S(1)} custom-call(bf16[1,128,1024]{2,1,0:T(8,128)(2,1)S(1)} %copy-done.2, s32[16,256]{1,0:T(8,128)S(1)} %limits.1.limit_ref, bf16[128,2048]{1,0:T(8,128)(2,1)S(1)} %copy-done.1, bf16[128,2048]{1,0:T(8,128)(2,1)S(1)} %collective-permute-done.1.refs_1_, ...), custom_call_target="tpu_custom_call" | custom-call | flops 1 | bytes 1 | tf_op jit(solution)/shard_map/probs_last/pallas_call | solution.py:48
  30.2 0.1 collective-permute-done.13.refs_7_
  30.3 1.5 %heads_last.1 = (bf16[128,256]{1,0:T(8,128)(2,1)S(1)}, bf16[128,256]{1,0:T(8,128)(2,1)S(1)}, bf16[128,256]{1,0:T(8,128)(2,1)S(1)}) custom-call(bf16[1,128,2048]{2,1,0:T(8,128)(2,1)S(1)} %copy-done, bf16[1,128,1024]{2,1,0:T(8,128)(2,1)S(1)} %copy-done.2, f32[3,384,256]{2,1,0:T(8,128)S(1)} %probs_last.1.prob_ref, bf16[128,384]{1,0:T(8,128)(2,1)S(1)} %turn.1.mine_ref, ...), custom_call_target="tpu_custom_call" | custom-call | flops 1 | bytes 1 | tf_op jit(solution)/shard_map/heads_last/pallas_call | solution.py:48
  31.8 1.9 %collective-permute-done.11.refs_3_ = bf16[2,128,768]{2,1,0:T(8,128)(2,1)S(1)} collective-permute-done((bf16[2,128,768]{2,1,0:T(8,128)(2,1)S(1)}, bf16[2,128,768]{2,1,0:T(8,128)(2,1)S(1)}, u32[]{:S(2)}, u32[]{:S(2)}) %collective-permute-start.11) | collective-permute-done | bytes 393248 | tf_op jit(solution)/shard_map/ppermute | solution.py:461
  33.8 1.0 %finish.1 = (bf16[1,128,1024]{2,1,0:T(8,128)(2,1)}, bf16[1,128,1024]{2,1,0:T(8,128)(2,1)}, bf16[1,128,1024]{2,1,0:T(8,128)(2,1)}) custom-call(bf16[128,768]{1,0:T(8,128)(2,1)S(1)} %get-tuple-element.51.refs_0_, f32[2,128,768]{2,1,0:T(8,128)S(1)} %get-tuple-element.52.refs_1_, bf16[2,128,768]{2,1,0:T(8,128)(2,1)S(1)} %collective-permute-done.10.refs_2_, ...), custom_call_target="tpu_custom_call" | custom-call | flops 1 | bytes 1 | tf_op jit(solution)/shard_map/finish/pallas_call | solution.py:48
  (29 shorter events, 0.4 us)
Async XLA Ops:
  0.6 16.0 %collective-permute-start = (bf16[256,2048]{1,0:T(8,128)(2,1)}, bf16[256,2048]{1,0:T(8,128)(2,1)S(1)}, u32[]{:S(2)}, u32[]{:S(2)}) collective-permute-start(bf16[256,2048]{1,0:T(8,128)(2,1)} %refs_3_.1), channel_id=1, source_target_pairs={{0,1},{1,0},{2,3},{3,2},{4,6},{5,7},{6,4},{7,5},{8,9},{9,8},{10,11... | collective-permute-start | bytes 3145736 | tf_op jit(solution)/shard_map/ppermute | solution.py:457
  5.0 9.1 %copy-start.5 = (s32[8,4]{0,1:T(4,128)S(1)}, s32[8,4]{0,1:T(4,128)}, u32[]{:S(2)}) copy-start(s32[8,4]{0,1:T(4,128)} %param.12) | copy-start | bytes 388
  5.0 9.1 %copy-start.6 = (s32[1,8]{1,0:T(1,128)S(1)}, s32[1,8]{1,0:T(1,128)}, u32[]{:S(2)}) copy-start(s32[1,8]{1,0:T(1,128)} %val_ref.1) | copy-start | bytes 100
  5.0 4.2 %collective-permute-start.1 = (bf16[128,2048]{1,0:T(8,128)(2,1)}, bf16[128,2048]{1,0:T(8,128)(2,1)S(1)}, u32[]{:S(2)}, u32[]{:S(2)}) collective-permute-start(bf16[128,2048]{1,0:T(8,128)(2,1)} %get-tuple-element.34.refs_0_), channel_id=1, source_target_pairs={{0,4},{4,0},{8,12},{12,8},{16,20},{20,16},{24,28},{28,24},{1,5},{5... | collective-permute-start | bytes 1572872 | tf_op jit(solution)/shard_map/ppermute | solution.py:467
  6.0 10.7 %collective-permute-start.2 = (bf16[128,2048]{1,0:T(8,128)(2,1)}, bf16[128,2048]{1,0:T(8,128)(2,1)S(1)}, u32[]{:S(2)}, u32[]{:S(2)}) collective-permute-start(bf16[128,2048]{1,0:T(8,128)(2,1)} %get-tuple-element.34.refs_0_), channel_id=1, source_target_pairs={{4,8},{8,4},{12,16},{16,12},{20,24},{24,20},{5,9},{9,5},{13,17},{1... | collective-permute-start | bytes 1572872 | tf_op jit(solution)/shard_map/ppermute | solution.py:467
  9.1 9.6 %collective-permute-start.6 = (bf16[128,2304]{1,0:T(8,128)(2,1)}, bf16[128,2304]{1,0:T(8,128)(2,1)S(1)}, u32[]{:S(2)}, u32[]{:S(2)}) collective-permute-start(bf16[128,2304]{1,0:T(8,128)(2,1)} %get-tuple-element.41.refs_0_), channel_id=1, source_target_pairs={{0,4},{4,0},{8,12},{12,8},{16,20},{20,16},{24,28},{28,24},{1,5},{5... | collective-permute-start | bytes 1769480 | tf_op jit(solution)/shard_map/ppermute | solution.py:470
  9.2 1.1 %copy-start.4 = (bf16[128,2304]{1,0:T(8,128)(2,1)S(1)}, bf16[128,2304]{1,0:T(8,128)(2,1)}, u32[]{:S(2)}) copy-start(bf16[128,2304]{1,0:T(8,128)(2,1)} %get-tuple-element.41.refs_0_) | copy-start | bytes 1769476
  10.2 8.6 %copy-start.3 = (bf16[256,2048]{1,0:T(8,128)(2,1)S(1)}, bf16[256,2048]{1,0:T(8,128)(2,1)}, u32[]{:S(2)}) copy-start(bf16[256,2048]{1,0:T(8,128)(2,1)} %refs_3_.1) | copy-start | bytes 3145732
  10.3 8.6 %copy-start = (bf16[1,128,2048]{2,1,0:T(8,128)(2,1)S(1)}, bf16[1,128,2048]{2,1,0:T(8,128)(2,1)}, u32[]{:S(2)}) copy-start(bf16[1,128,2048]{2,1,0:T(8,128)(2,1)} %dy_ref.9) | copy-start | bytes 1572868
  10.3 8.6 %copy-start.1 = (bf16[128,2048]{1,0:T(8,128)(2,1)S(1)}, bf16[128,2048]{1,0:T(8,128)(2,1)}, u32[]{:S(2)}) copy-start(bf16[128,2048]{1,0:T(8,128)(2,1)} %get-tuple-element.34.refs_0_) | copy-start | bytes 1572868
  10.3 8.6 %copy-start.2 = (bf16[1,128,1024]{2,1,0:T(8,128)(2,1)S(1)}, bf16[1,128,1024]{2,1,0:T(8,128)(2,1)}, u32[]{:S(2)}) copy-start(bf16[1,128,1024]{2,1,0:T(8,128)(2,1)} %q_ref.9) | copy-start | bytes 786436
  10.3 14.4 %collective-permute-start.9 = (bf16[128,2816]{1,0:T(8,128)(2,1)S(1)}, bf16[128,2816]{1,0:T(8,128)(2,1)S(1)}, u32[]{:S(2)}, u32[]{:S(2)}) collective-permute-start(bf16[128,2816]{1,0:T(8,128)(2,1)S(1)} %hand_far.1), channel_id=1, source_target_pairs={{4,8},{8,4},{12,16},{16,12},{20,24},{24,20},{5,9},{9,5},{13,17},{1... | collective-permute-start | bytes 2162696 | tf_op jit(solution)/shard_map/ppermute | solution.py:471
  16.8 3.5 %collective-permute-start.7 = (bf16[128,2048]{1,0:T(8,128)(2,1)S(1)}, bf16[128,2048]{1,0:T(8,128)(2,1)S(1)}, u32[]{:S(2)}, u32[]{:S(2)}) collective-permute-start(bf16[128,2048]{1,0:T(8,128)(2,1)S(1)} %get-tuple-element.42), channel_id=1, source_target_pairs={{0,4},{4,0},{8,12},{12,8},{16,20},{20,16},{24,28},{28,24},{1,5},{5... | collective-permute-start | bytes 1572872 | tf_op jit(solution)/shard_map/ppermute | solution.py:479
  16.9 4.2 %collective-permute-start.8 = (bf16[128,2048]{1,0:T(8,128)(2,1)S(1)}, bf16[128,2048]{1,0:T(8,128)(2,1)S(1)}, u32[]{:S(2)}, u32[]{:S(2)}) collective-permute-start(bf16[128,2048]{1,0:T(8,128)(2,1)S(1)} %get-tuple-element.43), channel_id=1, source_target_pairs={{0,4},{4,0},{8,12},{12,8},{16,20},{20,16},{24,28},{28,24},{1,5},{5... | collective-permute-start | bytes 1572872 | tf_op jit(solution)/shard_map/ppermute | solution.py:479
  17.4 10.9 %collective-permute-start.3 = (bf16[64,2048]{1,0:T(8,128)(2,1)S(1)}, bf16[64,2048]{1,0:T(8,128)(2,1)S(1)}, u32[]{:S(2)}, u32[]{:S(2)}) collective-permute-start(bf16[64,2048]{1,0:T(8,128)(2,1)S(1)} %get-tuple-element.36), channel_id=1, source_target_pairs={{0,2},{1,3},{2,0},{3,1},{4,5},{5,4},{6,7},{7,6},{8,10},{9,11},{10,... | collective-permute-start | bytes 786440 | tf_op jit(solution)/shard_map/ppermute | solution.py:457
  18.7 9.6 %collective-permute-start.4 = (bf16[64,2048]{1,0:T(8,128)(2,1)S(1)}, bf16[64,2048]{1,0:T(8,128)(2,1)S(1)}, u32[]{:S(2)}, u32[]{:S(2)}) collective-permute-start(bf16[64,2048]{1,0:T(8,128)(2,1)S(1)} %get-tuple-element.37), channel_id=1, source_target_pairs={{0,2},{1,3},{2,0},{3,1},{4,5},{5,4},{6,7},{7,6},{8,10},{9,11},{10,... | collective-permute-start | bytes 786440 | tf_op jit(solution)/shard_map/ppermute | solution.py:457
  20.3 8.0 %collective-permute-start.5 = (bf16[128,512]{1,0:T(8,128)(2,1)S(1)}, bf16[128,512]{1,0:T(8,128)(2,1)S(1)}, u32[]{:S(2)}, u32[]{:S(2)}) collective-permute-start(bf16[128,512]{1,0:T(8,128)(2,1)S(1)} %hand_near.1), channel_id=1, source_target_pairs={{0,4},{4,0},{8,12},{12,8},{16,20},{20,16},{24,28},{28,24},{1,5},{5... | collective-permute-start | bytes 393224 | tf_op jit(solution)/shard_map/ppermute | solution.py:476
  24.7 7.1 %collective-permute-start.10 = (bf16[2,128,768]{2,1,0:T(8,128)(2,1)S(1)}, bf16[2,128,768]{2,1,0:T(8,128)(2,1)S(1)}, u32[]{:S(2)}, u32[]{:S(2)}) collective-permute-start(bf16[2,128,768]{2,1,0:T(8,128)(2,1)S(1)} %get-tuple-element.55), channel_id=1, source_target_pairs={{0,4},{4,0},{8,12},{12,8},{16,20},{20,16},{24,28},{28,24},{1,5},{5... | collective-permute-start | bytes 1179656 | tf_op jit(solution)/shard_map/ppermute | solution.py:462
  24.7 9.1 %collective-permute-start.11 = (bf16[2,128,768]{2,1,0:T(8,128)(2,1)S(1)}, bf16[2,128,768]{2,1,0:T(8,128)(2,1)S(1)}, u32[]{:S(2)}, u32[]{:S(2)}) collective-permute-start(bf16[2,128,768]{2,1,0:T(8,128)(2,1)S(1)} %get-tuple-element.56), channel_id=1, source_target_pairs={{4,8},{8,4},{12,16},{16,12},{20,24},{24,20},{5,9},{9,5},{13,17},{1... | collective-permute-start | bytes 1179656 | tf_op jit(solution)/shard_map/ppermute | solution.py:461
  28.3 1.9 %collective-permute-start.12 = (bf16[64,2048]{1,0:T(8,128)(2,1)S(1)}, bf16[64,2048]{1,0:T(8,128)(2,1)S(1)}, u32[]{:S(2)}, u32[]{:S(2)}) collective-permute-start(bf16[64,2048]{1,0:T(8,128)(2,1)S(1)} %collective-permute-done.3.refs_0_), channel_id=1, source_target_pairs={{0,4},{4,0},{8,12},{12,8},{16,20},{20,16},{24,28},{28,24},{1,5},{5... | collective-permute-start | bytes 786440 | tf_op jit(solution)/shard_map/ppermute | solution.py:495
  28.4 1.9 %collective-permute-start.13 = (bf16[64,2048]{1,0:T(8,128)(2,1)S(1)}, bf16[64,2048]{1,0:T(8,128)(2,1)S(1)}, u32[]{:S(2)}, u32[]{:S(2)}) collective-permute-start(bf16[64,2048]{1,0:T(8,128)(2,1)S(1)} %collective-permute-done.4.refs_1_), channel_id=1, source_target_pairs={{0,4},{4,0},{8,12},{12,8},{16,20},{20,16},{24,28},{28,24},{1,5},{5... | collective-permute-start | bytes 786440 | tf_op jit(solution)/shard_map/ppermute | solution.py:495

commit v11 on v10

--- a/solution.py
+++ b/solution.py
@@ -9,7 +9,7 @@
 
 HD = 128
 PAIR = 2 * HD
-PIECE = 64
+PIECE = 32
 BRIEF = pl.CostEstimate(flops=1, bytes_accessed=1, transcendentals=0)
 F32 = jnp.float32
 BF16 = jnp.bfloat16
@@ -93,30 +93,15 @@
     return call(limits_kernel, "limits", shape, [SMEM] * 2, VMEM, [], pattern.T, valid)
 
 
-def join_kernel(last, k_ref, v_ref, dy_ref, q_ref, kv_ref, both_ref, kv, both, sems):
-    core, group = place()
-    tok, depth = dy_ref.shape[1:]
-    width = k_ref.shape[2]
-    steps = []
-    for sources, held, target in (
-        (((k_ref, slice(None), width), (v_ref, slice(None), width)), kv, kv_ref),
-        (
-            ((dy_ref, slice(None), depth), (q_ref, columns(last(core, group)), PAIR)),
-            both,
-            both_ref,
-        ),
-    ):
+def join_kernel(k_ref, v_ref, kv_ref, kv, sems):
+    tok, width = k_ref.shape[1:]
+    arrivals, moves = [], []
+    for side, ref in enumerate((k_ref, v_ref)):
         for row in range(0, tok, PIECE):
-            rows = pl.ds(row, PIECE)
-            to = 0
-            for source, cols, size in sources:
-                at = (rows, pl.ds(to, size))
-                steps.append((source.at[0, rows, cols], held.at[at], target.at[at]))
-                to += size
-    arrivals, moves = [], []
-    for i, (source, held, target) in enumerate(steps):
-        arrivals.append(pltpu.make_async_copy(source, held, sems.at[0, i]))
-        moves.append(pltpu.make_async_copy(held, target, sems.at[1, i]))
+            rows, i = pl.ds(row, PIECE), len(moves)
+            at = (rows, pl.ds(side * width, width))
+            arrivals.append(pltpu.make_async_copy(ref.at[0, rows, :], kv.at[at], sems.at[0, i]))
+            moves.append(pltpu.make_async_copy(kv.at[at], kv_ref.at[at], sems.at[1, i]))
     for copy in arrivals:
         copy.start()
     for arrival, move in zip(arrivals, moves):
@@ -126,58 +111,70 @@
         move.wait()
 
 
-def join(last, keys, values, d_out, queries):
-    tok, depth = d_out.shape[1:]
-    kv, both = (tok, 2 * keys.shape[2]), (tok, depth + PAIR)
+def join(keys, values):
+    tok, width = keys.shape[1:]
+    kv = (tok, 2 * width)
     return pl.pallas_call(
-        functools.partial(join_kernel, last),
-        out_shape=(jax.ShapeDtypeStruct(kv, BF16), jax.ShapeDtypeStruct(both, BF16)),
-        in_specs=[HBM] * 4,
-        out_specs=(ANY,) * 2,
+        join_kernel,
+        out_shape=jax.ShapeDtypeStruct(kv, BF16),
+        in_specs=[HBM] * 2,
+        out_specs=ANY,
         scratch_shapes=[
             pltpu.VMEM(kv, BF16),
-            pltpu.VMEM(both, BF16),
-            pltpu.SemaphoreType.DMA((2, 4 * (tok // PIECE))),
+            pltpu.SemaphoreType.DMA((2, 2 * (tok // PIECE))),
         ],
         cost_estimate=BRIEF,
         compiler_params=WIDE,
         name="join",
-    )(keys, values, d_out, queries)
-
-
-def hand_on_kernel(last, *refs):
+    )(keys, values)
+
+
+def hand_on_kernel(last, n_whole, *refs):
     core, group = place()
-    *before, kv_ref, out_ref = refs
+    whole, cut, out_ref = refs[:n_whole], refs[n_whole:-1], refs[-1]
     chunk = last(core, group)
-    cols = [columns(chunk), columns(chunk + kv_ref.shape[1] // (2 * PAIR))]
+    pieces = [ref[0] for ref in whole]
+    for ref in cut:
+        if ref.ndim == 3:
+            pieces.append(ref[0, :, columns(chunk)])
+        else:
+            pieces.append(ref[:, columns(chunk)])
+            pieces.append(ref[:, columns(chunk + ref.shape[1] // (2 * PAIR))])
     to = 0
-    for piece in [ref[...] for ref in before] + [kv_ref[:, at] for at in cols]:
+    for piece in pieces:
         out_ref[:, to : to + piece.shape[1]] = piece
         to += piece.shape[1]
 
 
-def hand_on(name, last, kv, *before):
-    width = sum(x.shape[1] for x in before) + 2 * PAIR
-    shape = jax.ShapeDtypeStruct((kv.shape[0], width), BF16)
-    kernel = functools.partial(hand_on_kernel, last)
-    return call(kernel, name, shape, [VMEM] * (len(before) + 1), VMEM, [], *before, kv)
+def hand_on(name, last, whole, cut):
+    width = sum(x.shape[2] for x in whole) + sum(PAIR * (1 if x.ndim == 3 else 2) for x in cut)
+    shape = jax.ShapeDtypeStruct((cut[0].shape[-2], width), BF16)
+    kernel = functools.partial(hand_on_kernel, last, len(whole))
+    return call(kernel, name, shape, [VMEM] * (len(whole) + len(cut)), VMEM, [], *whole, *cut)
 
 
 def onward_kernel(w_ref, *out_refs):
     core, _ = place()
     half = w_ref.shape[0] // 2
     start = pl.multiple_of(core * half, half)
-    for i, ref in enumerate(out_refs[:2]):
-        rows = ref.shape[0]
-        ref[...] = w_ref[pl.ds(start + i * rows, rows), :]
-    for ref, first in zip(out_refs[2:], (start, half - start)):
+    for ref, first in zip(out_refs, (start, half - start)):
         ref[...] = w_ref[pl.ds(pl.multiple_of(first, half), half), :]
 
 
 def onward(got):
     rows, depth = got.shape
-    shapes = [jax.ShapeDtypeStruct((rows // part, depth), BF16) for part in (4, 4, 2, 2)]
-    return call(onward_kernel, "onward", tuple(shapes), [VMEM], (VMEM,) * 4, [], got)
+    shapes = [jax.ShapeDtypeStruct((rows // part, depth), BF16) for part in (2, 2)]
+    return call(onward_kernel, "onward", tuple(shapes), [VMEM], (VMEM,) * 2, [], got)
+
+
+def split_kernel(x_ref, *out_refs):
+    for i, ref in enumerate(out_refs):
+        ref[...] = x_ref[i * ref.shape[0] : (i + 1) * ref.shape[0], :]
+
+
+def split(x):
+    half = jax.ShapeDtypeStruct((x.shape[0] // 2, x.shape[1]), BF16)
+    return call(split_kernel, "split", (half, half), [VMEM], (VMEM,) * 2, [], x)
 
 
 def diagonal(x):
@@ -462,18 +459,18 @@
         return dq, own, near(to_core), back
 
     last = lambda core, group: group ^ 3 if n_fsdp == 4 else 0
-    kv, both = join(last, keys, values, d_out, queries)
+    kv = join(keys, values)
     limits = limits_of(pattern, valid)
     far_kv, near_kv = far(kv), near(kv)
     if n_fsdp == 4 and n_chunks == 4 and w_out.shape[0] == PAIR:
         got = cross(w_out, (1, 2))
-        near_both = near(both)
-        far_both = far(hand_on("hand_far", last, near_kv, both))
+        message = hand_on("hand_far", last, [d_out], [queries, near_kv])
+        far_both, near_both = far(message), near(message)
         early = got, near_kv, far_kv, limits
         got, near_kv, far_kv, limits = lax.optimization_barrier(early)
-        *pieces, mine, other = onward(got)
-        got_d = [cross(piece, (2, 1)) for piece in pieces]
-        near_next = near(hand_on("hand_near", last, far_kv))
+        mine, other = onward(got)
+        got_d = cross(mine, (2, 1))
+        near_next = near(hand_on("hand_near", last, [], [far_kv]))
         ours = d_out, queries, limits, (kv, near_kv, far_kv)
         own = heads("heads_own", lambda core, group: [(group, 0, ((0, 0, PAIR),), 0)], [w_out], (), *ours)
         near_got = near(mine), near(other)
@@ -488,11 +485,12 @@
             own,
             *ours,
         )
-        got_d, near_next, dq = lax.optimization_barrier((got_d, near_next, side[0]))
-        far_both, messages = lax.optimization_barrier((far_both, side[2:]))
-        sums = exchange((dq, side[1], *messages))
+        got_d, near_next, far_both, dq = lax.optimization_barrier(
+            (got_d, near_next, far_both, side[0])
+        )
+        sums = exchange((dq, *side[1:]))
         halo = near_both, far_both, near_next
-        third = last_heads(last, *ours, halo, got_d, [near(x) for x in got_d])
+        third = last_heads(last, *ours, halo, [got_d], [near(x) for x in split(got_d)])
         order = lambda core, group: [group, group ^ 1, group ^ 2, group ^ 3]
         return finish(order, [sums, third], queries.shape)
     full = lax.all_gather(w_out, "fsdp", axis=0, tiled=True)

time: 35 us -> 33.6 us (0.960)
  local copies, waits for them, and re-layouts: 1.09 us -> 0.03 us
    ppermute x2, waiting for transfers between devices: 1.95 us -> 3.13 us  [body(): far_kv, near_kv = (far(kv), near(kv))]
    unnamed x14 -> x12, local copies, waits for them, and re-layouts: 1.09 us -> 0.03 us
    ppermute x5, waiting for transfers between devices: 1.49 us -> 0.47 us  [the longest x2 0.46 us: body(): near(x)]
    ppermute x1, starting transfers between devices: 3.59 us -> 3.12 us  [exchange(): back = far(to_far)]
    ppermute x3 -> x2, starting transfers between devices: 3.6 us -> 3.79 us  [cross(): return lax.ppermute(x, ('seq', 'fsdp'), pairs)]
    pallas_call x10 -> x11, Pallas kernels: 8.31 us -> 8.33 us  [call(): pl.pallas_call(kernel, out_shape=out_shape, in_specs=in_specs, out_specs=...]
  transfers between devices with their start and end apart: 14 -> 13, of which waited for: 4 -> 4; matrix products, arithmetic and copies ran while one was open for 0% -> 0% of each run, Pallas kernels for 27% -> 27%
where the time goes in v11:
time: 33.6 us; the launch traced here: 33.3 us
  starting transfers between devices  16.7 us (50%)
  Pallas kernels  10.2 us (30%)
  waiting for transfers between devices  5.52 us (16%)
  between operations  0.89 us (3%)
    pallas_call x11, Pallas kernels, call(): pl.pallas_call(kernel, out_shape=out_shape, in_specs=in_specs, out_specs=...  8.33 us
    ppermute x2, starting transfers between devices, body(): far_kv, near_kv = (far(kv), near(kv))  4.09 us
    ppermute x2, starting transfers between devices, cross(): return lax.ppermute(x, ('seq', 'fsdp'), pairs)  3.79 us
    ppermute x2, starting transfers between devices, body(): far_both, near_both = (far(message), near(message))  3.65 us
    ppermute x2, waiting for transfers between devices, body(): far_kv, near_kv = (far(kv), near(kv))  3.13 us
    ppermute x1, starting transfers between devices, exchange(): back = far(to_far)  3.12 us
    ppermute x1, waiting for transfers between devices, exchange(): back = far(to_far)  1.9 us
    pallas_call x1, Pallas kernels, join(): pl.pallas_call(join_kernel, out_shape=jax.ShapeDtypeStruct(kv, BF16), in_...  1.84 us
  transfers between devices with their start and end apart: 13, of which 4 were waited for; matrix products, arithmetic and copies ran while one was open for 0% of the time, Pallas kernels for 27%

profile of v11, /device:TPU:1, one launch (start us, length us, event | category | flops | bytes accessed | tf_op | source)
XLA Modules:
  0.0 33.3 jit_solution(11205873358987399786)
XLA Ops:
  0.7 2.1 %collective-permute-start = (bf16[256,2048]{1,0:T(8,128)(2,1)}, bf16[256,2048]{1,0:T(8,128)(2,1)S(1)}, u32[]{:S(2)}, u32[]{:S(2)}) collective-permute-start(bf16[256,2048]{1,0:T(8,128)(2,1)} %refs_3_.1), channel_id=1, source_target_pairs={{0,1},{1,0},{2,3},{3,2},{4,6},{5,7},{6,4},{7,5},{8,9},{9,8},{10,11... | collective-permute-start | bytes 3145736 | tf_op jit(solution)/shard_map/ppermute | solution.py:454
  2.8 1.8 %join.1.refs_0_ = bf16[128,2048]{1,0:T(8,128)(2,1)} custom-call(bf16[1,128,1024]{2,1,0:T(8,128)(2,1)} %k_ref.1, bf16[1,128,1024]{2,1,0:T(8,128)(2,1)} %v_ref.1), custom_call_target="tpu_custom_call" | custom-call | flops 1 | bytes 1 | tf_op jit(solution)/shard_map/join/pallas_call | solution.py:117
  4.7 1.0 %collective-permute-start.1 = (bf16[128,2048]{1,0:T(8,128)(2,1)}, bf16[128,2048]{1,0:T(8,128)(2,1)S(1)}, u32[]{:S(2)}, u32[]{:S(2)}) collective-permute-start(bf16[128,2048]{1,0:T(8,128)(2,1)} %join.1.refs_0_), channel_id=1, source_target_pairs={{0,4},{4,0},{8,12},{12,8},{16,20},{20,16},{24,28},{28,24},{1,5},{5... | collective-permute-start | bytes 1572872 | tf_op jit(solution)/shard_map/ppermute | solution.py:464
  5.7 3.1 %collective-permute-start.2 = (bf16[128,2048]{1,0:T(8,128)(2,1)}, bf16[128,2048]{1,0:T(8,128)(2,1)S(1)}, u32[]{:S(2)}, u32[]{:S(2)}) collective-permute-start(bf16[128,2048]{1,0:T(8,128)(2,1)} %join.1.refs_0_), channel_id=1, source_target_pairs={{4,8},{8,4},{12,16},{16,12},{20,24},{24,20},{5,9},{9,5},{13,17},{1... | collective-permute-start | bytes 1572872 | tf_op jit(solution)/shard_map/ppermute | solution.py:464
  8.9 0.1 collective-permute-start.6
  9.0 3.6 %collective-permute-start.5 = (bf16[128,2816]{1,0:T(8,128)(2,1)S(1)}, bf16[128,2816]{1,0:T(8,128)(2,1)S(1)}, u32[]{:S(2)}, u32[]{:S(2)}) collective-permute-start(bf16[128,2816]{1,0:T(8,128)(2,1)S(1)} %hand_far.1), channel_id=1, source_target_pairs={{4,8},{8,4},{12,16},{16,12},{20,24},{24,20},{5,9},{9,5},{13,17},{1... | collective-permute-start | bytes 2162696 | tf_op jit(solution)/shard_map/ppermute | solution.py:468
  12.6 0.6 %limits.1.limit_ref = s32[16,256]{1,0:T(8,128)S(1)} custom-call(s32[4,8]{1,0:T(4,128)S(1)} %bitcast.1, s32[1,8]{1,0:T(1,128)S(1)} %copy-done.5), custom_call_target="tpu_custom_call" | custom-call | flops 1 | bytes 1 | tf_op jit(solution)/shard_map/limits/pallas_call | solution.py:48
  13.2 3.1 %collective-permute-done.2.refs_0_.refs_2_ = bf16[128,2048]{1,0:T(8,128)(2,1)S(1)} collective-permute-done((bf16[128,2048]{1,0:T(8,128)(2,1)}, bf16[128,2048]{1,0:T(8,128)(2,1)S(1)}, u32[]{:S(2)}, u32[]{:S(2)}) %collective-permute-start.2) | collective-permute-done | bytes 524320 | tf_op jit(solution)/shard_map/ppermute | solution.py:464
  16.4 0.4 %collective-permute-start.7 = (bf16[128,2048]{1,0:T(8,128)(2,1)S(1)}, bf16[128,2048]{1,0:T(8,128)(2,1)S(1)}, u32[]{:S(2)}, u32[]{:S(2)}) collective-permute-start(bf16[128,2048]{1,0:T(8,128)(2,1)S(1)} %get-tuple-element.30), channel_id=1, source_target_pairs={{0,4},{4,0},{8,12},{12,8},{16,20},{20,16},{24,28},{28,24},{1,5},{5... | collective-permute-start | bytes 1572872 | tf_op jit(solution)/shard_map/ppermute | solution.py:476
  16.8 0.2 collective-permute-start.8
  17.0 1.7 %collective-permute-start.3 = (bf16[128,2048]{1,0:T(8,128)(2,1)S(1)}, bf16[128,2048]{1,0:T(8,128)(2,1)S(1)}, u32[]{:S(2)}, u32[]{:S(2)}) collective-permute-start(bf16[128,2048]{1,0:T(8,128)(2,1)S(1)} %get-tuple-element.30), channel_id=1, source_target_pairs={{0,2},{1,3},{2,0},{3,1},{4,5},{5,4},{6,7},{7,6},{8,10},{9,11},{10,... | collective-permute-start | bytes 1572872 | tf_op jit(solution)/shard_map/ppermute | solution.py:454
  18.7 1.4 %heads_own.1 = (bf16[128,256]{1,0:T(8,128)(2,1)S(1)}, f32[2,128,256]{2,1,0:T(8,128)S(1)}, bf16[2,128,256]{2,1,0:T(8,128)(2,1)S(1)}, bf16[2,128,256]{2,1,0:T(8,128)(2,1)S(1)}) custom-call(bf16[1,128,2048]{2,1,0:T(8,128)(2,1)S(1)} %copy-done, bf16[1,128,1024]{2,1,0:T(8,128)(2,1)S(1)} %copy-done.2, s32[16,256]{1,0:T(8,128)S(1)} %limits.1.limit_ref, ...), custom_call_target="tpu_custom_call" | custom-call | flops 1 | bytes 1 | tf_op jit(solution)/shard_map/heads_own/pallas_call | solution.py:48
  20.1 0.8 %collective-permute-start.4 = (bf16[128,512]{1,0:T(8,128)(2,1)S(1)}, bf16[128,512]{1,0:T(8,128)(2,1)S(1)}, u32[]{:S(2)}, u32[]{:S(2)}) collective-permute-start(bf16[128,512]{1,0:T(8,128)(2,1)S(1)} %hand_near.1), channel_id=1, source_target_pairs={{0,4},{4,0},{8,12},{12,8},{16,20},{20,16},{24,28},{28,24},{1,5},{5... | collective-permute-start | bytes 393224 | tf_op jit(solution)/shard_map/ppermute | solution.py:473
  21.0 2.2 %heads_side.1 = (bf16[128,768]{1,0:T(8,128)(2,1)S(1)}, f32[2,128,768]{2,1,0:T(8,128)S(1)}, bf16[2,128,768]{2,1,0:T(8,128)(2,1)S(1)}, bf16[2,128,768]{2,1,0:T(8,128)(2,1)S(1)}) custom-call(bf16[1,128,2048]{2,1,0:T(8,128)(2,1)S(1)} %copy-done, bf16[1,128,1024]{2,1,0:T(8,128)(2,1)S(1)} %copy-done.2, s32[16,256]{1,0:T(8,128)S(1)} %limits.1.limit_ref, ...), custom_call_target="tpu_custom_call" | custom-call | flops 1 | bytes 1 | tf_op jit(solution)/shard_map/heads_side/pallas_call | solution.py:48
  23.2 3.1 %collective-permute-start.10 = (bf16[2,128,768]{2,1,0:T(8,128)(2,1)S(1)}, bf16[2,128,768]{2,1,0:T(8,128)(2,1)S(1)}, u32[]{:S(2)}, u32[]{:S(2)}) collective-permute-start(bf16[2,128,768]{2,1,0:T(8,128)(2,1)S(1)} %get-tuple-element.45), channel_id=1, source_target_pairs={{4,8},{8,4},{12,16},{16,12},{20,24},{24,20},{5,9},{9,5},{13,17},{1... | collective-permute-start | bytes 1179656 | tf_op jit(solution)/shard_map/ppermute | solution.py:458
  26.5 0.5 %collective-permute-start.11 = (bf16[64,2048]{1,0:T(8,128)(2,1)S(1)}, bf16[64,2048]{1,0:T(8,128)(2,1)S(1)}, u32[]{:S(2)}, u32[]{:S(2)}) collective-permute-start(bf16[64,2048]{1,0:T(8,128)(2,1)S(1)} %get-tuple-element.50), channel_id=1, source_target_pairs={{0,4},{4,0},{8,12},{12,8},{16,20},{20,16},{24,28},{28,24},{1,5},{5... | collective-permute-start | bytes 786440 | tf_op jit(solution)/shard_map/ppermute | solution.py:493
  27.0 0.1 collective-permute-start.12
  27.1 0.6 %turn.1.mine_ref = bf16[128,384]{1,0:T(8,128)(2,1)S(1)} custom-call(bf16[1,128,2048]{2,1,0:T(8,128)(2,1)S(1)} %copy-done, bf16[128,2816]{1,0:T(8,128)(2,1)S(1)} %collective-permute-done.6.refs_3_.near_both, bf16[128,2816]{1,0:T(8,128)(2,1)S(1)} %collective-permute-done.5.refs_4_.far_both, bf16[128,2048]{1,0:T(8,128)(2,1)S(1)} %collective-permute-done.3.refs_0_.x_ref), custom_call_target="tpu_custom_call" | custom-call | flops 1 | bytes 1 | tf_op jit(solution)/shard_map/turn/pallas_call | solution.py:48
  27.7 0.7 %probs_last.1.prob_ref = f32[3,384,256]{2,1,0:T(8,128)S(1)} custom-call(bf16[1,128,1024]{2,1,0:T(8,128)(2,1)S(1)} %copy-done.2, s32[16,256]{1,0:T(8,128)S(1)} %limits.1.limit_ref, bf16[128,2048]{1,0:T(8,128)(2,1)S(1)} %copy-done.1, bf16[128,2048]{1,0:T(8,128)(2,1)S(1)} %collective-permute-done.1.refs_2_.refs_1_, ...), custom_call_target="tpu_custom_call" | custom-call | flops 1 | bytes 1 | tf_op jit(solution)/shard_map/probs_last/pallas_call | solution.py:48
  28.4 0.1 collective-permute-done.11.refs_6_
  28.5 0.4 %collective-permute-done.12.refs_7_ = bf16[64,2048]{1,0:T(8,128)(2,1)S(1)} collective-permute-done((bf16[64,2048]{1,0:T(8,128)(2,1)S(1)}, bf16[64,2048]{1,0:T(8,128)(2,1)S(1)}, u32[]{:S(2)}, u32[]{:S(2)}) %collective-permute-start.12) | collective-permute-done | bytes 262176 | tf_op jit(solution)/shard_map/ppermute | solution.py:493
  28.9 1.5 %heads_last.1 = (bf16[128,256]{1,0:T(8,128)(2,1)S(1)}, bf16[128,256]{1,0:T(8,128)(2,1)S(1)}, bf16[128,256]{1,0:T(8,128)(2,1)S(1)}) custom-call(bf16[1,128,2048]{2,1,0:T(8,128)(2,1)S(1)} %copy-done, bf16[1,128,1024]{2,1,0:T(8,128)(2,1)S(1)} %copy-done.2, f32[3,384,256]{2,1,0:T(8,128)S(1)} %probs_last.1.prob_ref, bf16[128,384]{1,0:T(8,128)(2,1)S(1)} %turn.1.mine_ref, ...), custom_call_target="tpu_custom_call" | custom-call | flops 1 | bytes 1 | tf_op jit(solution)/shard_map/heads_last/pallas_call | solution.py:48
  30.4 1.9 %collective-permute-done.10.refs_3_ = bf16[2,128,768]{2,1,0:T(8,128)(2,1)S(1)} collective-permute-done((bf16[2,128,768]{2,1,0:T(8,128)(2,1)S(1)}, bf16[2,128,768]{2,1,0:T(8,128)(2,1)S(1)}, u32[]{:S(2)}, u32[]{:S(2)}) %collective-permute-start.10) | collective-permute-done | bytes 393248 | tf_op jit(solution)/shard_map/ppermute | solution.py:458
  32.3 1.0 %finish.1 = (bf16[1,128,1024]{2,1,0:T(8,128)(2,1)}, bf16[1,128,1024]{2,1,0:T(8,128)(2,1)}, bf16[1,128,1024]{2,1,0:T(8,128)(2,1)}) custom-call(bf16[128,768]{1,0:T(8,128)(2,1)S(1)} %get-tuple-element.42.refs_0_, f32[2,128,768]{2,1,0:T(8,128)S(1)} %get-tuple-element.43.refs_1_, bf16[2,128,768]{2,1,0:T(8,128)(2,1)S(1)} %collective-permute-done.9.refs_2_, ...), custom_call_target="tpu_custom_call" | custom-call | flops 1 | bytes 1 | tf_op jit(solution)/shard_map/finish/pallas_call | solution.py:48
  (26 shorter events, 0.3 us)
Async XLA Ops:
  0.6 8.1 %copy-start = (bf16[1,128,2048]{2,1,0:T(8,128)(2,1)S(1)}, bf16[1,128,2048]{2,1,0:T(8,128)(2,1)}, u32[]{:S(2)}) copy-start(bf16[1,128,2048]{2,1,0:T(8,128)(2,1)} %dy_ref.7) | copy-start | bytes 1572868
  0.6 8.1 %copy-start.2 = (bf16[1,128,1024]{2,1,0:T(8,128)(2,1)S(1)}, bf16[1,128,1024]{2,1,0:T(8,128)(2,1)}, u32[]{:S(2)}) copy-start(bf16[1,128,1024]{2,1,0:T(8,128)(2,1)} %q_ref.7) | copy-start | bytes 786436
  0.7 15.7 %collective-permute-start = (bf16[256,2048]{1,0:T(8,128)(2,1)}, bf16[256,2048]{1,0:T(8,128)(2,1)S(1)}, u32[]{:S(2)}, u32[]{:S(2)}) collective-permute-start(bf16[256,2048]{1,0:T(8,128)(2,1)} %refs_3_.1), channel_id=1, source_target_pairs={{0,1},{1,0},{2,3},{3,2},{4,6},{5,7},{6,4},{7,5},{8,9},{9,8},{10,11... | collective-permute-start | bytes 3145736 | tf_op jit(solution)/shard_map/ppermute | solution.py:454
  4.6 7.9 %copy-start.4 = (s32[8,4]{0,1:T(4,128)S(1)}, s32[8,4]{0,1:T(4,128)}, u32[]{:S(2)}) copy-start(s32[8,4]{0,1:T(4,128)} %param.12) | copy-start | bytes 388
  4.6 7.9 %copy-start.5 = (s32[1,8]{1,0:T(1,128)S(1)}, s32[1,8]{1,0:T(1,128)}, u32[]{:S(2)}) copy-start(s32[1,8]{1,0:T(1,128)} %val_ref.1) | copy-start | bytes 100
  4.7 4.1 %collective-permute-start.1 = (bf16[128,2048]{1,0:T(8,128)(2,1)}, bf16[128,2048]{1,0:T(8,128)(2,1)S(1)}, u32[]{:S(2)}, u32[]{:S(2)}) collective-permute-start(bf16[128,2048]{1,0:T(8,128)(2,1)} %join.1.refs_0_), channel_id=1, source_target_pairs={{0,4},{4,0},{8,12},{12,8},{16,20},{20,16},{24,28},{28,24},{1,5},{5... | collective-permute-start | bytes 1572872 | tf_op jit(solution)/shard_map/ppermute | solution.py:464
  5.7 10.7 %collective-permute-start.2 = (bf16[128,2048]{1,0:T(8,128)(2,1)}, bf16[128,2048]{1,0:T(8,128)(2,1)S(1)}, u32[]{:S(2)}, u32[]{:S(2)}) collective-permute-start(bf16[128,2048]{1,0:T(8,128)(2,1)} %join.1.refs_0_), channel_id=1, source_target_pairs={{4,8},{8,4},{12,16},{16,12},{20,24},{24,20},{5,9},{9,5},{13,17},{1... | collective-permute-start | bytes 1572872 | tf_op jit(solution)/shard_map/ppermute | solution.py:464
  8.9 9.8 %copy-start.1 = (bf16[128,2048]{1,0:T(8,128)(2,1)S(1)}, bf16[128,2048]{1,0:T(8,128)(2,1)}, u32[]{:S(2)}) copy-start(bf16[128,2048]{1,0:T(8,128)(2,1)} %join.1.refs_0_) | copy-start | bytes 1572868
  8.9 9.8 %copy-start.3 = (bf16[256,2048]{1,0:T(8,128)(2,1)S(1)}, bf16[256,2048]{1,0:T(8,128)(2,1)}, u32[]{:S(2)}) copy-start(bf16[256,2048]{1,0:T(8,128)(2,1)} %refs_3_.1) | copy-start | bytes 3145732
  8.9 11.3 %collective-permute-start.6 = (bf16[128,2816]{1,0:T(8,128)(2,1)S(1)}, bf16[128,2816]{1,0:T(8,128)(2,1)S(1)}, u32[]{:S(2)}, u32[]{:S(2)}) collective-permute-start(bf16[128,2816]{1,0:T(8,128)(2,1)S(1)} %hand_far.1), channel_id=1, source_target_pairs={{0,4},{4,0},{8,12},{12,8},{16,20},{20,16},{24,28},{28,24},{1,5},{5... | collective-permute-start | bytes 2162696 | tf_op jit(solution)/shard_map/ppermute | solution.py:468
  9.0 17.5 %collective-permute-start.5 = (bf16[128,2816]{1,0:T(8,128)(2,1)S(1)}, bf16[128,2816]{1,0:T(8,128)(2,1)S(1)}, u32[]{:S(2)}, u32[]{:S(2)}) collective-permute-start(bf16[128,2816]{1,0:T(8,128)(2,1)S(1)} %hand_far.1), channel_id=1, source_target_pairs={{4,8},{8,4},{12,16},{16,12},{20,24},{24,20},{5,9},{9,5},{13,17},{1... | collective-permute-start | bytes 2162696 | tf_op jit(solution)/shard_map/ppermute | solution.py:468
  16.4 4.5 %collective-permute-start.7 = (bf16[128,2048]{1,0:T(8,128)(2,1)S(1)}, bf16[128,2048]{1,0:T(8,128)(2,1)S(1)}, u32[]{:S(2)}, u32[]{:S(2)}) collective-permute-start(bf16[128,2048]{1,0:T(8,128)(2,1)S(1)} %get-tuple-element.30), channel_id=1, source_target_pairs={{0,4},{4,0},{8,12},{12,8},{16,20},{20,16},{24,28},{28,24},{1,5},{5... | collective-permute-start | bytes 1572872 | tf_op jit(solution)/shard_map/ppermute | solution.py:476
  16.8 4.1 %collective-permute-start.8 = (bf16[128,2048]{1,0:T(8,128)(2,1)S(1)}, bf16[128,2048]{1,0:T(8,128)(2,1)S(1)}, u32[]{:S(2)}, u32[]{:S(2)}) collective-permute-start(bf16[128,2048]{1,0:T(8,128)(2,1)S(1)} %get-tuple-element.34), channel_id=1, source_target_pairs={{0,4},{4,0},{8,12},{12,8},{16,20},{20,16},{24,28},{28,24},{1,5},{5... | collective-permute-start | bytes 1572872 | tf_op jit(solution)/shard_map/ppermute | solution.py:476
  17.0 9.4 %collective-permute-start.3 = (bf16[128,2048]{1,0:T(8,128)(2,1)S(1)}, bf16[128,2048]{1,0:T(8,128)(2,1)S(1)}, u32[]{:S(2)}, u32[]{:S(2)}) collective-permute-start(bf16[128,2048]{1,0:T(8,128)(2,1)S(1)} %get-tuple-element.30), channel_id=1, source_target_pairs={{0,2},{1,3},{2,0},{3,1},{4,5},{5,4},{6,7},{7,6},{8,10},{9,11},{10,... | collective-permute-start | bytes 1572872 | tf_op jit(solution)/shard_map/ppermute | solution.py:454
  20.1 6.3 %collective-permute-start.4 = (bf16[128,512]{1,0:T(8,128)(2,1)S(1)}, bf16[128,512]{1,0:T(8,128)(2,1)S(1)}, u32[]{:S(2)}, u32[]{:S(2)}) collective-permute-start(bf16[128,512]{1,0:T(8,128)(2,1)S(1)} %hand_near.1), channel_id=1, source_target_pairs={{0,4},{4,0},{8,12},{12,8},{16,20},{20,16},{24,28},{28,24},{1,5},{5... | collective-permute-start | bytes 393224 | tf_op jit(solution)/shard_map/ppermute | solution.py:473
  23.2 9.1 %collective-permute-start.10 = (bf16[2,128,768]{2,1,0:T(8,128)(2,1)S(1)}, bf16[2,128,768]{2,1,0:T(8,128)(2,1)S(1)}, u32[]{:S(2)}, u32[]{:S(2)}) collective-permute-start(bf16[2,128,768]{2,1,0:T(8,128)(2,1)S(1)} %get-tuple-element.45), channel_id=1, source_target_pairs={{4,8},{8,4},{12,16},{16,12},{20,24},{24,20},{5,9},{9,5},{13,17},{1... | collective-permute-start | bytes 1179656 | tf_op jit(solution)/shard_map/ppermute | solution.py:458
  26.3 6.0 %collective-permute-start.9 = (bf16[2,128,768]{2,1,0:T(8,128)(2,1)S(1)}, bf16[2,128,768]{2,1,0:T(8,128)(2,1)S(1)}, u32[]{:S(2)}, u32[]{:S(2)}) collective-permute-start(bf16[2,128,768]{2,1,0:T(8,128)(2,1)S(1)} %get-tuple-element.44), channel_id=1, source_target_pairs={{0,4},{4,0},{8,12},{12,8},{16,20},{20,16},{24,28},{28,24},{1,5},{5... | collective-permute-start | bytes 1179656 | tf_op jit(solution)/shard_map/ppermute | solution.py:459
  26.5 2.0 %collective-permute-start.11 = (bf16[64,2048]{1,0:T(8,128)(2,1)S(1)}, bf16[64,2048]{1,0:T(8,128)(2,1)S(1)}, u32[]{:S(2)}, u32[]{:S(2)}) collective-permute-start(bf16[64,2048]{1,0:T(8,128)(2,1)S(1)} %get-tuple-element.50), channel_id=1, source_target_pairs={{0,4},{4,0},{8,12},{12,8},{16,20},{20,16},{24,28},{28,24},{1,5},{5... | collective-permute-start | bytes 786440 | tf_op jit(solution)/shard_map/ppermute | solution.py:493
  27.0 1.8 %collective-permute-start.12 = (bf16[64,2048]{1,0:T(8,128)(2,1)S(1)}, bf16[64,2048]{1,0:T(8,128)(2,1)S(1)}, u32[]{:S(2)}, u32[]{:S(2)}) collective-permute-start(bf16[64,2048]{1,0:T(8,128)(2,1)S(1)} %get-tuple-element.51), channel_id=1, source_target_pairs={{0,4},{4,0},{8,12},{12,8},{16,20},{20,16},{24,28},{28,24},{1,5},{5... | collective-permute-start | bytes 786440 | tf_op jit(solution)/shard_map/ppermute | solution.py:493

commit v12 on v11

--- a/solution.py
+++ b/solution.py
@@ -153,18 +153,22 @@
     return call(kernel, name, shape, [VMEM] * (len(whole) + len(cut)), VMEM, [], *whole, *cut)
 
 
-def onward_kernel(w_ref, *out_refs):
-    core, _ = place()
-    half = w_ref.shape[0] // 2
-    start = pl.multiple_of(core * half, half)
-    for ref, first in zip(out_refs, (start, half - start)):
-        ref[...] = w_ref[pl.ds(pl.multiple_of(first, half), half), :]
-
-
-def onward(got):
+def onward_kernel(last, w_ref, kv_ref, mine_ref, *both_refs):
+    core, group = place()
+    half, depth = mine_ref.shape
+    chunk = last(core, group)
+    mine_ref[...] = w_ref[pl.ds(pl.multiple_of(core * half, half), half), :]
+    for side, (ref, which) in enumerate(zip(both_refs, (core, 1 - core))):
+        ref[:, :depth] = w_ref[pl.ds(pl.multiple_of(which * half, half), half), :]
+        ref[:, depth:] = kv_ref[:, columns(chunk + side * (kv_ref.shape[1] // (2 * PAIR)))]
+
+
+def onward(last, got, kv):
     rows, depth = got.shape
-    shapes = [jax.ShapeDtypeStruct((rows // part, depth), BF16) for part in (2, 2)]
-    return call(onward_kernel, "onward", tuple(shapes), [VMEM], (VMEM,) * 2, [], got)
+    half, wide = (rows // 2, depth), (rows // 2, depth + PAIR)
+    shapes = tuple(jax.ShapeDtypeStruct(shape, BF16) for shape in (half, wide, wide))
+    kernel = functools.partial(onward_kernel, last)
+    return call(kernel, "onward", shapes, [VMEM] * 2, (VMEM,) * 3, [], got, kv)
 
 
 def split_kernel(x_ref, *out_refs):
@@ -232,43 +236,43 @@
     return jnp.concatenate([ref[:, cols] for ref in refs], axis=0)
 
 
-def heads_kernel(steps, carried, dy_ref, q_ref, limit_ref, *refs):
+def heads_kernel(steps, messages, dy_ref, q_ref, limit_ref, *refs):
     core, group = place()
-    kv_refs, w_refs = refs[:3], refs[3 : -4 - carried]
-    earlier, outs = refs[-4 - carried : -4], refs[-4:]
-    dq_ref, own_ref, to_core_ref, to_far_ref = outs
-    for old, out in zip(earlier, outs):
-        out[..., : old.shape[-1]] = old[...]
-    tok = q_ref.shape[1]
-    values_at = kv_refs[0].shape[1] // (2 * PAIR)
+    k_refs, w_refs = refs[:3], refs[3 : -4 - messages]
+    earlier, (dq_ref, own_ref, *message_refs) = refs[-4 - messages : -4], refs[-4:]
+    for old, out in zip(earlier, message_refs):
+        out[...] = old[...]
+    tok, depth = q_ref.shape[1], dy_ref.shape[2]
+    values_at = k_refs[0].shape[1] // (2 * PAIR)
     open_keys = key_mask(limit_ref, tok, 0, 3)
-    for chunk, slot, pieces, lead in steps(core, group):
-        cols, dest = columns(chunk), columns(slot)
-        w = jnp.concatenate([w_refs[i][row : row + rows, :] for i, row, rows in pieces], axis=0)
+    for chunk, slot, message_slot, pieces, lead in steps(core, group):
+        cols, dest, message_dest = columns(chunk), columns(slot), columns(message_slot)
+        w = jnp.concatenate([w_refs[i][row : row + rows, :depth] for i, row, rows in pieces], axis=0)
         d = diagonal_turned(*in_order(dot(w, dy_ref[0], NT).astype(BF16), lead))
         qd = diagonal(q_ref[0, :, cols])
-        k, v = stacked(kv_refs, cols), stacked(kv_refs, columns(chunk + values_at))
+        k, v = stacked(k_refs, cols), stacked(k_refs, columns(chunk + values_at))
         prob = prob_of(k, qd, open_keys)
         prob_b = prob.astype(BF16)
         d_score = score_grad(prob, prob_b, v, d)
         dq_ref[:, dest] = query_grad(d_score, k, tok)
         for side, grad in enumerate((dot(d_score, qd, NN) * SCALE, dot(prob_b, d, NT))):
             own_ref[side, :, dest] = grad[:tok]
-            to_core_ref[side, :, dest] = grad[tok : 2 * tok].astype(BF16)
-            to_far_ref[side, :, dest] = grad[2 * tok :].astype(BF16)
-
-
-def heads(name, steps, weights, earlier, d_out, q, limits, blocks):
+            for i, ref in enumerate(message_refs, 1):
+                ref[side, :, message_dest] = grad[i * tok : (i + 1) * tok].astype(BF16)
+
+
+def heads(name, steps, places, weights, earlier, d_out, q, limits, blocks):
     tok = q.shape[1]
-    width = len(steps(0, 0)) * PAIR + (earlier[0].shape[1] if earlier else 0)
+    width = len(steps(0, 0)) * PAIR
+    message = jax.ShapeDtypeStruct((2, tok, places * PAIR), BF16)
     return call(
         functools.partial(heads_kernel, steps, len(earlier)),
         name,
         (
             jax.ShapeDtypeStruct((tok, width), BF16),
             jax.ShapeDtypeStruct((2, tok, width), F32),
-            jax.ShapeDtypeStruct((2, tok, width), BF16),
-            jax.ShapeDtypeStruct((2, tok, width), BF16),
+            message,
+            message,
         ),
         [VMEM] * (6 + len(weights) + len(earlier)),
         (VMEM,) * 4,
@@ -287,7 +291,7 @@
     value_cols = columns(last(*place()) + kv_refs[0].shape[1] // (2 * PAIR))
     depth = far_both.shape[1] - 3 * PAIR
     own, near, far = ([ref[:, at] for at in (cols, value_cols)] for ref in kv_refs)
-    past_near = [near_next[:, :PAIR], near_next[:, PAIR:]]
+    past_near = [ref[:, depth:] for ref in near_next]
     past_far = [far_both[:, depth + PAIR : depth + 2 * PAIR], far_both[:, depth + 2 * PAIR :]]
     at_queries = slice(depth, depth + PAIR)
     return (
@@ -302,7 +306,8 @@
 
 
 def probs_kernel(last, q_ref, limit_ref, *refs):
-    *kv_refs, near_both, far_both, near_next, prob_ref = refs
+    *kv_refs, near_both, far_both = refs[:5]
+    near_next, prob_ref = refs[5:7], refs[7]
     tok = q_ref.shape[1]
     blocks = last_parts(last, q_ref, near_both, far_both, near_next, kv_refs)
     for block, (q, parts) in enumerate(blocks):
@@ -321,7 +326,8 @@
 def last_kernel(last, dy_ref, q_ref, prob_ref, mine_ref, *refs):
     core, _ = place()
     kv_refs = refs[:3]
-    near_both, far_both, near_next, *w_refs, dq_ref, dk_ref, dv_ref = refs[3:]
+    near_both, far_both, *near_next = refs[3:7]
+    *w_refs, dq_ref, dk_ref, dv_ref = refs[7:]
     tok, depth = q_ref.shape[1], dy_ref.shape[2]
     w = jnp.concatenate([ref[...] for ref in w_refs], axis=0)
     dy = jnp.concatenate([dy_ref[0], near_both[:, :depth], far_both[:, :depth]], axis=0)
@@ -347,13 +353,13 @@
     dv_ref[...] = dot(probs, jnp.concatenate(cotangents, axis=1), NT).astype(BF16)
 
 
-def last_heads(last, d_out, q, limits, blocks, halo, mine, other):
+def last_probs(last, q, limits, blocks, halo):
     tok = q.shape[1]
-    prob = call(
+    return call(
         functools.partial(probs_kernel, last),
         "probs_last",
         jax.ShapeDtypeStruct((3, 3 * tok, PAIR), F32),
-        [VMEM] * 8,
+        [VMEM] * 9,
         VMEM,
         [],
         q,
@@ -361,6 +367,10 @@
         *blocks,
         *halo,
     )
+
+
+def last_heads(last, prob, d_out, q, blocks, halo, mine, other):
+    tok = q.shape[1]
     turned = call(
         turn_kernel,
         "turn",
@@ -376,7 +386,7 @@
         functools.partial(last_kernel, last),
         "heads_last",
         (jax.ShapeDtypeStruct((tok, PAIR), BF16),) * 3,
-        [VMEM] * (10 + len(other)),
+        [VMEM] * (11 + len(other)),
         (VMEM,) * 3,
         [],
         d_out,
@@ -389,54 +399,84 @@
     )
 
 
-def finish_kernel(chunks, widths, *refs):
-    core, group = place()
-    outs, stage, sems = refs[-5:-2], refs[-2], refs[-1]
-    tok = stage.shape[1]
-    copies = []
-    slot = at = 0
-    for width, summed in widths:
-        part = refs[at : at + (3 if summed else 4)]
-        at += len(part)
+class Columns:
+    def __init__(self, stage, sems):
+        self.stage, self.sems, self.copies = stage, sems, []
+
+    def put(self, out_ref, chunk, value):
+        at = len(self.copies)
+        self.stage[at] = value
+        target = out_ref.at[0, :, columns(chunk)]
+        copy = pltpu.make_async_copy(self.stage.at[at], target, self.sems.at[at])
+        copy.start()
+        self.copies.append(copy)
+
+    def wait(self):
+        for copy in self.copies:
+            copy.wait()
+
+
+def scratch_of(count, tok):
+    return [pltpu.VMEM((count, tok, PAIR), BF16), pltpu.SemaphoreType.DMA((count,))]
+
+
+def settle_kernel(order, widths, *refs):
+    outs, to = refs[-5:-2], Columns(*refs[-2:])
+    pairs = order(*place())
+    for part, width in enumerate(widths):
         for step in range(width // PAIR):
             cols = slice(step * PAIR, (step + 1) * PAIR)
-            dest = columns(chunks(core, group)[slot])
-            stage[3 * slot] = part[0][:, cols]
-            for side in range(2):
-                if summed:
-                    total = part[1 + side][:, cols]
-                else:
-                    _, own, near, far = part
-                    total = own[side, :, cols] + near[side, :, cols].astype(F32)
-                    total = (total + far[side, :, cols].astype(F32)).astype(BF16)
-                stage[3 * slot + 1 + side] = total
-            for index in range(3):
-                copy = pltpu.make_async_copy(
-                    stage.at[3 * slot + index], outs[index].at[0, :, dest], sems.at[3 * slot + index]
-                )
-                copy.start()
-                copies.append(copy)
-            slot += 1
-    for copy in copies:
-        copy.wait()
-
-
-def finish(chunks, parts, shape):
-    count = len(chunks(0, 0))
-    ins = [x for part in parts for x in part]
-    widths = tuple((part[0].shape[1], len(part) == 3) for part in parts)
+            to.put(outs[0], pairs[part][step][0], refs[part][:, cols])
+    for out_ref, ref in zip(outs[1:], refs[len(widths) : -5]):
+        to.put(out_ref, pairs[-1][0][0], ref[...])
+    to.wait()
+
+
+def settle(order, d_queries, last, shape):
+    widths = tuple(x.shape[1] for x in d_queries)
+    count = sum(widths) // PAIR + len(last)
+    ins = [*d_queries, *last]
     return call(
-        functools.partial(finish_kernel, chunks, widths),
-        "finish",
+        functools.partial(settle_kernel, order, widths),
+        "settle",
         (jax.ShapeDtypeStruct(shape, BF16),) * 3,
         [VMEM] * len(ins),
         (ANY,) * 3,
-        [
-            pltpu.VMEM((3 * count, shape[1], PAIR), BF16),
-            pltpu.SemaphoreType.DMA((3 * count,)),
-        ],
+        scratch_of(count, shape[1]),
         *ins,
     )
+
+
+def finish_kernel(order, widths, far, near, *refs):
+    outs, to = refs[-4:-2], Columns(*refs[-2:])
+    pairs = order(*place())
+    for part, width in enumerate(widths):
+        own = refs[part]
+        for step in range(width // PAIR):
+            cols = slice(step * PAIR, (step + 1) * PAIR)
+            chunk, message_slot = pairs[part][step]
+            at = columns(message_slot)
+            for side, out_ref in enumerate(outs):
+                total = own[side, :, cols] + near[side, :, at].astype(F32)
+                to.put(out_ref, chunk, (total + far[side, :, at].astype(F32)).astype(BF16))
+    to.wait()
+
+
+def finish(order, far, near, parts, old):
+    shape = old[0].shape
+    widths = tuple(x.shape[2] for x in parts)
+    ins = [far, near, *parts]
+    return pl.pallas_call(
+        functools.partial(finish_kernel, order, widths),
+        out_shape=(jax.ShapeDtypeStruct(shape, BF16),) * 2,
+        in_specs=[VMEM] * len(ins) + [ANY] * 2,
+        out_specs=(ANY,) * 2,
+        scratch_shapes=scratch_of(2 * sum(widths) // PAIR, shape[1]),
+        input_output_aliases={len(ins): 0, len(ins) + 1: 1},
+        cost_estimate=BRIEF,
+        compiler_params=PARAMS,
+        name="finish",
+    )(*ins, *old)
 
 
 def body(queries, keys, values, d_out, w_out, pattern, valid):
@@ -452,11 +492,6 @@
             for g in range(n_fsdp)
         ]
         return lax.ppermute(x, ("seq", "fsdp"), pairs)
-
-    def exchange(part):
-        dq, own, to_core, to_far = part
-        back = far(to_far)
-        return dq, own, near(to_core), back
 
     last = lambda core, group: group ^ 3 if n_fsdp == 4 else 0
     kv = join(keys, values)
@@ -468,38 +503,51 @@
         far_both, near_both = far(message), near(message)
         early = got, near_kv, far_kv, limits
         got, near_kv, far_kv, limits = lax.optimization_barrier(early)
-        mine, other = onward(got)
+        ours = d_out, queries, limits, (kv, near_kv, far_kv)
+        mine, *both = onward(last, got, far_kv)
         got_d = cross(mine, (2, 1))
-        near_next = near(hand_on("hand_near", last, [], [far_kv]))
-        ours = d_out, queries, limits, (kv, near_kv, far_kv)
-        own = heads("heads_own", lambda core, group: [(group, 0, ((0, 0, PAIR),), 0)], [w_out], (), *ours)
-        near_got = near(mine), near(other)
-        near_both, near_got = lax.optimization_barrier((near_both, near_got))
-        side = heads(
-            "heads_side",
+        near_got = [near(x) for x in both]
+        first = heads(
+            "heads_first",
             lambda core, group: [
-                (group ^ (1 + core), 1 + core, ((0, 0, HD), (0, HD, HD)), 0),
-                (group ^ (2 - core), 2 - core, ((1, 0, HD), (2, 0, HD)), 1 - core),
+                (group, 0, 0, ((0, 0, PAIR),), 0),
+                (group ^ (1 + core), 1, 1 + core, ((1, 0, PAIR),), 0),
             ],
-            [got, *near_got],
-            own,
+            3,
+            [w_out, got],
+            (),
             *ours,
         )
-        got_d, near_next, far_both, dq = lax.optimization_barrier(
-            (got_d, near_next, far_both, side[0])
+        near_both, near_got, dq = lax.optimization_barrier((near_both, near_got, first[0]))
+        second = heads(
+            "heads_second",
+            lambda core, group: [(group ^ (2 - core), 0, 2 - core, ((0, 0, HD), (1, 0, HD)), 1 - core)],
+            3,
+            near_got,
+            first[2:],
+            *ours,
         )
-        sums = exchange((dq, *side[1:]))
-        halo = near_both, far_both, near_next
-        third = last_heads(last, *ours, halo, [got_d], [near(x) for x in split(got_d)])
-        order = lambda core, group: [group, group ^ 1, group ^ 2, group ^ 3]
-        return finish(order, [sums, third], queries.shape)
+        halo = near_both, far_both, *near_got
+        prob = last_probs(last, *ours[1:], halo)
+        got_d, halo, prob, second_dq = lax.optimization_barrier((got_d, halo, prob, second[0]))
+        sums = far(second[3]), near(second[2])
+        third = last_heads(last, prob, *ours[:2], ours[3], halo, [got_d], [near(x) for x in split(got_d)])
+        order = lambda core, group: [
+            [(group, 0), (group ^ (1 + core), 1 + core)],
+            [(group ^ (2 - core), 2 - core)],
+            [(group ^ 3, 0)],
+        ]
+        d_queries, *old = settle(order, (dq, second_dq, third[0]), third[1:], queries.shape)
+        return d_queries, *finish(order, *sums, (first[1], second[1]), old)
     full = lax.all_gather(w_out, "fsdp", axis=0, tiled=True)
     ours = d_out, queries, limits, (kv, near_kv, far_kv)
     steps = lambda core, group: [
-        (i, i, ((0, i * PAIR, PAIR),), 0) for i in range(n_chunks)
+        (i, i, i, ((0, i * PAIR, PAIR),), 0) for i in range(n_chunks)
     ]
-    part = exchange(heads("heads_all", steps, [full], (), *ours))
-    return finish(lambda core, group: list(range(n_chunks)), [part], queries.shape)
+    dq, own, to_core, to_far = heads("heads_all", steps, n_chunks, [full], (), *ours)
+    order = lambda core, group: [[(i, i) for i in range(n_chunks)]]
+    d_queries, *old = settle(order, (dq,), (), queries.shape)
+    return d_queries, *finish(order, far(to_far), near(to_core), (own,), old)
 
 
 def solution(mesh):

time: 33.6 us -> 32.9 us (0.979)
  waiting for transfers between devices: 5.52 us -> 4.19 us
  Pallas kernels: 10.2 us -> 10.8 us
    ppermute x5 -> x4, waiting for transfers between devices: 1.91 us -> 0.18 us  [the longest x2 0.18 us: body(): sums = (far(second[3]), near(second[2]))]
    pallas_call x0 -> x1, Pallas kernels: none -> 0.82 us  [finish(): pl.pallas_call(functools.partial(finish_kernel, order, widths), out_shape...]
    ppermute x2, waiting for transfers between devices: 0.46 us -> 0.86 us  [body(): near(x)]
    pallas_call x11 -> x10, Pallas kernels: 8.33 us -> 8.15 us  [call(): pl.pallas_call(kernel, out_shape=out_shape, in_specs=in_specs, out_specs=...]
    ppermute x5 -> x4, starting transfers between devices: 4.57 us -> 4.47 us  [the longest x2 3.9 us: body(): sums = (far(second[3]), near(second[2]))]
  transfers between devices with their start and end apart: 13 -> 12, of which waited for: 4 -> 4; matrix products, arithmetic and copies ran while one was open for 0% -> 0% of each run, Pallas kernels for 27% -> 31%
where the time goes in v12:
time: 32.9 us; the launch traced here: 32.5 us
  starting transfers between devices  16.6 us (50%)
  Pallas kernels  10.8 us (33%)
  waiting for transfers between devices  4.19 us (13%)
  between operations  0.88 us (3%)
    pallas_call x10, Pallas kernels, call(): pl.pallas_call(kernel, out_shape=out_shape, in_specs=in_specs, out_specs=...  8.15 us
    ppermute x2, starting transfers between devices, body(): far_kv, near_kv = (far(kv), near(kv))  4.09 us
    ppermute x2, starting transfers between devices, body(): sums = (far(second[3]), near(second[2]))  3.9 us
    ppermute x2, starting transfers between devices, cross(): return lax.ppermute(x, ('seq', 'fsdp'), pairs)  3.8 us
    ppermute x2, starting transfers between devices, body(): far_both, near_both = (far(message), near(message))  3.65 us
    ppermute x2, waiting for transfers between devices, body(): far_kv, near_kv = (far(kv), near(kv))  3.13 us
    pallas_call x1, Pallas kernels, join(): pl.pallas_call(join_kernel, out_shape=jax.ShapeDtypeStruct(kv, BF16), in_...  1.83 us
    ppermute x2, waiting for transfers between devices, body(): near(x)  0.86 us
  transfers between devices with their start and end apart: 12, of which 4 were waited for; matrix products, arithmetic and copies ran while one was open for 0% of the time, Pallas kernels for 31%

profile of v12, /device:TPU:1, one launch (start us, length us, event | category | flops | bytes accessed | tf_op | source)
XLA Modules:
  0.0 32.5 jit_solution(9745021427057411156)
XLA Ops:
  0.7 2.1 %collective-permute-start.2 = (bf16[256,2048]{1,0:T(8,128)(2,1)}, bf16[256,2048]{1,0:T(8,128)(2,1)S(1)}, u32[]{:S(2)}, u32[]{:S(2)}) collective-permute-start(bf16[256,2048]{1,0:T(8,128)(2,1)} %refs_3_.1), channel_id=1, source_target_pairs={{0,1},{1,0},{2,3},{3,2},{4,6},{5,7},{6,4},{7,5},{8,9},{9,8},{10,11... | collective-permute-start | bytes 3145736 | tf_op jit(solution)/shard_map/ppermute | solution.py:494
  2.8 1.8 %join.1.refs_0_ = bf16[128,2048]{1,0:T(8,128)(2,1)} custom-call(bf16[1,128,1024]{2,1,0:T(8,128)(2,1)} %k_ref.1, bf16[1,128,1024]{2,1,0:T(8,128)(2,1)} %v_ref.1), custom_call_target="tpu_custom_call" | custom-call | flops 1 | bytes 1 | tf_op jit(solution)/shard_map/join/pallas_call | solution.py:117
  4.7 1.0 %collective-permute-start = (bf16[128,2048]{1,0:T(8,128)(2,1)}, bf16[128,2048]{1,0:T(8,128)(2,1)S(1)}, u32[]{:S(2)}, u32[]{:S(2)}) collective-permute-start(bf16[128,2048]{1,0:T(8,128)(2,1)} %join.1.refs_0_), channel_id=1, source_target_pairs={{0,4},{4,0},{8,12},{12,8},{16,20},{20,16},{24,28},{28,24},{1,5},{5... | collective-permute-start | bytes 1572872 | tf_op jit(solution)/shard_map/ppermute | solution.py:499
  5.6 3.1 %collective-permute-start.3 = (bf16[128,2048]{1,0:T(8,128)(2,1)}, bf16[128,2048]{1,0:T(8,128)(2,1)S(1)}, u32[]{:S(2)}, u32[]{:S(2)}) collective-permute-start(bf16[128,2048]{1,0:T(8,128)(2,1)} %join.1.refs_0_), channel_id=1, source_target_pairs={{4,8},{8,4},{12,16},{16,12},{20,24},{24,20},{5,9},{9,5},{13,17},{1... | collective-permute-start | bytes 1572872 | tf_op jit(solution)/shard_map/ppermute | solution.py:499
  9.0 3.6 %collective-permute-start.7 = (bf16[128,2816]{1,0:T(8,128)(2,1)S(1)}, bf16[128,2816]{1,0:T(8,128)(2,1)S(1)}, u32[]{:S(2)}, u32[]{:S(2)}) collective-permute-start(bf16[128,2816]{1,0:T(8,128)(2,1)S(1)} %hand_far.1), channel_id=1, source_target_pairs={{4,8},{8,4},{12,16},{16,12},{20,24},{24,20},{5,9},{9,5},{13,17},{1... | collective-permute-start | bytes 2162696 | tf_op jit(solution)/shard_map/ppermute | solution.py:503
  12.6 0.6 %limits.1.limit_ref = s32[16,256]{1,0:T(8,128)S(1)} custom-call(s32[4,8]{1,0:T(4,128)S(1)} %bitcast.1, s32[1,8]{1,0:T(1,128)S(1)} %copy-done.5), custom_call_target="tpu_custom_call" | custom-call | flops 1 | bytes 1 | tf_op jit(solution)/shard_map/limits/pallas_call | solution.py:48
  13.2 3.1 %collective-permute-done.3.kv_ref.refs_2_ = bf16[128,2048]{1,0:T(8,128)(2,1)S(1)} collective-permute-done((bf16[128,2048]{1,0:T(8,128)(2,1)}, bf16[128,2048]{1,0:T(8,128)(2,1)S(1)}, u32[]{:S(2)}, u32[]{:S(2)}) %collective-permute-start.3) | collective-permute-done | bytes 524320 | tf_op jit(solution)/shard_map/ppermute | solution.py:499
  16.3 0.1 onward.1
  16.5 0.4 %collective-permute-start.4 = (bf16[128,2304]{1,0:T(8,128)(2,1)S(1)}, bf16[128,2304]{1,0:T(8,128)(2,1)S(1)}, u32[]{:S(2)}, u32[]{:S(2)}) collective-permute-start(bf16[128,2304]{1,0:T(8,128)(2,1)S(1)} %get-tuple-element.41), channel_id=1, source_target_pairs={{0,4},{4,0},{8,12},{12,8},{16,20},{20,16},{24,28},{28,24},{1,5},{5... | collective-permute-start | bytes 1769480 | tf_op jit(solution)/shard_map/ppermute | solution.py:509
  16.9 0.2 collective-permute-start.5
  17.0 1.7 %collective-permute-start.6 = (bf16[128,2048]{1,0:T(8,128)(2,1)S(1)}, bf16[128,2048]{1,0:T(8,128)(2,1)S(1)}, u32[]{:S(2)}, u32[]{:S(2)}) collective-permute-start(bf16[128,2048]{1,0:T(8,128)(2,1)S(1)} %get-tuple-element.47), channel_id=1, source_target_pairs={{0,2},{1,3},{2,0},{3,1},{4,5},{5,4},{6,7},{7,6},{8,10},{9,11},{10,... | collective-permute-start | bytes 1572872 | tf_op jit(solution)/shard_map/ppermute | solution.py:494
  18.7 2.2 %heads_first.1 = (bf16[128,512]{1,0:T(8,128)(2,1)S(1)}, f32[2,128,512]{2,1,0:T(8,128)S(1)}, bf16[2,128,768]{2,1,0:T(8,128)(2,1)S(1)}, bf16[2,128,768]{2,1,0:T(8,128)(2,1)S(1)}) custom-call(bf16[1,128,2048]{2,1,0:T(8,128)(2,1)S(1)} %copy-done, bf16[1,128,1024]{2,1,0:T(8,128)(2,1)S(1)} %copy-done.2, s32[16,256]{1,0:T(8,128)S(1)} %limits.1.limit_ref, ...), custom_call_target="tpu_custom_call" | custom-call | flops 1 | bytes 1 | tf_op jit(solution)/shard_map/heads_first/pallas_call | solution.py:48
  21.0 1.5 %heads_second.1 = (bf16[128,256]{1,0:T(8,128)(2,1)S(1)}, f32[2,128,256]{2,1,0:T(8,128)S(1)}, bf16[2,128,768]{2,1,0:T(8,128)(2,1)S(1)}, bf16[2,128,768]{2,1,0:T(8,128)(2,1)S(1)}) custom-call(bf16[1,128,2048]{2,1,0:T(8,128)(2,1)S(1)} %copy-done, bf16[1,128,1024]{2,1,0:T(8,128)(2,1)S(1)} %copy-done.2, s32[16,256]{1,0:T(8,128)S(1)} %limits.1.limit_ref, ...), custom_call_target="tpu_custom_call" | custom-call | flops 1 | bytes 1 | tf_op jit(solution)/shard_map/heads_second/pallas_call | solution.py:48
  22.4 3.8 %collective-permute-start.10 = (bf16[2,128,768]{2,1,0:T(8,128)(2,1)S(1)}, bf16[2,128,768]{2,1,0:T(8,128)(2,1)S(1)}, u32[]{:S(2)}, u32[]{:S(2)}) collective-permute-start(bf16[2,128,768]{2,1,0:T(8,128)(2,1)S(1)} %get-tuple-element.67), channel_id=1, source_target_pairs={{4,8},{8,4},{12,16},{16,12},{20,24},{24,20},{5,9},{9,5},{13,17},{1... | collective-permute-start | bytes 1179656 | tf_op jit(solution)/shard_map/ppermute | solution.py:533
  26.4 0.7 %probs_last.1.prob_ref = f32[3,384,256]{2,1,0:T(8,128)S(1)} custom-call(bf16[1,128,1024]{2,1,0:T(8,128)(2,1)S(1)} %copy-done.2, s32[16,256]{1,0:T(8,128)S(1)} %limits.1.limit_ref, bf16[128,2048]{1,0:T(8,128)(2,1)S(1)} %copy-done.1, bf16[128,2048]{1,0:T(8,128)(2,1)S(1)} %collective-permute-done.refs_2_.refs_1_, ...), custom_call_target="tpu_custom_call" | custom-call | flops 1 | bytes 1 | tf_op jit(solution)/shard_map/probs_last/pallas_call | solution.py:48
  27.1 0.6 %collective-permute-start.8 = (bf16[64,2048]{1,0:T(8,128)(2,1)S(1)}, bf16[64,2048]{1,0:T(8,128)(2,1)S(1)}, u32[]{:S(2)}, u32[]{:S(2)}) collective-permute-start(bf16[64,2048]{1,0:T(8,128)(2,1)S(1)} %get-tuple-element.61), channel_id=1, source_target_pairs={{0,4},{4,0},{8,12},{12,8},{16,20},{20,16},{24,28},{28,24},{1,5},{5... | collective-permute-start | bytes 786440 | tf_op jit(solution)/shard_map/ppermute | solution.py:534
  27.7 0.1 collective-permute-start.9
  27.8 0.6 %turn.1.mine_ref = bf16[128,384]{1,0:T(8,128)(2,1)S(1)} custom-call(bf16[1,128,2048]{2,1,0:T(8,128)(2,1)S(1)} %copy-done, bf16[128,2816]{1,0:T(8,128)(2,1)S(1)} %collective-permute-done.1.refs_3_.near_both, bf16[128,2816]{1,0:T(8,128)(2,1)S(1)} %collective-permute-done.7.refs_4_.far_both, bf16[128,2048]{1,0:T(8,128)(2,1)S(1)} %collective-permute-done.6.refs_0_.x_ref), custom_call_target="tpu_custom_call" | custom-call | flops 1 | bytes 1 | tf_op jit(solution)/shard_map/turn/pallas_call | solution.py:48
  28.4 0.5 %collective-permute-done.8.refs_7_ = bf16[64,2048]{1,0:T(8,128)(2,1)S(1)} collective-permute-done((bf16[64,2048]{1,0:T(8,128)(2,1)S(1)}, bf16[64,2048]{1,0:T(8,128)(2,1)S(1)}, u32[]{:S(2)}, u32[]{:S(2)}) %collective-permute-start.8) | collective-permute-done | bytes 262176 | tf_op jit(solution)/shard_map/ppermute | solution.py:534
  28.8 0.4 %collective-permute-done.9.refs_8_ = bf16[64,2048]{1,0:T(8,128)(2,1)S(1)} collective-permute-done((bf16[64,2048]{1,0:T(8,128)(2,1)S(1)}, bf16[64,2048]{1,0:T(8,128)(2,1)S(1)}, u32[]{:S(2)}, u32[]{:S(2)}) %collective-permute-start.9) | collective-permute-done | bytes 262176 | tf_op jit(solution)/shard_map/ppermute | solution.py:534
  29.2 1.5 %heads_last.1 = (bf16[128,256]{1,0:T(8,128)(2,1)S(1)}, bf16[128,256]{1,0:T(8,128)(2,1)S(1)}, bf16[128,256]{1,0:T(8,128)(2,1)S(1)}) custom-call(bf16[1,128,2048]{2,1,0:T(8,128)(2,1)S(1)} %copy-done, bf16[1,128,1024]{2,1,0:T(8,128)(2,1)S(1)} %copy-done.2, f32[3,384,256]{2,1,0:T(8,128)S(1)} %probs_last.1.prob_ref, bf16[128,384]{1,0:T(8,128)(2,1)S(1)} %turn.1.mine_ref, ...), custom_call_target="tpu_custom_call" | custom-call | flops 1 | bytes 1 | tf_op jit(solution)/shard_map/heads_last/pallas_call | solution.py:48
  30.7 0.8 %settle.1 = (bf16[1,128,1024]{2,1,0:T(8,128)(2,1)}, bf16[1,128,1024]{2,1,0:T(8,128)(2,1)}, bf16[1,128,1024]{2,1,0:T(8,128)(2,1)}) custom-call(bf16[128,512]{1,0:T(8,128)(2,1)S(1)} %get-tuple-element.46.refs_0_, bf16[128,256]{1,0:T(8,128)(2,1)S(1)} %get-tuple-element.54.refs_1_, bf16[128,256]{1,0:T(8,128)(2,1)S(1)} %get-tuple-element.63.refs_2_, ...), custom_call_target="tpu_custom_call" | custom-call | flops 1 | bytes 1 | tf_op jit(solution)/shard_map/settle/pallas_call | solution.py:48
  31.6 0.2 collective-permute-done.10.far
  31.7 0.8 %finish.1 = (bf16[1,128,1024]{2,1,0:T(8,128)(2,1)}, bf16[1,128,1024]{2,1,0:T(8,128)(2,1)}) custom-call(bf16[2,128,768]{2,1,0:T(8,128)(2,1)S(1)} %collective-permute-done.10.far, bf16[2,128,768]{2,1,0:T(8,128)(2,1)S(1)} %collective-permute-done.11.near, f32[2,128,512]{2,1,0:T(8,128)S(1)} %get-tuple-element.69.refs_0_, ...), custom_call_target="tpu_custom_call", output_to_operand_aliasing={{0}: (4, {}), {1}: (5, {})} | custom-call | flops 1 | bytes 1 | tf_op jit(solution)/shard_map/finish/pallas_call | solution.py:469
  (24 shorter events, 0.3 us)
Async XLA Ops:
  0.6 8.1 %copy-start = (bf16[1,128,2048]{2,1,0:T(8,128)(2,1)S(1)}, bf16[1,128,2048]{2,1,0:T(8,128)(2,1)}, u32[]{:S(2)}) copy-start(bf16[1,128,2048]{2,1,0:T(8,128)(2,1)} %dy_ref.7) | copy-start | bytes 1572868
  0.6 8.1 %copy-start.2 = (bf16[1,128,1024]{2,1,0:T(8,128)(2,1)S(1)}, bf16[1,128,1024]{2,1,0:T(8,128)(2,1)}, u32[]{:S(2)}) copy-start(bf16[1,128,1024]{2,1,0:T(8,128)(2,1)} %q_ref.7) | copy-start | bytes 786436
  0.7 15.7 %collective-permute-start.2 = (bf16[256,2048]{1,0:T(8,128)(2,1)}, bf16[256,2048]{1,0:T(8,128)(2,1)S(1)}, u32[]{:S(2)}, u32[]{:S(2)}) collective-permute-start(bf16[256,2048]{1,0:T(8,128)(2,1)} %refs_3_.1), channel_id=1, source_target_pairs={{0,1},{1,0},{2,3},{3,2},{4,6},{5,7},{6,4},{7,5},{8,9},{9,8},{10,11... | collective-permute-start | bytes 3145736 | tf_op jit(solution)/shard_map/ppermute | solution.py:494
  4.6 7.9 %copy-start.4 = (s32[8,4]{0,1:T(4,128)S(1)}, s32[8,4]{0,1:T(4,128)}, u32[]{:S(2)}) copy-start(s32[8,4]{0,1:T(4,128)} %param.12) | copy-start | bytes 388
  4.6 7.9 %copy-start.5 = (s32[1,8]{1,0:T(1,128)S(1)}, s32[1,8]{1,0:T(1,128)}, u32[]{:S(2)}) copy-start(s32[1,8]{1,0:T(1,128)} %val_ref.1) | copy-start | bytes 100
  4.7 4.1 %collective-permute-start = (bf16[128,2048]{1,0:T(8,128)(2,1)}, bf16[128,2048]{1,0:T(8,128)(2,1)S(1)}, u32[]{:S(2)}, u32[]{:S(2)}) collective-permute-start(bf16[128,2048]{1,0:T(8,128)(2,1)} %join.1.refs_0_), channel_id=1, source_target_pairs={{0,4},{4,0},{8,12},{12,8},{16,20},{20,16},{24,28},{28,24},{1,5},{5... | collective-permute-start | bytes 1572872 | tf_op jit(solution)/shard_map/ppermute | solution.py:499
  5.6 10.7 %collective-permute-start.3 = (bf16[128,2048]{1,0:T(8,128)(2,1)}, bf16[128,2048]{1,0:T(8,128)(2,1)S(1)}, u32[]{:S(2)}, u32[]{:S(2)}) collective-permute-start(bf16[128,2048]{1,0:T(8,128)(2,1)} %join.1.refs_0_), channel_id=1, source_target_pairs={{4,8},{8,4},{12,16},{16,12},{20,24},{24,20},{5,9},{9,5},{13,17},{1... | collective-permute-start | bytes 1572872 | tf_op jit(solution)/shard_map/ppermute | solution.py:499
  8.9 9.9 %copy-start.1 = (bf16[128,2048]{1,0:T(8,128)(2,1)S(1)}, bf16[128,2048]{1,0:T(8,128)(2,1)}, u32[]{:S(2)}) copy-start(bf16[128,2048]{1,0:T(8,128)(2,1)} %join.1.refs_0_) | copy-start | bytes 1572868
  8.9 9.8 %copy-start.3 = (bf16[256,2048]{1,0:T(8,128)(2,1)S(1)}, bf16[256,2048]{1,0:T(8,128)(2,1)}, u32[]{:S(2)}) copy-start(bf16[256,2048]{1,0:T(8,128)(2,1)} %refs_3_.1) | copy-start | bytes 3145732
  8.9 12.1 %collective-permute-start.1 = (bf16[128,2816]{1,0:T(8,128)(2,1)S(1)}, bf16[128,2816]{1,0:T(8,128)(2,1)S(1)}, u32[]{:S(2)}, u32[]{:S(2)}) collective-permute-start(bf16[128,2816]{1,0:T(8,128)(2,1)S(1)} %hand_far.1), channel_id=1, source_target_pairs={{0,4},{4,0},{8,12},{12,8},{16,20},{20,16},{24,28},{28,24},{1,5},{5... | collective-permute-start | bytes 2162696 | tf_op jit(solution)/shard_map/ppermute | solution.py:503
  9.0 17.4 %collective-permute-start.7 = (bf16[128,2816]{1,0:T(8,128)(2,1)S(1)}, bf16[128,2816]{1,0:T(8,128)(2,1)S(1)}, u32[]{:S(2)}, u32[]{:S(2)}) collective-permute-start(bf16[128,2816]{1,0:T(8,128)(2,1)S(1)} %hand_far.1), channel_id=1, source_target_pairs={{4,8},{8,4},{12,16},{16,12},{20,24},{24,20},{5,9},{9,5},{13,17},{1... | collective-permute-start | bytes 2162696 | tf_op jit(solution)/shard_map/ppermute | solution.py:503
  16.5 4.5 %collective-permute-start.4 = (bf16[128,2304]{1,0:T(8,128)(2,1)S(1)}, bf16[128,2304]{1,0:T(8,128)(2,1)S(1)}, u32[]{:S(2)}, u32[]{:S(2)}) collective-permute-start(bf16[128,2304]{1,0:T(8,128)(2,1)S(1)} %get-tuple-element.41), channel_id=1, source_target_pairs={{0,4},{4,0},{8,12},{12,8},{16,20},{20,16},{24,28},{28,24},{1,5},{5... | collective-permute-start | bytes 1769480 | tf_op jit(solution)/shard_map/ppermute | solution.py:509
  16.9 4.1 %collective-permute-start.5 = (bf16[128,2304]{1,0:T(8,128)(2,1)S(1)}, bf16[128,2304]{1,0:T(8,128)(2,1)S(1)}, u32[]{:S(2)}, u32[]{:S(2)}) collective-permute-start(bf16[128,2304]{1,0:T(8,128)(2,1)S(1)} %get-tuple-element.42), channel_id=1, source_target_pairs={{0,4},{4,0},{8,12},{12,8},{16,20},{20,16},{24,28},{28,24},{1,5},{5... | collective-permute-start | bytes 1769480 | tf_op jit(solution)/shard_map/ppermute | solution.py:509
  17.0 10.0 %collective-permute-start.6 = (bf16[128,2048]{1,0:T(8,128)(2,1)S(1)}, bf16[128,2048]{1,0:T(8,128)(2,1)S(1)}, u32[]{:S(2)}, u32[]{:S(2)}) collective-permute-start(bf16[128,2048]{1,0:T(8,128)(2,1)S(1)} %get-tuple-element.47), channel_id=1, source_target_pairs={{0,2},{1,3},{2,0},{3,1},{4,5},{5,4},{6,7},{7,6},{8,10},{9,11},{10,... | collective-permute-start | bytes 1572872 | tf_op jit(solution)/shard_map/ppermute | solution.py:494
  22.4 9.3 %collective-permute-start.10 = (bf16[2,128,768]{2,1,0:T(8,128)(2,1)S(1)}, bf16[2,128,768]{2,1,0:T(8,128)(2,1)S(1)}, u32[]{:S(2)}, u32[]{:S(2)}) collective-permute-start(bf16[2,128,768]{2,1,0:T(8,128)(2,1)S(1)} %get-tuple-element.67), channel_id=1, source_target_pairs={{4,8},{8,4},{12,16},{16,12},{20,24},{24,20},{5,9},{9,5},{13,17},{1... | collective-permute-start | bytes 1179656 | tf_op jit(solution)/shard_map/ppermute | solution.py:533
  26.3 5.4 %collective-permute-start.11 = (bf16[2,128,768]{2,1,0:T(8,128)(2,1)S(1)}, bf16[2,128,768]{2,1,0:T(8,128)(2,1)S(1)}, u32[]{:S(2)}, u32[]{:S(2)}) collective-permute-start(bf16[2,128,768]{2,1,0:T(8,128)(2,1)S(1)} %get-tuple-element.68), channel_id=1, source_target_pairs={{0,4},{4,0},{8,12},{12,8},{16,20},{20,16},{24,28},{28,24},{1,5},{5... | collective-permute-start | bytes 1179656 | tf_op jit(solution)/shard_map/ppermute | solution.py:533
  27.1 1.7 %collective-permute-start.8 = (bf16[64,2048]{1,0:T(8,128)(2,1)S(1)}, bf16[64,2048]{1,0:T(8,128)(2,1)S(1)}, u32[]{:S(2)}, u32[]{:S(2)}) collective-permute-start(bf16[64,2048]{1,0:T(8,128)(2,1)S(1)} %get-tuple-element.61), channel_id=1, source_target_pairs={{0,4},{4,0},{8,12},{12,8},{16,20},{20,16},{24,28},{28,24},{1,5},{5... | collective-permute-start | bytes 786440 | tf_op jit(solution)/shard_map/ppermute | solution.py:534
  27.7 1.5 %collective-permute-start.9 = (bf16[64,2048]{1,0:T(8,128)(2,1)S(1)}, bf16[64,2048]{1,0:T(8,128)(2,1)S(1)}, u32[]{:S(2)}, u32[]{:S(2)}) collective-permute-start(bf16[64,2048]{1,0:T(8,128)(2,1)S(1)} %get-tuple-element.62), channel_id=1, source_target_pairs={{0,4},{4,0},{8,12},{12,8},{16,20},{20,16},{24,28},{28,24},{1,5},{5... | collective-permute-start | bytes 786440 | tf_op jit(solution)/shard_map/ppermute | solution.py:534

commit v13 on v12

--- a/solution.py
+++ b/solution.py
@@ -153,6 +153,15 @@
     return call(kernel, name, shape, [VMEM] * (len(whole) + len(cut)), VMEM, [], *whole, *cut)
 
 
+def turned_kernel(dy_ref, out_ref):
+    out_ref[...] = dy_ref[0].T
+
+
+def turned_rows(d_out):
+    shape = jax.ShapeDtypeStruct(d_out.shape[:0:-1], BF16)
+    return call(turned_kernel, "turned", shape, [VMEM], VMEM, [], d_out)
+
+
 def onward_kernel(last, w_ref, kv_ref, mine_ref, *both_refs):
     core, group = place()
     half, depth = mine_ref.shape
@@ -242,13 +251,13 @@
     earlier, (dq_ref, own_ref, *message_refs) = refs[-4 - messages : -4], refs[-4:]
     for old, out in zip(earlier, message_refs):
         out[...] = old[...]
-    tok, depth = q_ref.shape[1], dy_ref.shape[2]
+    tok, depth = q_ref.shape[1], dy_ref.shape[0]
     values_at = k_refs[0].shape[1] // (2 * PAIR)
     open_keys = key_mask(limit_ref, tok, 0, 3)
     for chunk, slot, message_slot, pieces, lead in steps(core, group):
         cols, dest, message_dest = columns(chunk), columns(slot), columns(message_slot)
         w = jnp.concatenate([w_refs[i][row : row + rows, :depth] for i, row, rows in pieces], axis=0)
-        d = diagonal_turned(*in_order(dot(w, dy_ref[0], NT).astype(BF16), lead))
+        d = diagonal_turned(*in_order(dot(w, dy_ref[...], NN).astype(BF16), lead))
         qd = diagonal(q_ref[0, :, cols])
         k, v = stacked(k_refs, cols), stacked(k_refs, columns(chunk + values_at))
         prob = prob_of(k, qd, open_keys)
@@ -307,31 +316,36 @@
 
 def probs_kernel(last, q_ref, limit_ref, *refs):
     *kv_refs, near_both, far_both = refs[:5]
-    near_next, prob_ref = refs[5:7], refs[7]
+    near_next, prob_ref, turned_ref = refs[5:7], refs[7], refs[8]
     tok = q_ref.shape[1]
+    depth = turned_ref.shape[0]
+    turned_ref[:, :tok] = near_both[:, :depth].T
+    turned_ref[:, tok:] = far_both[:, :depth].T
     blocks = last_parts(last, q_ref, near_both, far_both, near_next, kv_refs)
     for block, (q, parts) in enumerate(blocks):
         open_keys = key_mask(limit_ref, tok, 3 * block, 3)
         prob_ref[block] = prob_of(joined(parts, 0), diagonal(q), open_keys)
 
 
-def turn_kernel(dy_ref, near_both, far_both, *refs):
+def turn_kernel(rows_ref, far_ref, *refs):
     *w_refs, out_ref = refs
-    depth = dy_ref.shape[2]
     w = jnp.concatenate([ref[...] for ref in w_refs], axis=0)
-    dy = jnp.concatenate([dy_ref[0], near_both[:, :depth], far_both[:, :depth]], axis=0)
-    out_ref[...] = dot(w, dy, NT).astype(BF16)
-
-
-def last_kernel(last, dy_ref, q_ref, prob_ref, mine_ref, *refs):
+    out_ref[...] = three_blocks(w, rows_ref, far_ref)
+
+
+def three_blocks(w, rows_ref, far_ref):
+    parts = [dot(w, ref[...], NN).astype(BF16) for ref in (rows_ref, far_ref)]
+    return jnp.concatenate(parts, axis=1)
+
+
+def last_kernel(last, rows_ref, far_rows_ref, q_ref, prob_ref, mine_ref, *refs):
     core, _ = place()
     kv_refs = refs[:3]
     near_both, far_both, *near_next = refs[3:7]
     *w_refs, dq_ref, dk_ref, dv_ref = refs[7:]
-    tok, depth = q_ref.shape[1], dy_ref.shape[2]
+    tok = q_ref.shape[1]
     w = jnp.concatenate([ref[...] for ref in w_refs], axis=0)
-    dy = jnp.concatenate([dy_ref[0], near_both[:, :depth], far_both[:, :depth]], axis=0)
-    other = dot(w, dy, NT).astype(BF16)
+    other = three_blocks(w, rows_ref, far_rows_ref)
     turned = in_order(jnp.concatenate([mine_ref[...], other], axis=0), core)
     probs, scores, queries, cotangents = [], [], [], []
     blocks = last_parts(last, q_ref, near_both, far_both, near_next, kv_refs)
@@ -355,12 +369,16 @@
 
 def last_probs(last, q, limits, blocks, halo):
     tok = q.shape[1]
+    depth = halo[1].shape[1] - 3 * PAIR
     return call(
         functools.partial(probs_kernel, last),
         "probs_last",
-        jax.ShapeDtypeStruct((3, 3 * tok, PAIR), F32),
+        (
+            jax.ShapeDtypeStruct((3, 3 * tok, PAIR), F32),
+            jax.ShapeDtypeStruct((depth, 2 * tok), BF16),
+        ),
         [VMEM] * 9,
-        VMEM,
+        (VMEM,) * 2,
         [],
         q,
         limits,
@@ -369,27 +387,28 @@
     )
 
 
-def last_heads(last, prob, d_out, q, blocks, halo, mine, other):
+def last_heads(last, prob, far_rows, rows, q, blocks, halo, mine, other):
     tok = q.shape[1]
     turned = call(
         turn_kernel,
         "turn",
         jax.ShapeDtypeStruct((HD, 3 * tok), BF16),
-        [VMEM] * (3 + len(mine)),
+        [VMEM] * (2 + len(mine)),
         VMEM,
         [],
-        d_out,
-        *halo[:2],
+        rows,
+        far_rows,
         *mine,
     )
     return call(
         functools.partial(last_kernel, last),
         "heads_last",
         (jax.ShapeDtypeStruct((tok, PAIR), BF16),) * 3,
-        [VMEM] * (11 + len(other)),
+        [VMEM] * (12 + len(other)),
         (VMEM,) * 3,
         [],
-        d_out,
+        rows,
+        far_rows,
         q,
         prob,
         turned,
@@ -501,9 +520,9 @@
         got = cross(w_out, (1, 2))
         message = hand_on("hand_far", last, [d_out], [queries, near_kv])
         far_both, near_both = far(message), near(message)
-        early = got, near_kv, far_kv, limits
-        got, near_kv, far_kv, limits = lax.optimization_barrier(early)
-        ours = d_out, queries, limits, (kv, near_kv, far_kv)
+        early = got, near_kv, far_kv, limits, turned_rows(d_out)
+        got, near_kv, far_kv, limits, rows = lax.optimization_barrier(early)
+        ours = rows, queries, limits, (kv, near_kv, far_kv)
         mine, *both = onward(last, got, far_kv)
         got_d = cross(mine, (2, 1))
         near_got = [near(x) for x in both]
@@ -528,10 +547,10 @@
             *ours,
         )
         halo = near_both, far_both, *near_got
-        prob = last_probs(last, *ours[1:], halo)
+        prob, far_rows = last_probs(last, *ours[1:], halo)
         got_d, halo, prob, second_dq = lax.optimization_barrier((got_d, halo, prob, second[0]))
         sums = far(second[3]), near(second[2])
-        third = last_heads(last, prob, *ours[:2], ours[3], halo, [got_d], [near(x) for x in split(got_d)])
+        third = last_heads(last, prob, far_rows, *ours[:2], ours[3], halo, [got_d], [near(x) for x in split(got_d)])
         order = lambda core, group: [
             [(group, 0), (group ^ (1 + core), 1 + core)],
             [(group ^ (2 - core), 2 - core)],
@@ -540,7 +559,7 @@
         d_queries, *old = settle(order, (dq, second_dq, third[0]), third[1:], queries.shape)
         return d_queries, *finish(order, *sums, (first[1], second[1]), old)
     full = lax.all_gather(w_out, "fsdp", axis=0, tiled=True)
-    ours = d_out, queries, limits, (kv, near_kv, far_kv)
+    ours = turned_rows(d_out), queries, limits, (kv, near_kv, far_kv)
     steps = lambda core, group: [
         (i, i, i, ((0, i * PAIR, PAIR),), 0) for i in range(n_chunks)
     ]

time: 32.9 us -> 32.3 us (0.982)
  Pallas kernels: 10.8 us -> 10.1 us
    pallas_call x10 -> x11, Pallas kernels: 8.15 us -> 7.42 us  [call(): pl.pallas_call(kernel, out_shape=out_shape, in_specs=in_specs, out_specs=...]
  transfers between devices with their start and end apart: 12 -> 12, of which waited for: 4 -> 4; matrix products, arithmetic and copies ran while one was open for 0% -> 0% of each run, Pallas kernels for 31% -> 29%
where the time goes in v13:
time: 32.3 us; the launch traced here: 32.1 us
  starting transfers between devices  16.7 us (52%)
  Pallas kernels  10.1 us (31%)
  waiting for transfers between devices  4.4 us (14%)
  between operations  0.89 us (3%)
    pallas_call x11, Pallas kernels, call(): pl.pallas_call(kernel, out_shape=out_shape, in_specs=in_specs, out_specs=...  7.42 us
    ppermute x2, starting transfers between devices, body(): far_kv, near_kv = (far(kv), near(kv))  4.09 us
    ppermute x2, starting transfers between devices, body(): sums = (far(second[3]), near(second[2]))  3.9 us
    ppermute x2, starting transfers between devices, cross(): return lax.ppermute(x, ('seq', 'fsdp'), pairs)  3.79 us
    ppermute x2, starting transfers between devices, body(): far_both, near_both = (far(message), near(message))  3.66 us
    ppermute x2, waiting for transfers between devices, body(): far_kv, near_kv = (far(kv), near(kv))  2.93 us
    pallas_call x1, Pallas kernels, join(): pl.pallas_call(join_kernel, out_shape=jax.ShapeDtypeStruct(kv, BF16), in_...  1.84 us
    ppermute x2, waiting for transfers between devices, body(): near(x)  1.02 us
  transfers between devices with their start and end apart: 12, of which 4 were waited for; matrix products, arithmetic and copies ran while one was open for 0% of the time, Pallas kernels for 29%

profile of v13, /device:TPU:1, one launch (start us, length us, event | category | flops | bytes accessed | tf_op | source)
XLA Modules:
  0.0 32.1 jit_solution(6914500639762879086)
XLA Ops:
  0.7 2.1 %collective-permute-start.2 = (bf16[256,2048]{1,0:T(8,128)(2,1)}, bf16[256,2048]{1,0:T(8,128)(2,1)S(1)}, u32[]{:S(2)}, u32[]{:S(2)}) collective-permute-start(bf16[256,2048]{1,0:T(8,128)(2,1)} %refs_3_.1), channel_id=1, source_target_pairs={{0,1},{1,0},{2,3},{3,2},{4,6},{5,7},{6,4},{7,5},{8,9},{9,8},{10,11... | collective-permute-start | bytes 3145736 | tf_op jit(solution)/shard_map/ppermute | solution.py:513
  2.8 1.8 %join.1.refs_0_ = bf16[128,2048]{1,0:T(8,128)(2,1)} custom-call(bf16[1,128,1024]{2,1,0:T(8,128)(2,1)} %k_ref.1, bf16[1,128,1024]{2,1,0:T(8,128)(2,1)} %v_ref.1), custom_call_target="tpu_custom_call" | custom-call | flops 1 | bytes 1 | tf_op jit(solution)/shard_map/join/pallas_call | solution.py:117
  4.7 1.0 %collective-permute-start = (bf16[128,2048]{1,0:T(8,128)(2,1)}, bf16[128,2048]{1,0:T(8,128)(2,1)S(1)}, u32[]{:S(2)}, u32[]{:S(2)}) collective-permute-start(bf16[128,2048]{1,0:T(8,128)(2,1)} %join.1.refs_0_), channel_id=1, source_target_pairs={{0,4},{4,0},{8,12},{12,8},{16,20},{20,16},{24,28},{28,24},{1,5},{5... | collective-permute-start | bytes 1572872 | tf_op jit(solution)/shard_map/ppermute | solution.py:518
  5.6 3.1 %collective-permute-start.3 = (bf16[128,2048]{1,0:T(8,128)(2,1)}, bf16[128,2048]{1,0:T(8,128)(2,1)S(1)}, u32[]{:S(2)}, u32[]{:S(2)}) collective-permute-start(bf16[128,2048]{1,0:T(8,128)(2,1)} %join.1.refs_0_), channel_id=1, source_target_pairs={{4,8},{8,4},{12,16},{16,12},{20,24},{24,20},{5,9},{9,5},{13,17},{1... | collective-permute-start | bytes 1572872 | tf_op jit(solution)/shard_map/ppermute | solution.py:518
  9.0 0.2 turned.1.dy_ref.rows_ref
  9.2 3.6 %collective-permute-start.7 = (bf16[128,2816]{1,0:T(8,128)(2,1)S(1)}, bf16[128,2816]{1,0:T(8,128)(2,1)S(1)}, u32[]{:S(2)}, u32[]{:S(2)}) collective-permute-start(bf16[128,2816]{1,0:T(8,128)(2,1)S(1)} %hand_far.1), channel_id=1, source_target_pairs={{4,8},{8,4},{12,16},{16,12},{20,24},{24,20},{5,9},{9,5},{13,17},{1... | collective-permute-start | bytes 2162696 | tf_op jit(solution)/shard_map/ppermute | solution.py:522
  12.8 0.6 %limits.1.limit_ref = s32[16,256]{1,0:T(8,128)S(1)} custom-call(s32[4,8]{1,0:T(4,128)S(1)} %bitcast.1, s32[1,8]{1,0:T(1,128)S(1)} %copy-done.5), custom_call_target="tpu_custom_call" | custom-call | flops 1 | bytes 1 | tf_op jit(solution)/shard_map/limits/pallas_call | solution.py:48
  13.4 2.9 %collective-permute-done.3.kv_ref.refs_2_ = bf16[128,2048]{1,0:T(8,128)(2,1)S(1)} collective-permute-done((bf16[128,2048]{1,0:T(8,128)(2,1)}, bf16[128,2048]{1,0:T(8,128)(2,1)S(1)}, u32[]{:S(2)}, u32[]{:S(2)}) %collective-permute-start.3) | collective-permute-done | bytes 524320 | tf_op jit(solution)/shard_map/ppermute | solution.py:518
  16.4 0.1 onward.1
  16.5 0.4 %collective-permute-start.4 = (bf16[128,2304]{1,0:T(8,128)(2,1)S(1)}, bf16[128,2304]{1,0:T(8,128)(2,1)S(1)}, u32[]{:S(2)}, u32[]{:S(2)}) collective-permute-start(bf16[128,2304]{1,0:T(8,128)(2,1)S(1)} %get-tuple-element.44), channel_id=1, source_target_pairs={{0,4},{4,0},{8,12},{12,8},{16,20},{20,16},{24,28},{28,24},{1,5},{5... | collective-permute-start | bytes 1769480 | tf_op jit(solution)/shard_map/ppermute | solution.py:528
  16.9 0.2 collective-permute-start.5
  17.0 1.7 %collective-permute-start.6 = (bf16[128,2048]{1,0:T(8,128)(2,1)S(1)}, bf16[128,2048]{1,0:T(8,128)(2,1)S(1)}, u32[]{:S(2)}, u32[]{:S(2)}) collective-permute-start(bf16[128,2048]{1,0:T(8,128)(2,1)S(1)} %get-tuple-element.51), channel_id=1, source_target_pairs={{0,2},{1,3},{2,0},{3,1},{4,5},{5,4},{6,7},{7,6},{8,10},{9,11},{10,... | collective-permute-start | bytes 1572872 | tf_op jit(solution)/shard_map/ppermute | solution.py:513
  18.7 2.1 %heads_first.1 = (bf16[128,512]{1,0:T(8,128)(2,1)S(1)}, f32[2,128,512]{2,1,0:T(8,128)S(1)}, bf16[2,128,768]{2,1,0:T(8,128)(2,1)S(1)}, bf16[2,128,768]{2,1,0:T(8,128)(2,1)S(1)}) custom-call(bf16[2048,128]{1,0:T(8,128)(2,1)S(1)} %turned.1.dy_ref.rows_ref, bf16[1,128,1024]{2,1,0:T(8,128)(2,1)S(1)} %copy-done.1, s32[16,256]{1,0:T(8,128)S(1)} %limits.1.limit_ref, ...), custom_call_target="tpu_custom_call" | custom-call | flops 1 | bytes 1 | tf_op jit(solution)/shard_map/heads_first/pallas_call | solution.py:48
  20.9 1.1 %heads_second.1 = (bf16[128,256]{1,0:T(8,128)(2,1)S(1)}, f32[2,128,256]{2,1,0:T(8,128)S(1)}, bf16[2,128,768]{2,1,0:T(8,128)(2,1)S(1)}, bf16[2,128,768]{2,1,0:T(8,128)(2,1)S(1)}) custom-call(bf16[2048,128]{1,0:T(8,128)(2,1)S(1)} %turned.1.dy_ref.rows_ref, bf16[1,128,1024]{2,1,0:T(8,128)(2,1)S(1)} %copy-done.1, s32[16,256]{1,0:T(8,128)S(1)} %limits.1.limit_ref, ...), custom_call_target="tpu_custom_call" | custom-call | flops 1 | bytes 1 | tf_op jit(solution)/shard_map/heads_second/pallas_call | solution.py:48
  21.9 3.8 %collective-permute-start.10 = (bf16[2,128,768]{2,1,0:T(8,128)(2,1)S(1)}, bf16[2,128,768]{2,1,0:T(8,128)(2,1)S(1)}, u32[]{:S(2)}, u32[]{:S(2)}) collective-permute-start(bf16[2,128,768]{2,1,0:T(8,128)(2,1)S(1)} %get-tuple-element.73), channel_id=1, source_target_pairs={{4,8},{8,4},{12,16},{16,12},{20,24},{24,20},{5,9},{9,5},{13,17},{1... | collective-permute-start | bytes 1179656 | tf_op jit(solution)/shard_map/ppermute | solution.py:552
  25.9 0.7 %probs_last.1 = (f32[3,384,256]{2,1,0:T(8,128)S(1)}, bf16[2048,256]{1,0:T(8,128)(2,1)S(1)}) custom-call(bf16[1,128,1024]{2,1,0:T(8,128)(2,1)S(1)} %copy-done.1, s32[16,256]{1,0:T(8,128)S(1)} %limits.1.limit_ref, bf16[128,2048]{1,0:T(8,128)(2,1)S(1)} %copy-done, bf16[128,2048]{1,0:T(8,128)(2,1)S(1)} %collective-permute-done.refs_2_.refs_1_, ...), custom_call_target="tpu_custom_call" | custom-call | flops 1 | bytes 1 | tf_op jit(solution)/shard_map/probs_last/pallas_call | solution.py:48
  26.7 0.6 %collective-permute-start.8 = (bf16[64,2048]{1,0:T(8,128)(2,1)S(1)}, bf16[64,2048]{1,0:T(8,128)(2,1)S(1)}, u32[]{:S(2)}, u32[]{:S(2)}) collective-permute-start(bf16[64,2048]{1,0:T(8,128)(2,1)S(1)} %get-tuple-element.67), channel_id=1, source_target_pairs={{0,4},{4,0},{8,12},{12,8},{16,20},{20,16},{24,28},{28,24},{1,5},{5... | collective-permute-start | bytes 786440 | tf_op jit(solution)/shard_map/ppermute | solution.py:553
  27.3 0.4 %turn.1.mine_ref = bf16[128,384]{1,0:T(8,128)(2,1)S(1)} custom-call(bf16[2048,128]{1,0:T(8,128)(2,1)S(1)} %turned.1.dy_ref.rows_ref, bf16[2048,256]{1,0:T(8,128)(2,1)S(1)} %get-tuple-element.60.far_ref.far_rows_ref, bf16[128,2048]{1,0:T(8,128)(2,1)S(1)} %collective-permute-done.6.refs_0_.x_ref), custom_call_target="tpu_custom_call" | custom-call | flops 1 | bytes 1 | tf_op jit(solution)/shard_map/turn/pallas_call | solution.py:48
  27.7 0.6 %collective-permute-done.8.refs_7_ = bf16[64,2048]{1,0:T(8,128)(2,1)S(1)} collective-permute-done((bf16[64,2048]{1,0:T(8,128)(2,1)S(1)}, bf16[64,2048]{1,0:T(8,128)(2,1)S(1)}, u32[]{:S(2)}, u32[]{:S(2)}) %collective-permute-start.8) | collective-permute-done | bytes 262176 | tf_op jit(solution)/shard_map/ppermute | solution.py:553
  28.4 0.4 %collective-permute-done.9.refs_8_ = bf16[64,2048]{1,0:T(8,128)(2,1)S(1)} collective-permute-done((bf16[64,2048]{1,0:T(8,128)(2,1)S(1)}, bf16[64,2048]{1,0:T(8,128)(2,1)S(1)}, u32[]{:S(2)}, u32[]{:S(2)}) %collective-permute-start.9) | collective-permute-done | bytes 262176 | tf_op jit(solution)/shard_map/ppermute | solution.py:553
  28.8 1.2 %heads_last.1 = (bf16[128,256]{1,0:T(8,128)(2,1)S(1)}, bf16[128,256]{1,0:T(8,128)(2,1)S(1)}, bf16[128,256]{1,0:T(8,128)(2,1)S(1)}) custom-call(bf16[2048,128]{1,0:T(8,128)(2,1)S(1)} %turned.1.dy_ref.rows_ref, bf16[2048,256]{1,0:T(8,128)(2,1)S(1)} %get-tuple-element.60.far_ref.far_rows_ref, bf16[1,128,1024]{2,1,0:T(8,128)(2,1)S(1)} %copy-done.1, ...), custom_call_target="tpu_custom_call" | custom-call | flops 1 | bytes 1 | tf_op jit(solution)/shard_map/heads_last/pallas_call | solution.py:48
  30.0 0.8 %settle.1 = (bf16[1,128,1024]{2,1,0:T(8,128)(2,1)}, bf16[1,128,1024]{2,1,0:T(8,128)(2,1)}, bf16[1,128,1024]{2,1,0:T(8,128)(2,1)}) custom-call(bf16[128,512]{1,0:T(8,128)(2,1)S(1)} %get-tuple-element.50.refs_0_, bf16[128,256]{1,0:T(8,128)(2,1)S(1)} %get-tuple-element.59.refs_1_, bf16[128,256]{1,0:T(8,128)(2,1)S(1)} %get-tuple-element.69.refs_2_, ...), custom_call_target="tpu_custom_call" | custom-call | flops 1 | bytes 1 | tf_op jit(solution)/shard_map/settle/pallas_call | solution.py:48
  30.8 0.4 %collective-permute-done.10.far = bf16[2,128,768]{2,1,0:T(8,128)(2,1)S(1)} collective-permute-done((bf16[2,128,768]{2,1,0:T(8,128)(2,1)S(1)}, bf16[2,128,768]{2,1,0:T(8,128)(2,1)S(1)}, u32[]{:S(2)}, u32[]{:S(2)}) %collective-permute-start.10) | collective-permute-done | bytes 393248 | tf_op jit(solution)/shard_map/ppermute | solution.py:552
  31.2 0.8 %finish.1 = (bf16[1,128,1024]{2,1,0:T(8,128)(2,1)}, bf16[1,128,1024]{2,1,0:T(8,128)(2,1)}) custom-call(bf16[2,128,768]{2,1,0:T(8,128)(2,1)S(1)} %collective-permute-done.10.far, bf16[2,128,768]{2,1,0:T(8,128)(2,1)S(1)} %collective-permute-done.11.near, f32[2,128,512]{2,1,0:T(8,128)S(1)} %get-tuple-element.75.refs_0_, ...), custom_call_target="tpu_custom_call", output_to_operand_aliasing={{0}: (4, {}), {1}: (5, {})} | custom-call | flops 1 | bytes 1 | tf_op jit(solution)/shard_map/finish/pallas_call | solution.py:488
  (25 shorter events, 0.4 us)
Async XLA Ops:
  0.6 8.1 %copy-start.1 = (bf16[1,128,1024]{2,1,0:T(8,128)(2,1)S(1)}, bf16[1,128,1024]{2,1,0:T(8,128)(2,1)}, u32[]{:S(2)}) copy-start(bf16[1,128,1024]{2,1,0:T(8,128)(2,1)} %q_ref.7) | copy-start | bytes 786436
  0.6 8.1 %copy-start.2 = (bf16[1,128,2048]{2,1,0:T(8,128)(2,1)S(1)}, bf16[1,128,2048]{2,1,0:T(8,128)(2,1)}, u32[]{:S(2)}) copy-start(bf16[1,128,2048]{2,1,0:T(8,128)(2,1)} %dy_ref.1) | copy-start | bytes 1572868
  0.7 15.7 %collective-permute-start.2 = (bf16[256,2048]{1,0:T(8,128)(2,1)}, bf16[256,2048]{1,0:T(8,128)(2,1)S(1)}, u32[]{:S(2)}, u32[]{:S(2)}) collective-permute-start(bf16[256,2048]{1,0:T(8,128)(2,1)} %refs_3_.1), channel_id=1, source_target_pairs={{0,1},{1,0},{2,3},{3,2},{4,6},{5,7},{6,4},{7,5},{8,9},{9,8},{10,11... | collective-permute-start | bytes 3145736 | tf_op jit(solution)/shard_map/ppermute | solution.py:513
  4.6 8.1 %copy-start.4 = (s32[8,4]{0,1:T(4,128)S(1)}, s32[8,4]{0,1:T(4,128)}, u32[]{:S(2)}) copy-start(s32[8,4]{0,1:T(4,128)} %param.12) | copy-start | bytes 388
  4.6 8.1 %copy-start.5 = (s32[1,8]{1,0:T(1,128)S(1)}, s32[1,8]{1,0:T(1,128)}, u32[]{:S(2)}) copy-start(s32[1,8]{1,0:T(1,128)} %val_ref.1) | copy-start | bytes 100
  4.7 4.1 %collective-permute-start = (bf16[128,2048]{1,0:T(8,128)(2,1)}, bf16[128,2048]{1,0:T(8,128)(2,1)S(1)}, u32[]{:S(2)}, u32[]{:S(2)}) collective-permute-start(bf16[128,2048]{1,0:T(8,128)(2,1)} %join.1.refs_0_), channel_id=1, source_target_pairs={{0,4},{4,0},{8,12},{12,8},{16,20},{20,16},{24,28},{28,24},{1,5},{5... | collective-permute-start | bytes 1572872 | tf_op jit(solution)/shard_map/ppermute | solution.py:518
  5.6 10.7 %collective-permute-start.3 = (bf16[128,2048]{1,0:T(8,128)(2,1)}, bf16[128,2048]{1,0:T(8,128)(2,1)S(1)}, u32[]{:S(2)}, u32[]{:S(2)}) collective-permute-start(bf16[128,2048]{1,0:T(8,128)(2,1)} %join.1.refs_0_), channel_id=1, source_target_pairs={{4,8},{8,4},{12,16},{16,12},{20,24},{24,20},{5,9},{9,5},{13,17},{1... | collective-permute-start | bytes 1572872 | tf_op jit(solution)/shard_map/ppermute | solution.py:518
  8.9 9.9 %copy-start = (bf16[128,2048]{1,0:T(8,128)(2,1)S(1)}, bf16[128,2048]{1,0:T(8,128)(2,1)}, u32[]{:S(2)}) copy-start(bf16[128,2048]{1,0:T(8,128)(2,1)} %join.1.refs_0_) | copy-start | bytes 1572868
  8.9 9.8 %copy-start.3 = (bf16[256,2048]{1,0:T(8,128)(2,1)S(1)}, bf16[256,2048]{1,0:T(8,128)(2,1)}, u32[]{:S(2)}) copy-start(bf16[256,2048]{1,0:T(8,128)(2,1)} %refs_3_.1) | copy-start | bytes 3145732
  8.9 11.9 %collective-permute-start.1 = (bf16[128,2816]{1,0:T(8,128)(2,1)S(1)}, bf16[128,2816]{1,0:T(8,128)(2,1)S(1)}, u32[]{:S(2)}, u32[]{:S(2)}) collective-permute-start(bf16[128,2816]{1,0:T(8,128)(2,1)S(1)} %hand_far.1), channel_id=1, source_target_pairs={{0,4},{4,0},{8,12},{12,8},{16,20},{20,16},{24,28},{28,24},{1,5},{5... | collective-permute-start | bytes 2162696 | tf_op jit(solution)/shard_map/ppermute | solution.py:522
  9.2 16.7 %collective-permute-start.7 = (bf16[128,2816]{1,0:T(8,128)(2,1)S(1)}, bf16[128,2816]{1,0:T(8,128)(2,1)S(1)}, u32[]{:S(2)}, u32[]{:S(2)}) collective-permute-start(bf16[128,2816]{1,0:T(8,128)(2,1)S(1)} %hand_far.1), channel_id=1, source_target_pairs={{4,8},{8,4},{12,16},{16,12},{20,24},{24,20},{5,9},{9,5},{13,17},{1... | collective-permute-start | bytes 2162696 | tf_op jit(solution)/shard_map/ppermute | solution.py:522
  16.5 4.4 %collective-permute-start.4 = (bf16[128,2304]{1,0:T(8,128)(2,1)S(1)}, bf16[128,2304]{1,0:T(8,128)(2,1)S(1)}, u32[]{:S(2)}, u32[]{:S(2)}) collective-permute-start(bf16[128,2304]{1,0:T(8,128)(2,1)S(1)} %get-tuple-element.44), channel_id=1, source_target_pairs={{0,4},{4,0},{8,12},{12,8},{16,20},{20,16},{24,28},{28,24},{1,5},{5... | collective-permute-start | bytes 1769480 | tf_op jit(solution)/shard_map/ppermute | solution.py:528
  16.9 4.0 %collective-permute-start.5 = (bf16[128,2304]{1,0:T(8,128)(2,1)S(1)}, bf16[128,2304]{1,0:T(8,128)(2,1)S(1)}, u32[]{:S(2)}, u32[]{:S(2)}) collective-permute-start(bf16[128,2304]{1,0:T(8,128)(2,1)S(1)} %get-tuple-element.45), channel_id=1, source_target_pairs={{0,4},{4,0},{8,12},{12,8},{16,20},{20,16},{24,28},{28,24},{1,5},{5... | collective-permute-start | bytes 1769480 | tf_op jit(solution)/shard_map/ppermute | solution.py:528
  17.0 9.6 %collective-permute-start.6 = (bf16[128,2048]{1,0:T(8,128)(2,1)S(1)}, bf16[128,2048]{1,0:T(8,128)(2,1)S(1)}, u32[]{:S(2)}, u32[]{:S(2)}) collective-permute-start(bf16[128,2048]{1,0:T(8,128)(2,1)S(1)} %get-tuple-element.51), channel_id=1, source_target_pairs={{0,2},{1,3},{2,0},{3,1},{4,5},{5,4},{6,7},{7,6},{8,10},{9,11},{10,... | collective-permute-start | bytes 1572872 | tf_op jit(solution)/shard_map/ppermute | solution.py:513
  21.9 9.3 %collective-permute-start.10 = (bf16[2,128,768]{2,1,0:T(8,128)(2,1)S(1)}, bf16[2,128,768]{2,1,0:T(8,128)(2,1)S(1)}, u32[]{:S(2)}, u32[]{:S(2)}) collective-permute-start(bf16[2,128,768]{2,1,0:T(8,128)(2,1)S(1)} %get-tuple-element.73), channel_id=1, source_target_pairs={{4,8},{8,4},{12,16},{16,12},{20,24},{24,20},{5,9},{9,5},{13,17},{1... | collective-permute-start | bytes 1179656 | tf_op jit(solution)/shard_map/ppermute | solution.py:552
  25.8 5.4 %collective-permute-start.11 = (bf16[2,128,768]{2,1,0:T(8,128)(2,1)S(1)}, bf16[2,128,768]{2,1,0:T(8,128)(2,1)S(1)}, u32[]{:S(2)}, u32[]{:S(2)}) collective-permute-start(bf16[2,128,768]{2,1,0:T(8,128)(2,1)S(1)} %get-tuple-element.74), channel_id=1, source_target_pairs={{0,4},{4,0},{8,12},{12,8},{16,20},{20,16},{24,28},{28,24},{1,5},{5... | collective-permute-start | bytes 1179656 | tf_op jit(solution)/shard_map/ppermute | solution.py:552
  26.7 1.7 %collective-permute-start.8 = (bf16[64,2048]{1,0:T(8,128)(2,1)S(1)}, bf16[64,2048]{1,0:T(8,128)(2,1)S(1)}, u32[]{:S(2)}, u32[]{:S(2)}) collective-permute-start(bf16[64,2048]{1,0:T(8,128)(2,1)S(1)} %get-tuple-element.67), channel_id=1, source_target_pairs={{0,4},{4,0},{8,12},{12,8},{16,20},{20,16},{24,28},{28,24},{1,5},{5... | collective-permute-start | bytes 786440 | tf_op jit(solution)/shard_map/ppermute | solution.py:553
  27.2 1.5 %collective-permute-start.9 = (bf16[64,2048]{1,0:T(8,128)(2,1)S(1)}, bf16[64,2048]{1,0:T(8,128)(2,1)S(1)}, u32[]{:S(2)}, u32[]{:S(2)}) collective-permute-start(bf16[64,2048]{1,0:T(8,128)(2,1)S(1)} %get-tuple-element.68), channel_id=1, source_target_pairs={{0,4},{4,0},{8,12},{12,8},{16,20},{20,16},{24,28},{28,24},{1,5},{5... | collective-permute-start | bytes 786440 | tf_op jit(solution)/shard_map/ppermute | solution.py:553

commit v14 on v13

--- a/solution.py
+++ b/solution.py
@@ -42,6 +42,10 @@
 
 def columns(chunk):
     return pl.ds(pl.multiple_of(chunk * PAIR, PAIR), PAIR)
+
+
+def head_columns(first, head):
+    return pl.ds(pl.multiple_of(first + head * HD, HD), HD)
 
 
 def call(kernel, name, out_shape, in_specs, out_specs, scratch, *args):
@@ -327,46 +331,6 @@
         prob_ref[block] = prob_of(joined(parts, 0), diagonal(q), open_keys)
 
 
-def turn_kernel(rows_ref, far_ref, *refs):
-    *w_refs, out_ref = refs
-    w = jnp.concatenate([ref[...] for ref in w_refs], axis=0)
-    out_ref[...] = three_blocks(w, rows_ref, far_ref)
-
-
-def three_blocks(w, rows_ref, far_ref):
-    parts = [dot(w, ref[...], NN).astype(BF16) for ref in (rows_ref, far_ref)]
-    return jnp.concatenate(parts, axis=1)
-
-
-def last_kernel(last, rows_ref, far_rows_ref, q_ref, prob_ref, mine_ref, *refs):
-    core, _ = place()
-    kv_refs = refs[:3]
-    near_both, far_both, *near_next = refs[3:7]
-    *w_refs, dq_ref, dk_ref, dv_ref = refs[7:]
-    tok = q_ref.shape[1]
-    w = jnp.concatenate([ref[...] for ref in w_refs], axis=0)
-    other = three_blocks(w, rows_ref, far_rows_ref)
-    turned = in_order(jnp.concatenate([mine_ref[...], other], axis=0), core)
-    probs, scores, queries, cotangents = [], [], [], []
-    blocks = last_parts(last, q_ref, near_both, far_both, near_next, kv_refs)
-    for block, (q, parts) in enumerate(blocks):
-        qd = diagonal(q)
-        d = diagonal_turned(*[half[:, block * tok : (block + 1) * tok] for half in turned])
-        prob = prob_ref[block]
-        prob_b = prob.astype(BF16)
-        d_score = score_grad(prob, prob_b, joined(parts, 1), d)
-        if block == 0:
-            dq_ref[...] = query_grad(d_score, joined(parts, 0), tok)
-        mine = slice(0, tok) if block == 0 else slice(tok, 2 * tok)
-        probs.append(prob_b[mine])
-        scores.append(d_score[mine])
-        queries.append(qd)
-        cotangents.append(d)
-    scores, probs = jnp.concatenate(scores, axis=1), jnp.concatenate(probs, axis=1)
-    dk_ref[...] = (dot(scores, jnp.concatenate(queries, axis=0), NN) * SCALE).astype(BF16)
-    dv_ref[...] = dot(probs, jnp.concatenate(cotangents, axis=1), NT).astype(BF16)
-
-
 def last_probs(last, q, limits, blocks, halo):
     tok = q.shape[1]
     depth = halo[1].shape[1] - 3 * PAIR
@@ -387,34 +351,60 @@
     )
 
 
-def last_heads(last, prob, far_rows, rows, q, blocks, halo, mine, other):
+def last_kernel(last, first, rows_ref, far_rows_ref, q_ref, prob_ref, *refs):
+    core, group = place()
+    head = core if first else 1 - core
+    kv_refs, (near_both, far_both, *near_next) = refs[:3], refs[3:7]
+    *w_refs, dq_ref, dk_ref, dv_ref = refs[7:]
+    tok, depth = q_ref.shape[1], rows_ref.shape[0]
+    w = jnp.concatenate([ref[...] for ref in w_refs], axis=0)
+    turned = [dot(w, ref[...], NN).astype(BF16) for ref in (rows_ref, far_rows_ref)]
+    turned = jnp.concatenate(turned, axis=1)
+    start = last(core, group) * PAIR
+    values_at = kv_refs[0].shape[1] // 2
+    own, near, far = (
+        [ref[:, head_columns(at, head)] for at in (start, start + values_at)] for ref in kv_refs
+    )
+    past_near = [ref[:, head_columns(depth, head)] for ref in near_next]
+    past_far = [far_both[:, head_columns(depth + i * PAIR, head)] for i in (1, 2)]
+    blocks = (
+        (q_ref[0, :, head_columns(start, head)], (own, near, far)),
+        (near_both[:, head_columns(depth, head)], (near, own, past_near)),
+        (far_both[:, head_columns(depth, head)], (far, own, past_far)),
+    )
+    probs, scores, queries = [], [], []
+    for block, (q, parts) in enumerate(blocks):
+        prob = prob_ref[block, :, head_columns(0, head)]
+        prob_b = prob.astype(BF16)
+        d = turned[:, block * tok : (block + 1) * tok]
+        d_score = score_grad(prob, prob_b, joined(parts, 1), d)
+        if block == 0:
+            dq_ref[...] = (dot(d_score, joined(parts, 0), TN) * SCALE).astype(BF16)
+        mine = slice(0, tok) if block == 0 else slice(tok, 2 * tok)
+        probs.append(prob_b[mine])
+        scores.append(d_score[mine])
+        queries.append(q)
+    scores, probs = jnp.concatenate(scores, axis=1), jnp.concatenate(probs, axis=1)
+    dk_ref[...] = (dot(scores, jnp.concatenate(queries, axis=0), NN) * SCALE).astype(BF16)
+    dv_ref[...] = dot(probs, turned, NT).astype(BF16)
+
+
+def last_head(last, first, prob, far_rows, rows, q, blocks, halo, w):
     tok = q.shape[1]
-    turned = call(
-        turn_kernel,
-        "turn",
-        jax.ShapeDtypeStruct((HD, 3 * tok), BF16),
-        [VMEM] * (2 + len(mine)),
-        VMEM,
-        [],
-        rows,
-        far_rows,
-        *mine,
-    )
     return call(
-        functools.partial(last_kernel, last),
-        "heads_last",
-        (jax.ShapeDtypeStruct((tok, PAIR), BF16),) * 3,
-        [VMEM] * (12 + len(other)),
+        functools.partial(last_kernel, last, first),
+        "heads_last" if first else "heads_end",
+        (jax.ShapeDtypeStruct((tok, HD), BF16),) * 3,
+        [VMEM] * (11 + len(w)),
         (VMEM,) * 3,
         [],
         rows,
         far_rows,
         q,
         prob,
-        turned,
         *blocks,
         *halo,
-        *other,
+        *w,
     )
 
 
@@ -422,11 +412,15 @@
     def __init__(self, stage, sems):
         self.stage, self.sems, self.copies = stage, sems, []
 
-    def put(self, out_ref, chunk, value):
+    def put(self, out_ref, chunk, value, head=None):
         at = len(self.copies)
-        self.stage[at] = value
-        target = out_ref.at[0, :, columns(chunk)]
-        copy = pltpu.make_async_copy(self.stage.at[at], target, self.sems.at[at])
+        if head is None:
+            held, target = self.stage.at[at], out_ref.at[0, :, columns(chunk)]
+        else:
+            held = self.stage.at[at, :, pl.ds(0, HD)]
+            target = out_ref.at[0, :, head_columns(chunk * PAIR, head)]
+        held[...] = value
+        copy = pltpu.make_async_copy(held, target, self.sems.at[at])
         copy.start()
         self.copies.append(copy)
 
@@ -440,62 +434,61 @@
 
 
 def settle_kernel(order, widths, *refs):
-    outs, to = refs[-5:-2], Columns(*refs[-2:])
+    out_ref, to = refs[-3], Columns(*refs[-2:])
     pairs = order(*place())
     for part, width in enumerate(widths):
         for step in range(width // PAIR):
             cols = slice(step * PAIR, (step + 1) * PAIR)
-            to.put(outs[0], pairs[part][step][0], refs[part][:, cols])
-    for out_ref, ref in zip(outs[1:], refs[len(widths) : -5]):
-        to.put(out_ref, pairs[-1][0][0], ref[...])
+            to.put(out_ref, pairs[part][step][0], refs[part][:, cols])
     to.wait()
 
 
-def settle(order, d_queries, last, shape):
+def settle(order, d_queries, shape):
     widths = tuple(x.shape[1] for x in d_queries)
-    count = sum(widths) // PAIR + len(last)
-    ins = [*d_queries, *last]
     return call(
         functools.partial(settle_kernel, order, widths),
         "settle",
-        (jax.ShapeDtypeStruct(shape, BF16),) * 3,
-        [VMEM] * len(ins),
-        (ANY,) * 3,
-        scratch_of(count, shape[1]),
-        *ins,
-    )
-
-
-def finish_kernel(order, widths, far, near, *refs):
-    outs, to = refs[-4:-2], Columns(*refs[-2:])
+        jax.ShapeDtypeStruct(shape, BF16),
+        [VMEM] * len(d_queries),
+        ANY,
+        scratch_of(sum(widths) // PAIR, shape[1]),
+        *d_queries,
+    )
+
+
+def finish_kernel(order, last, widths, n_last, far, near, *refs):
+    outs, to = refs[-5:-2], Columns(*refs[-2:])
     pairs = order(*place())
+    core, group = place()
+    for i, ref in enumerate(refs[len(widths) : len(widths) + n_last]):
+        to.put(outs[i % 3], last(core, group), ref[...], core if i < 3 else 1 - core)
     for part, width in enumerate(widths):
         own = refs[part]
         for step in range(width // PAIR):
             cols = slice(step * PAIR, (step + 1) * PAIR)
             chunk, message_slot = pairs[part][step]
             at = columns(message_slot)
-            for side, out_ref in enumerate(outs):
+            for side, out_ref in enumerate(outs[1:]):
                 total = own[side, :, cols] + near[side, :, at].astype(F32)
                 to.put(out_ref, chunk, (total + far[side, :, at].astype(F32)).astype(BF16))
     to.wait()
 
 
-def finish(order, far, near, parts, old):
-    shape = old[0].shape
+def finish(order, last, far, near, parts, third, d_queries):
+    shape = d_queries.shape
     widths = tuple(x.shape[2] for x in parts)
-    ins = [far, near, *parts]
+    ins = [far, near, *parts, *third]
     return pl.pallas_call(
-        functools.partial(finish_kernel, order, widths),
-        out_shape=(jax.ShapeDtypeStruct(shape, BF16),) * 2,
-        in_specs=[VMEM] * len(ins) + [ANY] * 2,
-        out_specs=(ANY,) * 2,
-        scratch_shapes=scratch_of(2 * sum(widths) // PAIR, shape[1]),
-        input_output_aliases={len(ins): 0, len(ins) + 1: 1},
+        functools.partial(finish_kernel, order, last, widths, len(third)),
+        out_shape=(jax.ShapeDtypeStruct(shape, BF16),) * 3,
+        in_specs=[VMEM] * len(ins) + [ANY],
+        out_specs=(ANY,) * 3,
+        scratch_shapes=scratch_of(2 * sum(widths) // PAIR + len(third), shape[1]),
+        input_output_aliases={len(ins): 0},
         cost_estimate=BRIEF,
         compiler_params=PARAMS,
         name="finish",
-    )(*ins, *old)
+    )(*ins, d_queries)
 
 
 def body(queries, keys, values, d_out, w_out, pattern, valid):
@@ -520,21 +513,21 @@
         got = cross(w_out, (1, 2))
         message = hand_on("hand_far", last, [d_out], [queries, near_kv])
         far_both, near_both = far(message), near(message)
-        early = got, near_kv, far_kv, limits, turned_rows(d_out)
-        got, near_kv, far_kv, limits, rows = lax.optimization_barrier(early)
+        rows = turned_rows(d_out)
+        ours = rows, queries, limits, (kv, near_kv, far_kv)
+        own = heads("heads_own", lambda core, group: [(group, 0, 0, ((0, 0, PAIR),), 0)], 3, [w_out], (), *ours)
+        early = got, near_kv, far_kv, limits, rows, own[0]
+        got, near_kv, far_kv, limits, rows, own_dq = lax.optimization_barrier(early)
         ours = rows, queries, limits, (kv, near_kv, far_kv)
         mine, *both = onward(last, got, far_kv)
         got_d = cross(mine, (2, 1))
         near_got = [near(x) for x in both]
         first = heads(
             "heads_first",
-            lambda core, group: [
-                (group, 0, 0, ((0, 0, PAIR),), 0),
-                (group ^ (1 + core), 1, 1 + core, ((1, 0, PAIR),), 0),
-            ],
+            lambda core, group: [(group ^ (1 + core), 0, 1 + core, ((0, 0, PAIR),), 0)],
             3,
-            [w_out, got],
-            (),
+            [got],
+            own[2:],
             *ours,
         )
         near_both, near_got, dq = lax.optimization_barrier((near_both, near_got, first[0]))
@@ -548,16 +541,18 @@
         )
         halo = near_both, far_both, *near_got
         prob, far_rows = last_probs(last, *ours[1:], halo)
-        got_d, halo, prob, second_dq = lax.optimization_barrier((got_d, halo, prob, second[0]))
+        order = lambda core, group: [
+            [(group, 0)],
+            [(group ^ (1 + core), 1 + core)],
+            [(group ^ (2 - core), 2 - core)],
+        ]
+        placed = settle(order, (own_dq, dq, second[0]), queries.shape)
+        got_d, halo, prob, placed = lax.optimization_barrier((got_d, halo, prob, placed))
         sums = far(second[3]), near(second[2])
-        third = last_heads(last, prob, far_rows, *ours[:2], ours[3], halo, [got_d], [near(x) for x in split(got_d)])
-        order = lambda core, group: [
-            [(group, 0), (group ^ (1 + core), 1 + core)],
-            [(group ^ (2 - core), 2 - core)],
-            [(group ^ 3, 0)],
-        ]
-        d_queries, *old = settle(order, (dq, second_dq, third[0]), third[1:], queries.shape)
-        return d_queries, *finish(order, *sums, (first[1], second[1]), old)
+        edge = [near(x) for x in split(got_d)]
+        known = prob, far_rows, *ours[:2], ours[3], halo
+        third = *last_head(last, True, *known, [got_d]), *last_head(last, False, *known, edge)
+        return finish(order, last, *sums, (own[1], first[1], second[1]), third, placed)
     full = lax.all_gather(w_out, "fsdp", axis=0, tiled=True)
     ours = turned_rows(d_out), queries, limits, (kv, near_kv, far_kv)
     steps = lambda core, group: [
@@ -565,8 +560,8 @@
     ]
     dq, own, to_core, to_far = heads("heads_all", steps, n_chunks, [full], (), *ours)
     order = lambda core, group: [[(i, i) for i in range(n_chunks)]]
-    d_queries, *old = settle(order, (dq,), (), queries.shape)
-    return d_queries, *finish(order, far(to_far), near(to_core), (own,), old)
+    placed = settle(order, (dq,), queries.shape)
+    return finish(order, last, far(to_far), near(to_core), (own,), (), placed)
 
 
 def solution(mesh):

time: 32.3 us -> 32 us (level)
  starting transfers between devices: 16.7 us -> 15.8 us
  Pallas kernels: 10.1 us -> 10.5 us
    ppermute x2, starting transfers between devices: 3.79 us -> 2.87 us  [cross(): return lax.ppermute(x, ('seq', 'fsdp'), pairs)]
    ppermute x2, waiting for transfers between devices: 1.02 us -> 0.46 us  [body(): edge = [near(x) for x in split(got_d)]]
    ppermute x2, waiting for transfers between devices: 0.01 us -> 0.5 us  [body(): near_got = [near(x) for x in both]]
    pallas_call x11 -> x12, Pallas kernels: 7.42 us -> 7.71 us  [call(): pl.pallas_call(kernel, out_shape=out_shape, in_specs=in_specs, out_specs=...]
  transfers between devices with their start and end apart: 12 -> 12, of which waited for: 4 -> 5; matrix products, arithmetic and copies ran while one was open for 0% -> 0% of each run, Pallas kernels for 29% -> 30%
where the time goes in v14:
time: 32 us; the launch traced here: 31.7 us
  starting transfers between devices  15.8 us (49%)
  Pallas kernels  10.5 us (33%)
  waiting for transfers between devices  4.54 us (14%)
  between operations  0.9 us (3%)
    pallas_call x12, Pallas kernels, call(): pl.pallas_call(kernel, out_shape=out_shape, in_specs=in_specs, out_specs=...  7.71 us
    ppermute x2, starting transfers between devices, body(): far_kv, near_kv = (far(kv), near(kv))  4.23 us
    ppermute x2, starting transfers between devices, body(): sums = (far(second[3]), near(second[2]))  3.84 us
    ppermute x2, starting transfers between devices, body(): far_both, near_both = (far(message), near(message))  3.66 us
    ppermute x2, starting transfers between devices, cross(): return lax.ppermute(x, ('seq', 'fsdp'), pairs)  2.87 us
    ppermute x2, waiting for transfers between devices, body(): far_kv, near_kv = (far(kv), near(kv))  2.82 us
    pallas_call x1, Pallas kernels, join(): pl.pallas_call(join_kernel, out_shape=jax.ShapeDtypeStruct(kv, BF16), in_...  1.84 us
    pallas_call x1, Pallas kernels, finish(): pl.pallas_call(functools.partial(finish_kernel, order, last, widths, len(...  0.92 us
  transfers between devices with their start and end apart: 12, of which 5 were waited for; matrix products, arithmetic and copies ran while one was open for 0% of the time, Pallas kernels for 30%

profile of v14, /device:TPU:1, one launch (start us, length us, event | category | flops | bytes accessed | tf_op | source)
XLA Modules:
  0.0 31.7 jit_solution(4256393844717773723)
XLA Ops:
  0.7 2.1 %collective-permute-start = (bf16[256,2048]{1,0:T(8,128)(2,1)}, bf16[256,2048]{1,0:T(8,128)(2,1)S(1)}, u32[]{:S(2)}, u32[]{:S(2)}) collective-permute-start(bf16[256,2048]{1,0:T(8,128)(2,1)} %refs_3_.1), channel_id=1, source_target_pairs={{0,1},{1,0},{2,3},{3,2},{4,6},{5,7},{6,4},{7,5},{8,9},{9,8},{10,11... | collective-permute-start | bytes 3145736 | tf_op jit(solution)/shard_map/ppermute | solution.py:506
  2.8 1.8 %join.1.refs_0_ = bf16[128,2048]{1,0:T(8,128)(2,1)} custom-call(bf16[1,128,1024]{2,1,0:T(8,128)(2,1)} %k_ref.1, bf16[1,128,1024]{2,1,0:T(8,128)(2,1)} %v_ref.1), custom_call_target="tpu_custom_call" | custom-call | flops 1 | bytes 1 | tf_op jit(solution)/shard_map/join/pallas_call | solution.py:121
  4.7 1.0 %collective-permute-start.1 = (bf16[128,2048]{1,0:T(8,128)(2,1)}, bf16[128,2048]{1,0:T(8,128)(2,1)S(1)}, u32[]{:S(2)}, u32[]{:S(2)}) collective-permute-start(bf16[128,2048]{1,0:T(8,128)(2,1)} %join.1.refs_0_), channel_id=1, source_target_pairs={{0,4},{4,0},{8,12},{12,8},{16,20},{20,16},{24,28},{28,24},{1,5},{5... | collective-permute-start | bytes 1572872 | tf_op jit(solution)/shard_map/ppermute | solution.py:511
  5.7 3.2 %collective-permute-start.2 = (bf16[128,2048]{1,0:T(8,128)(2,1)}, bf16[128,2048]{1,0:T(8,128)(2,1)S(1)}, u32[]{:S(2)}, u32[]{:S(2)}) collective-permute-start(bf16[128,2048]{1,0:T(8,128)(2,1)} %join.1.refs_0_), channel_id=1, source_target_pairs={{4,8},{8,4},{12,16},{16,12},{20,24},{24,20},{5,9},{9,5},{13,17},{1... | collective-permute-start | bytes 1572872 | tf_op jit(solution)/shard_map/ppermute | solution.py:511
  9.1 0.2 turned.1.dy_ref.rows_ref
  9.3 0.6 %limits.1.limit_ref = s32[16,256]{1,0:T(8,128)S(1)} custom-call(s32[4,8]{1,0:T(4,128)S(1)} %bitcast.1, s32[1,8]{1,0:T(1,128)S(1)} %copy-done.5), custom_call_target="tpu_custom_call" | custom-call | flops 1 | bytes 1 | tf_op jit(solution)/shard_map/limits/pallas_call | solution.py:52
  10.0 3.6 %collective-permute-start.8 = (bf16[128,2816]{1,0:T(8,128)(2,1)S(1)}, bf16[128,2816]{1,0:T(8,128)(2,1)S(1)}, u32[]{:S(2)}, u32[]{:S(2)}) collective-permute-start(bf16[128,2816]{1,0:T(8,128)(2,1)S(1)} %hand_far.1), channel_id=1, source_target_pairs={{4,8},{8,4},{12,16},{16,12},{20,24},{24,20},{5,9},{9,5},{13,17},{1... | collective-permute-start | bytes 2162696 | tf_op jit(solution)/shard_map/ppermute | solution.py:515
  13.6 2.8 %collective-permute-done.2.refs_2_.kv_ref = bf16[128,2048]{1,0:T(8,128)(2,1)S(1)} collective-permute-done((bf16[128,2048]{1,0:T(8,128)(2,1)}, bf16[128,2048]{1,0:T(8,128)(2,1)S(1)}, u32[]{:S(2)}, u32[]{:S(2)}) %collective-permute-start.2) | collective-permute-done | bytes 524320 | tf_op jit(solution)/shard_map/ppermute | solution.py:511
  16.4 1.1 %heads_own.1 = (bf16[128,256]{1,0:T(8,128)(2,1)S(1)}, f32[2,128,256]{2,1,0:T(8,128)S(1)}, bf16[2,128,768]{2,1,0:T(8,128)(2,1)S(1)}, bf16[2,128,768]{2,1,0:T(8,128)(2,1)S(1)}) custom-call(bf16[2048,128]{1,0:T(8,128)(2,1)S(1)} %turned.1.dy_ref.rows_ref, bf16[1,128,1024]{2,1,0:T(8,128)(2,1)S(1)} %copy-done.1, s32[16,256]{1,0:T(8,128)S(1)} %limits.1.limit_ref, ...), custom_call_target="tpu_custom_call" | custom-call | flops 1 | bytes 1 | tf_op jit(solution)/shard_map/heads_own/pallas_call | solution.py:52
  17.5 0.1 onward.1
  17.7 0.5 %collective-permute-start.5 = (bf16[128,2304]{1,0:T(8,128)(2,1)S(1)}, bf16[128,2304]{1,0:T(8,128)(2,1)S(1)}, u32[]{:S(2)}, u32[]{:S(2)}) collective-permute-start(bf16[128,2304]{1,0:T(8,128)(2,1)S(1)} %get-tuple-element.52), channel_id=1, source_target_pairs={{0,4},{4,0},{8,12},{12,8},{16,20},{20,16},{24,28},{28,24},{1,5},{5... | collective-permute-start | bytes 1769480 | tf_op jit(solution)/shard_map/ppermute | solution.py:524
  18.2 0.7 %collective-permute-start.9 = (bf16[128,2048]{1,0:T(8,128)(2,1)S(1)}, bf16[128,2048]{1,0:T(8,128)(2,1)S(1)}, u32[]{:S(2)}, u32[]{:S(2)}) collective-permute-start(bf16[128,2048]{1,0:T(8,128)(2,1)S(1)} %get-tuple-element.67), channel_id=1, source_target_pairs={{0,2},{1,3},{2,0},{3,1},{4,5},{5,4},{6,7},{7,6},{8,10},{9,11},{10,... | collective-permute-start | bytes 1572872 | tf_op jit(solution)/shard_map/ppermute | solution.py:506
  18.9 1.1 %heads_first.1 = (bf16[128,256]{1,0:T(8,128)(2,1)S(1)}, f32[2,128,256]{2,1,0:T(8,128)S(1)}, bf16[2,128,768]{2,1,0:T(8,128)(2,1)S(1)}, bf16[2,128,768]{2,1,0:T(8,128)(2,1)S(1)}) custom-call(bf16[2048,128]{1,0:T(8,128)(2,1)S(1)} %turned.1.dy_ref.rows_ref, bf16[1,128,1024]{2,1,0:T(8,128)(2,1)S(1)} %copy-done.1, s32[16,256]{1,0:T(8,128)S(1)} %limits.1.limit_ref, ...), custom_call_target="tpu_custom_call" | custom-call | flops 1 | bytes 1 | tf_op jit(solution)/shard_map/heads_first/pallas_call | solution.py:52
  20.0 0.5 %collective-permute-done.5.refs_4_.refs_6_ = bf16[128,2304]{1,0:T(8,128)(2,1)S(1)} collective-permute-done((bf16[128,2304]{1,0:T(8,128)(2,1)S(1)}, bf16[128,2304]{1,0:T(8,128)(2,1)S(1)}, u32[]{:S(2)}, u32[]{:S(2)}) %collective-permute-start.5) | collective-permute-done | bytes 589856 | tf_op jit(solution)/shard_map/ppermute | solution.py:524
  20.5 1.1 %heads_second.1 = (bf16[128,256]{1,0:T(8,128)(2,1)S(1)}, f32[2,128,256]{2,1,0:T(8,128)S(1)}, bf16[2,128,768]{2,1,0:T(8,128)(2,1)S(1)}, bf16[2,128,768]{2,1,0:T(8,128)(2,1)S(1)}) custom-call(bf16[2048,128]{1,0:T(8,128)(2,1)S(1)} %turned.1.dy_ref.rows_ref, bf16[1,128,1024]{2,1,0:T(8,128)(2,1)S(1)} %copy-done.1, s32[16,256]{1,0:T(8,128)S(1)} %limits.1.limit_ref, ...), custom_call_target="tpu_custom_call" | custom-call | flops 1 | bytes 1 | tf_op jit(solution)/shard_map/heads_second/pallas_call | solution.py:52
  21.6 3.8 %collective-permute-start.6 = (bf16[2,128,768]{2,1,0:T(8,128)(2,1)S(1)}, bf16[2,128,768]{2,1,0:T(8,128)(2,1)S(1)}, u32[]{:S(2)}, u32[]{:S(2)}) collective-permute-start(bf16[2,128,768]{2,1,0:T(8,128)(2,1)S(1)} %get-tuple-element.60), channel_id=1, source_target_pairs={{4,8},{8,4},{12,16},{16,12},{20,24},{24,20},{5,9},{9,5},{13,17},{1... | collective-permute-start | bytes 1179656 | tf_op jit(solution)/shard_map/ppermute | solution.py:551
  25.4 0.7 %settle.1.refs_9_ = bf16[1,128,1024]{2,1,0:T(8,128)(2,1)} custom-call(bf16[128,256]{1,0:T(8,128)(2,1)S(1)} %get-tuple-element.69.refs_0_, bf16[128,256]{1,0:T(8,128)(2,1)S(1)} %get-tuple-element.70.refs_1_, bf16[128,256]{1,0:T(8,128)(2,1)S(1)} %get-tuple-element.71.refs_2_), custom_call_target="tpu_custom_call" | custom-call | flops 1 | bytes 1 | tf_op jit(solution)/shard_map/settle/pallas_call | solution.py:52
  26.2 0.7 %probs_last.1 = (f32[3,384,256]{2,1,0:T(8,128)S(1)}, bf16[2048,256]{1,0:T(8,128)(2,1)S(1)}) custom-call(bf16[1,128,1024]{2,1,0:T(8,128)(2,1)S(1)} %copy-done.1, s32[16,256]{1,0:T(8,128)S(1)} %limits.1.limit_ref, bf16[128,2048]{1,0:T(8,128)(2,1)S(1)} %copy-done, bf16[128,2048]{1,0:T(8,128)(2,1)S(1)} %collective-permute-done.1.refs_1_.refs_2_, ...), custom_call_target="tpu_custom_call" | custom-call | flops 1 | bytes 1 | tf_op jit(solution)/shard_map/probs_last/pallas_call | solution.py:52
  27.0 0.6 %collective-permute-start.10 = (bf16[64,2048]{1,0:T(8,128)(2,1)S(1)}, bf16[64,2048]{1,0:T(8,128)(2,1)S(1)}, u32[]{:S(2)}, u32[]{:S(2)}) collective-permute-start(bf16[64,2048]{1,0:T(8,128)(2,1)S(1)} %get-tuple-element.81), channel_id=1, source_target_pairs={{0,4},{4,0},{8,12},{12,8},{16,20},{20,16},{24,28},{28,24},{1,5},{5... | collective-permute-start | bytes 786440 | tf_op jit(solution)/shard_map/ppermute | solution.py:552
  27.6 1.0 %heads_last.1 = (bf16[128,128]{1,0:T(8,128)(2,1)S(1)}, bf16[128,128]{1,0:T(8,128)(2,1)S(1)}, bf16[128,128]{1,0:T(8,128)(2,1)S(1)}) custom-call(bf16[2048,128]{1,0:T(8,128)(2,1)S(1)} %turned.1.dy_ref.rows_ref, bf16[2048,256]{1,0:T(8,128)(2,1)S(1)} %get-tuple-element.66.far_rows_ref, bf16[1,128,1024]{2,1,0:T(8,128)(2,1)S(1)} %copy-done.1, ...), custom_call_target="tpu_custom_call" | custom-call | flops 1 | bytes 1 | tf_op jit(solution)/shard_map/heads_last/pallas_call | solution.py:52
  28.7 0.4 %collective-permute-done.11.refs_8_ = bf16[64,2048]{1,0:T(8,128)(2,1)S(1)} collective-permute-done((bf16[64,2048]{1,0:T(8,128)(2,1)S(1)}, bf16[64,2048]{1,0:T(8,128)(2,1)S(1)}, u32[]{:S(2)}, u32[]{:S(2)}) %collective-permute-start.11) | collective-permute-done | bytes 262176 | tf_op jit(solution)/shard_map/ppermute | solution.py:552
  29.1 1.0 %heads_end.1 = (bf16[128,128]{1,0:T(8,128)(2,1)S(1)}, bf16[128,128]{1,0:T(8,128)(2,1)S(1)}, bf16[128,128]{1,0:T(8,128)(2,1)S(1)}) custom-call(bf16[2048,128]{1,0:T(8,128)(2,1)S(1)} %turned.1.dy_ref.rows_ref, bf16[2048,256]{1,0:T(8,128)(2,1)S(1)} %get-tuple-element.66.far_rows_ref, bf16[1,128,1024]{2,1,0:T(8,128)(2,1)S(1)} %copy-done.1, ...), custom_call_target="tpu_custom_call" | custom-call | flops 1 | bytes 1 | tf_op jit(solution)/shard_map/heads_end/pallas_call | solution.py:52
  30.1 0.7 %collective-permute-done.6.far = bf16[2,128,768]{2,1,0:T(8,128)(2,1)S(1)} collective-permute-done((bf16[2,128,768]{2,1,0:T(8,128)(2,1)S(1)}, bf16[2,128,768]{2,1,0:T(8,128)(2,1)S(1)}, u32[]{:S(2)}, u32[]{:S(2)}) %collective-permute-start.6) | collective-permute-done | bytes 393248 | tf_op jit(solution)/shard_map/ppermute | solution.py:551
  30.8 0.9 %finish.1 = (bf16[1,128,1024]{2,1,0:T(8,128)(2,1)}, bf16[1,128,1024]{2,1,0:T(8,128)(2,1)}, bf16[1,128,1024]{2,1,0:T(8,128)(2,1)}) custom-call(bf16[2,128,768]{2,1,0:T(8,128)(2,1)S(1)} %collective-permute-done.6.far, bf16[2,128,768]{2,1,0:T(8,128)(2,1)S(1)} %collective-permute-done.7.near, ...), custom_call_target="tpu_custom_call", output_to_operand_aliasing={{0}: (11, {})} | custom-call | flops 1 | bytes 1 | tf_op jit(solution)/shard_map/finish/pallas_call | solution.py:481
  (26 shorter events, 0.5 us)
Async XLA Ops:
  0.6 8.3 %copy-start.1 = (bf16[1,128,1024]{2,1,0:T(8,128)(2,1)S(1)}, bf16[1,128,1024]{2,1,0:T(8,128)(2,1)}, u32[]{:S(2)}) copy-start(bf16[1,128,1024]{2,1,0:T(8,128)(2,1)} %q_ref.11) | copy-start | bytes 786436
  0.6 8.3 %copy-start.2 = (bf16[1,128,2048]{2,1,0:T(8,128)(2,1)S(1)}, bf16[1,128,2048]{2,1,0:T(8,128)(2,1)}, u32[]{:S(2)}) copy-start(bf16[1,128,2048]{2,1,0:T(8,128)(2,1)} %refs_0_.1) | copy-start | bytes 1572868
  0.7 16.8 %collective-permute-start = (bf16[256,2048]{1,0:T(8,128)(2,1)}, bf16[256,2048]{1,0:T(8,128)(2,1)S(1)}, u32[]{:S(2)}, u32[]{:S(2)}) collective-permute-start(bf16[256,2048]{1,0:T(8,128)(2,1)} %refs_3_.1), channel_id=1, source_target_pairs={{0,1},{1,0},{2,3},{3,2},{4,6},{5,7},{6,4},{7,5},{8,9},{9,8},{10,11... | collective-permute-start | bytes 3145736 | tf_op jit(solution)/shard_map/ppermute | solution.py:506
  4.6 4.7 %copy-start.4 = (s32[8,4]{0,1:T(4,128)S(1)}, s32[8,4]{0,1:T(4,128)}, u32[]{:S(2)}) copy-start(s32[8,4]{0,1:T(4,128)} %param.12) | copy-start | bytes 388
  4.6 4.7 %copy-start.5 = (s32[1,8]{1,0:T(1,128)S(1)}, s32[1,8]{1,0:T(1,128)}, u32[]{:S(2)}) copy-start(s32[1,8]{1,0:T(1,128)} %val_ref.1) | copy-start | bytes 100
  4.7 11.7 %copy-start = (bf16[128,2048]{1,0:T(8,128)(2,1)S(1)}, bf16[128,2048]{1,0:T(8,128)(2,1)}, u32[]{:S(2)}) copy-start(bf16[128,2048]{1,0:T(8,128)(2,1)} %join.1.refs_0_) | copy-start | bytes 1572868
  4.7 11.7 %copy-start.3 = (bf16[256,2048]{1,0:T(8,128)(2,1)S(1)}, bf16[256,2048]{1,0:T(8,128)(2,1)}, u32[]{:S(2)}) copy-start(bf16[256,2048]{1,0:T(8,128)(2,1)} %refs_3_.1) | copy-start | bytes 3145732
  4.7 4.2 %collective-permute-start.1 = (bf16[128,2048]{1,0:T(8,128)(2,1)}, bf16[128,2048]{1,0:T(8,128)(2,1)S(1)}, u32[]{:S(2)}, u32[]{:S(2)}) collective-permute-start(bf16[128,2048]{1,0:T(8,128)(2,1)} %join.1.refs_0_), channel_id=1, source_target_pairs={{0,4},{4,0},{8,12},{12,8},{16,20},{20,16},{24,28},{28,24},{1,5},{5... | collective-permute-start | bytes 1572872 | tf_op jit(solution)/shard_map/ppermute | solution.py:511
  5.7 10.7 %collective-permute-start.2 = (bf16[128,2048]{1,0:T(8,128)(2,1)}, bf16[128,2048]{1,0:T(8,128)(2,1)S(1)}, u32[]{:S(2)}, u32[]{:S(2)}) collective-permute-start(bf16[128,2048]{1,0:T(8,128)(2,1)} %join.1.refs_0_), channel_id=1, source_target_pairs={{4,8},{8,4},{12,16},{16,12},{20,24},{24,20},{5,9},{9,5},{13,17},{1... | collective-permute-start | bytes 1572872 | tf_op jit(solution)/shard_map/ppermute | solution.py:511
  9.0 11.0 %collective-permute-start.3 = (bf16[128,2816]{1,0:T(8,128)(2,1)S(1)}, bf16[128,2816]{1,0:T(8,128)(2,1)S(1)}, u32[]{:S(2)}, u32[]{:S(2)}) collective-permute-start(bf16[128,2816]{1,0:T(8,128)(2,1)S(1)} %hand_far.1), channel_id=1, source_target_pairs={{0,4},{4,0},{8,12},{12,8},{16,20},{20,16},{24,28},{28,24},{1,5},{5... | collective-permute-start | bytes 2162696 | tf_op jit(solution)/shard_map/ppermute | solution.py:515
  10.0 16.2 %collective-permute-start.8 = (bf16[128,2816]{1,0:T(8,128)(2,1)S(1)}, bf16[128,2816]{1,0:T(8,128)(2,1)S(1)}, u32[]{:S(2)}, u32[]{:S(2)}) collective-permute-start(bf16[128,2816]{1,0:T(8,128)(2,1)S(1)} %hand_far.1), channel_id=1, source_target_pairs={{4,8},{8,4},{12,16},{16,12},{20,24},{24,20},{5,9},{9,5},{13,17},{1... | collective-permute-start | bytes 2162696 | tf_op jit(solution)/shard_map/ppermute | solution.py:515
  17.6 2.4 %collective-permute-start.4 = (bf16[128,2304]{1,0:T(8,128)(2,1)S(1)}, bf16[128,2304]{1,0:T(8,128)(2,1)S(1)}, u32[]{:S(2)}, u32[]{:S(2)}) collective-permute-start(bf16[128,2304]{1,0:T(8,128)(2,1)S(1)} %get-tuple-element.51), channel_id=1, source_target_pairs={{0,4},{4,0},{8,12},{12,8},{16,20},{20,16},{24,28},{28,24},{1,5},{5... | collective-permute-start | bytes 1769480 | tf_op jit(solution)/shard_map/ppermute | solution.py:524
  17.7 2.8 %collective-permute-start.5 = (bf16[128,2304]{1,0:T(8,128)(2,1)S(1)}, bf16[128,2304]{1,0:T(8,128)(2,1)S(1)}, u32[]{:S(2)}, u32[]{:S(2)}) collective-permute-start(bf16[128,2304]{1,0:T(8,128)(2,1)S(1)} %get-tuple-element.52), channel_id=1, source_target_pairs={{0,4},{4,0},{8,12},{12,8},{16,20},{20,16},{24,28},{28,24},{1,5},{5... | collective-permute-start | bytes 1769480 | tf_op jit(solution)/shard_map/ppermute | solution.py:524
  18.2 8.8 %collective-permute-start.9 = (bf16[128,2048]{1,0:T(8,128)(2,1)S(1)}, bf16[128,2048]{1,0:T(8,128)(2,1)S(1)}, u32[]{:S(2)}, u32[]{:S(2)}) collective-permute-start(bf16[128,2048]{1,0:T(8,128)(2,1)S(1)} %get-tuple-element.67), channel_id=1, source_target_pairs={{0,2},{1,3},{2,0},{3,1},{4,5},{5,4},{6,7},{7,6},{8,10},{9,11},{10,... | collective-permute-start | bytes 1572872 | tf_op jit(solution)/shard_map/ppermute | solution.py:506
  21.6 9.2 %collective-permute-start.6 = (bf16[2,128,768]{2,1,0:T(8,128)(2,1)S(1)}, bf16[2,128,768]{2,1,0:T(8,128)(2,1)S(1)}, u32[]{:S(2)}, u32[]{:S(2)}) collective-permute-start(bf16[2,128,768]{2,1,0:T(8,128)(2,1)S(1)} %get-tuple-element.60), channel_id=1, source_target_pairs={{4,8},{8,4},{12,16},{16,12},{20,24},{24,20},{5,9},{9,5},{13,17},{1... | collective-permute-start | bytes 1179656 | tf_op jit(solution)/shard_map/ppermute | solution.py:551
  25.4 5.4 %collective-permute-start.7 = (bf16[2,128,768]{2,1,0:T(8,128)(2,1)S(1)}, bf16[2,128,768]{2,1,0:T(8,128)(2,1)S(1)}, u32[]{:S(2)}, u32[]{:S(2)}) collective-permute-start(bf16[2,128,768]{2,1,0:T(8,128)(2,1)S(1)} %get-tuple-element.61), channel_id=1, source_target_pairs={{0,4},{4,0},{8,12},{12,8},{16,20},{20,16},{24,28},{28,24},{1,5},{5... | collective-permute-start | bytes 1179656 | tf_op jit(solution)/shard_map/ppermute | solution.py:551
  27.0 1.7 %collective-permute-start.10 = (bf16[64,2048]{1,0:T(8,128)(2,1)S(1)}, bf16[64,2048]{1,0:T(8,128)(2,1)S(1)}, u32[]{:S(2)}, u32[]{:S(2)}) collective-permute-start(bf16[64,2048]{1,0:T(8,128)(2,1)S(1)} %get-tuple-element.81), channel_id=1, source_target_pairs={{0,4},{4,0},{8,12},{12,8},{16,20},{20,16},{24,28},{28,24},{1,5},{5... | collective-permute-start | bytes 786440 | tf_op jit(solution)/shard_map/ppermute | solution.py:552
  27.5 1.5 %collective-permute-start.11 = (bf16[64,2048]{1,0:T(8,128)(2,1)S(1)}, bf16[64,2048]{1,0:T(8,128)(2,1)S(1)}, u32[]{:S(2)}, u32[]{:S(2)}) collective-permute-start(bf16[64,2048]{1,0:T(8,128)(2,1)S(1)} %get-tuple-element.82), channel_id=1, source_target_pairs={{0,4},{4,0},{8,12},{12,8},{16,20},{20,16},{24,28},{28,24},{1,5},{5... | collective-permute-start | bytes 786440 | tf_op jit(solution)/shard_map/ppermute | solution.py:552

commit v15 on v14

--- a/solution.py
+++ b/solution.py
@@ -9,19 +9,16 @@
 
 HD = 128
 PAIR = 2 * HD
-PIECE = 32
 BRIEF = pl.CostEstimate(flops=1, bytes_accessed=1, transcendentals=0)
 F32 = jnp.float32
 BF16 = jnp.bfloat16
 NT = (((1,), (1,)), ((), ()))
 NN = (((1,), (0,)), ((), ()))
 TN = (((0,), (0,)), ((), ()))
-HBM = pl.BlockSpec(memory_space=pltpu.HBM)
 ANY = pl.BlockSpec(memory_space=pl.ANY)
 VMEM = pl.BlockSpec(memory_space=pltpu.VMEM)
 SMEM = pl.BlockSpec(memory_space=pltpu.SMEM)
 PARAMS = pltpu.CompilerParams(vmem_limit_bytes=40 * 2**20)
-WIDE = pltpu.CompilerParams(vmem_limit_bytes=58 * 2**20)
 SCALE = HD ** (-0.5)
 
 
@@ -97,40 +94,16 @@
     return call(limits_kernel, "limits", shape, [SMEM] * 2, VMEM, [], pattern.T, valid)
 
 
-def join_kernel(k_ref, v_ref, kv_ref, kv, sems):
-    tok, width = k_ref.shape[1:]
-    arrivals, moves = [], []
-    for side, ref in enumerate((k_ref, v_ref)):
-        for row in range(0, tok, PIECE):
-            rows, i = pl.ds(row, PIECE), len(moves)
-            at = (rows, pl.ds(side * width, width))
-            arrivals.append(pltpu.make_async_copy(ref.at[0, rows, :], kv.at[at], sems.at[0, i]))
-            moves.append(pltpu.make_async_copy(kv.at[at], kv_ref.at[at], sems.at[1, i]))
-    for copy in arrivals:
-        copy.start()
-    for arrival, move in zip(arrivals, moves):
-        arrival.wait()
-        move.start()
-    for move in moves:
-        move.wait()
+def join_kernel(k_ref, v_ref, kv_ref):
+    width = k_ref.shape[2]
+    kv_ref[:, :width] = k_ref[0]
+    kv_ref[:, width:] = v_ref[0]
 
 
 def join(keys, values):
     tok, width = keys.shape[1:]
-    kv = (tok, 2 * width)
-    return pl.pallas_call(
-        join_kernel,
-        out_shape=jax.ShapeDtypeStruct(kv, BF16),
-        in_specs=[HBM] * 2,
-        out_specs=ANY,
-        scratch_shapes=[
-            pltpu.VMEM(kv, BF16),
-            pltpu.SemaphoreType.DMA((2, 2 * (tok // PIECE))),
-        ],
-        cost_estimate=BRIEF,
-        compiler_params=WIDE,
-        name="join",
-    )(keys, values)
+    shape = jax.ShapeDtypeStruct((tok, 2 * width), BF16)
+    return call(join_kernel, "join", shape, [VMEM] * 2, VMEM, [], keys, values)
 
 
 def hand_on_kernel(last, n_whole, *refs):
@@ -157,13 +130,16 @@
     return call(kernel, name, shape, [VMEM] * (len(whole) + len(cut)), VMEM, [], *whole, *cut)
 
 
-def turned_kernel(dy_ref, out_ref):
+def turned_kernel(dy_ref, w_ref, out_ref, d_ref):
     out_ref[...] = dy_ref[0].T
-
-
-def turned_rows(d_out):
-    shape = jax.ShapeDtypeStruct(d_out.shape[:0:-1], BF16)
-    return call(turned_kernel, "turned", shape, [VMEM], VMEM, [], d_out)
+    d_ref[...] = dot(w_ref[...], out_ref[...], NN).astype(BF16)
+
+
+def turned_rows(d_out, w_out):
+    depth, tok = d_out.shape[:0:-1]
+    shapes = (depth, tok), (w_out.shape[0], tok)
+    shapes = tuple(jax.ShapeDtypeStruct(shape, BF16) for shape in shapes)
+    return call(turned_kernel, "turned", shapes, [VMEM] * 2, (VMEM,) * 2, [], d_out, w_out)
 
 
 def onward_kernel(last, w_ref, kv_ref, mine_ref, *both_refs):
@@ -261,7 +237,9 @@
     for chunk, slot, message_slot, pieces, lead in steps(core, group):
         cols, dest, message_dest = columns(chunk), columns(slot), columns(message_slot)
         w = jnp.concatenate([w_refs[i][row : row + rows, :depth] for i, row, rows in pieces], axis=0)
-        d = diagonal_turned(*in_order(dot(w, dy_ref[...], NN).astype(BF16), lead))
+        if w_refs[pieces[0][0]].shape[1] >= depth:
+            w = dot(w, dy_ref[...], NN).astype(BF16)
+        d = diagonal_turned(*in_order(w, lead))
         qd = diagonal(q_ref[0, :, cols])
         k, v = stacked(k_refs, cols), stacked(k_refs, columns(chunk + values_at))
         prob = prob_of(k, qd, open_keys)
@@ -513,9 +491,9 @@
         got = cross(w_out, (1, 2))
         message = hand_on("hand_far", last, [d_out], [queries, near_kv])
         far_both, near_both = far(message), near(message)
-        rows = turned_rows(d_out)
+        rows, d_own = turned_rows(d_out, w_out)
         ours = rows, queries, limits, (kv, near_kv, far_kv)
-        own = heads("heads_own", lambda core, group: [(group, 0, 0, ((0, 0, PAIR),), 0)], 3, [w_out], (), *ours)
+        own = heads("heads_own", lambda core, group: [(group, 0, 0, ((0, 0, PAIR),), 0)], 3, [d_own], (), *ours)
         early = got, near_kv, far_kv, limits, rows, own[0]
         got, near_kv, far_kv, limits, rows, own_dq = lax.optimization_barrier(early)
         ours = rows, queries, limits, (kv, near_kv, far_kv)
@@ -554,7 +532,7 @@
         third = *last_head(last, True, *known, [got_d]), *last_head(last, False, *known, edge)
         return finish(order, last, *sums, (own[1], first[1], second[1]), third, placed)
     full = lax.all_gather(w_out, "fsdp", axis=0, tiled=True)
-    ours = turned_rows(d_out), queries, limits, (kv, near_kv, far_kv)
+    ours = turned_rows(d_out, w_out)[0], queries, limits, (kv, near_kv, far_kv)
     steps = lambda core, group: [
         (i, i, i, ((0, i * PAIR, PAIR),), 0) for i in range(n_chunks)
     ]

time: 32 us -> 31.6 us (0.988)
  local copies, waits for them, and re-layouts: 0.03 us -> 1.97 us
  Pallas kernels: 10.5 us -> 8.77 us
  waiting for transfers between devices: 4.54 us -> 3.89 us
    unnamed x12 -> x14, local copies, waits for them, and re-layouts: 0.03 us -> 1.97 us
    pallas_call x1 -> x0, Pallas kernels: 1.84 us -> none  [join(): pl.pallas_call(join_kernel, out_shape=jax.ShapeDtypeStruct(kv, BF16), in_...]
    ppermute x2, waiting for transfers between devices: 2.82 us -> 2.35 us  [body(): far_kv, near_kv = (far(kv), near(kv))]
    pallas_call x12 -> x13, Pallas kernels: 7.71 us -> 7.85 us  [call(): pl.pallas_call(kernel, out_shape=out_shape, in_specs=in_specs, out_specs=...]
  transfers between devices with their start and end apart: 12 -> 12, of which waited for: 5 -> 5; matrix products, arithmetic and copies ran while one was open for 0% -> 0% of each run, Pallas kernels for 30% -> 25%
where the time goes in v15:
time: 31.6 us; the launch traced here: 31.4 us
  starting transfers between devices  15.8 us (50%)
  Pallas kernels  8.77 us (28%)
  waiting for transfers between devices  3.89 us (12%)
  local copies, waits for them, and re-layouts  1.97 us (6%)
  between operations  0.88 us (3%)
    pallas_call x13, Pallas kernels, call(): pl.pallas_call(kernel, out_shape=out_shape, in_specs=in_specs, out_specs=...  7.85 us
    ppermute x2, starting transfers between devices, body(): far_kv, near_kv = (far(kv), near(kv))  4.23 us
    ppermute x2, starting transfers between devices, body(): sums = (far(second[3]), near(second[2]))  3.74 us
    ppermute x2, starting transfers between devices, body(): far_both, near_both = (far(message), near(message))  3.62 us
    ppermute x2, starting transfers between devices, cross(): return lax.ppermute(x, ('seq', 'fsdp'), pairs)  2.96 us
    ppermute x2, waiting for transfers between devices, body(): far_kv, near_kv = (far(kv), near(kv))  2.35 us
    unnamed x14, local copies, waits for them, and re-layouts  1.97 us
    pallas_call x1, Pallas kernels, finish(): pl.pallas_call(functools.partial(finish_kernel, order, last, widths, len(...  0.92 us
  transfers between devices with their start and end apart: 12, of which 5 were waited for; matrix products, arithmetic and copies ran while one was open for 0% of the time, Pallas kernels for 25%

profile of v15, /device:TPU:1, one launch (start us, length us, event | category | flops | bytes accessed | tf_op | source)
XLA Modules:
  0.0 31.4 jit_solution(12975819602887980626)
XLA Ops:
  0.7 2.1 %collective-permute-start = (bf16[256,2048]{1,0:T(8,128)(2,1)}, bf16[256,2048]{1,0:T(8,128)(2,1)S(1)}, u32[]{:S(2)}, u32[]{:S(2)}) collective-permute-start(bf16[256,2048]{1,0:T(8,128)(2,1)} %w_ref.1), channel_id=1, source_target_pairs={{0,1},{1,0},{2,3},{3,2},{4,6},{5,7},{6,4},{7,5},{8,9},{9,8},{10,11... | collective-permute-start | bytes 3145736 | tf_op jit(solution)/shard_map/ppermute | solution.py:484
  2.8 0.9 %copy-done.3 = bf16[1,128,1024]{2,1,0:T(8,128)(2,1)S(1)} copy-done((bf16[1,128,1024]{2,1,0:T(8,128)(2,1)S(1)}, bf16[1,128,1024]{2,1,0:T(8,128)(2,1)}, u32[]{:S(2)}) %copy-start.3) | copy-done | bytes 262168
  3.7 0.9 %copy-done.4 = bf16[1,128,1024]{2,1,0:T(8,128)(2,1)S(1)} copy-done((bf16[1,128,1024]{2,1,0:T(8,128)(2,1)S(1)}, bf16[1,128,1024]{2,1,0:T(8,128)(2,1)}, u32[]{:S(2)}) %copy-start.4) | copy-done | bytes 262168
  4.7 1.0 %collective-permute-start.1 = (bf16[128,2048]{1,0:T(8,128)(2,1)S(1)}, bf16[128,2048]{1,0:T(8,128)(2,1)S(1)}, u32[]{:S(2)}, u32[]{:S(2)}) collective-permute-start(bf16[128,2048]{1,0:T(8,128)(2,1)S(1)} %join.1.refs_0_), channel_id=1, source_target_pairs={{0,4},{4,0},{8,12},{12,8},{16,20},{20,16},{24,28},{28,24},{1,5},{5... | collective-permute-start | bytes 1572872 | tf_op jit(solution)/shard_map/ppermute | solution.py:489
  5.7 3.2 %collective-permute-start.2 = (bf16[128,2048]{1,0:T(8,128)(2,1)S(1)}, bf16[128,2048]{1,0:T(8,128)(2,1)S(1)}, u32[]{:S(2)}, u32[]{:S(2)}) collective-permute-start(bf16[128,2048]{1,0:T(8,128)(2,1)S(1)} %join.1.refs_0_), channel_id=1, source_target_pairs={{4,8},{8,4},{12,16},{16,12},{20,24},{24,20},{5,9},{9,5},{13,17},{1... | collective-permute-start | bytes 1572872 | tf_op jit(solution)/shard_map/ppermute | solution.py:489
  9.2 0.5 %turned.1 = (bf16[2048,128]{1,0:T(8,128)(2,1)S(1)}, bf16[256,128]{1,0:T(8,128)(2,1)S(1)}) custom-call(bf16[1,128,2048]{2,1,0:T(8,128)(2,1)S(1)} %copy-done.1, bf16[256,2048]{1,0:T(8,128)(2,1)S(1)} %copy-done.2), custom_call_target="tpu_custom_call" | custom-call | flops 1 | bytes 1 | tf_op jit(solution)/shard_map/turned/pallas_call | solution.py:49
  9.8 0.6 %limits.1.limit_ref = s32[16,256]{1,0:T(8,128)S(1)} custom-call(s32[4,8]{1,0:T(4,128)S(1)} %bitcast.1, s32[1,8]{1,0:T(1,128)S(1)} %copy-done.6), custom_call_target="tpu_custom_call" | custom-call | flops 1 | bytes 1 | tf_op jit(solution)/shard_map/limits/pallas_call | solution.py:49
  10.4 3.5 %collective-permute-start.8 = (bf16[128,2816]{1,0:T(8,128)(2,1)S(1)}, bf16[128,2816]{1,0:T(8,128)(2,1)S(1)}, u32[]{:S(2)}, u32[]{:S(2)}) collective-permute-start(bf16[128,2816]{1,0:T(8,128)(2,1)S(1)} %hand_far.1), channel_id=1, source_target_pairs={{4,8},{8,4},{12,16},{16,12},{20,24},{24,20},{5,9},{9,5},{13,17},{1... | collective-permute-start | bytes 2162696 | tf_op jit(solution)/shard_map/ppermute | solution.py:493
  14.0 2.3 %collective-permute-done.2.refs_2_.kv_ref = bf16[128,2048]{1,0:T(8,128)(2,1)S(1)} collective-permute-done((bf16[128,2048]{1,0:T(8,128)(2,1)S(1)}, bf16[128,2048]{1,0:T(8,128)(2,1)S(1)}, u32[]{:S(2)}, u32[]{:S(2)}) %collective-permute-start.2) | collective-permute-done | bytes 524320 | tf_op jit(solution)/shard_map/ppermute | solution.py:489
  16.3 0.8 %heads_own.1 = (bf16[128,256]{1,0:T(8,128)(2,1)S(1)}, f32[2,128,256]{2,1,0:T(8,128)S(1)}, bf16[2,128,768]{2,1,0:T(8,128)(2,1)S(1)}, bf16[2,128,768]{2,1,0:T(8,128)(2,1)S(1)}) custom-call(bf16[2048,128]{1,0:T(8,128)(2,1)S(1)} %get-tuple-element.50.dy_ref.rows_ref, bf16[1,128,1024]{2,1,0:T(8,128)(2,1)S(1)} %copy-done, s32[16,256]{1,0:T(8,128)S(1)} %limits.1.limit_ref, ...), custom_call_target="tpu_custom_call" | custom-call | flops 1 | bytes 1 | tf_op jit(solution)/shard_map/heads_own/pallas_call | solution.py:49
  17.4 0.5 %collective-permute-start.5 = (bf16[128,2304]{1,0:T(8,128)(2,1)S(1)}, bf16[128,2304]{1,0:T(8,128)(2,1)S(1)}, u32[]{:S(2)}, u32[]{:S(2)}) collective-permute-start(bf16[128,2304]{1,0:T(8,128)(2,1)S(1)} %get-tuple-element.56), channel_id=1, source_target_pairs={{0,4},{4,0},{8,12},{12,8},{16,20},{20,16},{24,28},{28,24},{1,5},{5... | collective-permute-start | bytes 1769480 | tf_op jit(solution)/shard_map/ppermute | solution.py:502
  17.9 0.8 %collective-permute-start.9 = (bf16[128,2048]{1,0:T(8,128)(2,1)S(1)}, bf16[128,2048]{1,0:T(8,128)(2,1)S(1)}, u32[]{:S(2)}, u32[]{:S(2)}) collective-permute-start(bf16[128,2048]{1,0:T(8,128)(2,1)S(1)} %get-tuple-element.71), channel_id=1, source_target_pairs={{0,2},{1,3},{2,0},{3,1},{4,5},{5,4},{6,7},{7,6},{8,10},{9,11},{10,... | collective-permute-start | bytes 1572872 | tf_op jit(solution)/shard_map/ppermute | solution.py:484
  18.7 1.1 %heads_first.1 = (bf16[128,256]{1,0:T(8,128)(2,1)S(1)}, f32[2,128,256]{2,1,0:T(8,128)S(1)}, bf16[2,128,768]{2,1,0:T(8,128)(2,1)S(1)}, bf16[2,128,768]{2,1,0:T(8,128)(2,1)S(1)}) custom-call(bf16[2048,128]{1,0:T(8,128)(2,1)S(1)} %get-tuple-element.50.dy_ref.rows_ref, bf16[1,128,1024]{2,1,0:T(8,128)(2,1)S(1)} %copy-done, s32[16,256]{1,0:T(8,128)S(1)} %limits.1.limit_ref, ...), custom_call_target="tpu_custom_call" | custom-call | flops 1 | bytes 1 | tf_op jit(solution)/shard_map/heads_first/pallas_call | solution.py:49
  19.8 0.4 %collective-permute-done.5.refs_4_.refs_6_ = bf16[128,2304]{1,0:T(8,128)(2,1)S(1)} collective-permute-done((bf16[128,2304]{1,0:T(8,128)(2,1)S(1)}, bf16[128,2304]{1,0:T(8,128)(2,1)S(1)}, u32[]{:S(2)}, u32[]{:S(2)}) %collective-permute-start.5) | collective-permute-done | bytes 589856 | tf_op jit(solution)/shard_map/ppermute | solution.py:502
  20.2 1.1 %heads_second.1 = (bf16[128,256]{1,0:T(8,128)(2,1)S(1)}, f32[2,128,256]{2,1,0:T(8,128)S(1)}, bf16[2,128,768]{2,1,0:T(8,128)(2,1)S(1)}, bf16[2,128,768]{2,1,0:T(8,128)(2,1)S(1)}) custom-call(bf16[2048,128]{1,0:T(8,128)(2,1)S(1)} %get-tuple-element.50.dy_ref.rows_ref, bf16[1,128,1024]{2,1,0:T(8,128)(2,1)S(1)} %copy-done, s32[16,256]{1,0:T(8,128)S(1)} %limits.1.limit_ref, ...), custom_call_target="tpu_custom_call" | custom-call | flops 1 | bytes 1 | tf_op jit(solution)/shard_map/heads_second/pallas_call | solution.py:49
  21.3 3.7 %collective-permute-start.6 = (bf16[2,128,768]{2,1,0:T(8,128)(2,1)S(1)}, bf16[2,128,768]{2,1,0:T(8,128)(2,1)S(1)}, u32[]{:S(2)}, u32[]{:S(2)}) collective-permute-start(bf16[2,128,768]{2,1,0:T(8,128)(2,1)S(1)} %get-tuple-element.64), channel_id=1, source_target_pairs={{4,8},{8,4},{12,16},{16,12},{20,24},{24,20},{5,9},{9,5},{13,17},{1... | collective-permute-start | bytes 1179656 | tf_op jit(solution)/shard_map/ppermute | solution.py:529
  25.1 0.7 %settle.1.refs_9_ = bf16[1,128,1024]{2,1,0:T(8,128)(2,1)} custom-call(bf16[128,256]{1,0:T(8,128)(2,1)S(1)} %get-tuple-element.73.refs_0_, bf16[128,256]{1,0:T(8,128)(2,1)S(1)} %get-tuple-element.74.refs_1_, bf16[128,256]{1,0:T(8,128)(2,1)S(1)} %get-tuple-element.75.refs_2_), custom_call_target="tpu_custom_call" | custom-call | flops 1 | bytes 1 | tf_op jit(solution)/shard_map/settle/pallas_call | solution.py:49
  25.8 0.7 %probs_last.1 = (f32[3,384,256]{2,1,0:T(8,128)S(1)}, bf16[2048,256]{1,0:T(8,128)(2,1)S(1)}) custom-call(bf16[1,128,1024]{2,1,0:T(8,128)(2,1)S(1)} %copy-done, s32[16,256]{1,0:T(8,128)S(1)} %limits.1.limit_ref, bf16[128,2048]{1,0:T(8,128)(2,1)S(1)} %join.1.refs_0_, bf16[128,2048]{1,0:T(8,128)(2,1)S(1)} %collective-permute-done.1.refs_1_.refs_2_, ...), custom_call_target="tpu_custom_call" | custom-call | flops 1 | bytes 1 | tf_op jit(solution)/shard_map/probs_last/pallas_call | solution.py:49
  26.6 0.6 %collective-permute-start.10 = (bf16[64,2048]{1,0:T(8,128)(2,1)S(1)}, bf16[64,2048]{1,0:T(8,128)(2,1)S(1)}, u32[]{:S(2)}, u32[]{:S(2)}) collective-permute-start(bf16[64,2048]{1,0:T(8,128)(2,1)S(1)} %get-tuple-element.85), channel_id=1, source_target_pairs={{0,4},{4,0},{8,12},{12,8},{16,20},{20,16},{24,28},{28,24},{1,5},{5... | collective-permute-start | bytes 786440 | tf_op jit(solution)/shard_map/ppermute | solution.py:530
  27.3 1.0 %heads_last.1 = (bf16[128,128]{1,0:T(8,128)(2,1)S(1)}, bf16[128,128]{1,0:T(8,128)(2,1)S(1)}, bf16[128,128]{1,0:T(8,128)(2,1)S(1)}) custom-call(bf16[2048,128]{1,0:T(8,128)(2,1)S(1)} %get-tuple-element.50.dy_ref.rows_ref, bf16[2048,256]{1,0:T(8,128)(2,1)S(1)} %get-tuple-element.70.far_rows_ref, bf16[1,128,1024]{2,1,0:T(8,128)(2,1)S(1)} %copy-done, ...), custom_call_target="tpu_custom_call" | custom-call | flops 1 | bytes 1 | tf_op jit(solution)/shard_map/heads_last/pallas_call | solution.py:49
  28.4 0.4 %collective-permute-done.11.refs_8_ = bf16[64,2048]{1,0:T(8,128)(2,1)S(1)} collective-permute-done((bf16[64,2048]{1,0:T(8,128)(2,1)S(1)}, bf16[64,2048]{1,0:T(8,128)(2,1)S(1)}, u32[]{:S(2)}, u32[]{:S(2)}) %collective-permute-start.11) | collective-permute-done | bytes 262176 | tf_op jit(solution)/shard_map/ppermute | solution.py:530
  28.8 1.0 %heads_end.1 = (bf16[128,128]{1,0:T(8,128)(2,1)S(1)}, bf16[128,128]{1,0:T(8,128)(2,1)S(1)}, bf16[128,128]{1,0:T(8,128)(2,1)S(1)}) custom-call(bf16[2048,128]{1,0:T(8,128)(2,1)S(1)} %get-tuple-element.50.dy_ref.rows_ref, bf16[2048,256]{1,0:T(8,128)(2,1)S(1)} %get-tuple-element.70.far_rows_ref, bf16[1,128,1024]{2,1,0:T(8,128)(2,1)S(1)} %copy-done, ...), custom_call_target="tpu_custom_call" | custom-call | flops 1 | bytes 1 | tf_op jit(solution)/shard_map/heads_end/pallas_call | solution.py:49
  29.8 0.7 %collective-permute-done.6.far = bf16[2,128,768]{2,1,0:T(8,128)(2,1)S(1)} collective-permute-done((bf16[2,128,768]{2,1,0:T(8,128)(2,1)S(1)}, bf16[2,128,768]{2,1,0:T(8,128)(2,1)S(1)}, u32[]{:S(2)}, u32[]{:S(2)}) %collective-permute-start.6) | collective-permute-done | bytes 393248 | tf_op jit(solution)/shard_map/ppermute | solution.py:529
  30.4 0.9 %finish.1 = (bf16[1,128,1024]{2,1,0:T(8,128)(2,1)}, bf16[1,128,1024]{2,1,0:T(8,128)(2,1)}, bf16[1,128,1024]{2,1,0:T(8,128)(2,1)}) custom-call(bf16[2,128,768]{2,1,0:T(8,128)(2,1)S(1)} %collective-permute-done.6.far, bf16[2,128,768]{2,1,0:T(8,128)(2,1)S(1)} %collective-permute-done.7.near, ...), custom_call_target="tpu_custom_call", output_to_operand_aliasing={{0}: (11, {})} | custom-call | flops 1 | bytes 1 | tf_op jit(solution)/shard_map/finish/pallas_call | solution.py:459
  (28 shorter events, 0.7 us)
Async XLA Ops:
  0.6 8.4 %copy-start = (bf16[1,128,1024]{2,1,0:T(8,128)(2,1)S(1)}, bf16[1,128,1024]{2,1,0:T(8,128)(2,1)}, u32[]{:S(2)}) copy-start(bf16[1,128,1024]{2,1,0:T(8,128)(2,1)} %q_ref.11) | copy-start | bytes 786436
  0.6 8.4 %copy-start.1 = (bf16[1,128,2048]{2,1,0:T(8,128)(2,1)S(1)}, bf16[1,128,2048]{2,1,0:T(8,128)(2,1)}, u32[]{:S(2)}) copy-start(bf16[1,128,2048]{2,1,0:T(8,128)(2,1)} %refs_0_.1) | copy-start | bytes 1572868
  0.7 16.5 %collective-permute-start = (bf16[256,2048]{1,0:T(8,128)(2,1)}, bf16[256,2048]{1,0:T(8,128)(2,1)S(1)}, u32[]{:S(2)}, u32[]{:S(2)}) collective-permute-start(bf16[256,2048]{1,0:T(8,128)(2,1)} %w_ref.1), channel_id=1, source_target_pairs={{0,1},{1,0},{2,3},{3,2},{4,6},{5,7},{6,4},{7,5},{8,9},{9,8},{10,11... | collective-permute-start | bytes 3145736 | tf_op jit(solution)/shard_map/ppermute | solution.py:484
  2.8 0.9 %copy-start.3 = (bf16[1,128,1024]{2,1,0:T(8,128)(2,1)S(1)}, bf16[1,128,1024]{2,1,0:T(8,128)(2,1)}, u32[]{:S(2)}) copy-start(bf16[1,128,1024]{2,1,0:T(8,128)(2,1)} %k_ref.1) | copy-start | bytes 786436
  3.7 0.9 %copy-start.4 = (bf16[1,128,1024]{2,1,0:T(8,128)(2,1)S(1)}, bf16[1,128,1024]{2,1,0:T(8,128)(2,1)}, u32[]{:S(2)}) copy-start(bf16[1,128,1024]{2,1,0:T(8,128)(2,1)} %v_ref.1) | copy-start | bytes 786436
  4.7 4.5 %copy-start.2 = (bf16[256,2048]{1,0:T(8,128)(2,1)S(1)}, bf16[256,2048]{1,0:T(8,128)(2,1)}, u32[]{:S(2)}) copy-start(bf16[256,2048]{1,0:T(8,128)(2,1)} %w_ref.1) | copy-start | bytes 3145732
  4.7 4.2 %collective-permute-start.1 = (bf16[128,2048]{1,0:T(8,128)(2,1)S(1)}, bf16[128,2048]{1,0:T(8,128)(2,1)S(1)}, u32[]{:S(2)}, u32[]{:S(2)}) collective-permute-start(bf16[128,2048]{1,0:T(8,128)(2,1)S(1)} %join.1.refs_0_), channel_id=1, source_target_pairs={{0,4},{4,0},{8,12},{12,8},{16,20},{20,16},{24,28},{28,24},{1,5},{5... | collective-permute-start | bytes 1572872 | tf_op jit(solution)/shard_map/ppermute | solution.py:489
  5.7 10.6 %collective-permute-start.2 = (bf16[128,2048]{1,0:T(8,128)(2,1)S(1)}, bf16[128,2048]{1,0:T(8,128)(2,1)S(1)}, u32[]{:S(2)}, u32[]{:S(2)}) collective-permute-start(bf16[128,2048]{1,0:T(8,128)(2,1)S(1)} %join.1.refs_0_), channel_id=1, source_target_pairs={{4,8},{8,4},{12,16},{16,12},{20,24},{24,20},{5,9},{9,5},{13,17},{1... | collective-permute-start | bytes 1572872 | tf_op jit(solution)/shard_map/ppermute | solution.py:489
  9.1 0.7 %copy-start.5 = (s32[8,4]{0,1:T(4,128)S(1)}, s32[8,4]{0,1:T(4,128)}, u32[]{:S(2)}) copy-start(s32[8,4]{0,1:T(4,128)} %param.12) | copy-start | bytes 388
  9.1 0.7 %copy-start.6 = (s32[1,8]{1,0:T(1,128)S(1)}, s32[1,8]{1,0:T(1,128)}, u32[]{:S(2)}) copy-start(s32[1,8]{1,0:T(1,128)} %val_ref.1) | copy-start | bytes 100
  9.1 10.7 %collective-permute-start.3 = (bf16[128,2816]{1,0:T(8,128)(2,1)S(1)}, bf16[128,2816]{1,0:T(8,128)(2,1)S(1)}, u32[]{:S(2)}, u32[]{:S(2)}) collective-permute-start(bf16[128,2816]{1,0:T(8,128)(2,1)S(1)} %hand_far.1), channel_id=1, source_target_pairs={{0,4},{4,0},{8,12},{12,8},{16,20},{20,16},{24,28},{28,24},{1,5},{5... | collective-permute-start | bytes 2162696 | tf_op jit(solution)/shard_map/ppermute | solution.py:493
  10.4 15.4 %collective-permute-start.8 = (bf16[128,2816]{1,0:T(8,128)(2,1)S(1)}, bf16[128,2816]{1,0:T(8,128)(2,1)S(1)}, u32[]{:S(2)}, u32[]{:S(2)}) collective-permute-start(bf16[128,2816]{1,0:T(8,128)(2,1)S(1)} %hand_far.1), channel_id=1, source_target_pairs={{4,8},{8,4},{12,16},{16,12},{20,24},{24,20},{5,9},{9,5},{13,17},{1... | collective-permute-start | bytes 2162696 | tf_op jit(solution)/shard_map/ppermute | solution.py:493
  17.3 2.5 %collective-permute-start.4 = (bf16[128,2304]{1,0:T(8,128)(2,1)S(1)}, bf16[128,2304]{1,0:T(8,128)(2,1)S(1)}, u32[]{:S(2)}, u32[]{:S(2)}) collective-permute-start(bf16[128,2304]{1,0:T(8,128)(2,1)S(1)} %get-tuple-element.55), channel_id=1, source_target_pairs={{0,4},{4,0},{8,12},{12,8},{16,20},{20,16},{24,28},{28,24},{1,5},{5... | collective-permute-start | bytes 1769480 | tf_op jit(solution)/shard_map/ppermute | solution.py:502
  17.4 2.8 %collective-permute-start.5 = (bf16[128,2304]{1,0:T(8,128)(2,1)S(1)}, bf16[128,2304]{1,0:T(8,128)(2,1)S(1)}, u32[]{:S(2)}, u32[]{:S(2)}) collective-permute-start(bf16[128,2304]{1,0:T(8,128)(2,1)S(1)} %get-tuple-element.56), channel_id=1, source_target_pairs={{0,4},{4,0},{8,12},{12,8},{16,20},{20,16},{24,28},{28,24},{1,5},{5... | collective-permute-start | bytes 1769480 | tf_op jit(solution)/shard_map/ppermute | solution.py:502
  17.9 8.7 %collective-permute-start.9 = (bf16[128,2048]{1,0:T(8,128)(2,1)S(1)}, bf16[128,2048]{1,0:T(8,128)(2,1)S(1)}, u32[]{:S(2)}, u32[]{:S(2)}) collective-permute-start(bf16[128,2048]{1,0:T(8,128)(2,1)S(1)} %get-tuple-element.71), channel_id=1, source_target_pairs={{0,2},{1,3},{2,0},{3,1},{4,5},{5,4},{6,7},{7,6},{8,10},{9,11},{10,... | collective-permute-start | bytes 1572872 | tf_op jit(solution)/shard_map/ppermute | solution.py:484
  21.3 9.1 %collective-permute-start.6 = (bf16[2,128,768]{2,1,0:T(8,128)(2,1)S(1)}, bf16[2,128,768]{2,1,0:T(8,128)(2,1)S(1)}, u32[]{:S(2)}, u32[]{:S(2)}) collective-permute-start(bf16[2,128,768]{2,1,0:T(8,128)(2,1)S(1)} %get-tuple-element.64), channel_id=1, source_target_pairs={{4,8},{8,4},{12,16},{16,12},{20,24},{24,20},{5,9},{9,5},{13,17},{1... | collective-permute-start | bytes 1179656 | tf_op jit(solution)/shard_map/ppermute | solution.py:529
  25.0 5.4 %collective-permute-start.7 = (bf16[2,128,768]{2,1,0:T(8,128)(2,1)S(1)}, bf16[2,128,768]{2,1,0:T(8,128)(2,1)S(1)}, u32[]{:S(2)}, u32[]{:S(2)}) collective-permute-start(bf16[2,128,768]{2,1,0:T(8,128)(2,1)S(1)} %get-tuple-element.65), channel_id=1, source_target_pairs={{0,4},{4,0},{8,12},{12,8},{16,20},{20,16},{24,28},{28,24},{1,5},{5... | collective-permute-start | bytes 1179656 | tf_op jit(solution)/shard_map/ppermute | solution.py:529
  26.6 1.8 %collective-permute-start.10 = (bf16[64,2048]{1,0:T(8,128)(2,1)S(1)}, bf16[64,2048]{1,0:T(8,128)(2,1)S(1)}, u32[]{:S(2)}, u32[]{:S(2)}) collective-permute-start(bf16[64,2048]{1,0:T(8,128)(2,1)S(1)} %get-tuple-element.85), channel_id=1, source_target_pairs={{0,4},{4,0},{8,12},{12,8},{16,20},{20,16},{24,28},{28,24},{1,5},{5... | collective-permute-start | bytes 786440 | tf_op jit(solution)/shard_map/ppermute | solution.py:530
  27.2 1.5 %collective-permute-start.11 = (bf16[64,2048]{1,0:T(8,128)(2,1)S(1)}, bf16[64,2048]{1,0:T(8,128)(2,1)S(1)}, u32[]{:S(2)}, u32[]{:S(2)}) collective-permute-start(bf16[64,2048]{1,0:T(8,128)(2,1)S(1)} %get-tuple-element.86), channel_id=1, source_target_pairs={{0,4},{4,0},{8,12},{12,8},{16,20},{20,16},{24,28},{28,24},{1,5},{5... | collective-permute-start | bytes 786440 | tf_op jit(solution)/shard_map/ppermute | solution.py:530

commit v16 on v15

--- a/solution.py
+++ b/solution.py
@@ -298,7 +298,7 @@
 
 def probs_kernel(last, q_ref, limit_ref, *refs):
     *kv_refs, near_both, far_both = refs[:5]
-    near_next, prob_ref, turned_ref = refs[5:7], refs[7], refs[8]
+    near_next, (prob_ref, attended_ref, turned_ref) = refs[5:7], refs[7:]
     tok = q_ref.shape[1]
     depth = turned_ref.shape[0]
     turned_ref[:, :tok] = near_both[:, :depth].T
@@ -306,7 +306,10 @@
     blocks = last_parts(last, q_ref, near_both, far_both, near_next, kv_refs)
     for block, (q, parts) in enumerate(blocks):
         open_keys = key_mask(limit_ref, tok, 3 * block, 3)
-        prob_ref[block] = prob_of(joined(parts, 0), diagonal(q), open_keys)
+        prob = prob_of(joined(parts, 0), diagonal(q), open_keys)
+        prob_ref[block] = prob
+        out = dot(joined(parts, 1), prob.astype(BF16), TN)
+        attended_ref[block] = jnp.concatenate([out[:HD, :tok], out[HD:, tok:]], axis=1)
 
 
 def last_probs(last, q, limits, blocks, halo):
@@ -317,10 +320,11 @@
         "probs_last",
         (
             jax.ShapeDtypeStruct((3, 3 * tok, PAIR), F32),
+            jax.ShapeDtypeStruct((3, HD, 2 * tok), F32),
             jax.ShapeDtypeStruct((depth, 2 * tok), BF16),
         ),
         [VMEM] * 9,
-        (VMEM,) * 2,
+        (VMEM,) * 3,
         [],
         q,
         limits,
@@ -329,7 +333,7 @@
     )
 
 
-def last_kernel(last, first, rows_ref, far_rows_ref, q_ref, prob_ref, *refs):
+def last_kernel(last, first, rows_ref, far_rows_ref, q_ref, prob_ref, attended_ref, *refs):
     core, group = place()
     head = core if first else 1 - core
     kv_refs, (near_both, far_both, *near_next) = refs[:3], refs[3:7]
@@ -352,34 +356,38 @@
     )
     probs, scores, queries = [], [], []
     for block, (q, parts) in enumerate(blocks):
-        prob = prob_ref[block, :, head_columns(0, head)]
-        prob_b = prob.astype(BF16)
         d = turned[:, block * tok : (block + 1) * tok]
-        d_score = score_grad(prob, prob_b, joined(parts, 1), d)
+        lanes = head_columns(0, head)
+        delta = jnp.sum(d.astype(F32) * attended_ref[block, :, lanes], axis=0, keepdims=True)
+        if block == 0:
+            prob, v = prob_ref[block, :, lanes], joined(parts, 1)
+        else:
+            prob, v = prob_ref[block, tok : 2 * tok, lanes], parts[1][1]
+        d_score = (prob * (dot(v, d, NN) - delta)).astype(BF16)
         if block == 0:
             dq_ref[...] = (dot(d_score, joined(parts, 0), TN) * SCALE).astype(BF16)
-        mine = slice(0, tok) if block == 0 else slice(tok, 2 * tok)
-        probs.append(prob_b[mine])
-        scores.append(d_score[mine])
+        probs.append(prob[:tok].astype(BF16))
+        scores.append(d_score[:tok])
         queries.append(q)
     scores, probs = jnp.concatenate(scores, axis=1), jnp.concatenate(probs, axis=1)
     dk_ref[...] = (dot(scores, jnp.concatenate(queries, axis=0), NN) * SCALE).astype(BF16)
     dv_ref[...] = dot(probs, turned, NT).astype(BF16)
 
 
-def last_head(last, first, prob, far_rows, rows, q, blocks, halo, w):
+def last_head(last, first, prob, attended, far_rows, rows, q, blocks, halo, w):
     tok = q.shape[1]
     return call(
         functools.partial(last_kernel, last, first),
         "heads_last" if first else "heads_end",
         (jax.ShapeDtypeStruct((tok, HD), BF16),) * 3,
-        [VMEM] * (11 + len(w)),
+        [VMEM] * (12 + len(w)),
         (VMEM,) * 3,
         [],
         rows,
         far_rows,
         q,
         prob,
+        attended,
         *blocks,
         *halo,
         *w,
@@ -518,7 +526,7 @@
             *ours,
         )
         halo = near_both, far_both, *near_got
-        prob, far_rows = last_probs(last, *ours[1:], halo)
+        prob, attended, far_rows = last_probs(last, *ours[1:], halo)
         order = lambda core, group: [
             [(group, 0)],
             [(group ^ (1 + core), 1 + core)],
@@ -528,7 +536,7 @@
         got_d, halo, prob, placed = lax.optimization_barrier((got_d, halo, prob, placed))
         sums = far(second[3]), near(second[2])
         edge = [near(x) for x in split(got_d)]
-        known = prob, far_rows, *ours[:2], ours[3], halo
+        known = prob, attended, far_rows, *ours[:2], ours[3], halo
         third = *last_head(last, True, *known, [got_d]), *last_head(last, False, *known, edge)
         return finish(order, last, *sums, (own[1], first[1], second[1]), third, placed)
     full = lax.all_gather(w_out, "fsdp", axis=0, tiled=True)

time: 31.6 us -> 31.6 us (level)
  transfers between devices with their start and end apart: 12 -> 12, of which waited for: 5 -> 5; matrix products, arithmetic and copies ran while one was open for 0% -> 0% of each run, Pallas kernels for 25% -> 26%
where the time goes in v16:
time: 31.6 us; the launch traced here: 31.4 us
  starting transfers between devices  15.8 us (50%)
  Pallas kernels  8.95 us (28%)
  waiting for transfers between devices  3.8 us (12%)
  local copies, waits for them, and re-layouts  1.97 us (6%)
  between operations  0.88 us (3%)
    pallas_call x13, Pallas kernels, call(): pl.pallas_call(kernel, out_shape=out_shape, in_specs=in_specs, out_specs=...  8.03 us
    ppermute x2, starting transfers between devices, body(): far_kv, near_kv = (far(kv), near(kv))  4.23 us
    ppermute x2, starting transfers between devices, body(): sums = (far(second[3]), near(second[2]))  3.74 us
    ppermute x2, starting transfers between devices, body(): far_both, near_both = (far(message), near(message))  3.62 us
    ppermute x2, starting transfers between devices, cross(): return lax.ppermute(x, ('seq', 'fsdp'), pairs)  2.96 us
    ppermute x2, waiting for transfers between devices, body(): far_kv, near_kv = (far(kv), near(kv))  2.35 us
    unnamed x14, local copies, waits for them, and re-layouts  1.97 us
    pallas_call x1, Pallas kernels, finish(): pl.pallas_call(functools.partial(finish_kernel, order, last, widths, len(...  0.92 us
  transfers between devices with their start and end apart: 12, of which 5 were waited for; matrix products, arithmetic and copies ran while one was open for 0% of the time, Pallas kernels for 26%

profile of v16, /device:TPU:1, one launch (start us, length us, event | category | flops | bytes accessed | tf_op | source)
XLA Modules:
  0.0 31.4 jit_solution(4148900712424468078)
XLA Ops:
  0.7 2.1 %collective-permute-start = (bf16[256,2048]{1,0:T(8,128)(2,1)}, bf16[256,2048]{1,0:T(8,128)(2,1)S(1)}, u32[]{:S(2)}, u32[]{:S(2)}) collective-permute-start(bf16[256,2048]{1,0:T(8,128)(2,1)} %w_ref.1), channel_id=1, source_target_pairs={{0,1},{1,0},{2,3},{3,2},{4,6},{5,7},{6,4},{7,5},{8,9},{9,8},{10,11... | collective-permute-start | bytes 3145736 | tf_op jit(solution)/shard_map/ppermute | solution.py:492
  2.8 0.9 %copy-done.3 = bf16[1,128,1024]{2,1,0:T(8,128)(2,1)S(1)} copy-done((bf16[1,128,1024]{2,1,0:T(8,128)(2,1)S(1)}, bf16[1,128,1024]{2,1,0:T(8,128)(2,1)}, u32[]{:S(2)}) %copy-start.3) | copy-done | bytes 262168
  3.7 0.9 %copy-done.4 = bf16[1,128,1024]{2,1,0:T(8,128)(2,1)S(1)} copy-done((bf16[1,128,1024]{2,1,0:T(8,128)(2,1)S(1)}, bf16[1,128,1024]{2,1,0:T(8,128)(2,1)}, u32[]{:S(2)}) %copy-start.4) | copy-done | bytes 262168
  4.7 1.0 %collective-permute-start.1 = (bf16[128,2048]{1,0:T(8,128)(2,1)S(1)}, bf16[128,2048]{1,0:T(8,128)(2,1)S(1)}, u32[]{:S(2)}, u32[]{:S(2)}) collective-permute-start(bf16[128,2048]{1,0:T(8,128)(2,1)S(1)} %join.1.refs_0_), channel_id=1, source_target_pairs={{0,4},{4,0},{8,12},{12,8},{16,20},{20,16},{24,28},{28,24},{1,5},{5... | collective-permute-start | bytes 1572872 | tf_op jit(solution)/shard_map/ppermute | solution.py:497
  5.7 3.2 %collective-permute-start.2 = (bf16[128,2048]{1,0:T(8,128)(2,1)S(1)}, bf16[128,2048]{1,0:T(8,128)(2,1)S(1)}, u32[]{:S(2)}, u32[]{:S(2)}) collective-permute-start(bf16[128,2048]{1,0:T(8,128)(2,1)S(1)} %join.1.refs_0_), channel_id=1, source_target_pairs={{4,8},{8,4},{12,16},{16,12},{20,24},{24,20},{5,9},{9,5},{13,17},{1... | collective-permute-start | bytes 1572872 | tf_op jit(solution)/shard_map/ppermute | solution.py:497
  9.2 0.5 %turned.1 = (bf16[2048,128]{1,0:T(8,128)(2,1)S(1)}, bf16[256,128]{1,0:T(8,128)(2,1)S(1)}) custom-call(bf16[1,128,2048]{2,1,0:T(8,128)(2,1)S(1)} %copy-done.1, bf16[256,2048]{1,0:T(8,128)(2,1)S(1)} %copy-done.2), custom_call_target="tpu_custom_call" | custom-call | flops 1 | bytes 1 | tf_op jit(solution)/shard_map/turned/pallas_call | solution.py:49
  9.8 0.6 %limits.1.limit_ref = s32[16,256]{1,0:T(8,128)S(1)} custom-call(s32[4,8]{1,0:T(4,128)S(1)} %bitcast.1, s32[1,8]{1,0:T(1,128)S(1)} %copy-done.6), custom_call_target="tpu_custom_call" | custom-call | flops 1 | bytes 1 | tf_op jit(solution)/shard_map/limits/pallas_call | solution.py:49
  10.4 3.5 %collective-permute-start.8 = (bf16[128,2816]{1,0:T(8,128)(2,1)S(1)}, bf16[128,2816]{1,0:T(8,128)(2,1)S(1)}, u32[]{:S(2)}, u32[]{:S(2)}) collective-permute-start(bf16[128,2816]{1,0:T(8,128)(2,1)S(1)} %hand_far.1), channel_id=1, source_target_pairs={{4,8},{8,4},{12,16},{16,12},{20,24},{24,20},{5,9},{9,5},{13,17},{1... | collective-permute-start | bytes 2162696 | tf_op jit(solution)/shard_map/ppermute | solution.py:501
  14.0 2.3 %collective-permute-done.2.refs_2_.kv_ref = bf16[128,2048]{1,0:T(8,128)(2,1)S(1)} collective-permute-done((bf16[128,2048]{1,0:T(8,128)(2,1)S(1)}, bf16[128,2048]{1,0:T(8,128)(2,1)S(1)}, u32[]{:S(2)}, u32[]{:S(2)}) %collective-permute-start.2) | collective-permute-done | bytes 524320 | tf_op jit(solution)/shard_map/ppermute | solution.py:497
  16.3 0.8 %heads_own.1 = (bf16[128,256]{1,0:T(8,128)(2,1)S(1)}, f32[2,128,256]{2,1,0:T(8,128)S(1)}, bf16[2,128,768]{2,1,0:T(8,128)(2,1)S(1)}, bf16[2,128,768]{2,1,0:T(8,128)(2,1)S(1)}) custom-call(bf16[2048,128]{1,0:T(8,128)(2,1)S(1)} %get-tuple-element.51.dy_ref.rows_ref, bf16[1,128,1024]{2,1,0:T(8,128)(2,1)S(1)} %copy-done, s32[16,256]{1,0:T(8,128)S(1)} %limits.1.limit_ref, ...), custom_call_target="tpu_custom_call" | custom-call | flops 1 | bytes 1 | tf_op jit(solution)/shard_map/heads_own/pallas_call | solution.py:49
  17.4 0.5 %collective-permute-start.5 = (bf16[128,2304]{1,0:T(8,128)(2,1)S(1)}, bf16[128,2304]{1,0:T(8,128)(2,1)S(1)}, u32[]{:S(2)}, u32[]{:S(2)}) collective-permute-start(bf16[128,2304]{1,0:T(8,128)(2,1)S(1)} %get-tuple-element.57), channel_id=1, source_target_pairs={{0,4},{4,0},{8,12},{12,8},{16,20},{20,16},{24,28},{28,24},{1,5},{5... | collective-permute-start | bytes 1769480 | tf_op jit(solution)/shard_map/ppermute | solution.py:510
  17.9 0.8 %collective-permute-start.9 = (bf16[128,2048]{1,0:T(8,128)(2,1)S(1)}, bf16[128,2048]{1,0:T(8,128)(2,1)S(1)}, u32[]{:S(2)}, u32[]{:S(2)}) collective-permute-start(bf16[128,2048]{1,0:T(8,128)(2,1)S(1)} %get-tuple-element.72), channel_id=1, source_target_pairs={{0,2},{1,3},{2,0},{3,1},{4,5},{5,4},{6,7},{7,6},{8,10},{9,11},{10,... | collective-permute-start | bytes 1572872 | tf_op jit(solution)/shard_map/ppermute | solution.py:492
  18.7 1.1 %heads_first.1 = (bf16[128,256]{1,0:T(8,128)(2,1)S(1)}, f32[2,128,256]{2,1,0:T(8,128)S(1)}, bf16[2,128,768]{2,1,0:T(8,128)(2,1)S(1)}, bf16[2,128,768]{2,1,0:T(8,128)(2,1)S(1)}) custom-call(bf16[2048,128]{1,0:T(8,128)(2,1)S(1)} %get-tuple-element.51.dy_ref.rows_ref, bf16[1,128,1024]{2,1,0:T(8,128)(2,1)S(1)} %copy-done, s32[16,256]{1,0:T(8,128)S(1)} %limits.1.limit_ref, ...), custom_call_target="tpu_custom_call" | custom-call | flops 1 | bytes 1 | tf_op jit(solution)/shard_map/heads_first/pallas_call | solution.py:49
  19.8 0.4 %collective-permute-done.5.refs_4_.refs_6_ = bf16[128,2304]{1,0:T(8,128)(2,1)S(1)} collective-permute-done((bf16[128,2304]{1,0:T(8,128)(2,1)S(1)}, bf16[128,2304]{1,0:T(8,128)(2,1)S(1)}, u32[]{:S(2)}, u32[]{:S(2)}) %collective-permute-start.5) | collective-permute-done | bytes 589856 | tf_op jit(solution)/shard_map/ppermute | solution.py:510
  20.2 1.1 %heads_second.1 = (bf16[128,256]{1,0:T(8,128)(2,1)S(1)}, f32[2,128,256]{2,1,0:T(8,128)S(1)}, bf16[2,128,768]{2,1,0:T(8,128)(2,1)S(1)}, bf16[2,128,768]{2,1,0:T(8,128)(2,1)S(1)}) custom-call(bf16[2048,128]{1,0:T(8,128)(2,1)S(1)} %get-tuple-element.51.dy_ref.rows_ref, bf16[1,128,1024]{2,1,0:T(8,128)(2,1)S(1)} %copy-done, s32[16,256]{1,0:T(8,128)S(1)} %limits.1.limit_ref, ...), custom_call_target="tpu_custom_call" | custom-call | flops 1 | bytes 1 | tf_op jit(solution)/shard_map/heads_second/pallas_call | solution.py:49
  21.3 3.7 %collective-permute-start.6 = (bf16[2,128,768]{2,1,0:T(8,128)(2,1)S(1)}, bf16[2,128,768]{2,1,0:T(8,128)(2,1)S(1)}, u32[]{:S(2)}, u32[]{:S(2)}) collective-permute-start(bf16[2,128,768]{2,1,0:T(8,128)(2,1)S(1)} %get-tuple-element.65), channel_id=1, source_target_pairs={{4,8},{8,4},{12,16},{16,12},{20,24},{24,20},{5,9},{9,5},{13,17},{1... | collective-permute-start | bytes 1179656 | tf_op jit(solution)/shard_map/ppermute | solution.py:537
  25.1 0.7 %settle.1.refs_9_ = bf16[1,128,1024]{2,1,0:T(8,128)(2,1)} custom-call(bf16[128,256]{1,0:T(8,128)(2,1)S(1)} %get-tuple-element.74.refs_0_, bf16[128,256]{1,0:T(8,128)(2,1)S(1)} %get-tuple-element.75.refs_1_, bf16[128,256]{1,0:T(8,128)(2,1)S(1)} %get-tuple-element.76.refs_2_), custom_call_target="tpu_custom_call" | custom-call | flops 1 | bytes 1 | tf_op jit(solution)/shard_map/settle/pallas_call | solution.py:49
  25.8 1.0 %probs_last.1 = (f32[3,384,256]{2,1,0:T(8,128)S(1)}, f32[3,128,256]{2,1,0:T(8,128)S(1)}, bf16[2048,256]{1,0:T(8,128)(2,1)S(1)}) custom-call(bf16[1,128,1024]{2,1,0:T(8,128)(2,1)S(1)} %copy-done, s32[16,256]{1,0:T(8,128)S(1)} %limits.1.limit_ref, bf16[128,2048]{1,0:T(8,128)(2,1)S(1)} %join.1.refs_0_, ...), custom_call_target="tpu_custom_call" | custom-call | flops 1 | bytes 1 | tf_op jit(solution)/shard_map/probs_last/pallas_call | solution.py:49
  26.9 0.6 %collective-permute-start.10 = (bf16[64,2048]{1,0:T(8,128)(2,1)S(1)}, bf16[64,2048]{1,0:T(8,128)(2,1)S(1)}, u32[]{:S(2)}, u32[]{:S(2)}) collective-permute-start(bf16[64,2048]{1,0:T(8,128)(2,1)S(1)} %get-tuple-element.87), channel_id=1, source_target_pairs={{0,4},{4,0},{8,12},{12,8},{16,20},{20,16},{24,28},{28,24},{1,5},{5... | collective-permute-start | bytes 786440 | tf_op jit(solution)/shard_map/ppermute | solution.py:538
  27.5 0.9 %heads_last.1 = (bf16[128,128]{1,0:T(8,128)(2,1)S(1)}, bf16[128,128]{1,0:T(8,128)(2,1)S(1)}, bf16[128,128]{1,0:T(8,128)(2,1)S(1)}) custom-call(bf16[2048,128]{1,0:T(8,128)(2,1)S(1)} %get-tuple-element.51.dy_ref.rows_ref, bf16[2048,256]{1,0:T(8,128)(2,1)S(1)} %get-tuple-element.71.far_rows_ref, bf16[1,128,1024]{2,1,0:T(8,128)(2,1)S(1)} %copy-done, ...), custom_call_target="tpu_custom_call" | custom-call | flops 1 | bytes 1 | tf_op jit(solution)/shard_map/heads_last/pallas_call | solution.py:49
  28.6 0.4 %collective-permute-done.11.refs_8_ = bf16[64,2048]{1,0:T(8,128)(2,1)S(1)} collective-permute-done((bf16[64,2048]{1,0:T(8,128)(2,1)S(1)}, bf16[64,2048]{1,0:T(8,128)(2,1)S(1)}, u32[]{:S(2)}, u32[]{:S(2)}) %collective-permute-start.11) | collective-permute-done | bytes 262176 | tf_op jit(solution)/shard_map/ppermute | solution.py:538
  29.0 0.9 %heads_end.1 = (bf16[128,128]{1,0:T(8,128)(2,1)S(1)}, bf16[128,128]{1,0:T(8,128)(2,1)S(1)}, bf16[128,128]{1,0:T(8,128)(2,1)S(1)}) custom-call(bf16[2048,128]{1,0:T(8,128)(2,1)S(1)} %get-tuple-element.51.dy_ref.rows_ref, bf16[2048,256]{1,0:T(8,128)(2,1)S(1)} %get-tuple-element.71.far_rows_ref, bf16[1,128,1024]{2,1,0:T(8,128)(2,1)S(1)} %copy-done, ...), custom_call_target="tpu_custom_call" | custom-call | flops 1 | bytes 1 | tf_op jit(solution)/shard_map/heads_end/pallas_call | solution.py:49
  29.9 0.5 %collective-permute-done.6.far = bf16[2,128,768]{2,1,0:T(8,128)(2,1)S(1)} collective-permute-done((bf16[2,128,768]{2,1,0:T(8,128)(2,1)S(1)}, bf16[2,128,768]{2,1,0:T(8,128)(2,1)S(1)}, u32[]{:S(2)}, u32[]{:S(2)}) %collective-permute-start.6) | collective-permute-done | bytes 393248 | tf_op jit(solution)/shard_map/ppermute | solution.py:537
  30.4 0.9 %finish.1 = (bf16[1,128,1024]{2,1,0:T(8,128)(2,1)}, bf16[1,128,1024]{2,1,0:T(8,128)(2,1)}, bf16[1,128,1024]{2,1,0:T(8,128)(2,1)}) custom-call(bf16[2,128,768]{2,1,0:T(8,128)(2,1)S(1)} %collective-permute-done.6.far, bf16[2,128,768]{2,1,0:T(8,128)(2,1)S(1)} %collective-permute-done.7.near, ...), custom_call_target="tpu_custom_call", output_to_operand_aliasing={{0}: (11, {})} | custom-call | flops 1 | bytes 1 | tf_op jit(solution)/shard_map/finish/pallas_call | solution.py:467
  (28 shorter events, 0.8 us)
Async XLA Ops:
  0.6 8.4 %copy-start = (bf16[1,128,1024]{2,1,0:T(8,128)(2,1)S(1)}, bf16[1,128,1024]{2,1,0:T(8,128)(2,1)}, u32[]{:S(2)}) copy-start(bf16[1,128,1024]{2,1,0:T(8,128)(2,1)} %q_ref.11) | copy-start | bytes 786436
  0.6 8.4 %copy-start.1 = (bf16[1,128,2048]{2,1,0:T(8,128)(2,1)S(1)}, bf16[1,128,2048]{2,1,0:T(8,128)(2,1)}, u32[]{:S(2)}) copy-start(bf16[1,128,2048]{2,1,0:T(8,128)(2,1)} %refs_0_.1) | copy-start | bytes 1572868
  0.7 16.5 %collective-permute-start = (bf16[256,2048]{1,0:T(8,128)(2,1)}, bf16[256,2048]{1,0:T(8,128)(2,1)S(1)}, u32[]{:S(2)}, u32[]{:S(2)}) collective-permute-start(bf16[256,2048]{1,0:T(8,128)(2,1)} %w_ref.1), channel_id=1, source_target_pairs={{0,1},{1,0},{2,3},{3,2},{4,6},{5,7},{6,4},{7,5},{8,9},{9,8},{10,11... | collective-permute-start | bytes 3145736 | tf_op jit(solution)/shard_map/ppermute | solution.py:492
  2.8 0.9 %copy-start.3 = (bf16[1,128,1024]{2,1,0:T(8,128)(2,1)S(1)}, bf16[1,128,1024]{2,1,0:T(8,128)(2,1)}, u32[]{:S(2)}) copy-start(bf16[1,128,1024]{2,1,0:T(8,128)(2,1)} %k_ref.1) | copy-start | bytes 786436
  3.7 0.9 %copy-start.4 = (bf16[1,128,1024]{2,1,0:T(8,128)(2,1)S(1)}, bf16[1,128,1024]{2,1,0:T(8,128)(2,1)}, u32[]{:S(2)}) copy-start(bf16[1,128,1024]{2,1,0:T(8,128)(2,1)} %v_ref.1) | copy-start | bytes 786436
  4.7 4.5 %copy-start.2 = (bf16[256,2048]{1,0:T(8,128)(2,1)S(1)}, bf16[256,2048]{1,0:T(8,128)(2,1)}, u32[]{:S(2)}) copy-start(bf16[256,2048]{1,0:T(8,128)(2,1)} %w_ref.1) | copy-start | bytes 3145732
  4.7 4.2 %collective-permute-start.1 = (bf16[128,2048]{1,0:T(8,128)(2,1)S(1)}, bf16[128,2048]{1,0:T(8,128)(2,1)S(1)}, u32[]{:S(2)}, u32[]{:S(2)}) collective-permute-start(bf16[128,2048]{1,0:T(8,128)(2,1)S(1)} %join.1.refs_0_), channel_id=1, source_target_pairs={{0,4},{4,0},{8,12},{12,8},{16,20},{20,16},{24,28},{28,24},{1,5},{5... | collective-permute-start | bytes 1572872 | tf_op jit(solution)/shard_map/ppermute | solution.py:497
  5.7 10.6 %collective-permute-start.2 = (bf16[128,2048]{1,0:T(8,128)(2,1)S(1)}, bf16[128,2048]{1,0:T(8,128)(2,1)S(1)}, u32[]{:S(2)}, u32[]{:S(2)}) collective-permute-start(bf16[128,2048]{1,0:T(8,128)(2,1)S(1)} %join.1.refs_0_), channel_id=1, source_target_pairs={{4,8},{8,4},{12,16},{16,12},{20,24},{24,20},{5,9},{9,5},{13,17},{1... | collective-permute-start | bytes 1572872 | tf_op jit(solution)/shard_map/ppermute | solution.py:497
  9.1 0.7 %copy-start.5 = (s32[8,4]{0,1:T(4,128)S(1)}, s32[8,4]{0,1:T(4,128)}, u32[]{:S(2)}) copy-start(s32[8,4]{0,1:T(4,128)} %param.12) | copy-start | bytes 388
  9.1 0.7 %copy-start.6 = (s32[1,8]{1,0:T(1,128)S(1)}, s32[1,8]{1,0:T(1,128)}, u32[]{:S(2)}) copy-start(s32[1,8]{1,0:T(1,128)} %val_ref.1) | copy-start | bytes 100
  9.1 10.7 %collective-permute-start.3 = (bf16[128,2816]{1,0:T(8,128)(2,1)S(1)}, bf16[128,2816]{1,0:T(8,128)(2,1)S(1)}, u32[]{:S(2)}, u32[]{:S(2)}) collective-permute-start(bf16[128,2816]{1,0:T(8,128)(2,1)S(1)} %hand_far.1), channel_id=1, source_target_pairs={{0,4},{4,0},{8,12},{12,8},{16,20},{20,16},{24,28},{28,24},{1,5},{5... | collective-permute-start | bytes 2162696 | tf_op jit(solution)/shard_map/ppermute | solution.py:501
  10.4 15.4 %collective-permute-start.8 = (bf16[128,2816]{1,0:T(8,128)(2,1)S(1)}, bf16[128,2816]{1,0:T(8,128)(2,1)S(1)}, u32[]{:S(2)}, u32[]{:S(2)}) collective-permute-start(bf16[128,2816]{1,0:T(8,128)(2,1)S(1)} %hand_far.1), channel_id=1, source_target_pairs={{4,8},{8,4},{12,16},{16,12},{20,24},{24,20},{5,9},{9,5},{13,17},{1... | collective-permute-start | bytes 2162696 | tf_op jit(solution)/shard_map/ppermute | solution.py:501
  17.3 2.5 %collective-permute-start.4 = (bf16[128,2304]{1,0:T(8,128)(2,1)S(1)}, bf16[128,2304]{1,0:T(8,128)(2,1)S(1)}, u32[]{:S(2)}, u32[]{:S(2)}) collective-permute-start(bf16[128,2304]{1,0:T(8,128)(2,1)S(1)} %get-tuple-element.56), channel_id=1, source_target_pairs={{0,4},{4,0},{8,12},{12,8},{16,20},{20,16},{24,28},{28,24},{1,5},{5... | collective-permute-start | bytes 1769480 | tf_op jit(solution)/shard_map/ppermute | solution.py:510
  17.4 2.8 %collective-permute-start.5 = (bf16[128,2304]{1,0:T(8,128)(2,1)S(1)}, bf16[128,2304]{1,0:T(8,128)(2,1)S(1)}, u32[]{:S(2)}, u32[]{:S(2)}) collective-permute-start(bf16[128,2304]{1,0:T(8,128)(2,1)S(1)} %get-tuple-element.57), channel_id=1, source_target_pairs={{0,4},{4,0},{8,12},{12,8},{16,20},{20,16},{24,28},{28,24},{1,5},{5... | collective-permute-start | bytes 1769480 | tf_op jit(solution)/shard_map/ppermute | solution.py:510
  17.9 9.0 %collective-permute-start.9 = (bf16[128,2048]{1,0:T(8,128)(2,1)S(1)}, bf16[128,2048]{1,0:T(8,128)(2,1)S(1)}, u32[]{:S(2)}, u32[]{:S(2)}) collective-permute-start(bf16[128,2048]{1,0:T(8,128)(2,1)S(1)} %get-tuple-element.72), channel_id=1, source_target_pairs={{0,2},{1,3},{2,0},{3,1},{4,5},{5,4},{6,7},{7,6},{8,10},{9,11},{10,... | collective-permute-start | bytes 1572872 | tf_op jit(solution)/shard_map/ppermute | solution.py:492
  21.3 9.1 %collective-permute-start.6 = (bf16[2,128,768]{2,1,0:T(8,128)(2,1)S(1)}, bf16[2,128,768]{2,1,0:T(8,128)(2,1)S(1)}, u32[]{:S(2)}, u32[]{:S(2)}) collective-permute-start(bf16[2,128,768]{2,1,0:T(8,128)(2,1)S(1)} %get-tuple-element.65), channel_id=1, source_target_pairs={{4,8},{8,4},{12,16},{16,12},{20,24},{24,20},{5,9},{9,5},{13,17},{1... | collective-permute-start | bytes 1179656 | tf_op jit(solution)/shard_map/ppermute | solution.py:537
  25.0 5.4 %collective-permute-start.7 = (bf16[2,128,768]{2,1,0:T(8,128)(2,1)S(1)}, bf16[2,128,768]{2,1,0:T(8,128)(2,1)S(1)}, u32[]{:S(2)}, u32[]{:S(2)}) collective-permute-start(bf16[2,128,768]{2,1,0:T(8,128)(2,1)S(1)} %get-tuple-element.66), channel_id=1, source_target_pairs={{0,4},{4,0},{8,12},{12,8},{16,20},{20,16},{24,28},{28,24},{1,5},{5... | collective-permute-start | bytes 1179656 | tf_op jit(solution)/shard_map/ppermute | solution.py:537
  26.9 1.7 %collective-permute-start.10 = (bf16[64,2048]{1,0:T(8,128)(2,1)S(1)}, bf16[64,2048]{1,0:T(8,128)(2,1)S(1)}, u32[]{:S(2)}, u32[]{:S(2)}) collective-permute-start(bf16[64,2048]{1,0:T(8,128)(2,1)S(1)} %get-tuple-element.87), channel_id=1, source_target_pairs={{0,4},{4,0},{8,12},{12,8},{16,20},{20,16},{24,28},{28,24},{1,5},{5... | collective-permute-start | bytes 786440 | tf_op jit(solution)/shard_map/ppermute | solution.py:538
  27.5 1.5 %collective-permute-start.11 = (bf16[64,2048]{1,0:T(8,128)(2,1)S(1)}, bf16[64,2048]{1,0:T(8,128)(2,1)S(1)}, u32[]{:S(2)}, u32[]{:S(2)}) collective-permute-start(bf16[64,2048]{1,0:T(8,128)(2,1)S(1)} %get-tuple-element.88), channel_id=1, source_target_pairs={{0,4},{4,0},{8,12},{12,8},{16,20},{20,16},{24,28},{28,24},{1,5},{5... | collective-permute-start | bytes 786440 | tf_op jit(solution)/shard_map/ppermute | solution.py:538

commit v17 on v16

--- a/solution.py
+++ b/solution.py
@@ -398,15 +398,11 @@
     def __init__(self, stage, sems):
         self.stage, self.sems, self.copies = stage, sems, []
 
-    def put(self, out_ref, chunk, value, head=None):
+    def put(self, out_ref, chunk, value):
         at = len(self.copies)
-        if head is None:
-            held, target = self.stage.at[at], out_ref.at[0, :, columns(chunk)]
-        else:
-            held = self.stage.at[at, :, pl.ds(0, HD)]
-            target = out_ref.at[0, :, head_columns(chunk * PAIR, head)]
-        held[...] = value
-        copy = pltpu.make_async_copy(held, target, self.sems.at[at])
+        self.stage[at] = value
+        target = out_ref.at[0, :, columns(chunk)]
+        copy = pltpu.make_async_copy(self.stage.at[at], target, self.sems.at[at])
         copy.start()
         self.copies.append(copy)
 
@@ -443,21 +439,37 @@
 
 
 def finish_kernel(order, last, widths, n_last, far, near, *refs):
-    outs, to = refs[-5:-2], Columns(*refs[-2:])
-    pairs = order(*place())
     core, group = place()
-    for i, ref in enumerate(refs[len(widths) : len(widths) + n_last]):
-        to.put(outs[i % 3], last(core, group), ref[...], core if i < 3 else 1 - core)
-    for part, width in enumerate(widths):
-        own = refs[part]
-        for step in range(width // PAIR):
-            cols = slice(step * PAIR, (step + 1) * PAIR)
-            chunk, message_slot = pairs[part][step]
-            at = columns(message_slot)
-            for side, out_ref in enumerate(outs[1:]):
-                total = own[side, :, cols] + near[side, :, at].astype(F32)
-                to.put(out_ref, chunk, (total + far[side, :, at].astype(F32)).astype(BF16))
-    to.wait()
+    pairs = order(core, group)
+    ends = refs[len(widths) : len(widths) + n_last]
+    outs, (stage, sems) = refs[-5:-2], refs[-2:]
+    start = last(core, group) * PAIR
+    copies = []
+
+    def send(held, target):
+        copies.append(pltpu.make_async_copy(held, target, sems.at[len(copies)]))
+        copies[-1].start()
+
+    for side in range(3):
+        for i, ref in enumerate(ends[side::3]):
+            stage[side, :, head_columns(start, core if i == 0 else 1 - core)] = ref[...]
+        if side == 0:
+            if ends:
+                cols = columns(last(core, group))
+                send(stage.at[0, :, cols], outs[0].at[0, :, cols])
+            continue
+        for part, width in enumerate(widths):
+            own = refs[part]
+            for step in range(width // PAIR):
+                cols = slice(step * PAIR, (step + 1) * PAIR)
+                chunk, message_slot = pairs[part][step]
+                at = columns(message_slot)
+                total = own[side - 1, :, cols] + near[side - 1, :, at].astype(F32)
+                total = (total + far[side - 1, :, at].astype(F32)).astype(BF16)
+                stage[side, :, columns(chunk)] = total
+        send(stage.at[side], outs[side].at[0])
+    for copy in copies:
+        copy.wait()
 
 
 def finish(order, last, far, near, parts, third, d_queries):
@@ -469,7 +481,7 @@
         out_shape=(jax.ShapeDtypeStruct(shape, BF16),) * 3,
         in_specs=[VMEM] * len(ins) + [ANY],
         out_specs=(ANY,) * 3,
-        scratch_shapes=scratch_of(2 * sum(widths) // PAIR + len(third), shape[1]),
+        scratch_shapes=[pltpu.VMEM((3, *shape[1:]), BF16), pltpu.SemaphoreType.DMA((3,))],
         input_output_aliases={len(ins): 0},
         cost_estimate=BRIEF,
         compiler_params=PARAMS,

time: 31.6 us -> 31.6 us (level)
  no operation moved by 1% of the time
where the time goes in v17:
time: 31.6 us; the launch traced here: 31.3 us
  starting transfers between devices  15.8 us (50%)
  Pallas kernels  8.95 us (28%)
  waiting for transfers between devices  3.8 us (12%)
  local copies, waits for them, and re-layouts  1.97 us (6%)
  between operations  0.88 us (3%)
    pallas_call x13, Pallas kernels, call(): pl.pallas_call(kernel, out_shape=out_shape, in_specs=in_specs, out_specs=...  8.03 us
    ppermute x2, starting transfers between devices, body(): far_kv, near_kv = (far(kv), near(kv))  4.23 us
    ppermute x2, starting transfers between devices, body(): sums = (far(second[3]), near(second[2]))  3.74 us
    ppermute x2, starting transfers between devices, body(): far_both, near_both = (far(message), near(message))  3.62 us
    ppermute x2, starting transfers between devices, cross(): return lax.ppermute(x, ('seq', 'fsdp'), pairs)  2.96 us
    ppermute x2, waiting for transfers between devices, body(): far_kv, near_kv = (far(kv), near(kv))  2.35 us
    unnamed x14, local copies, waits for them, and re-layouts  1.97 us
    pallas_call x1, Pallas kernels, finish(): pl.pallas_call(functools.partial(finish_kernel, order, last, widths, len(...  0.92 us
  transfers between devices with their start and end apart: 12, of which 5 were waited for; matrix products, arithmetic and copies ran while one was open for 0% of the time, Pallas kernels for 26%

profile of v17, /device:TPU:1, one launch (start us, length us, event | category | flops | bytes accessed | tf_op | source)
XLA Modules:
  0.0 31.3 jit_solution(1569881298512916664)
XLA Ops:
  0.7 2.1 %collective-permute-start = (bf16[256,2048]{1,0:T(8,128)(2,1)}, bf16[256,2048]{1,0:T(8,128)(2,1)S(1)}, u32[]{:S(2)}, u32[]{:S(2)}) collective-permute-start(bf16[256,2048]{1,0:T(8,128)(2,1)} %w_ref.1), channel_id=1, source_target_pairs={{0,1},{1,0},{2,3},{3,2},{4,6},{5,7},{6,4},{7,5},{8,9},{9,8},{10,11... | collective-permute-start | bytes 3145736 | tf_op jit(solution)/shard_map/ppermute | solution.py:504
  2.8 0.9 %copy-done.3 = bf16[1,128,1024]{2,1,0:T(8,128)(2,1)S(1)} copy-done((bf16[1,128,1024]{2,1,0:T(8,128)(2,1)S(1)}, bf16[1,128,1024]{2,1,0:T(8,128)(2,1)}, u32[]{:S(2)}) %copy-start.3) | copy-done | bytes 262168
  3.7 0.9 %copy-done.4 = bf16[1,128,1024]{2,1,0:T(8,128)(2,1)S(1)} copy-done((bf16[1,128,1024]{2,1,0:T(8,128)(2,1)S(1)}, bf16[1,128,1024]{2,1,0:T(8,128)(2,1)}, u32[]{:S(2)}) %copy-start.4) | copy-done | bytes 262168
  4.7 1.0 %collective-permute-start.1 = (bf16[128,2048]{1,0:T(8,128)(2,1)S(1)}, bf16[128,2048]{1,0:T(8,128)(2,1)S(1)}, u32[]{:S(2)}, u32[]{:S(2)}) collective-permute-start(bf16[128,2048]{1,0:T(8,128)(2,1)S(1)} %join.1.refs_0_), channel_id=1, source_target_pairs={{0,4},{4,0},{8,12},{12,8},{16,20},{20,16},{24,28},{28,24},{1,5},{5... | collective-permute-start | bytes 1572872 | tf_op jit(solution)/shard_map/ppermute | solution.py:509
  5.7 3.2 %collective-permute-start.2 = (bf16[128,2048]{1,0:T(8,128)(2,1)S(1)}, bf16[128,2048]{1,0:T(8,128)(2,1)S(1)}, u32[]{:S(2)}, u32[]{:S(2)}) collective-permute-start(bf16[128,2048]{1,0:T(8,128)(2,1)S(1)} %join.1.refs_0_), channel_id=1, source_target_pairs={{4,8},{8,4},{12,16},{16,12},{20,24},{24,20},{5,9},{9,5},{13,17},{1... | collective-permute-start | bytes 1572872 | tf_op jit(solution)/shard_map/ppermute | solution.py:509
  9.2 0.5 %turned.1 = (bf16[2048,128]{1,0:T(8,128)(2,1)S(1)}, bf16[256,128]{1,0:T(8,128)(2,1)S(1)}) custom-call(bf16[1,128,2048]{2,1,0:T(8,128)(2,1)S(1)} %copy-done.1, bf16[256,2048]{1,0:T(8,128)(2,1)S(1)} %copy-done.2), custom_call_target="tpu_custom_call" | custom-call | flops 1 | bytes 1 | tf_op jit(solution)/shard_map/turned/pallas_call | solution.py:49
  9.8 0.6 %limits.1.limit_ref = s32[16,256]{1,0:T(8,128)S(1)} custom-call(s32[4,8]{1,0:T(4,128)S(1)} %bitcast.1, s32[1,8]{1,0:T(1,128)S(1)} %copy-done.6), custom_call_target="tpu_custom_call" | custom-call | flops 1 | bytes 1 | tf_op jit(solution)/shard_map/limits/pallas_call | solution.py:49
  10.4 3.5 %collective-permute-start.8 = (bf16[128,2816]{1,0:T(8,128)(2,1)S(1)}, bf16[128,2816]{1,0:T(8,128)(2,1)S(1)}, u32[]{:S(2)}, u32[]{:S(2)}) collective-permute-start(bf16[128,2816]{1,0:T(8,128)(2,1)S(1)} %hand_far.1), channel_id=1, source_target_pairs={{4,8},{8,4},{12,16},{16,12},{20,24},{24,20},{5,9},{9,5},{13,17},{1... | collective-permute-start | bytes 2162696 | tf_op jit(solution)/shard_map/ppermute | solution.py:513
  14.0 2.3 %collective-permute-done.2.refs_2_.kv_ref = bf16[128,2048]{1,0:T(8,128)(2,1)S(1)} collective-permute-done((bf16[128,2048]{1,0:T(8,128)(2,1)S(1)}, bf16[128,2048]{1,0:T(8,128)(2,1)S(1)}, u32[]{:S(2)}, u32[]{:S(2)}) %collective-permute-start.2) | collective-permute-done | bytes 524320 | tf_op jit(solution)/shard_map/ppermute | solution.py:509
  16.3 0.8 %heads_own.1 = (bf16[128,256]{1,0:T(8,128)(2,1)S(1)}, f32[2,128,256]{2,1,0:T(8,128)S(1)}, bf16[2,128,768]{2,1,0:T(8,128)(2,1)S(1)}, bf16[2,128,768]{2,1,0:T(8,128)(2,1)S(1)}) custom-call(bf16[2048,128]{1,0:T(8,128)(2,1)S(1)} %get-tuple-element.51.dy_ref.rows_ref, bf16[1,128,1024]{2,1,0:T(8,128)(2,1)S(1)} %copy-done, s32[16,256]{1,0:T(8,128)S(1)} %limits.1.limit_ref, ...), custom_call_target="tpu_custom_call" | custom-call | flops 1 | bytes 1 | tf_op jit(solution)/shard_map/heads_own/pallas_call | solution.py:49
  17.4 0.5 %collective-permute-start.5 = (bf16[128,2304]{1,0:T(8,128)(2,1)S(1)}, bf16[128,2304]{1,0:T(8,128)(2,1)S(1)}, u32[]{:S(2)}, u32[]{:S(2)}) collective-permute-start(bf16[128,2304]{1,0:T(8,128)(2,1)S(1)} %get-tuple-element.57), channel_id=1, source_target_pairs={{0,4},{4,0},{8,12},{12,8},{16,20},{20,16},{24,28},{28,24},{1,5},{5... | collective-permute-start | bytes 1769480 | tf_op jit(solution)/shard_map/ppermute | solution.py:522
  17.9 0.8 %collective-permute-start.9 = (bf16[128,2048]{1,0:T(8,128)(2,1)S(1)}, bf16[128,2048]{1,0:T(8,128)(2,1)S(1)}, u32[]{:S(2)}, u32[]{:S(2)}) collective-permute-start(bf16[128,2048]{1,0:T(8,128)(2,1)S(1)} %get-tuple-element.72), channel_id=1, source_target_pairs={{0,2},{1,3},{2,0},{3,1},{4,5},{5,4},{6,7},{7,6},{8,10},{9,11},{10,... | collective-permute-start | bytes 1572872 | tf_op jit(solution)/shard_map/ppermute | solution.py:504
  18.7 1.1 %heads_first.1 = (bf16[128,256]{1,0:T(8,128)(2,1)S(1)}, f32[2,128,256]{2,1,0:T(8,128)S(1)}, bf16[2,128,768]{2,1,0:T(8,128)(2,1)S(1)}, bf16[2,128,768]{2,1,0:T(8,128)(2,1)S(1)}) custom-call(bf16[2048,128]{1,0:T(8,128)(2,1)S(1)} %get-tuple-element.51.dy_ref.rows_ref, bf16[1,128,1024]{2,1,0:T(8,128)(2,1)S(1)} %copy-done, s32[16,256]{1,0:T(8,128)S(1)} %limits.1.limit_ref, ...), custom_call_target="tpu_custom_call" | custom-call | flops 1 | bytes 1 | tf_op jit(solution)/shard_map/heads_first/pallas_call | solution.py:49
  19.8 0.4 %collective-permute-done.5.refs_4_.refs_6_ = bf16[128,2304]{1,0:T(8,128)(2,1)S(1)} collective-permute-done((bf16[128,2304]{1,0:T(8,128)(2,1)S(1)}, bf16[128,2304]{1,0:T(8,128)(2,1)S(1)}, u32[]{:S(2)}, u32[]{:S(2)}) %collective-permute-start.5) | collective-permute-done | bytes 589856 | tf_op jit(solution)/shard_map/ppermute | solution.py:522
  20.2 1.1 %heads_second.1 = (bf16[128,256]{1,0:T(8,128)(2,1)S(1)}, f32[2,128,256]{2,1,0:T(8,128)S(1)}, bf16[2,128,768]{2,1,0:T(8,128)(2,1)S(1)}, bf16[2,128,768]{2,1,0:T(8,128)(2,1)S(1)}) custom-call(bf16[2048,128]{1,0:T(8,128)(2,1)S(1)} %get-tuple-element.51.dy_ref.rows_ref, bf16[1,128,1024]{2,1,0:T(8,128)(2,1)S(1)} %copy-done, s32[16,256]{1,0:T(8,128)S(1)} %limits.1.limit_ref, ...), custom_call_target="tpu_custom_call" | custom-call | flops 1 | bytes 1 | tf_op jit(solution)/shard_map/heads_second/pallas_call | solution.py:49
  21.3 3.7 %collective-permute-start.6 = (bf16[2,128,768]{2,1,0:T(8,128)(2,1)S(1)}, bf16[2,128,768]{2,1,0:T(8,128)(2,1)S(1)}, u32[]{:S(2)}, u32[]{:S(2)}) collective-permute-start(bf16[2,128,768]{2,1,0:T(8,128)(2,1)S(1)} %get-tuple-element.65), channel_id=1, source_target_pairs={{4,8},{8,4},{12,16},{16,12},{20,24},{24,20},{5,9},{9,5},{13,17},{1... | collective-permute-start | bytes 1179656 | tf_op jit(solution)/shard_map/ppermute | solution.py:549
  25.1 0.7 %settle.1.refs_9_ = bf16[1,128,1024]{2,1,0:T(8,128)(2,1)} custom-call(bf16[128,256]{1,0:T(8,128)(2,1)S(1)} %get-tuple-element.74.refs_0_, bf16[128,256]{1,0:T(8,128)(2,1)S(1)} %get-tuple-element.75.refs_1_, bf16[128,256]{1,0:T(8,128)(2,1)S(1)} %get-tuple-element.76.refs_2_), custom_call_target="tpu_custom_call" | custom-call | flops 1 | bytes 1 | tf_op jit(solution)/shard_map/settle/pallas_call | solution.py:49
  25.8 1.0 %probs_last.1 = (f32[3,384,256]{2,1,0:T(8,128)S(1)}, f32[3,128,256]{2,1,0:T(8,128)S(1)}, bf16[2048,256]{1,0:T(8,128)(2,1)S(1)}) custom-call(bf16[1,128,1024]{2,1,0:T(8,128)(2,1)S(1)} %copy-done, s32[16,256]{1,0:T(8,128)S(1)} %limits.1.limit_ref, bf16[128,2048]{1,0:T(8,128)(2,1)S(1)} %join.1.refs_0_, ...), custom_call_target="tpu_custom_call" | custom-call | flops 1 | bytes 1 | tf_op jit(solution)/shard_map/probs_last/pallas_call | solution.py:49
  26.9 0.6 %collective-permute-start.10 = (bf16[64,2048]{1,0:T(8,128)(2,1)S(1)}, bf16[64,2048]{1,0:T(8,128)(2,1)S(1)}, u32[]{:S(2)}, u32[]{:S(2)}) collective-permute-start(bf16[64,2048]{1,0:T(8,128)(2,1)S(1)} %get-tuple-element.87), channel_id=1, source_target_pairs={{0,4},{4,0},{8,12},{12,8},{16,20},{20,16},{24,28},{28,24},{1,5},{5... | collective-permute-start | bytes 786440 | tf_op jit(solution)/shard_map/ppermute | solution.py:550
  27.5 0.9 %heads_last.1 = (bf16[128,128]{1,0:T(8,128)(2,1)S(1)}, bf16[128,128]{1,0:T(8,128)(2,1)S(1)}, bf16[128,128]{1,0:T(8,128)(2,1)S(1)}) custom-call(bf16[2048,128]{1,0:T(8,128)(2,1)S(1)} %get-tuple-element.51.dy_ref.rows_ref, bf16[2048,256]{1,0:T(8,128)(2,1)S(1)} %get-tuple-element.71.far_rows_ref, bf16[1,128,1024]{2,1,0:T(8,128)(2,1)S(1)} %copy-done, ...), custom_call_target="tpu_custom_call" | custom-call | flops 1 | bytes 1 | tf_op jit(solution)/shard_map/heads_last/pallas_call | solution.py:49
  28.6 0.4 %collective-permute-done.11.refs_8_ = bf16[64,2048]{1,0:T(8,128)(2,1)S(1)} collective-permute-done((bf16[64,2048]{1,0:T(8,128)(2,1)S(1)}, bf16[64,2048]{1,0:T(8,128)(2,1)S(1)}, u32[]{:S(2)}, u32[]{:S(2)}) %collective-permute-start.11) | collective-permute-done | bytes 262176 | tf_op jit(solution)/shard_map/ppermute | solution.py:550
  29.0 0.9 %heads_end.1 = (bf16[128,128]{1,0:T(8,128)(2,1)S(1)}, bf16[128,128]{1,0:T(8,128)(2,1)S(1)}, bf16[128,128]{1,0:T(8,128)(2,1)S(1)}) custom-call(bf16[2048,128]{1,0:T(8,128)(2,1)S(1)} %get-tuple-element.51.dy_ref.rows_ref, bf16[2048,256]{1,0:T(8,128)(2,1)S(1)} %get-tuple-element.71.far_rows_ref, bf16[1,128,1024]{2,1,0:T(8,128)(2,1)S(1)} %copy-done, ...), custom_call_target="tpu_custom_call" | custom-call | flops 1 | bytes 1 | tf_op jit(solution)/shard_map/heads_end/pallas_call | solution.py:49
  29.9 0.5 %collective-permute-done.6.far = bf16[2,128,768]{2,1,0:T(8,128)(2,1)S(1)} collective-permute-done((bf16[2,128,768]{2,1,0:T(8,128)(2,1)S(1)}, bf16[2,128,768]{2,1,0:T(8,128)(2,1)S(1)}, u32[]{:S(2)}, u32[]{:S(2)}) %collective-permute-start.6) | collective-permute-done | bytes 393248 | tf_op jit(solution)/shard_map/ppermute | solution.py:549
  30.4 0.9 %finish.1 = (bf16[1,128,1024]{2,1,0:T(8,128)(2,1)}, bf16[1,128,1024]{2,1,0:T(8,128)(2,1)}, bf16[1,128,1024]{2,1,0:T(8,128)(2,1)}) custom-call(bf16[2,128,768]{2,1,0:T(8,128)(2,1)S(1)} %collective-permute-done.6.far, bf16[2,128,768]{2,1,0:T(8,128)(2,1)S(1)} %collective-permute-done.7.near, ...), custom_call_target="tpu_custom_call", output_to_operand_aliasing={{0}: (11, {})} | custom-call | flops 1 | bytes 1 | tf_op jit(solution)/shard_map/finish/pallas_call | solution.py:479
  (28 shorter events, 0.8 us)
Async XLA Ops:
  0.6 8.4 %copy-start = (bf16[1,128,1024]{2,1,0:T(8,128)(2,1)S(1)}, bf16[1,128,1024]{2,1,0:T(8,128)(2,1)}, u32[]{:S(2)}) copy-start(bf16[1,128,1024]{2,1,0:T(8,128)(2,1)} %q_ref.11) | copy-start | bytes 786436
  0.6 8.4 %copy-start.1 = (bf16[1,128,2048]{2,1,0:T(8,128)(2,1)S(1)}, bf16[1,128,2048]{2,1,0:T(8,128)(2,1)}, u32[]{:S(2)}) copy-start(bf16[1,128,2048]{2,1,0:T(8,128)(2,1)} %refs_0_.1) | copy-start | bytes 1572868
  0.7 16.5 %collective-permute-start = (bf16[256,2048]{1,0:T(8,128)(2,1)}, bf16[256,2048]{1,0:T(8,128)(2,1)S(1)}, u32[]{:S(2)}, u32[]{:S(2)}) collective-permute-start(bf16[256,2048]{1,0:T(8,128)(2,1)} %w_ref.1), channel_id=1, source_target_pairs={{0,1},{1,0},{2,3},{3,2},{4,6},{5,7},{6,4},{7,5},{8,9},{9,8},{10,11... | collective-permute-start | bytes 3145736 | tf_op jit(solution)/shard_map/ppermute | solution.py:504
  2.8 0.9 %copy-start.3 = (bf16[1,128,1024]{2,1,0:T(8,128)(2,1)S(1)}, bf16[1,128,1024]{2,1,0:T(8,128)(2,1)}, u32[]{:S(2)}) copy-start(bf16[1,128,1024]{2,1,0:T(8,128)(2,1)} %k_ref.1) | copy-start | bytes 786436
  3.7 0.9 %copy-start.4 = (bf16[1,128,1024]{2,1,0:T(8,128)(2,1)S(1)}, bf16[1,128,1024]{2,1,0:T(8,128)(2,1)}, u32[]{:S(2)}) copy-start(bf16[1,128,1024]{2,1,0:T(8,128)(2,1)} %v_ref.1) | copy-start | bytes 786436
  4.7 4.5 %copy-start.2 = (bf16[256,2048]{1,0:T(8,128)(2,1)S(1)}, bf16[256,2048]{1,0:T(8,128)(2,1)}, u32[]{:S(2)}) copy-start(bf16[256,2048]{1,0:T(8,128)(2,1)} %w_ref.1) | copy-start | bytes 3145732
  4.7 4.2 %collective-permute-start.1 = (bf16[128,2048]{1,0:T(8,128)(2,1)S(1)}, bf16[128,2048]{1,0:T(8,128)(2,1)S(1)}, u32[]{:S(2)}, u32[]{:S(2)}) collective-permute-start(bf16[128,2048]{1,0:T(8,128)(2,1)S(1)} %join.1.refs_0_), channel_id=1, source_target_pairs={{0,4},{4,0},{8,12},{12,8},{16,20},{20,16},{24,28},{28,24},{1,5},{5... | collective-permute-start | bytes 1572872 | tf_op jit(solution)/shard_map/ppermute | solution.py:509
  5.7 10.6 %collective-permute-start.2 = (bf16[128,2048]{1,0:T(8,128)(2,1)S(1)}, bf16[128,2048]{1,0:T(8,128)(2,1)S(1)}, u32[]{:S(2)}, u32[]{:S(2)}) collective-permute-start(bf16[128,2048]{1,0:T(8,128)(2,1)S(1)} %join.1.refs_0_), channel_id=1, source_target_pairs={{4,8},{8,4},{12,16},{16,12},{20,24},{24,20},{5,9},{9,5},{13,17},{1... | collective-permute-start | bytes 1572872 | tf_op jit(solution)/shard_map/ppermute | solution.py:509
  9.1 0.7 %copy-start.5 = (s32[8,4]{0,1:T(4,128)S(1)}, s32[8,4]{0,1:T(4,128)}, u32[]{:S(2)}) copy-start(s32[8,4]{0,1:T(4,128)} %param.12) | copy-start | bytes 388
  9.1 0.7 %copy-start.6 = (s32[1,8]{1,0:T(1,128)S(1)}, s32[1,8]{1,0:T(1,128)}, u32[]{:S(2)}) copy-start(s32[1,8]{1,0:T(1,128)} %val_ref.1) | copy-start | bytes 100
  9.1 10.7 %collective-permute-start.3 = (bf16[128,2816]{1,0:T(8,128)(2,1)S(1)}, bf16[128,2816]{1,0:T(8,128)(2,1)S(1)}, u32[]{:S(2)}, u32[]{:S(2)}) collective-permute-start(bf16[128,2816]{1,0:T(8,128)(2,1)S(1)} %hand_far.1), channel_id=1, source_target_pairs={{0,4},{4,0},{8,12},{12,8},{16,20},{20,16},{24,28},{28,24},{1,5},{5... | collective-permute-start | bytes 2162696 | tf_op jit(solution)/shard_map/ppermute | solution.py:513
  10.4 15.4 %collective-permute-start.8 = (bf16[128,2816]{1,0:T(8,128)(2,1)S(1)}, bf16[128,2816]{1,0:T(8,128)(2,1)S(1)}, u32[]{:S(2)}, u32[]{:S(2)}) collective-permute-start(bf16[128,2816]{1,0:T(8,128)(2,1)S(1)} %hand_far.1), channel_id=1, source_target_pairs={{4,8},{8,4},{12,16},{16,12},{20,24},{24,20},{5,9},{9,5},{13,17},{1... | collective-permute-start | bytes 2162696 | tf_op jit(solution)/shard_map/ppermute | solution.py:513
  17.3 2.5 %collective-permute-start.4 = (bf16[128,2304]{1,0:T(8,128)(2,1)S(1)}, bf16[128,2304]{1,0:T(8,128)(2,1)S(1)}, u32[]{:S(2)}, u32[]{:S(2)}) collective-permute-start(bf16[128,2304]{1,0:T(8,128)(2,1)S(1)} %get-tuple-element.56), channel_id=1, source_target_pairs={{0,4},{4,0},{8,12},{12,8},{16,20},{20,16},{24,28},{28,24},{1,5},{5... | collective-permute-start | bytes 1769480 | tf_op jit(solution)/shard_map/ppermute | solution.py:522
  17.4 2.8 %collective-permute-start.5 = (bf16[128,2304]{1,0:T(8,128)(2,1)S(1)}, bf16[128,2304]{1,0:T(8,128)(2,1)S(1)}, u32[]{:S(2)}, u32[]{:S(2)}) collective-permute-start(bf16[128,2304]{1,0:T(8,128)(2,1)S(1)} %get-tuple-element.57), channel_id=1, source_target_pairs={{0,4},{4,0},{8,12},{12,8},{16,20},{20,16},{24,28},{28,24},{1,5},{5... | collective-permute-start | bytes 1769480 | tf_op jit(solution)/shard_map/ppermute | solution.py:522
  17.9 9.0 %collective-permute-start.9 = (bf16[128,2048]{1,0:T(8,128)(2,1)S(1)}, bf16[128,2048]{1,0:T(8,128)(2,1)S(1)}, u32[]{:S(2)}, u32[]{:S(2)}) collective-permute-start(bf16[128,2048]{1,0:T(8,128)(2,1)S(1)} %get-tuple-element.72), channel_id=1, source_target_pairs={{0,2},{1,3},{2,0},{3,1},{4,5},{5,4},{6,7},{7,6},{8,10},{9,11},{10,... | collective-permute-start | bytes 1572872 | tf_op jit(solution)/shard_map/ppermute | solution.py:504
  21.3 9.1 %collective-permute-start.6 = (bf16[2,128,768]{2,1,0:T(8,128)(2,1)S(1)}, bf16[2,128,768]{2,1,0:T(8,128)(2,1)S(1)}, u32[]{:S(2)}, u32[]{:S(2)}) collective-permute-start(bf16[2,128,768]{2,1,0:T(8,128)(2,1)S(1)} %get-tuple-element.65), channel_id=1, source_target_pairs={{4,8},{8,4},{12,16},{16,12},{20,24},{24,20},{5,9},{9,5},{13,17},{1... | collective-permute-start | bytes 1179656 | tf_op jit(solution)/shard_map/ppermute | solution.py:549
  25.0 5.4 %collective-permute-start.7 = (bf16[2,128,768]{2,1,0:T(8,128)(2,1)S(1)}, bf16[2,128,768]{2,1,0:T(8,128)(2,1)S(1)}, u32[]{:S(2)}, u32[]{:S(2)}) collective-permute-start(bf16[2,128,768]{2,1,0:T(8,128)(2,1)S(1)} %get-tuple-element.66), channel_id=1, source_target_pairs={{0,4},{4,0},{8,12},{12,8},{16,20},{20,16},{24,28},{28,24},{1,5},{5... | collective-permute-start | bytes 1179656 | tf_op jit(solution)/shard_map/ppermute | solution.py:549
  26.9 1.7 %collective-permute-start.10 = (bf16[64,2048]{1,0:T(8,128)(2,1)S(1)}, bf16[64,2048]{1,0:T(8,128)(2,1)S(1)}, u32[]{:S(2)}, u32[]{:S(2)}) collective-permute-start(bf16[64,2048]{1,0:T(8,128)(2,1)S(1)} %get-tuple-element.87), channel_id=1, source_target_pairs={{0,4},{4,0},{8,12},{12,8},{16,20},{20,16},{24,28},{28,24},{1,5},{5... | collective-permute-start | bytes 786440 | tf_op jit(solution)/shard_map/ppermute | solution.py:550
  27.5 1.5 %collective-permute-start.11 = (bf16[64,2048]{1,0:T(8,128)(2,1)S(1)}, bf16[64,2048]{1,0:T(8,128)(2,1)S(1)}, u32[]{:S(2)}, u32[]{:S(2)}) collective-permute-start(bf16[64,2048]{1,0:T(8,128)(2,1)S(1)} %get-tuple-element.88), channel_id=1, source_target_pairs={{0,4},{4,0},{8,12},{12,8},{16,20},{20,16},{24,28},{28,24},{1,5},{5... | collective-permute-start | bytes 786440 | tf_op jit(solution)/shard_map/ppermute | solution.py:550

commit v18 on v15

--- a/solution.py
+++ b/solution.py
@@ -525,7 +525,7 @@
             [(group ^ (2 - core), 2 - core)],
         ]
         placed = settle(order, (own_dq, dq, second[0]), queries.shape)
-        got_d, halo, prob, placed = lax.optimization_barrier((got_d, halo, prob, placed))
+        got_d, halo, placed = lax.optimization_barrier((got_d, halo, placed))
         sums = far(second[3]), near(second[2])
         edge = [near(x) for x in split(got_d)]
         known = prob, far_rows, *ours[:2], ours[3], halo

time: 31.6 us -> 31.7 us (level)
  starting transfers between devices: 15.8 us -> 16.2 us
  waiting for transfers between devices: 3.89 us -> 3.53 us
    ppermute x2, waiting for transfers between devices: 0.46 us -> 0.01 us  [body(): edge = [near(x) for x in split(got_d)]]
    ppermute x2, waiting for transfers between devices: 0.01 us -> 0.42 us  [cross(): return lax.ppermute(x, ('seq', 'fsdp'), pairs)]
    ppermute x2, starting transfers between devices: 0.73 us -> 1.08 us  [body(): edge = [near(x) for x in split(got_d)]]
  transfers between devices with their start and end apart: 12 -> 12, of which waited for: 5 -> 4; matrix products, arithmetic and copies ran while one was open for 0% -> 0% of each run, Pallas kernels for 25% -> 25%
where the time goes in v18:
time: 31.7 us; the launch traced here: 31.4 us
  starting transfers between devices  16.2 us (51%)
  Pallas kernels  8.77 us (28%)
  waiting for transfers between devices  3.53 us (11%)
  local copies, waits for them, and re-layouts  1.97 us (6%)
  between operations  0.89 us (3%)
    pallas_call x13, Pallas kernels, call(): pl.pallas_call(kernel, out_shape=out_shape, in_specs=in_specs, out_specs=...  7.85 us
    ppermute x2, starting transfers between devices, body(): far_kv, near_kv = (far(kv), near(kv))  4.23 us
    ppermute x2, starting transfers between devices, body(): sums = (far(second[3]), near(second[2]))  3.74 us
    ppermute x2, starting transfers between devices, body(): far_both, near_both = (far(message), near(message))  3.62 us
    ppermute x2, starting transfers between devices, cross(): return lax.ppermute(x, ('seq', 'fsdp'), pairs)  2.96 us
    ppermute x2, waiting for transfers between devices, body(): far_kv, near_kv = (far(kv), near(kv))  2.35 us
    unnamed x14, local copies, waits for them, and re-layouts  1.97 us
    ppermute x2, starting transfers between devices, body(): edge = [near(x) for x in split(got_d)]  1.08 us
  transfers between devices with their start and end apart: 12, of which 4 were waited for; matrix products, arithmetic and copies ran while one was open for 0% of the time, Pallas kernels for 25%

profile of v18, /device:TPU:1, one launch (start us, length us, event | category | flops | bytes accessed | tf_op | source)
XLA Modules:
  0.0 31.4 jit_solution(16370737839421121500)
XLA Ops:
  0.7 2.1 %collective-permute-start = (bf16[256,2048]{1,0:T(8,128)(2,1)}, bf16[256,2048]{1,0:T(8,128)(2,1)S(1)}, u32[]{:S(2)}, u32[]{:S(2)}) collective-permute-start(bf16[256,2048]{1,0:T(8,128)(2,1)} %w_ref.1), channel_id=1, source_target_pairs={{0,1},{1,0},{2,3},{3,2},{4,6},{5,7},{6,4},{7,5},{8,9},{9,8},{10,11... | collective-permute-start | bytes 3145736 | tf_op jit(solution)/shard_map/ppermute | solution.py:484
  2.8 0.9 %copy-done.3 = bf16[1,128,1024]{2,1,0:T(8,128)(2,1)S(1)} copy-done((bf16[1,128,1024]{2,1,0:T(8,128)(2,1)S(1)}, bf16[1,128,1024]{2,1,0:T(8,128)(2,1)}, u32[]{:S(2)}) %copy-start.3) | copy-done | bytes 262168
  3.7 0.9 %copy-done.4 = bf16[1,128,1024]{2,1,0:T(8,128)(2,1)S(1)} copy-done((bf16[1,128,1024]{2,1,0:T(8,128)(2,1)S(1)}, bf16[1,128,1024]{2,1,0:T(8,128)(2,1)}, u32[]{:S(2)}) %copy-start.4) | copy-done | bytes 262168
  4.7 1.0 %collective-permute-start.1 = (bf16[128,2048]{1,0:T(8,128)(2,1)S(1)}, bf16[128,2048]{1,0:T(8,128)(2,1)S(1)}, u32[]{:S(2)}, u32[]{:S(2)}) collective-permute-start(bf16[128,2048]{1,0:T(8,128)(2,1)S(1)} %join.1.refs_0_), channel_id=1, source_target_pairs={{0,4},{4,0},{8,12},{12,8},{16,20},{20,16},{24,28},{28,24},{1,5},{5... | collective-permute-start | bytes 1572872 | tf_op jit(solution)/shard_map/ppermute | solution.py:489
  5.7 3.2 %collective-permute-start.2 = (bf16[128,2048]{1,0:T(8,128)(2,1)S(1)}, bf16[128,2048]{1,0:T(8,128)(2,1)S(1)}, u32[]{:S(2)}, u32[]{:S(2)}) collective-permute-start(bf16[128,2048]{1,0:T(8,128)(2,1)S(1)} %join.1.refs_0_), channel_id=1, source_target_pairs={{4,8},{8,4},{12,16},{16,12},{20,24},{24,20},{5,9},{9,5},{13,17},{1... | collective-permute-start | bytes 1572872 | tf_op jit(solution)/shard_map/ppermute | solution.py:489
  9.2 0.5 %turned.1 = (bf16[2048,128]{1,0:T(8,128)(2,1)S(1)}, bf16[256,128]{1,0:T(8,128)(2,1)S(1)}) custom-call(bf16[1,128,2048]{2,1,0:T(8,128)(2,1)S(1)} %copy-done.1, bf16[256,2048]{1,0:T(8,128)(2,1)S(1)} %copy-done.2), custom_call_target="tpu_custom_call" | custom-call | flops 1 | bytes 1 | tf_op jit(solution)/shard_map/turned/pallas_call | solution.py:49
  9.8 0.6 %limits.1.limit_ref = s32[16,256]{1,0:T(8,128)S(1)} custom-call(s32[4,8]{1,0:T(4,128)S(1)} %bitcast.1, s32[1,8]{1,0:T(1,128)S(1)} %copy-done.6), custom_call_target="tpu_custom_call" | custom-call | flops 1 | bytes 1 | tf_op jit(solution)/shard_map/limits/pallas_call | solution.py:49
  10.4 3.5 %collective-permute-start.8 = (bf16[128,2816]{1,0:T(8,128)(2,1)S(1)}, bf16[128,2816]{1,0:T(8,128)(2,1)S(1)}, u32[]{:S(2)}, u32[]{:S(2)}) collective-permute-start(bf16[128,2816]{1,0:T(8,128)(2,1)S(1)} %hand_far.1), channel_id=1, source_target_pairs={{4,8},{8,4},{12,16},{16,12},{20,24},{24,20},{5,9},{9,5},{13,17},{1... | collective-permute-start | bytes 2162696 | tf_op jit(solution)/shard_map/ppermute | solution.py:493
  14.0 2.3 %collective-permute-done.2.refs_2_.kv_ref = bf16[128,2048]{1,0:T(8,128)(2,1)S(1)} collective-permute-done((bf16[128,2048]{1,0:T(8,128)(2,1)S(1)}, bf16[128,2048]{1,0:T(8,128)(2,1)S(1)}, u32[]{:S(2)}, u32[]{:S(2)}) %collective-permute-start.2) | collective-permute-done | bytes 524320 | tf_op jit(solution)/shard_map/ppermute | solution.py:489
  16.3 0.8 %heads_own.1 = (bf16[128,256]{1,0:T(8,128)(2,1)S(1)}, f32[2,128,256]{2,1,0:T(8,128)S(1)}, bf16[2,128,768]{2,1,0:T(8,128)(2,1)S(1)}, bf16[2,128,768]{2,1,0:T(8,128)(2,1)S(1)}) custom-call(bf16[2048,128]{1,0:T(8,128)(2,1)S(1)} %get-tuple-element.49.dy_ref.rows_ref, bf16[1,128,1024]{2,1,0:T(8,128)(2,1)S(1)} %copy-done, s32[16,256]{1,0:T(8,128)S(1)} %limits.1.limit_ref, ...), custom_call_target="tpu_custom_call" | custom-call | flops 1 | bytes 1 | tf_op jit(solution)/shard_map/heads_own/pallas_call | solution.py:49
  17.4 0.5 %collective-permute-start.5 = (bf16[128,2304]{1,0:T(8,128)(2,1)S(1)}, bf16[128,2304]{1,0:T(8,128)(2,1)S(1)}, u32[]{:S(2)}, u32[]{:S(2)}) collective-permute-start(bf16[128,2304]{1,0:T(8,128)(2,1)S(1)} %get-tuple-element.55), channel_id=1, source_target_pairs={{0,4},{4,0},{8,12},{12,8},{16,20},{20,16},{24,28},{28,24},{1,5},{5... | collective-permute-start | bytes 1769480 | tf_op jit(solution)/shard_map/ppermute | solution.py:502
  17.9 0.8 %collective-permute-start.9 = (bf16[128,2048]{1,0:T(8,128)(2,1)S(1)}, bf16[128,2048]{1,0:T(8,128)(2,1)S(1)}, u32[]{:S(2)}, u32[]{:S(2)}) collective-permute-start(bf16[128,2048]{1,0:T(8,128)(2,1)S(1)} %get-tuple-element.71), channel_id=1, source_target_pairs={{0,2},{1,3},{2,0},{3,1},{4,5},{5,4},{6,7},{7,6},{8,10},{9,11},{10,... | collective-permute-start | bytes 1572872 | tf_op jit(solution)/shard_map/ppermute | solution.py:484
  18.7 1.1 %heads_first.1 = (bf16[128,256]{1,0:T(8,128)(2,1)S(1)}, f32[2,128,256]{2,1,0:T(8,128)S(1)}, bf16[2,128,768]{2,1,0:T(8,128)(2,1)S(1)}, bf16[2,128,768]{2,1,0:T(8,128)(2,1)S(1)}) custom-call(bf16[2048,128]{1,0:T(8,128)(2,1)S(1)} %get-tuple-element.49.dy_ref.rows_ref, bf16[1,128,1024]{2,1,0:T(8,128)(2,1)S(1)} %copy-done, s32[16,256]{1,0:T(8,128)S(1)} %limits.1.limit_ref, ...), custom_call_target="tpu_custom_call" | custom-call | flops 1 | bytes 1 | tf_op jit(solution)/shard_map/heads_first/pallas_call | solution.py:49
  19.8 0.4 %collective-permute-done.5.refs_4_.refs_6_ = bf16[128,2304]{1,0:T(8,128)(2,1)S(1)} collective-permute-done((bf16[128,2304]{1,0:T(8,128)(2,1)S(1)}, bf16[128,2304]{1,0:T(8,128)(2,1)S(1)}, u32[]{:S(2)}, u32[]{:S(2)}) %collective-permute-start.5) | collective-permute-done | bytes 589856 | tf_op jit(solution)/shard_map/ppermute | solution.py:502
  20.2 1.1 %heads_second.1 = (bf16[128,256]{1,0:T(8,128)(2,1)S(1)}, f32[2,128,256]{2,1,0:T(8,128)S(1)}, bf16[2,128,768]{2,1,0:T(8,128)(2,1)S(1)}, bf16[2,128,768]{2,1,0:T(8,128)(2,1)S(1)}) custom-call(bf16[2048,128]{1,0:T(8,128)(2,1)S(1)} %get-tuple-element.49.dy_ref.rows_ref, bf16[1,128,1024]{2,1,0:T(8,128)(2,1)S(1)} %copy-done, s32[16,256]{1,0:T(8,128)S(1)} %limits.1.limit_ref, ...), custom_call_target="tpu_custom_call" | custom-call | flops 1 | bytes 1 | tf_op jit(solution)/shard_map/heads_second/pallas_call | solution.py:49
  21.3 3.7 %collective-permute-start.6 = (bf16[2,128,768]{2,1,0:T(8,128)(2,1)S(1)}, bf16[2,128,768]{2,1,0:T(8,128)(2,1)S(1)}, u32[]{:S(2)}, u32[]{:S(2)}) collective-permute-start(bf16[2,128,768]{2,1,0:T(8,128)(2,1)S(1)} %get-tuple-element.63), channel_id=1, source_target_pairs={{4,8},{8,4},{12,16},{16,12},{20,24},{24,20},{5,9},{9,5},{13,17},{1... | collective-permute-start | bytes 1179656 | tf_op jit(solution)/shard_map/ppermute | solution.py:529
  25.1 0.7 %settle.1.refs_9_ = bf16[1,128,1024]{2,1,0:T(8,128)(2,1)} custom-call(bf16[128,256]{1,0:T(8,128)(2,1)S(1)} %get-tuple-element.72.refs_0_, bf16[128,256]{1,0:T(8,128)(2,1)S(1)} %get-tuple-element.73.refs_1_, bf16[128,256]{1,0:T(8,128)(2,1)S(1)} %get-tuple-element.74.refs_2_), custom_call_target="tpu_custom_call" | custom-call | flops 1 | bytes 1 | tf_op jit(solution)/shard_map/settle/pallas_call | solution.py:49
  25.8 0.4 %collective-permute-done.9.refs_7_.x_ref = bf16[128,2048]{1,0:T(8,128)(2,1)S(1)} collective-permute-done((bf16[128,2048]{1,0:T(8,128)(2,1)S(1)}, bf16[128,2048]{1,0:T(8,128)(2,1)S(1)}, u32[]{:S(2)}, u32[]{:S(2)}) %collective-permute-start.9) | collective-permute-done | bytes 524320 | tf_op jit(solution)/shard_map/ppermute | solution.py:484
  26.2 1.0 %collective-permute-start.10 = (bf16[64,2048]{1,0:T(8,128)(2,1)S(1)}, bf16[64,2048]{1,0:T(8,128)(2,1)S(1)}, u32[]{:S(2)}, u32[]{:S(2)}) collective-permute-start(bf16[64,2048]{1,0:T(8,128)(2,1)S(1)} %get-tuple-element.83), channel_id=1, source_target_pairs={{0,4},{4,0},{8,12},{12,8},{16,20},{20,16},{24,28},{28,24},{1,5},{5... | collective-permute-start | bytes 786440 | tf_op jit(solution)/shard_map/ppermute | solution.py:530
  27.3 0.7 %probs_last.1 = (f32[3,384,256]{2,1,0:T(8,128)S(1)}, bf16[2048,256]{1,0:T(8,128)(2,1)S(1)}) custom-call(bf16[1,128,1024]{2,1,0:T(8,128)(2,1)S(1)} %copy-done, s32[16,256]{1,0:T(8,128)S(1)} %limits.1.limit_ref, bf16[128,2048]{1,0:T(8,128)(2,1)S(1)} %join.1.refs_0_, bf16[128,2048]{1,0:T(8,128)(2,1)S(1)} %collective-permute-done.1.refs_1_.refs_2_, ...), custom_call_target="tpu_custom_call" | custom-call | flops 1 | bytes 1 | tf_op jit(solution)/shard_map/probs_last/pallas_call | solution.py:49
  28.1 1.0 %heads_last.1 = (bf16[128,128]{1,0:T(8,128)(2,1)S(1)}, bf16[128,128]{1,0:T(8,128)(2,1)S(1)}, bf16[128,128]{1,0:T(8,128)(2,1)S(1)}) custom-call(bf16[2048,128]{1,0:T(8,128)(2,1)S(1)} %get-tuple-element.49.dy_ref.rows_ref, bf16[2048,256]{1,0:T(8,128)(2,1)S(1)} %get-tuple-element.69.far_rows_ref, bf16[1,128,1024]{2,1,0:T(8,128)(2,1)S(1)} %copy-done, ...), custom_call_target="tpu_custom_call" | custom-call | flops 1 | bytes 1 | tf_op jit(solution)/shard_map/heads_last/pallas_call | solution.py:49
  29.1 1.0 %heads_end.1 = (bf16[128,128]{1,0:T(8,128)(2,1)S(1)}, bf16[128,128]{1,0:T(8,128)(2,1)S(1)}, bf16[128,128]{1,0:T(8,128)(2,1)S(1)}) custom-call(bf16[2048,128]{1,0:T(8,128)(2,1)S(1)} %get-tuple-element.49.dy_ref.rows_ref, bf16[2048,256]{1,0:T(8,128)(2,1)S(1)} %get-tuple-element.69.far_rows_ref, bf16[1,128,1024]{2,1,0:T(8,128)(2,1)S(1)} %copy-done, ...), custom_call_target="tpu_custom_call" | custom-call | flops 1 | bytes 1 | tf_op jit(solution)/shard_map/heads_end/pallas_call | solution.py:49
  30.1 0.3 %collective-permute-done.6.far = bf16[2,128,768]{2,1,0:T(8,128)(2,1)S(1)} collective-permute-done((bf16[2,128,768]{2,1,0:T(8,128)(2,1)S(1)}, bf16[2,128,768]{2,1,0:T(8,128)(2,1)S(1)}, u32[]{:S(2)}, u32[]{:S(2)}) %collective-permute-start.6) | collective-permute-done | bytes 393248 | tf_op jit(solution)/shard_map/ppermute | solution.py:529
  30.4 0.9 %finish.1 = (bf16[1,128,1024]{2,1,0:T(8,128)(2,1)}, bf16[1,128,1024]{2,1,0:T(8,128)(2,1)}, bf16[1,128,1024]{2,1,0:T(8,128)(2,1)}) custom-call(bf16[2,128,768]{2,1,0:T(8,128)(2,1)S(1)} %collective-permute-done.6.far, bf16[2,128,768]{2,1,0:T(8,128)(2,1)S(1)} %collective-permute-done.7.near, ...), custom_call_target="tpu_custom_call", output_to_operand_aliasing={{0}: (11, {})} | custom-call | flops 1 | bytes 1 | tf_op jit(solution)/shard_map/finish/pallas_call | solution.py:459
  (28 shorter events, 0.6 us)
Async XLA Ops:
  0.6 8.4 %copy-start = (bf16[1,128,1024]{2,1,0:T(8,128)(2,1)S(1)}, bf16[1,128,1024]{2,1,0:T(8,128)(2,1)}, u32[]{:S(2)}) copy-start(bf16[1,128,1024]{2,1,0:T(8,128)(2,1)} %q_ref.11) | copy-start | bytes 786436
  0.6 8.4 %copy-start.1 = (bf16[1,128,2048]{2,1,0:T(8,128)(2,1)S(1)}, bf16[1,128,2048]{2,1,0:T(8,128)(2,1)}, u32[]{:S(2)}) copy-start(bf16[1,128,2048]{2,1,0:T(8,128)(2,1)} %refs_0_.1) | copy-start | bytes 1572868
  0.7 16.5 %collective-permute-start = (bf16[256,2048]{1,0:T(8,128)(2,1)}, bf16[256,2048]{1,0:T(8,128)(2,1)S(1)}, u32[]{:S(2)}, u32[]{:S(2)}) collective-permute-start(bf16[256,2048]{1,0:T(8,128)(2,1)} %w_ref.1), channel_id=1, source_target_pairs={{0,1},{1,0},{2,3},{3,2},{4,6},{5,7},{6,4},{7,5},{8,9},{9,8},{10,11... | collective-permute-start | bytes 3145736 | tf_op jit(solution)/shard_map/ppermute | solution.py:484
  2.8 0.9 %copy-start.3 = (bf16[1,128,1024]{2,1,0:T(8,128)(2,1)S(1)}, bf16[1,128,1024]{2,1,0:T(8,128)(2,1)}, u32[]{:S(2)}) copy-start(bf16[1,128,1024]{2,1,0:T(8,128)(2,1)} %k_ref.1) | copy-start | bytes 786436
  3.7 0.9 %copy-start.4 = (bf16[1,128,1024]{2,1,0:T(8,128)(2,1)S(1)}, bf16[1,128,1024]{2,1,0:T(8,128)(2,1)}, u32[]{:S(2)}) copy-start(bf16[1,128,1024]{2,1,0:T(8,128)(2,1)} %v_ref.1) | copy-start | bytes 786436
  4.7 4.5 %copy-start.2 = (bf16[256,2048]{1,0:T(8,128)(2,1)S(1)}, bf16[256,2048]{1,0:T(8,128)(2,1)}, u32[]{:S(2)}) copy-start(bf16[256,2048]{1,0:T(8,128)(2,1)} %w_ref.1) | copy-start | bytes 3145732
  4.7 4.2 %collective-permute-start.1 = (bf16[128,2048]{1,0:T(8,128)(2,1)S(1)}, bf16[128,2048]{1,0:T(8,128)(2,1)S(1)}, u32[]{:S(2)}, u32[]{:S(2)}) collective-permute-start(bf16[128,2048]{1,0:T(8,128)(2,1)S(1)} %join.1.refs_0_), channel_id=1, source_target_pairs={{0,4},{4,0},{8,12},{12,8},{16,20},{20,16},{24,28},{28,24},{1,5},{5... | collective-permute-start | bytes 1572872 | tf_op jit(solution)/shard_map/ppermute | solution.py:489
  5.7 10.6 %collective-permute-start.2 = (bf16[128,2048]{1,0:T(8,128)(2,1)S(1)}, bf16[128,2048]{1,0:T(8,128)(2,1)S(1)}, u32[]{:S(2)}, u32[]{:S(2)}) collective-permute-start(bf16[128,2048]{1,0:T(8,128)(2,1)S(1)} %join.1.refs_0_), channel_id=1, source_target_pairs={{4,8},{8,4},{12,16},{16,12},{20,24},{24,20},{5,9},{9,5},{13,17},{1... | collective-permute-start | bytes 1572872 | tf_op jit(solution)/shard_map/ppermute | solution.py:489
  9.1 0.7 %copy-start.5 = (s32[8,4]{0,1:T(4,128)S(1)}, s32[8,4]{0,1:T(4,128)}, u32[]{:S(2)}) copy-start(s32[8,4]{0,1:T(4,128)} %param.12) | copy-start | bytes 388
  9.1 0.7 %copy-start.6 = (s32[1,8]{1,0:T(1,128)S(1)}, s32[1,8]{1,0:T(1,128)}, u32[]{:S(2)}) copy-start(s32[1,8]{1,0:T(1,128)} %val_ref.1) | copy-start | bytes 100
  9.1 10.7 %collective-permute-start.3 = (bf16[128,2816]{1,0:T(8,128)(2,1)S(1)}, bf16[128,2816]{1,0:T(8,128)(2,1)S(1)}, u32[]{:S(2)}, u32[]{:S(2)}) collective-permute-start(bf16[128,2816]{1,0:T(8,128)(2,1)S(1)} %hand_far.1), channel_id=1, source_target_pairs={{0,4},{4,0},{8,12},{12,8},{16,20},{20,16},{24,28},{28,24},{1,5},{5... | collective-permute-start | bytes 2162696 | tf_op jit(solution)/shard_map/ppermute | solution.py:493
  10.4 15.4 %collective-permute-start.8 = (bf16[128,2816]{1,0:T(8,128)(2,1)S(1)}, bf16[128,2816]{1,0:T(8,128)(2,1)S(1)}, u32[]{:S(2)}, u32[]{:S(2)}) collective-permute-start(bf16[128,2816]{1,0:T(8,128)(2,1)S(1)} %hand_far.1), channel_id=1, source_target_pairs={{4,8},{8,4},{12,16},{16,12},{20,24},{24,20},{5,9},{9,5},{13,17},{1... | collective-permute-start | bytes 2162696 | tf_op jit(solution)/shard_map/ppermute | solution.py:493
  17.3 2.5 %collective-permute-start.4 = (bf16[128,2304]{1,0:T(8,128)(2,1)S(1)}, bf16[128,2304]{1,0:T(8,128)(2,1)S(1)}, u32[]{:S(2)}, u32[]{:S(2)}) collective-permute-start(bf16[128,2304]{1,0:T(8,128)(2,1)S(1)} %get-tuple-element.54), channel_id=1, source_target_pairs={{0,4},{4,0},{8,12},{12,8},{16,20},{20,16},{24,28},{28,24},{1,5},{5... | collective-permute-start | bytes 1769480 | tf_op jit(solution)/shard_map/ppermute | solution.py:502
  17.4 2.8 %collective-permute-start.5 = (bf16[128,2304]{1,0:T(8,128)(2,1)S(1)}, bf16[128,2304]{1,0:T(8,128)(2,1)S(1)}, u32[]{:S(2)}, u32[]{:S(2)}) collective-permute-start(bf16[128,2304]{1,0:T(8,128)(2,1)S(1)} %get-tuple-element.55), channel_id=1, source_target_pairs={{0,4},{4,0},{8,12},{12,8},{16,20},{20,16},{24,28},{28,24},{1,5},{5... | collective-permute-start | bytes 1769480 | tf_op jit(solution)/shard_map/ppermute | solution.py:502
  17.9 8.3 %collective-permute-start.9 = (bf16[128,2048]{1,0:T(8,128)(2,1)S(1)}, bf16[128,2048]{1,0:T(8,128)(2,1)S(1)}, u32[]{:S(2)}, u32[]{:S(2)}) collective-permute-start(bf16[128,2048]{1,0:T(8,128)(2,1)S(1)} %get-tuple-element.71), channel_id=1, source_target_pairs={{0,2},{1,3},{2,0},{3,1},{4,5},{5,4},{6,7},{7,6},{8,10},{9,11},{10,... | collective-permute-start | bytes 1572872 | tf_op jit(solution)/shard_map/ppermute | solution.py:484
  21.3 9.1 %collective-permute-start.6 = (bf16[2,128,768]{2,1,0:T(8,128)(2,1)S(1)}, bf16[2,128,768]{2,1,0:T(8,128)(2,1)S(1)}, u32[]{:S(2)}, u32[]{:S(2)}) collective-permute-start(bf16[2,128,768]{2,1,0:T(8,128)(2,1)S(1)} %get-tuple-element.63), channel_id=1, source_target_pairs={{4,8},{8,4},{12,16},{16,12},{20,24},{24,20},{5,9},{9,5},{13,17},{1... | collective-permute-start | bytes 1179656 | tf_op jit(solution)/shard_map/ppermute | solution.py:529
  25.0 5.4 %collective-permute-start.7 = (bf16[2,128,768]{2,1,0:T(8,128)(2,1)S(1)}, bf16[2,128,768]{2,1,0:T(8,128)(2,1)S(1)}, u32[]{:S(2)}, u32[]{:S(2)}) collective-permute-start(bf16[2,128,768]{2,1,0:T(8,128)(2,1)S(1)} %get-tuple-element.64), channel_id=1, source_target_pairs={{0,4},{4,0},{8,12},{12,8},{16,20},{20,16},{24,28},{28,24},{1,5},{5... | collective-permute-start | bytes 1179656 | tf_op jit(solution)/shard_map/ppermute | solution.py:529
  26.2 2.8 %collective-permute-start.10 = (bf16[64,2048]{1,0:T(8,128)(2,1)S(1)}, bf16[64,2048]{1,0:T(8,128)(2,1)S(1)}, u32[]{:S(2)}, u32[]{:S(2)}) collective-permute-start(bf16[64,2048]{1,0:T(8,128)(2,1)S(1)} %get-tuple-element.83), channel_id=1, source_target_pairs={{0,4},{4,0},{8,12},{12,8},{16,20},{20,16},{24,28},{28,24},{1,5},{5... | collective-permute-start | bytes 786440 | tf_op jit(solution)/shard_map/ppermute | solution.py:530
  27.2 1.8 %collective-permute-start.11 = (bf16[64,2048]{1,0:T(8,128)(2,1)S(1)}, bf16[64,2048]{1,0:T(8,128)(2,1)S(1)}, u32[]{:S(2)}, u32[]{:S(2)}) collective-permute-start(bf16[64,2048]{1,0:T(8,128)(2,1)S(1)} %get-tuple-element.84), channel_id=1, source_target_pairs={{0,4},{4,0},{8,12},{12,8},{16,20},{20,16},{24,28},{28,24},{1,5},{5... | collective-permute-start | bytes 786440 | tf_op jit(solution)/shard_map/ppermute | solution.py:530
